TPU v7x, 128 devices: a whole 4x4x4 slice. The times are simulated.
128 devices in a mesh: rep: 4 (over z_hi, core), fsdp: 32 (over z_lo, y, x).
Axes of the slice: x: 4, y: 4, z: 4 (z_hi: 2, z_lo: 2; z = z_hi * 2 + z_lo), core: 2. Of those that a mesh axis runs over, the one named last changes fastest.
Arguments:
- params: float32 [8192, 1024], P('fsdp'), may hold values from -6 to 6
- momentum: float32 [8192, 1024], P('fsdp'), may hold values from -6 to 6
- local_params: bfloat16 [4, 8192, 1024], P('rep', 'fsdp'), may hold values from -6 to 6
- exps: int32 [4], replicated, may hold values from 6 to 9
- inputs: bfloat16 [131072, 8192], P(('rep', 'fsdp')), may hold values from -24 to 24
- key_cotangent: bfloat16 [131072, 1024], P(('rep', 'fsdp')), may hold values from -0.03125 to 0.03125
Outputs:
- new_params: float32 [8192, 1024], P('fsdp')
- new_momentum: float32 [8192, 1024], P('fsdp')
- kv_grad: float32 [4, 8192, 1024], P('rep', 'fsdp')
All inputs are finite; a program needn't handle non-finite values.
Results may differ from a plain program's by a relative error of at most 0.0075.
Values sent between devices are 32-bit elements; how exact they have to be, the bound alone decides.
No kernel may reach another device: no remote copies, remote signals or barrier semaphores. Data moves between devices by JAX's collectives and lax.ppermute only.
A program may use at most 128 MiB of HBM per device.

v0:
```python
import jax
import jax.numpy as jnp
from jax import lax
from jax.sharding import PartitionSpec as P


def nesterov(weights, moment, outer_grad):
    fresh = 0.9 * moment + outer_grad
    return (weights - 0.7 * (outer_grad + 0.9 * fresh), fresh)


def local(params, momentum, local_params, exps, inputs, key_cotangent):
    groups = lax.axis_size("rep")
    group = lax.axis_index("rep")
    picked = jnp.sum(jnp.where(jnp.arange(groups) == group, exps, 0))
    scale_up = jnp.exp2(picked.astype(jnp.float32))
    delta = params - local_params[0].astype(jnp.float32)
    coded = jnp.clip(delta * scale_up, -448.0, 448.0).astype(jnp.bfloat16)
    decoded = coded.astype(jnp.float32) / scale_up
    total = lax.psum(decoded, "rep")
    new_params, new_momentum = nesterov(params, momentum, total / groups)
    product = lax.dot_general(
        inputs, key_cotangent, (((0,), (0,)), ((), ())), preferred_element_type=jnp.float32
    )
    kv_grad = lax.psum_scatter(product, "fsdp", scatter_dimension=0, tiled=True)
    return (new_params, new_momentum, kv_grad[None])


def solution(mesh):
    in_specs = (
        P("fsdp", None),
        P("fsdp", None),
        P("rep", "fsdp", None),
        P(),
        P(("rep", "fsdp"), None),
        P(("rep", "fsdp"), None),
    )
    out_specs = (P("fsdp", None), P("fsdp", None), P("rep", "fsdp", None))
    return jax.shard_map(local, mesh=mesh, in_specs=in_specs, out_specs=out_specs, check_vma=False)
```

profile of v0, /device:TPU:0, one launch (start us, length us, event | category | flops | bytes accessed | tf_op | source)
XLA Modules:
  0.0 419.8 jit_solution(15430865065460330300)
XLA Ops:
  8.0 0.0 copy-start
  8.0 0.0 all-reduce.2.cloned.1.call-start
  8.1 1.4 fusion.3
  10.2 2.5 convert_divide_fusion
  12.7 0.0 all-reduce.2.cloned.1.call-update
  12.8 0.0 reduce-scatter.2.cloned.1.call-start
  12.8 0.0 copy-done
  12.8 27.1 %fusion.4 = f32[8192,1024]{1,0:T(8,128)} fusion(bf16[1024,8192]{1,0:T(8,128)(2,1)} %param.10, bf16[1024,1024]{1,0:T(8,128)(2,1)S(1)} %copy-done), kind=kOutput, calls=%fused_computation.9 | convolution fusion | flops 17179869184 | bytes 52428800 | tf_op jit(solution)/shard_map/dot_general | solution.py:22
  39.9 0.0 copy-start.1
  39.9 0.0 reduce-scatter.2.cloned.1.call-update
  40.0 369.0 %all-reduce.2.cloned.1.call-done = f32[256,1024]{1,0:T(8,128)} async-done(((f32[256,1024]{1,0:T(8,128)}), f32[256,1024]{1,0:T(8,128)}) %all-reduce.2.cloned.1.call-update) | async-done | bytes 1048592 | tf_op jit(solution)/shard_map/psum | solution.py:20
  409.0 0.0 copy-done.1
  409.0 3.3 multiply_subtract_fusion
  412.3 0.0 reduce-scatter.2.cloned.1.call-done
Async XLA Ops:
  8.0 4.8 %copy-start = (bf16[1024,1024]{1,0:T(8,128)(2,1)S(1)}, bf16[1024,1024]{1,0:T(8,128)(2,1)}, u32[]{:S(2)}) copy-start(bf16[1024,1024]{1,0:T(8,128)(2,1)} %param.11) | copy-start | bytes 6291460
  8.0 401.0 %all-reduce.2.cloned.1.call-start = ((), (), s32[]{:S(2)}) async-start(), calls=%async_computation.1 | async-start | bytes 2097152 | tf_op jit(solution)/shard_map/psum | solution.py:20
  12.8 399.6 %reduce-scatter.2.cloned.1.call-start = ((), (), s32[]{:S(2)}) async-start(), calls=%async_computation.2 | async-start | bytes 34603008 | tf_op jit(solution)/shard_map/reduce_scatter | solution.py:25
  39.9 369.1 %copy-start.1 = (f32[256,1024]{1,0:T(8,128)S(1)}, f32[256,1024]{1,0:T(8,128)}, u32[]{:S(2)}) copy-start(f32[256,1024]{1,0:T(8,128)} %param.6) | copy-start | bytes 3145732
Sparse Core Ops, SparseCore 0:
  12.9 396.0 all-reduce.1
Sparse Core Ops, SparseCore 1:
  40.1 367.0 reduce-scatter.1
where the time goes:
time: 421 us; the launch traced here: 420 us
  waiting for transfers between devices  369 us (88%)
  matrix products  27.1 us (6%)
  between operations  16.2 us (4%)
  other arithmetic  7.28 us (2%)
    psum x1, waiting for transfers between devices, local(): total = lax.psum(decoded, 'rep')  369 us
    dot_general x1, matrix products, local(): lax.dot_general(inputs, key_cotangent, (((0,), (0,)), ((), ())), preferre...  27.1 us
  transfers between devices with their start and end apart: 2, of which 1 were waited for; matrix products, arithmetic and copies ran while one was open for 7% of the time, Pallas kernels for 0%

commit v1 on v0

v1 whole, which is shorter than its diff:
```python
import jax
import jax.numpy as jnp
from jax import lax
from jax.experimental import pallas as pl
from jax.experimental.pallas import tpu as pltpu
from jax.sharding import PartitionSpec as P

AXES = {"z": (16, 2), "y": (4, 4), "x": (1, 4)}

CHUNKS = (
    (176, "xyz", 1),
    (176, "xyz", -1),
    (176, "yxz", 1),
    (176, "yxz", -1),
    (80, "zxy", 1),
    (80, "zxy", -1),
    (80, "zyx", 1),
    (80, "zyx", -1),
)


def shift(axis, step):
    stride, size = AXES[axis]
    pairs = []
    for source in range(32):
        place = source // stride % size
        pairs.append((source, source + ((place + step) % size - place) * stride))
    return pairs


def send(array, axis, step):
    return lax.ppermute(array, "fsdp", shift(axis, step))


def blocks_of(fixed, free):
    out = []
    for dz in range(2) if "z" in free else [fixed["z"]]:
        for dy in range(4) if "y" in free else [fixed["y"]]:
            for dx in range(4) if "x" in free else [fixed["x"]]:
                out.append((dz, dy, dx))
    return out


class Piece:
    def __init__(self, chunk, blocks, terms):
        self.chunk, self.blocks, self.terms = chunk, blocks, terms


def multiply(inputs, keys, ids, segments):
    width = 256
    depth = inputs.shape[0]
    total = sum(len(seg[0].blocks) for seg in segments)
    rows, operands, in_specs, out_specs, out_shape, plan = [], [], [], [], [], []
    order = [b for seg in segments for b in seg[0].blocks]
    rows.append(ids(order))

    def spec(rows_n, row):
        return pl.BlockSpec((1, rows_n, width), lambda i, table, row=row: (table[row, i], 0, 0))

    start = 0
    flops = 0
    moved = total * depth * width * 2
    for seg in segments:
        count = len(seg[0].blocks)
        for piece in seg:
            key = keys[piece.chunk]
            height = key.shape[0]
            entry = [start, count, len(operands), len(piece.terms)]
            operands.append(key)
            in_specs.append(pl.BlockSpec((height, depth), lambda i, table: (0, 0)))
            for array, places in piece.terms:
                row = [places[piece.blocks[min(max(i - start, 0), count - 1)]] for i in range(total)]
                rows.append(jnp.array(row, jnp.int32))
                operands.append(array)
                in_specs.append(spec(height, len(rows) - 1))
            rows.append(jnp.array([min(max(i - start, 0), count - 1) for i in range(total)], jnp.int32))
            out_specs.append(spec(height, len(rows) - 1))
            out_shape.append(jax.ShapeDtypeStruct((count, height, width), jnp.float32))
            plan.append(entry)
            flops += 2 * count * height * width * depth
            moved += (1 + len(piece.terms)) * count * height * width * 4 + height * depth * 2
        start += count
    n_in = len(operands)

    def body(table, x_ref, *refs):
        ins, outs = refs[:n_in], refs[n_in:]
        step = pl.program_id(0)
        for (first, count, at, terms), out in zip(plan, outs):

            @pl.when((step >= first) & (step < first + count))
            def _(at=at, terms=terms, out=out):
                value = jnp.dot(ins[at][...], x_ref[...], preferred_element_type=jnp.float32)
                for term in range(terms):
                    value = value + ins[at + 1 + term][0]
                out[0] = value

    return pl.pallas_call(
        body,
        grid_spec=pltpu.PrefetchScalarGridSpec(
            num_scalar_prefetch=1,
            grid=(total,),
            in_specs=[pl.BlockSpec((depth, width), lambda i, table: (0, table[0, i]))] + in_specs,
            out_specs=out_specs,
        ),
        out_shape=out_shape,
        compiler_params=pltpu.CompilerParams(
            dimension_semantics=("arbitrary",), vmem_limit_bytes=40 * 1024 * 1024
        ),
        cost_estimate=pl.CostEstimate(flops=flops, bytes_accessed=moved, transcendentals=0),
    )(jnp.stack(rows), inputs, *operands)


def gradient(inputs, cotangent):
    me = lax.axis_index("fsdp")
    mine = (me // 16, me // 4 % 4, me % 4)

    def ids(order):
        at = jnp.array(order, jnp.int32)
        return (
            16 * ((mine[0] + at[:, 0]) % 2) + 4 * ((mine[1] + at[:, 1]) % 4) + (mine[2] + at[:, 2]) % 4
        ).astype(jnp.int32)

    keys, low = [], 0
    for height, _, _ in CHUNKS:
        keys.append(cotangent[:, low : low + height].T)
        low += height

    arrived = [[] for _ in CHUNKS]

    def piece(chunk, blocks):
        terms = []
        for array, places in arrived[chunk]:
            if all(b in places for b in blocks):
                terms.append((array, places))
            else:
                assert not any(b in places for b in blocks)
        return Piece(chunk, blocks, terms)

    def run(segments):
        return multiply(inputs, keys, ids, segments)

    def land(chunk, array, blocks, axis, step):
        at = "zyx".index(axis)
        places = {}
        for n, b in enumerate(blocks):
            moved = list(b)
            moved[at] = (moved[at] - step) % AXES[axis][1]
            places[tuple(moved)] = n
        arrived[chunk].append((send(array, axis, step), places))

    def selected(chunk, stage, offset):
        order = CHUNKS[chunk][1]
        fixed = {a: 0 for a in order[:stage]}
        fixed[order[stage]] = offset
        return blocks_of(fixed, order[stage + 1 :])

    def far(pair, stage):
        axis = CHUNKS[pair[0]][1][stage]
        if axis == "z":
            todo = [(c, 1, 1) for c in pair]
        else:
            todo = [(c, 2, CHUNKS[c][2]) for c in pair]
        blocks = selected(pair[0], stage, todo[0][1])
        for (c, _, step), array in zip(todo, run([[piece(c, blocks) for c in pair]])):
            land(c, array, blocks, axis, step)

    def near(pair, stage, turn):
        axis = CHUNKS[pair[0]][1][stage]
        if axis == "z":
            return
        segments, todo = [], []
        for c in pair:
            step = turn * CHUNKS[c][2]
            blocks = selected(c, stage, step % 4)
            segments.append([piece(c, blocks)])
            todo.append((c, blocks, step))
        for (c, blocks, step), array in zip(todo, run(segments)):
            land(c, array, blocks, axis, step)

    pairs = ((0, 1), (2, 3), (4, 5), (6, 7))
    for stage in range(3):
        for pair in pairs:
            far(pair, stage)
        for turn in (-1, 1):
            for pair in pairs:
                near(pair, stage, turn)
    own = [(0, 0, 0)]
    parts = []
    for pair in pairs:
        parts += run([[piece(c, own) for c in pair]])
    return jnp.concatenate([p[0] for p in parts], axis=0).T


def outer(params, momentum, local_params, exps):
    groups = lax.axis_size("rep")
    group = lax.axis_index("rep")
    picked = jnp.sum(jnp.where(jnp.arange(groups) == group, exps, 0))
    scale_up = jnp.left_shift(1, picked).astype(jnp.float32)
    delta = params - local_params[0].astype(jnp.float32)
    coded = jnp.clip(delta * scale_up, -448.0, 448.0).astype(jnp.bfloat16)
    decoded = coded.astype(jnp.float32) / scale_up
    core = group % 2
    half = decoded.shape[0] // 2
    kept = lax.dynamic_slice_in_dim(decoded, core * half, half, 0)
    given = lax.dynamic_slice_in_dim(decoded, (1 - core) * half, half, 0)
    other_core = [(r, r ^ 1) for r in range(4)]
    other_chip = [(r, r ^ 2) for r in range(4)]
    kept = kept + lax.ppermute(given, "rep", other_core)
    kept = kept + lax.ppermute(kept, "rep", other_chip)
    rest = lax.ppermute(kept, "rep", other_core)
    first = core == 0
    total = jnp.concatenate([jnp.where(first, kept, rest), jnp.where(first, rest, kept)], axis=0)
    outer_grad = total / groups
    fresh = 0.9 * momentum + outer_grad
    return params - 0.7 * (outer_grad + 0.9 * fresh), fresh


def local(params, momentum, local_params, exps, inputs, key_cotangent):
    new_params, new_momentum = outer(params, momentum, local_params, exps)
    kv_grad = gradient(inputs, key_cotangent)
    return (new_params, new_momentum, kv_grad[None])


def solution(mesh):
    in_specs = (
        P("fsdp", None),
        P("fsdp", None),
        P("rep", "fsdp", None),
        P(),
        P(("rep", "fsdp"), None),
        P(("rep", "fsdp"), None),
    )
    out_specs = (P("fsdp", None), P("fsdp", None), P("rep", "fsdp", None))
    return jax.shard_map(local, mesh=mesh, in_specs=in_specs, out_specs=out_specs, check_vma=False)
```

time: 421 us -> 451 us (1.071); the launches traced: 420 us -> 443 us
  waiting for transfers between devices: 369 us -> 97 us
  Pallas kernels: 0 us -> 196 us
  starting transfers between devices: 0.08 us -> 87.4 us
  local copies, waits for them, and re-layouts: 0.01 us -> 48.1 us
  matrix products: 27.1 us -> 0 us
  between operations: 16.2 us -> 2.53 us
  other arithmetic: 7.28 us -> 11.9 us
    psum x1 -> x0, waiting for transfers between devices: 369 us -> none  [local(): total = lax.psum(decoded, 'rep')]
    pallas_call x0 -> x32, Pallas kernels: none -> 196 us  [multiply(): pl.pallas_call(body, grid_spec=pltpu.PrefetchScalarGridSpec(num_scalar_pr...]
    ppermute x0 -> x59, waiting for transfers between devices: none -> 97 us  [the longest x1 57.4 us: outer(): kept = kept + lax.ppermute(kept, 'rep', other_chip)]
    ppermute x0 -> x59, starting transfers between devices: none -> 87.4 us  [the longest x56 83.7 us: send(): return lax.ppermute(array, 'fsdp', shift(axis, step))]
    unnamed x4 -> x204, local copies, waits for them, and re-layouts: 0.01 us -> 38 us
    dot_general x1 -> x0, matrix products: 27.1 us -> none  [local(): lax.dot_general(inputs, key_cotangent, (((0,), (0,)), ((), ())), preferre...]
    add x0 -> x14, other arithmetic: none -> 6.92 us  [the longest x12 3.6 us: ids(): 16 * ((mine[0] + at[:, 0]) % 2) + 4 * ((mine[1] + at[:, 1]) % 4)]
    slice x0 -> x2, local copies, waits for them, and re-layouts: none -> 5.94 us  [gradient(): keys.append(cotangent[:, low:low + height].T)]
  transfers between devices with their start and end apart: 2 -> 59, of which waited for: 1 -> 8; matrix products, arithmetic and copies ran while one was open for 7% -> 6% of each run, Pallas kernels for 0% -> 41%
where the time goes in v1:
time: 451 us; the launch traced here: 443 us
  Pallas kernels  196 us (43%)
  waiting for transfers between devices  97 us (22%)
  starting transfers between devices  87.4 us (19%)
  local copies, waits for them, and re-layouts  48.1 us (11%)
  other arithmetic  11.9 us (3%)
    pallas_call x32, Pallas kernels, multiply(): pl.pallas_call(body, grid_spec=pltpu.PrefetchScalarGridSpec(num_scalar_pr...  196 us
    ppermute x56, starting transfers between devices, send(): return lax.ppermute(array, 'fsdp', shift(axis, step))  83.7 us
    ppermute x1, waiting for transfers between devices, outer(): kept = kept + lax.ppermute(kept, 'rep', other_chip)  57.4 us
    ppermute x56, waiting for transfers between devices, send(): return lax.ppermute(array, 'fsdp', shift(axis, step))  39.6 us
    unnamed x204, local copies, waits for them, and re-layouts  38 us
  transfers between devices with their start and end apart: 59, of which 8 were waited for; matrix products, arithmetic and copies ran while one was open for 6% of the time, Pallas kernels for 41%

profile of v1, /device:TPU:0, one launch (start us, length us, event | category | flops | bytes accessed | tf_op | source)
XLA Modules:
  0.0 442.6 jit_solution(3307916500508444453)
XLA Ops:
  3.1 13.4 %shard_map.2269 = (f32[16,80,256]{2,1,0:T(8,128)}, f32[16,80,256]{2,1,0:T(8,128)}) custom-call(s32[3,16]{1,0:T(4,128)S(1)} %pad_add_fusion.8.table, bf16[1024,8192]{1,0:T(8,128)(2,1)} %x_ref.63, bf16[80,1024]{1,0:T(8,128)(2,1)S(1)} %bitcast.135, bf16[80,1024]{1,0:T(8,128)(2,1)S(1)} %bitcast.143), custom_call_target="tpu_custom_call" | custom-call | flops 1342177280 | bytes 11337728 | tf_op jit(solution)/shard_map/pallas_call | solution.py:97
  19.0 13.4 %shard_map.2261 = (f32[16,80,256]{2,1,0:T(8,128)}, f32[16,80,256]{2,1,0:T(8,128)}) custom-call(s32[3,16]{1,0:T(4,128)S(1)} %pad_add_fusion.8.table, bf16[1024,8192]{1,0:T(8,128)(2,1)} %x_ref.63, bf16[80,1024]{1,0:T(8,128)(2,1)S(1)} %bitcast.151, bf16[80,1024]{1,0:T(8,128)(2,1)S(1)} %bitcast.159), custom_call_target="tpu_custom_call" | custom-call | flops 1342177280 | bytes 11337728 | tf_op jit(solution)/shard_map/pallas_call | solution.py:97
  39.0 3.9 fusion.84
  46.1 8.1 %shard_map.2254 = (f32[8,176,256]{2,1,0:T(8,128)}, f32[8,176,256]{2,1,0:T(8,128)}) custom-call(s32[3,8]{1,0:T(4,128)S(1)} %get-tuple-element.184.table, bf16[1024,8192]{1,0:T(8,128)(2,1)} %x_ref.63, bf16[176,1024]{1,0:T(8,128)(2,1)S(1)} %bitcast.103, bf16[176,1024]{1,0:T(8,128)(2,1)S(1)} %bitcast.111), custom_call_target="tpu_custom_call" | custom-call | flops 1476395008 | bytes 7798784 | tf_op jit(solution)/shard_map/pallas_call | solution.py:97
  57.2 3.7 collective-permute-start.1
  60.9 57.4 %collective-permute-done.1 = f32[128,1024]{1,0:T(8,128)S(1)} collective-permute-done((f32[128,1024]{1,0:T(8,128)S(1)}, f32[128,1024]{1,0:T(8,128)S(1)}, u32[]{:S(2)}, u32[]{:S(2)}) %collective-permute-start.1) | collective-permute-done | bytes 524320 | tf_op jit(solution)/shard_map/ppermute | solution.py:209
  122.1 13.2 %shard_map.2253 = (f32[8,176,256]{2,1,0:T(8,128)}, f32[8,176,256]{2,1,0:T(8,128)}) custom-call(s32[3,16]{1,0:T(4,128)S(1)} %get-tuple-element.170.table, bf16[1024,8192]{1,0:T(8,128)(2,1)} %x_ref.63, bf16[176,1024]{1,0:T(8,128)(2,1)S(1)} %bitcast.104, bf16[176,1024]{1,0:T(8,128)(2,1)S(1)} %bitcast.112), custom_call_target="tpu_custom_call" | custom-call | flops 1476395008 | bytes 11993088 | tf_op jit(solution)/shard_map/pallas_call | solution.py:97
  143.3 8.1 %shard_map.2246 = (f32[8,176,256]{2,1,0:T(8,128)}, f32[8,176,256]{2,1,0:T(8,128)}) custom-call(s32[3,8]{1,0:T(4,128)S(1)} %get-tuple-element.185.table, bf16[1024,8192]{1,0:T(8,128)(2,1)} %x_ref.63, bf16[176,1024]{1,0:T(8,128)(2,1)S(1)} %bitcast.119, bf16[176,1024]{1,0:T(8,128)(2,1)S(1)} %bitcast.127), custom_call_target="tpu_custom_call" | custom-call | flops 1476395008 | bytes 7798784 | tf_op jit(solution)/shard_map/pallas_call | solution.py:97
  154.6 13.2 %shard_map.2245 = (f32[8,176,256]{2,1,0:T(8,128)}, f32[8,176,256]{2,1,0:T(8,128)}) custom-call(s32[3,16]{1,0:T(4,128)S(1)} %get-tuple-element.171.table, bf16[1024,8192]{1,0:T(8,128)(2,1)} %x_ref.63, bf16[176,1024]{1,0:T(8,128)(2,1)S(1)} %bitcast.120, bf16[176,1024]{1,0:T(8,128)(2,1)S(1)} %bitcast.128), custom_call_target="tpu_custom_call" | custom-call | flops 1476395008 | bytes 11993088 | tf_op jit(solution)/shard_map/pallas_call | solution.py:97
  169.5 13.8 %collective-permute-done.17.refs_1_ = f32[8,176,256]{2,1,0:T(8,128)} collective-permute-done((f32[8,176,256]{2,1,0:T(8,128)}, f32[8,176,256]{2,1,0:T(8,128)}, u32[]{:S(2)}, u32[]{:S(2)}) %collective-permute-start.17) | collective-permute-done | bytes 1441824 | tf_op jit(solution)/shard_map/ppermute | solution.py:32
  189.7 4.7 %shard_map.2271 = (f32[4,80,256]{2,1,0:T(8,128)}, f32[4,80,256]{2,1,0:T(8,128)}) custom-call(s32[5,4]{1,0:T(8,128)S(1)} %stack.985.table, bf16[1024,8192]{1,0:T(8,128)(2,1)} %x_ref.63, bf16[80,1024]{1,0:T(8,128)(2,1)S(1)} %bitcast.136, f32[16,80,256]{2,1,0:T(8,128)S(1)} %collective-permute-done.45.refs_1_, bf16[80,1024]{1,0:T(8,128)(2,1)S(1)} %bitcast.144, ...), custom_call_target="tpu_custom_call" | custom-call | flops 335544320 | bytes 3735552 | tf_op jit(solution)/shard_map/pallas_call | solution.py:97
  199.9 7.2 %shard_map.2270 = (f32[4,80,256]{2,1,0:T(8,128)}, f32[4,80,256]{2,1,0:T(8,128)}) custom-call(s32[5,8]{1,0:T(8,128)S(1)} %stack.973.table, bf16[1024,8192]{1,0:T(8,128)(2,1)} %x_ref.63, bf16[80,1024]{1,0:T(8,128)(2,1)S(1)} %bitcast.137, f32[16,80,256]{2,1,0:T(8,128)S(1)} %collective-permute-done.45.refs_1_, bf16[80,1024]{1,0:T(8,128)(2,1)S(1)} %bitcast.145, ...), custom_call_target="tpu_custom_call" | custom-call | flops 335544320 | bytes 5832704 | tf_op jit(solution)/shard_map/pallas_call | solution.py:97
  207.1 8.3 %collective-permute-done.3.refs_1_ = f32[8,176,256]{2,1,0:T(8,128)} collective-permute-done((f32[8,176,256]{2,1,0:T(8,128)}, f32[8,176,256]{2,1,0:T(8,128)}, u32[]{:S(2)}, u32[]{:S(2)}) %collective-permute-start.3) | collective-permute-done | bytes 1441824 | tf_op jit(solution)/shard_map/ppermute | solution.py:32
  217.6 4.7 %shard_map.2263 = (f32[4,80,256]{2,1,0:T(8,128)}, f32[4,80,256]{2,1,0:T(8,128)}) custom-call(s32[5,4]{1,0:T(8,128)S(1)} %stack.921.table, bf16[1024,8192]{1,0:T(8,128)(2,1)} %x_ref.63, bf16[80,1024]{1,0:T(8,128)(2,1)S(1)} %bitcast.152, f32[16,80,256]{2,1,0:T(8,128)S(1)} %collective-permute-done.31.refs_1_, bf16[80,1024]{1,0:T(8,128)(2,1)S(1)} %bitcast.160, ...), custom_call_target="tpu_custom_call" | custom-call | flops 335544320 | bytes 3735552 | tf_op jit(solution)/shard_map/pallas_call | solution.py:97
  225.8 7.1 %shard_map.2262 = (f32[4,80,256]{2,1,0:T(8,128)}, f32[4,80,256]{2,1,0:T(8,128)S(1)}) custom-call(s32[5,8]{1,0:T(8,128)S(1)} %stack.909.table, bf16[1024,8192]{1,0:T(8,128)(2,1)} %x_ref.63, bf16[80,1024]{1,0:T(8,128)(2,1)S(1)} %bitcast.153, f32[16,80,256]{2,1,0:T(8,128)S(1)} %collective-permute-done.31.refs_1_, bf16[80,1024]{1,0:T(8,128)(2,1)S(1)} %bitcast.161, ...), custom_call_target="tpu_custom_call" | custom-call | flops 335544320 | bytes 5832704 | tf_op jit(solution)/shard_map/pallas_call | solution.py:97
  238.5 7.5 %shard_map.2272 = (f32[4,80,256]{2,1,0:T(8,128)}, f32[4,80,256]{2,1,0:T(8,128)}) custom-call(s32[7,8]{1,0:T(8,128)S(1)} %stack.980.table, bf16[1024,8192]{1,0:T(8,128)(2,1)} %x_ref.63, bf16[80,1024]{1,0:T(8,128)(2,1)S(1)} %bitcast.138, f32[16,80,256]{2,1,0:T(8,128)S(1)} %collective-permute-done.45.refs_1_, f32[4,80,256]{2,1,0:T(8,128)} %collective-permute-done.48.refs_2_, ...), custom_call_target="tpu_custom_call" | custom-call | flops 335544320 | bytes 6488064 | tf_op jit(solution)/shard_map/pallas_call | solution.py:97
  249.3 13.9 %shard_map.2247 = (f32[8,176,256]{2,1,0:T(8,128)}, f32[8,176,256]{2,1,0:T(8,128)}) custom-call(s32[5,16]{1,0:T(8,128)S(1)} %stack.789.table, bf16[1024,8192]{1,0:T(8,128)(2,1)} %x_ref.63, bf16[176,1024]{1,0:T(8,128)(2,1)S(1)} %bitcast.121, f32[8,176,256]{2,1,0:T(8,128)} %collective-permute-done.4.refs_1_, bf16[176,1024]{1,0:T(8,128)(2,1)S(1)} %bitcast.129, ...), custom_call_target="tpu_custom_call" | custom-call | flops 1476395008 | bytes 14876672 | tf_op jit(solution)/shard_map/pallas_call | solution.py:97
  268.3 7.3 %shard_map.2264 = (f32[4,80,256]{2,1,0:T(8,128)S(1)}, f32[4,80,256]{2,1,0:T(8,128)}) custom-call(s32[7,8]{1,0:T(8,128)S(1)} %stack.916.table, bf16[1024,8192]{1,0:T(8,128)(2,1)} %x_ref.63, bf16[80,1024]{1,0:T(8,128)(2,1)S(1)} %bitcast.154, f32[16,80,256]{2,1,0:T(8,128)S(1)} %collective-permute-done.31.refs_1_, ...), custom_call_target="tpu_custom_call" | custom-call | flops 335544320 | bytes 6488064 | tf_op jit(solution)/shard_map/pallas_call | solution.py:97
  275.6 13.9 %shard_map.2255 = (f32[8,176,256]{2,1,0:T(8,128)}, f32[8,176,256]{2,1,0:T(8,128)}) custom-call(s32[5,16]{1,0:T(8,128)S(1)} %stack.849.table, bf16[1024,8192]{1,0:T(8,128)(2,1)} %x_ref.63, bf16[176,1024]{1,0:T(8,128)(2,1)S(1)} %bitcast.105, f32[8,176,256]{2,1,0:T(8,128)} %collective-permute-done.18.refs_1_, bf16[176,1024]{1,0:T(8,128)(2,1)S(1)} %bitcast.113, ...), custom_call_target="tpu_custom_call" | custom-call | flops 1476395008 | bytes 14876672 | tf_op jit(solution)/shard_map/pallas_call | solution.py:97
  292.8 7.4 %collective-permute-done.36.refs_3_ = f32[4,80,256]{2,1,0:T(8,128)S(1)} collective-permute-done((f32[4,80,256]{2,1,0:T(8,128)S(1)}, f32[4,80,256]{2,1,0:T(8,128)S(1)}, u32[]{:S(2)}, u32[]{:S(2)}) %collective-permute-start.36) | collective-permute-done | bytes 327712 | tf_op jit(solution)/shard_map/ppermute | solution.py:32
  308.3 6.0 %collective-permute-done.54.refs_4_ = f32[1,80,256]{2,1,0:T(8,128)} collective-permute-done((f32[1,80,256]{2,1,0:T(8,128)}, f32[1,80,256]{2,1,0:T(8,128)}, u32[]{:S(2)}, u32[]{:S(2)}) %collective-permute-start.54) | collective-permute-done | bytes 81952 | tf_op jit(solution)/shard_map/ppermute | solution.py:32
  328.6 3.2 collective-permute-start.41
  339.0 3.6 shard_map.2249
  345.9 9.3 %collective-permute-start.39 = (f32[1,80,256]{2,1,0:T(8,128)}, f32[1,80,256]{2,1,0:T(8,128)}, u32[]{:S(2)}, u32[]{:S(2)}) collective-permute-start(f32[1,80,256]{2,1,0:T(8,128)} %get-tuple-element.107), channel_id=1, source_target_pairs={{0,12},{1,13},{2,14},{3,15},{4,0},{5,1},{6,2},{7,3},{8,4},{9,5},{1... | collective-permute-start | bytes 245768 | tf_op jit(solution)/shard_map/ppermute | solution.py:32
  358.5 3.3 shard_map.2275
  362.3 3.5 shard_map.2257
  371.9 5.1 %shard_map.2248 = (f32[2,176,256]{2,1,0:T(8,128)}, f32[2,176,256]{2,1,0:T(8,128)}) custom-call(s32[7,4]{1,0:T(8,128)S(1)} %stack.799.table, bf16[1024,8192]{1,0:T(8,128)(2,1)} %x_ref.63, bf16[176,1024]{1,0:T(8,128)(2,1)S(1)} %bitcast.123, f32[8,176,256]{2,1,0:T(8,128)} %collective-permute-done.3.refs_1_, f32[8,176,256]{2,1,0:T(8,128)} %collective-permute-done.6.refs_2_, ...), custom_call_target="tpu_custom_call" | custom-call | flops 369098752 | bytes 4980736 | tf_op jit(solution)/shard_map/pallas_call | solution.py:97
  387.5 5.4 %shard_map.2250 = (f32[2,176,256]{2,1,0:T(8,128)}, f32[2,176,256]{2,1,0:T(8,128)}) custom-call(s32[9,4]{1,0:T(8,128)S(1)} %stack.808.table, bf16[1024,8192]{1,0:T(8,128)(2,1)} %x_ref.63, bf16[176,1024]{1,0:T(8,128)(2,1)S(1)} %bitcast.124, f32[8,176,256]{2,1,0:T(8,128)} %collective-permute-done.3.refs_1_, f32[8,176,256]{2,1,0:T(8,128)} %collective-permute-done.6.refs_2_, ...), custom_call_target="tpu_custom_call" | custom-call | flops 369098752 | bytes 5701632 | tf_op jit(solution)/shard_map/pallas_call | solution.py:97
  392.9 3.3 collective-permute-start.9
  396.2 3.2 collective-permute-start.14
  399.4 5.0 %shard_map.2256 = (f32[2,176,256]{2,1,0:T(8,128)}, f32[2,176,256]{2,1,0:T(8,128)S(1)}) custom-call(s32[7,4]{1,0:T(8,128)S(1)} %stack.859.table, bf16[1024,8192]{1,0:T(8,128)(2,1)} %x_ref.63, bf16[176,1024]{1,0:T(8,128)(2,1)S(1)} %bitcast.107, f32[8,176,256]{2,1,0:T(8,128)} %collective-permute-done.17.refs_1_, ...), custom_call_target="tpu_custom_call" | custom-call | flops 369098752 | bytes 4980736 | tf_op jit(solution)/shard_map/pallas_call | solution.py:97
  409.4 4.5 %shard_map.2258 = (f32[2,176,256]{2,1,0:T(8,128)S(1)}, f32[2,176,256]{2,1,0:T(8,128)S(1)}) custom-call(s32[9,4]{1,0:T(8,128)S(1)} %stack.868.table, bf16[1024,8192]{1,0:T(8,128)(2,1)} %x_ref.63, bf16[176,1024]{1,0:T(8,128)(2,1)S(1)} %bitcast.108, f32[8,176,256]{2,1,0:T(8,128)} %collective-permute-done.17.refs_1_, ...), custom_call_target="tpu_custom_call" | custom-call | flops 369098752 | bytes 5701632 | tf_op jit(solution)/shard_map/pallas_call | solution.py:97
  (382 shorter events, 154.6 us)
Async XLA Ops:
  16.6 101.7 %collective-permute-start.45 = (f32[16,80,256]{2,1,0:T(8,128)}, f32[16,80,256]{2,1,0:T(8,128)S(1)}, u32[]{:S(2)}, u32[]{:S(2)}) collective-permute-start(f32[16,80,256]{2,1,0:T(8,128)} %get-tuple-element.115), channel_id=1, source_target_pairs={{0,16},{1,17},{2,18},{3,19},{4,20},{5,21},{6,22},{7,23},{8,24},{9,... | collective-permute-start | bytes 3932168 | tf_op jit(solution)/shard_map/ppermute | solution.py:32
  18.6 116.7 %collective-permute-start.46 = (f32[16,80,256]{2,1,0:T(8,128)}, f32[16,80,256]{2,1,0:T(8,128)}, u32[]{:S(2)}, u32[]{:S(2)}) collective-permute-start(f32[16,80,256]{2,1,0:T(8,128)} %get-tuple-element.116), channel_id=1, source_target_pairs={{0,16},{1,17},{2,18},{3,19},{4,20},{5,21},{6,22},{7,23},{8,24},{9,... | collective-permute-start | bytes 3932168 | tf_op jit(solution)/shard_map/ppermute | solution.py:32
  32.4 103.6 %collective-permute-start.31 = (f32[16,80,256]{2,1,0:T(8,128)}, f32[16,80,256]{2,1,0:T(8,128)S(1)}, u32[]{:S(2)}, u32[]{:S(2)}) collective-permute-start(f32[16,80,256]{2,1,0:T(8,128)} %get-tuple-element.99), channel_id=1, source_target_pairs={{0,16},{1,17},{2,18},{3,19},{4,20},{5,21},{6,22},{7,23},{8,24},{9,... | collective-permute-start | bytes 3932168 | tf_op jit(solution)/shard_map/ppermute | solution.py:32
  54.2 98.6 %collective-permute-start.18 = (f32[8,176,256]{2,1,0:T(8,128)}, f32[8,176,256]{2,1,0:T(8,128)}, u32[]{:S(2)}, u32[]{:S(2)}) collective-permute-start(f32[8,176,256]{2,1,0:T(8,128)} %get-tuple-element.84), channel_id=1, source_target_pairs={{0,4},{1,5},{2,6},{3,7},{4,8},{5,9},{6,10},{7,11},{8,12},{9,13},{1... | collective-permute-start | bytes 4325384 | tf_op jit(solution)/shard_map/ppermute | solution.py:32
  57.2 61.1 %collective-permute-start.1 = (f32[128,1024]{1,0:T(8,128)S(1)}, f32[128,1024]{1,0:T(8,128)S(1)}, u32[]{:S(2)}, u32[]{:S(2)}) collective-permute-start(f32[128,1024]{1,0:T(8,128)S(1)} %dynamic-slice_add_fusion), channel_id=1, source_target_pairs={{0,64},{32,96},{64,0},{96,32},{1,65},{33,97},{65,1},{97,33},{2,66}... | collective-permute-start | bytes 1572872 | tf_op jit(solution)/shard_map/ppermute | solution.py:209
  118.3 33.0 %collective-permute-start.32 = (f32[16,80,256]{2,1,0:T(8,128)}, f32[16,80,256]{2,1,0:T(8,128)}, u32[]{:S(2)}, u32[]{:S(2)}) collective-permute-start(f32[16,80,256]{2,1,0:T(8,128)} %get-tuple-element.100), channel_id=1, source_target_pairs={{0,16},{1,17},{2,18},{3,19},{4,20},{5,21},{6,22},{7,23},{8,24},{9,... | collective-permute-start | bytes 3932168 | tf_op jit(solution)/shard_map/ppermute | solution.py:32
  119.1 48.8 %collective-permute-start.19 = (f32[8,176,256]{2,1,0:T(8,128)}, f32[8,176,256]{2,1,0:T(8,128)}, u32[]{:S(2)}, u32[]{:S(2)}) collective-permute-start(f32[8,176,256]{2,1,0:T(8,128)} %get-tuple-element.85), channel_id=1, source_target_pairs={{0,12},{1,13},{2,14},{3,15},{4,0},{5,1},{6,2},{7,3},{8,4},{9,5},{1... | collective-permute-start | bytes 4325384 | tf_op jit(solution)/shard_map/ppermute | solution.py:32
  135.3 48.0 %collective-permute-start.17 = (f32[8,176,256]{2,1,0:T(8,128)}, f32[8,176,256]{2,1,0:T(8,128)}, u32[]{:S(2)}, u32[]{:S(2)}) collective-permute-start(f32[8,176,256]{2,1,0:T(8,128)} %get-tuple-element.83), channel_id=1, source_target_pairs={{0,12},{1,13},{2,14},{3,15},{4,0},{5,1},{6,2},{7,3},{8,4},{9,5},{1... | collective-permute-start | bytes 4325384 | tf_op jit(solution)/shard_map/ppermute | solution.py:32
  136.1 50.8 %collective-permute-start.21 = (f32[8,176,256]{2,1,0:T(8,128)}, f32[8,176,256]{2,1,0:T(8,128)}, u32[]{:S(2)}, u32[]{:S(2)}) collective-permute-start(f32[8,176,256]{2,1,0:T(8,128)} %get-tuple-element.87), channel_id=1, source_target_pairs={{0,4},{1,5},{2,6},{3,7},{4,8},{5,9},{6,10},{7,11},{8,12},{9,13},{1... | collective-permute-start | bytes 4325384 | tf_op jit(solution)/shard_map/ppermute | solution.py:32
  151.3 43.0 %collective-permute-start.4 = (f32[8,176,256]{2,1,0:T(8,128)}, f32[8,176,256]{2,1,0:T(8,128)}, u32[]{:S(2)}, u32[]{:S(2)}) collective-permute-start(f32[8,176,256]{2,1,0:T(8,128)} %get-tuple-element.68), channel_id=1, source_target_pairs={{0,1},{1,2},{2,3},{3,0},{4,5},{5,6},{6,7},{7,4},{8,9},{9,10},{10,1... | collective-permute-start | bytes 4325384 | tf_op jit(solution)/shard_map/ppermute | solution.py:32
  152.8 42.6 %collective-permute-start.5 = (f32[8,176,256]{2,1,0:T(8,128)}, f32[8,176,256]{2,1,0:T(8,128)}, u32[]{:S(2)}, u32[]{:S(2)}) collective-permute-start(f32[8,176,256]{2,1,0:T(8,128)} %get-tuple-element.69), channel_id=1, source_target_pairs={{0,3},{1,0},{2,1},{3,2},{4,7},{5,4},{6,5},{7,6},{8,11},{9,8},{10,9... | collective-permute-start | bytes 4325384 | tf_op jit(solution)/shard_map/ppermute | solution.py:32
  167.9 47.5 %collective-permute-start.3 = (f32[8,176,256]{2,1,0:T(8,128)}, f32[8,176,256]{2,1,0:T(8,128)}, u32[]{:S(2)}, u32[]{:S(2)}) collective-permute-start(f32[8,176,256]{2,1,0:T(8,128)} %get-tuple-element.67), channel_id=1, source_target_pairs={{0,3},{1,0},{2,1},{3,2},{4,7},{5,4},{6,5},{7,6},{8,11},{9,8},{10,9... | collective-permute-start | bytes 4325384 | tf_op jit(solution)/shard_map/ppermute | solution.py:32
  183.3 39.0 %collective-permute-start.7 = (f32[8,176,256]{2,1,0:T(8,128)}, f32[8,176,256]{2,1,0:T(8,128)}, u32[]{:S(2)}, u32[]{:S(2)}) collective-permute-start(f32[8,176,256]{2,1,0:T(8,128)} %get-tuple-element.71), channel_id=1, source_target_pairs={{0,1},{1,2},{2,3},{3,0},{4,5},{5,6},{6,7},{7,4},{8,9},{9,10},{10,1... | collective-permute-start | bytes 4325384 | tf_op jit(solution)/shard_map/ppermute | solution.py:32
  186.8 35.6 %collective-permute-start.2 = (f32[128,1024]{1,0:T(8,128)}, f32[128,1024]{1,0:T(8,128)}, u32[]{:S(2)}, u32[]{:S(2)}) collective-permute-start(f32[128,1024]{1,0:T(8,128)} %add.2594), channel_id=1, source_target_pairs={{0,32},{32,0},{64,96},{96,64},{1,33},{33,1},{65,97},{97,65},{2,34}... | collective-permute-start | bytes 1572872 | tf_op jit(solution)/shard_map/ppermute | solution.py:210
  194.4 39.3 %collective-permute-start.48 = (f32[4,80,256]{2,1,0:T(8,128)}, f32[4,80,256]{2,1,0:T(8,128)}, u32[]{:S(2)}, u32[]{:S(2)}) collective-permute-start(f32[4,80,256]{2,1,0:T(8,128)} %get-tuple-element.118), channel_id=1, source_target_pairs={{0,4},{1,5},{2,6},{3,7},{4,8},{5,9},{6,10},{7,11},{8,12},{9,13},{1... | collective-permute-start | bytes 983048 | tf_op jit(solution)/shard_map/ppermute | solution.py:32
  195.5 39.9 %collective-permute-start.49 = (f32[4,80,256]{2,1,0:T(8,128)}, f32[4,80,256]{2,1,0:T(8,128)}, u32[]{:S(2)}, u32[]{:S(2)}) collective-permute-start(f32[4,80,256]{2,1,0:T(8,128)} %get-tuple-element.119), channel_id=1, source_target_pairs={{0,12},{1,13},{2,14},{3,15},{4,0},{5,1},{6,2},{7,3},{8,4},{9,5},{1... | collective-permute-start | bytes 983048 | tf_op jit(solution)/shard_map/ppermute | solution.py:32
  222.4 23.9 %collective-permute-start.34 = (f32[4,80,256]{2,1,0:T(8,128)}, f32[4,80,256]{2,1,0:T(8,128)}, u32[]{:S(2)}, u32[]{:S(2)}) collective-permute-start(f32[4,80,256]{2,1,0:T(8,128)} %get-tuple-element.102), channel_id=1, source_target_pairs={{0,1},{1,2},{2,3},{3,0},{4,5},{5,6},{6,7},{7,4},{8,9},{9,10},{10,1... | collective-permute-start | bytes 983048 | tf_op jit(solution)/shard_map/ppermute | solution.py:32
  233.6 29.5 %collective-permute-start.35 = (f32[4,80,256]{2,1,0:T(8,128)}, f32[4,80,256]{2,1,0:T(8,128)}, u32[]{:S(2)}, u32[]{:S(2)}) collective-permute-start(f32[4,80,256]{2,1,0:T(8,128)} %get-tuple-element.103), channel_id=1, source_target_pairs={{0,3},{1,0},{2,1},{3,2},{4,7},{5,4},{6,5},{7,6},{8,11},{9,8},{10,9... | collective-permute-start | bytes 983048 | tf_op jit(solution)/shard_map/ppermute | solution.py:32
  235.4 28.1 %collective-permute-start.33 = (f32[4,80,256]{2,1,0:T(8,128)}, f32[4,80,256]{2,1,0:T(8,128)}, u32[]{:S(2)}, u32[]{:S(2)}) collective-permute-start(f32[4,80,256]{2,1,0:T(8,128)} %get-tuple-element.101), channel_id=1, source_target_pairs={{0,3},{1,0},{2,1},{3,2},{4,7},{5,4},{6,5},{7,6},{8,11},{9,8},{10,9... | collective-permute-start | bytes 983048 | tf_op jit(solution)/shard_map/ppermute | solution.py:32
  237.2 38.4 %collective-permute-start.37 = (f32[4,80,256]{2,1,0:T(8,128)}, f32[4,80,256]{2,1,0:T(8,128)}, u32[]{:S(2)}, u32[]{:S(2)}) collective-permute-start(f32[4,80,256]{2,1,0:T(8,128)} %copy-done.45), channel_id=1, source_target_pairs={{0,1},{1,2},{2,3},{3,0},{4,5},{5,6},{6,7},{7,4},{8,9},{9,10},{10,1... | collective-permute-start | bytes 983048 | tf_op jit(solution)/shard_map/ppermute | solution.py:32
  246.0 43.5 %collective-permute-start.50 = (f32[4,80,256]{2,1,0:T(8,128)}, f32[4,80,256]{2,1,0:T(8,128)}, u32[]{:S(2)}, u32[]{:S(2)}) collective-permute-start(f32[4,80,256]{2,1,0:T(8,128)} %get-tuple-element.120), channel_id=1, source_target_pairs={{0,4},{1,5},{2,6},{3,7},{4,8},{5,9},{6,10},{7,11},{8,12},{9,13},{1... | collective-permute-start | bytes 983048 | tf_op jit(solution)/shard_map/ppermute | solution.py:32
  246.3 43.2 %collective-permute-start.52 = (f32[4,80,256]{2,1,0:T(8,128)}, f32[4,80,256]{2,1,0:T(8,128)}, u32[]{:S(2)}, u32[]{:S(2)}) collective-permute-start(f32[4,80,256]{2,1,0:T(8,128)} %get-tuple-element.122), channel_id=1, source_target_pairs={{0,12},{1,13},{2,14},{3,15},{4,0},{5,1},{6,2},{7,3},{8,4},{9,5},{1... | collective-permute-start | bytes 983048 | tf_op jit(solution)/shard_map/ppermute | solution.py:32
  263.2 65.4 %collective-permute-start.6 = (f32[8,176,256]{2,1,0:T(8,128)}, f32[8,176,256]{2,1,0:T(8,128)}, u32[]{:S(2)}, u32[]{:S(2)}) collective-permute-start(f32[8,176,256]{2,1,0:T(8,128)} %get-tuple-element.70), channel_id=1, source_target_pairs={{0,1},{1,2},{2,3},{3,0},{4,5},{5,6},{6,7},{7,4},{8,9},{9,10},{10,1... | collective-permute-start | bytes 4325384 | tf_op jit(solution)/shard_map/ppermute | solution.py:32
  263.5 65.1 %collective-permute-start.8 = (f32[8,176,256]{2,1,0:T(8,128)}, f32[8,176,256]{2,1,0:T(8,128)}, u32[]{:S(2)}, u32[]{:S(2)}) collective-permute-start(f32[8,176,256]{2,1,0:T(8,128)} %get-tuple-element.72), channel_id=1, source_target_pairs={{0,3},{1,0},{2,1},{3,2},{4,7},{5,4},{6,5},{7,6},{8,11},{9,8},{10,9... | collective-permute-start | bytes 4325384 | tf_op jit(solution)/shard_map/ppermute | solution.py:32
  275.6 24.6 %collective-permute-start.36 = (f32[4,80,256]{2,1,0:T(8,128)S(1)}, f32[4,80,256]{2,1,0:T(8,128)S(1)}, u32[]{:S(2)}, u32[]{:S(2)}) collective-permute-start(f32[4,80,256]{2,1,0:T(8,128)S(1)} %get-tuple-element.104), channel_id=1, source_target_pairs={{0,1},{1,2},{2,3},{3,0},{4,5},{5,6},{6,7},{7,4},{8,9},{9,10},{10,1... | collective-permute-start | bytes 983048 | tf_op jit(solution)/shard_map/ppermute | solution.py:32
  289.5 65.7 %collective-permute-start.20 = (f32[8,176,256]{2,1,0:T(8,128)}, f32[8,176,256]{2,1,0:T(8,128)}, u32[]{:S(2)}, u32[]{:S(2)}) collective-permute-start(f32[8,176,256]{2,1,0:T(8,128)} %get-tuple-element.86), channel_id=1, source_target_pairs={{0,4},{1,5},{2,6},{3,7},{4,8},{5,9},{6,10},{7,11},{8,12},{9,13},{1... | collective-permute-start | bytes 4325384 | tf_op jit(solution)/shard_map/ppermute | solution.py:32
  289.5 72.3 %collective-permute-start.22 = (f32[8,176,256]{2,1,0:T(8,128)}, f32[8,176,256]{2,1,0:T(8,128)}, u32[]{:S(2)}, u32[]{:S(2)}) collective-permute-start(f32[8,176,256]{2,1,0:T(8,128)} %get-tuple-element.88), channel_id=1, source_target_pairs={{0,12},{1,13},{2,14},{3,15},{4,0},{5,1},{6,2},{7,3},{8,4},{9,5},{1... | collective-permute-start | bytes 4325384 | tf_op jit(solution)/shard_map/ppermute | solution.py:32
  342.6 41.1 %collective-permute-start.10 = (f32[2,176,256]{2,1,0:T(8,128)}, f32[2,176,256]{2,1,0:T(8,128)}, u32[]{:S(2)}, u32[]{:S(2)}) collective-permute-start(f32[2,176,256]{2,1,0:T(8,128)} %get-tuple-element.74), channel_id=1, source_target_pairs={{0,4},{1,5},{2,6},{3,7},{4,8},{5,9},{6,10},{7,11},{8,12},{9,13},{1... | collective-permute-start | bytes 1081352 | tf_op jit(solution)/shard_map/ppermute | solution.py:32
  342.7 42.7 %collective-permute-start.11 = (f32[2,176,256]{2,1,0:T(8,128)}, f32[2,176,256]{2,1,0:T(8,128)}, u32[]{:S(2)}, u32[]{:S(2)}) collective-permute-start(f32[2,176,256]{2,1,0:T(8,128)} %get-tuple-element.75), channel_id=1, source_target_pairs={{0,12},{1,13},{2,14},{3,15},{4,0},{5,1},{6,2},{7,3},{8,4},{9,5},{1... | collective-permute-start | bytes 1081352 | tf_op jit(solution)/shard_map/ppermute | solution.py:32
  366.6 29.6 %collective-permute-start.24 = (f32[2,176,256]{2,1,0:T(8,128)}, f32[2,176,256]{2,1,0:T(8,128)}, u32[]{:S(2)}, u32[]{:S(2)}) collective-permute-start(f32[2,176,256]{2,1,0:T(8,128)} %get-tuple-element.90), channel_id=1, source_target_pairs={{0,1},{1,2},{2,3},{3,0},{4,5},{5,6},{6,7},{7,4},{8,9},{9,10},{10,1... | collective-permute-start | bytes 1081352 | tf_op jit(solution)/shard_map/ppermute | solution.py:32
  367.3 37.8 %collective-permute-start.25 = (f32[2,176,256]{2,1,0:T(8,128)}, f32[2,176,256]{2,1,0:T(8,128)}, u32[]{:S(2)}, u32[]{:S(2)}) collective-permute-start(f32[2,176,256]{2,1,0:T(8,128)} %copy-done.44), channel_id=1, source_target_pairs={{0,3},{1,0},{2,1},{3,2},{4,7},{5,4},{6,5},{7,6},{8,11},{9,8},{10,9... | collective-permute-start | bytes 1081352 | tf_op jit(solution)/shard_map/ppermute | solution.py:32
  377.0 30.3 %collective-permute-start.13 = (f32[2,176,256]{2,1,0:T(8,128)}, f32[2,176,256]{2,1,0:T(8,128)}, u32[]{:S(2)}, u32[]{:S(2)}) collective-permute-start(f32[2,176,256]{2,1,0:T(8,128)} %get-tuple-element.77), channel_id=1, source_target_pairs={{0,4},{1,5},{2,6},{3,7},{4,8},{5,9},{6,10},{7,11},{8,12},{9,13},{1... | collective-permute-start | bytes 1081352 | tf_op jit(solution)/shard_map/ppermute | solution.py:32
  (121 other events, 1005.1 us)

commit v2 on v0

v2 whole, which is shorter than its diff:
```python
import jax
import jax.numpy as jnp
from jax import lax
from jax.experimental import pallas as pl
from jax.experimental.pallas import tpu as pltpu
from jax.sharding import PartitionSpec as P

WIDTH = 256
ROW = 4
A = 224
B = 160
C = 128
X_RINGS = [[16 * z + 4 * y + x for x in range(4)] for z in range(2) for y in range(4)]

LONG = pl.CostEstimate(flops=10**11, bytes_accessed=10**8, transcendentals=0)


def multiply(inputs, keys, place, strips, wanted, swapped=False, after=()):
    depth = inputs.shape[0]
    span = ROW * WIDTH
    halves = 2

    def body(table, *refs):
        xs, ks, outs = refs[:halves], refs[halves : halves + len(keys)], refs[len(refs) - len(wanted) :]
        step = pl.program_id(0)
        part = depth // halves

        def emit(key, out):
            value = jnp.dot(ks[key][:, :part], xs[0][...], preferred_element_type=jnp.float32)
            value += jnp.dot(ks[key][:, part:], xs[1][...], preferred_element_type=jnp.float32)
            for x in range(ROW):
                piece = value[:, x * WIDTH : (x + 1) * WIDTH]
                if swapped:
                    out[x, 0] = piece
                else:
                    out[0, x] = piece

        for (key, first, count), out in zip(wanted, outs):
            if count == len(strips):
                emit(key, out)
            else:
                pl.when((step >= first) & (step < first + count))(lambda key=key, out=out: emit(key, out))

    def out_spec(key, first, count):
        rows = keys[key].shape[0]

        def at(i, table):
            n = jnp.clip(i - first, 0, count - 1)
            return (0, n, 0, 0) if swapped else (n, 0, 0, 0)

        return pl.BlockSpec((ROW, 1, rows, WIDTH) if swapped else (1, ROW, rows, WIDTH), at)

    shapes = [
        (ROW, n, keys[k].shape[0], WIDTH) if swapped else (n, ROW, keys[k].shape[0], WIDTH) for k, _, n in wanted
    ]
    table = 4 * ((place[0] + jnp.array([s[0] for s in strips])) % 2) + (
        place[1] + jnp.array([s[1] for s in strips])
    ) % 4
    return pl.pallas_call(
        body,
        grid_spec=pltpu.PrefetchScalarGridSpec(
            num_scalar_prefetch=1,
            grid=(len(strips),),
            in_specs=[
                pl.BlockSpec((depth // halves, span), lambda i, table, s=s: (s, table[i])) for s in range(halves)
            ]
            + [pl.BlockSpec(k.shape, lambda i, table: (0, 0)) for k in keys]
            + [pl.BlockSpec(memory_space=pl.ANY) for _ in after],
            out_specs=[out_spec(*w) for w in wanted],
        ),
        out_shape=[jax.ShapeDtypeStruct(s, jnp.float32) for s in shapes],
        compiler_params=pltpu.CompilerParams(
            dimension_semantics=("arbitrary",), vmem_limit_bytes=60 * 1024 * 1024
        ),
        cost_estimate=LONG,
    )(table.astype(jnp.int32), *[inputs] * halves, *keys, *after)


def along_y(array, step):
    return lax.ppermute(
        array, "fsdp", [(f, f // 16 * 16 + (f // 4 + step) % 4 * 4 + f % 4) for f in range(32)]
    )


def along_z(array):
    return lax.ppermute(array, "fsdp", [(f, (f + 16) % 32) for f in range(32)])


def over_x(array):
    return lax.psum_scatter(array, "fsdp", scatter_dimension=0, axis_index_groups=X_RINGS, tiled=True)[0]


def combine(body, arrays, shapes, after=()):
    def kernel(*refs):
        body(*refs[: len(arrays)], *refs[len(arrays) + len(after) :])

    return pl.pallas_call(
        kernel,
        in_specs=[pl.BlockSpec(memory_space=pltpu.VMEM)] * len(arrays)
        + [pl.BlockSpec(memory_space=pl.ANY)] * len(after),
        out_specs=[pl.BlockSpec(memory_space=pltpu.VMEM)] * len(shapes),
        out_shape=[jax.ShapeDtypeStruct(s, jnp.float32) for s in shapes],
        compiler_params=pltpu.CompilerParams(vmem_limit_bytes=60 * 1024 * 1024),
        cost_estimate=LONG,
    )(*arrays, *after)


def reduce_a(array, after):
    half = A // 2

    def part(ref, z, y, h):
        return ref[4 * z + y, h * half : (h + 1) * half, :]

    def first(a, up, down):
        for z in range(2):
            up[0, z], up[1, z] = part(a, z, 2, 0), part(a, z, 1, 1)
            down[0, z], down[1, z] = part(a, z, 2, 1), part(a, z, 3, 0)

    up, down = combine(first, [array], [(2, 2, half, WIDTH)] * 2, after)
    up_in, down_in = along_y(up, 1), along_y(down, -1)
    after = yield [up]

    def second(a, up_in, down_in, up, down):
        for z in range(2):
            up[z] = part(a, z, 1, 0) + up_in[0, z]
            down[z] = part(a, z, 3, 1) + down_in[0, z]

    up, down = combine(second, [array, up_in, down_in], [(2, half, WIDTH)] * 2, after)
    up_last, down_last = along_y(up, 1), along_y(down, -1)
    after = yield [up]

    def third(a, up_in, down_in, up_last, down_last, keep, cross):
        for z, out in enumerate((keep, cross)):
            out[:half, :] = part(a, z, 0, 0) + down_in[1, z] + up_last[z]
            out[half:, :] = part(a, z, 0, 1) + up_in[1, z] + down_last[z]

    keep, cross = combine(third, [array, up_in, down_in, up_last, down_last], [(A, WIDTH)] * 2, after)
    yield keep, along_z(cross), [keep]


def reduce_c(near, far, after):
    def part(refs, x, y, h):
        return refs[h][y, x] + refs[2][y, x, h * C : (h + 1) * C, :]

    def first(n0, n1, f, up, down):
        refs = (n0, n1, f)
        for x in range(ROW):
            up[0, x], up[1, x] = part(refs, x, 2, 0), part(refs, x, 1, 1)
            down[0, x], down[1, x] = part(refs, x, 2, 1), part(refs, x, 3, 0)

    up, down = combine(first, [*near, far], [(2, ROW, C, WIDTH)] * 2, after)
    up_in, down_in = along_y(up, 1), along_y(down, -1)
    after = yield [up]

    def second(n0, n1, f, up_in, down_in, up, down):
        refs = (n0, n1, f)
        for x in range(ROW):
            up[x] = part(refs, x, 1, 0) + up_in[0, x]
            down[x] = part(refs, x, 3, 1) + down_in[0, x]

    up, down = combine(second, [*near, far, up_in, down_in], [(ROW, C, WIDTH)] * 2, after)
    up_last, down_last = along_y(up, 1), along_y(down, -1)
    after = yield [up]

    def third(n0, n1, f, up_in, down_in, up_last, down_last, out):
        refs = (n0, n1, f)
        for x in range(ROW):
            out[x, :C, :] = part(refs, x, 0, 0) + down_in[1, x] + up_last[x]
            out[x, C:, :] = part(refs, x, 0, 1) + up_in[1, x] + down_last[x]

    (own,) = combine(
        third, [*near, far, up_in, down_in, up_last, down_last], [(ROW, 2 * C, WIDTH)], after
    )
    yield over_x(own), [own]


def local(params, momentum, local_params, exps, inputs, cotangent):
    groups = lax.axis_size("rep")
    group = lax.axis_index("rep")
    picked = jnp.sum(jnp.where(jnp.arange(groups) == group, exps, 0))
    scale_up = jnp.left_shift(1, picked).astype(jnp.float32)
    delta = params - local_params[0].astype(jnp.float32)
    coded = jnp.clip(delta * scale_up, -448.0, 448.0).astype(jnp.bfloat16)
    decoded = coded.astype(jnp.float32) / scale_up
    total = lax.psum(decoded, "rep")

    me = lax.axis_index("fsdp")
    place = (me // 16, me // 4 % 4)
    keys, low = [], 0
    for height in (A, A, B, B, C, C):
        keys.append(cotangent[:, low : low + height].T)
        low += height
    whole = [(z, y) for z in range(2) for y in range(4)]

    def run(*args, **kwargs):
        return multiply(inputs, *args[:1], place, *args[1:], **kwargs)

    (a1,) = run(keys[0:1], whole, [(0, 0, 8)], swapped=True, after=[decoded])
    a1_x = over_x(a1)
    b_far = run(keys[2:4], [(0, 2), (1, 2)], [(0, 0, 2), (1, 0, 2)], after=[a1])
    b_up1, b_down1 = along_y(b_far[0], 1), along_y(b_far[1], -1)
    (c_far,) = run(
        [jnp.concatenate(keys[4:6])], [(1, y) for y in range(4)], [(0, 0, 4)], after=b_far[:1]
    )
    c_z = along_z(c_far)
    (a2,) = run(keys[1:2], whole, [(0, 0, 8)], swapped=True, after=[c_far])
    a2_x = over_x(a2)
    rest = run(
        keys[2:6],
        [(1, 0), (0, 0), (0, 1), (0, 2), (0, 3)],
        [(0, 0, 2), (1, 0, 2), (2, 1, 4), (3, 1, 4)],
        after=[a2],
    )
    b_own, c_near = rest[:2], rest[2:]
    b_near = run(
        keys[2:4],
        [(0, 1), (1, 1), (0, 3), (1, 3)],
        [(0, 0, 2), (1, 0, 2), (0, 2, 2), (1, 2, 2)],
        after=rest[:1],
    )
    b_up2, b_down2 = along_y(b_near[1], 1), along_y(b_near[2], -1)

    def b_third(near0, near3, up1, down1, up, down):
        for z in range(2):
            for x in range(ROW):
                up[z, x] = near0[z, x] + up1[z, x]
                down[z, x] = near3[z, x] + down1[z, x]

    b_last = combine(
        b_third, [b_near[0], b_near[3], b_up1, b_down1], [(2, ROW, B, WIDTH)] * 2
    )
    b_up3, b_down3 = along_y(b_last[0], 1), along_y(b_last[1], -1)

    def nesterov(weights, moment, total, new_weights, fresh):
        outer_grad = total[...] / groups
        fresh[...] = 0.9 * moment[...] + outer_grad
        new_weights[...] = weights[...] - 0.7 * (outer_grad + 0.9 * fresh[...])

    new_params, new_momentum = combine(
        nesterov, [params, momentum, total], [params.shape] * 2, b_last[:1]
    )

    ring_1 = reduce_a(a1_x[:, :, :], [new_params])
    done = next(ring_1)

    def b_home(own0, own1, up2, down2, up3, down3, out):
        for z in range(2):
            for x in range(ROW):
                low = 2 * B * z
                out[x, low : low + B, :] = own0[1 - z, x] + down2[z, x] + up3[z, x]
                out[x, low + B : low + 2 * B, :] = own1[1 - z, x] + up2[z, x] + down3[z, x]

    (b_sum,) = combine(
        b_home, [*b_own, b_up2, b_down2, b_up3, b_down3], [(ROW, 4 * B, WIDTH)], done
    )
    b_x = over_x(b_sum)
    ring_c = reduce_c(c_near, c_z, [b_sum])
    done = next(ring_c)
    done = ring_1.send(done)
    done = ring_c.send(done)
    a1_keep, a1_in, done = ring_1.send(done)
    c_own, done = ring_c.send(done)
    ring_2 = reduce_a(a2_x, done)
    done = next(ring_2)
    done = ring_2.send(done)
    a2_keep, a2_in, done = ring_2.send(done)
    b_in = along_z(b_x[2 * B :])
    kv_grad = jnp.concatenate([a1_keep + a1_in, a2_keep + a2_in, b_x[: 2 * B] + b_in, c_own], axis=0).T
    return (new_params, new_momentum, kv_grad[None])


def solution(mesh):
    in_specs = (
        P("fsdp", None),
        P("fsdp", None),
        P("rep", "fsdp", None),
        P(),
        P(("rep", "fsdp"), None),
        P(("rep", "fsdp"), None),
    )
    out_specs = (P("fsdp", None), P("fsdp", None), P("rep", "fsdp", None))
    return jax.shard_map(local, mesh=mesh, in_specs=in_specs, out_specs=out_specs, check_vma=False)
```

time: 421 us -> 262 us (0.62)
  waiting for transfers between devices: 369 us -> 89.1 us
  Pallas kernels: 0 us -> 104 us
  matrix products: 27.1 us -> 0 us
  starting transfers between devices: 0.08 us -> 25.3 us
  local copies, waits for them, and re-layouts: 0.01 us -> 16.4 us
    psum x1, waiting for transfers between devices: 369 us -> 0.01 us  [local(): total = lax.psum(decoded, 'rep')]
    pallas_call x0 -> x18, Pallas kernels: none -> 104 us  [the longest x6 59 us: multiply(): pl.pallas_call(body, grid_spec=pltpu.PrefetchScalarGridSpec(num_scalar_pr...]
    ppermute x0 -> x22, waiting for transfers between devices: none -> 83.2 us  [the longest x18 78 us: along_y(): lax.ppermute(array, 'fsdp', [(f, f // 16 * 16 + (f // 4 + step) % 4 * 4 +...]
    dot_general x1 -> x0, matrix products: 27.1 us -> none  [local(): lax.dot_general(inputs, key_cotangent, (((0,), (0,)), ((), ())), preferre...]
    ppermute x0 -> x22, starting transfers between devices: none -> 25.1 us  [the longest x18 23.1 us: along_y(): lax.ppermute(array, 'fsdp', [(f, f // 16 * 16 + (f // 4 + step) % 4 * 4 +...]
    unnamed x4 -> x55, local copies, waits for them, and re-layouts: 0.01 us -> 12.5 us
    add x0 -> x8, other arithmetic: none -> 4.78 us  [the longest x5 2.73 us: multiply(): 4 * ((place[0] + jnp.array([s[0] for s in strips])) % 2)]
    reduce_scatter x1 -> x4, waiting for transfers between devices: 0.01 us -> 4.61 us  [over_x(): lax.psum_scatter(array, 'fsdp', scatter_dimension=0, axis_index_groups=X_...]
  transfers between devices with their start and end apart: 2 -> 27, of which waited for: 1 -> 13; matrix products, arithmetic and copies ran while one was open for 7% -> 4% of each run, Pallas kernels for 0% -> 35%
where the time goes in v2:
time: 262 us; the launch traced here: 260 us
  Pallas kernels  104 us (40%)
  waiting for transfers between devices  89.1 us (34%)
  starting transfers between devices  25.3 us (10%)
  between operations  16.6 us (6%)
  local copies, waits for them, and re-layouts  16.4 us (6%)
  other arithmetic  9.08 us (3%)
    ppermute x18, waiting for transfers between devices, along_y(): lax.ppermute(array, 'fsdp', [(f, f // 16 * 16 + (f // 4 + step) % 4 * 4 +...  78 us
    pallas_call x6, Pallas kernels, multiply(): pl.pallas_call(body, grid_spec=pltpu.PrefetchScalarGridSpec(num_scalar_pr...  59 us
    pallas_call x12, Pallas kernels, combine(): pl.pallas_call(kernel, in_specs=[pl.BlockSpec(memory_space=pltpu.VMEM)] *...  44.7 us
    ppermute x18, starting transfers between devices, along_y(): lax.ppermute(array, 'fsdp', [(f, f // 16 * 16 + (f // 4 + step) % 4 * 4 +...  23.1 us
    unnamed x55, local copies, waits for them, and re-layouts  12.5 us
  transfers between devices with their start and end apart: 27, of which 13 were waited for; matrix products, arithmetic and copies ran while one was open for 4% of the time, Pallas kernels for 35%

profile of v2, /device:TPU:0, one launch (start us, length us, event | category | flops | bytes accessed | tf_op | source)
XLA Modules:
  0.0 260.1 jit_solution(11412259427257532482)
XLA Ops:
  10.0 2.4 fusion.22
  15.2 13.3 %shard_map.193.refs_4_ = f32[4,8,224,256]{3,2,1,0:T(8,128)} custom-call(s32[8]{0:T(128)} %fusion.6.table, bf16[1024,8192]{1,0:T(8,128)(2,1)} %refs_1_.12, bf16[1024,8192]{1,0:T(8,128)(2,1)} %refs_1_.12, bf16[224,1024]{1,0:T(8,128)(2,1)} %bitcast.26, f32[256,1024]{1,0:T(8,128)} %convert_divide_fusion.refs_3_), custom_call_target="tpu_custom_call" | custom-call | flops 99999997952 | bytes 100000000 | tf_op jit(solution)/shard_map/pallas_call | solution.py:59
  33.6 5.0 %shard_map.194 = (f32[2,4,160,256]{3,2,1,0:T(8,128)}, f32[2,4,160,256]{3,2,1,0:T(8,128)}) custom-call(s32[2]{0:T(128)} %fusion.19.table, bf16[1024,8192]{1,0:T(8,128)(2,1)} %refs_1_.12, bf16[1024,8192]{1,0:T(8,128)(2,1)} %refs_1_.12, bf16[160,1024]{1,0:T(8,128)(2,1)} %bitcast.31, bf16[160,1024]{1,0:T(8,128)(2,1)} %bitcast.28, ...), custom_call_target="tpu_custom_call" | custom-call | flops 99999997952 | bytes 100000000 | tf_op jit(solution)/shard_map/pallas_call | solution.py:59
  38.5 3.1 %collective-permute-start.1 = (f32[2,4,160,256]{3,2,1,0:T(8,128)}, f32[2,4,160,256]{3,2,1,0:T(8,128)}, u32[]{:S(2)}, u32[]{:S(2)}) collective-permute-start(f32[2,4,160,256]{3,2,1,0:T(8,128)} %get-tuple-element.37), channel_id=1, source_target_pairs={{0,12},{1,13},{2,14},{3,15},{4,0},{5,1},{6,2},{7,3},{8,4},{9,5},{1... | collective-permute-start | bytes 3932168 | tf_op jit(solution)/shard_map/ppermute | solution.py:80
  44.2 8.1 %shard_map.195.refs_3_ = f32[4,4,256,256]{3,2,1,0:T(8,128)} custom-call(s32[4]{0:T(128)} %fusion.17.table, bf16[1024,8192]{1,0:T(8,128)(2,1)} %refs_1_.12, bf16[1024,8192]{1,0:T(8,128)(2,1)} %refs_1_.12, bf16[256,1024]{1,0:T(8,128)(2,1)} %pad_maximum_fusion.refs_2_, f32[2,4,160,256]{3,2,1,0:T(8,128)} %get-tuple-element.33.refs_3_), custom_call_target="tpu_custom_call" | custom-call | flops 99999997952 | bytes 100000000 | tf_op jit(solution)/shard_map/pallas_call | solution.py:59
  55.1 13.3 %shard_map.196.refs_6_ = f32[4,8,224,256]{3,2,1,0:T(8,128)} custom-call(s32[8]{0:T(128)} %fusion.6.table, bf16[1024,8192]{1,0:T(8,128)(2,1)} %refs_1_.12, bf16[1024,8192]{1,0:T(8,128)(2,1)} %refs_1_.12, bf16[224,1024]{1,0:T(8,128)(2,1)} %bitcast.27, f32[4,4,256,256]{3,2,1,0:T(8,128)} %shard_map.195.refs_3_), custom_call_target="tpu_custom_call" | custom-call | flops 99999997952 | bytes 100000000 | tf_op jit(solution)/shard_map/pallas_call | solution.py:59
  69.6 10.7 %shard_map.197 = (f32[2,4,160,256]{3,2,1,0:T(8,128)}, f32[2,4,160,256]{3,2,1,0:T(8,128)}, f32[4,4,128,256]{3,2,1,0:T(8,128)}, f32[4,4,128,256]{3,2,1,0:T(8,128)}) custom-call(s32[5]{0:T(128)} %fusion.5.table, bf16[1024,8192]{1,0:T(8,128)(2,1)} %refs_1_.12, bf16[1024,8192]{1,0:T(8,128)(2,1)} %refs_1_.12, bf16[160,1024]{1,0:T(8,128)(2,1)} %bitcast.32, ...), custom_call_target="tpu_custom_call" | custom-call | flops 99999997952 | bytes 100000000 | tf_op jit(solution)/shard_map/pallas_call | solution.py:59
  80.9 8.6 %shard_map.198 = (f32[2,4,160,256]{3,2,1,0:T(8,128)}, f32[2,4,160,256]{3,2,1,0:T(8,128)}, f32[2,4,160,256]{3,2,1,0:T(8,128)}, f32[2,4,160,256]{3,2,1,0:T(8,128)}) custom-call(s32[4]{0:T(128)} %fusion.4.table, bf16[1024,8192]{1,0:T(8,128)(2,1)} %refs_1_.12, bf16[1024,8192]{1,0:T(8,128)(2,1)} %refs_1_.12, bf16[160,1024]{1,0:T(8,128)(2,1)} %bitcast.33, ...), custom_call_target="tpu_custom_call" | custom-call | flops 99999997952 | bytes 100000000 | tf_op jit(solution)/shard_map/pallas_call | solution.py:59
  92.8 4.2 %shard_map.199 = (f32[2,4,160,256]{3,2,1,0:T(8,128)}, f32[2,4,160,256]{3,2,1,0:T(8,128)}) custom-call(f32[2,4,160,256]{3,2,1,0:T(8,128)} %get-tuple-element.35.refs_0_, f32[2,4,160,256]{3,2,1,0:T(8,128)} %get-tuple-element.36.refs_1_, f32[2,4,160,256]{3,2,1,0:T(8,128)} %collective-permute-done.refs_2_, f32[2,4,160,256]{3,2,1,0:T(8,128)} %collective-permute-done.1.refs_3_), custom_call_target="tpu_custom_call" | custom-call | flops 99999997952 | bytes 100000000 | tf_op jit(solution)/shard_map/pallas_call | solution.py:97
  99.1 3.4 %shard_map.200 = (f32[256,1024]{1,0:T(8,128)}, f32[256,1024]{1,0:T(8,128)}) custom-call(f32[256,1024]{1,0:T(8,128)} %refs_0_.13, f32[256,1024]{1,0:T(8,128)} %refs_1_.13, f32[256,1024]{1,0:T(8,128)} %all-reduce.2.cloned.1.call-done.refs_2_, f32[2,4,160,256]{3,2,1,0:T(8,128)} %get-tuple-element.38.refs_3_), custom_call_target="tpu_custom_call" | custom-call | flops 99999997952 | bytes 100000000 | tf_op jit(solution)/shard_map/pallas_call | solution.py:97
  102.5 4.6 %reduce-scatter.5.cloned.1.call-done = f32[1,8,224,256]{3,2,1,0:T(8,128)} async-done(((f32[4,8,224,256]{3,2,1,0:T(8,128)}), f32[1,8,224,256]{3,2,1,0:T(8,128)}) %reduce-scatter.5.cloned.1.call-update) | async-done | bytes 1835024 | tf_op jit(solution)/shard_map/reduce_scatter | solution.py:90
  107.0 2.5 shard_map.201
  109.6 13.2 %collective-permute-done.5.refs_2_ = f32[2,4,160,256]{3,2,1,0:T(8,128)} collective-permute-done((f32[2,4,160,256]{3,2,1,0:T(8,128)}, f32[2,4,160,256]{3,2,1,0:T(8,128)}, u32[]{:S(2)}, u32[]{:S(2)}) %collective-permute-start.5) | collective-permute-done | bytes 1310752 | tf_op jit(solution)/shard_map/ppermute | solution.py:80
  124.8 25.9 %collective-permute-done.8.refs_5_ = f32[2,4,160,256]{3,2,1,0:T(8,128)} collective-permute-done((f32[2,4,160,256]{3,2,1,0:T(8,128)}, f32[2,4,160,256]{3,2,1,0:T(8,128)}, u32[]{:S(2)}, u32[]{:S(2)}) %collective-permute-start.8) | collective-permute-done | bytes 1310752 | tf_op jit(solution)/shard_map/ppermute | solution.py:80
  150.8 5.4 %shard_map.202.refs_3_ = f32[4,640,256]{2,1,0:T(8,128)} custom-call(f32[2,4,160,256]{3,2,1,0:T(8,128)} %get-tuple-element.34.refs_4_.refs_0_, f32[2,4,160,256]{3,2,1,0:T(8,128)} %get-tuple-element.45.refs_1_, f32[2,4,160,256]{3,2,1,0:T(8,128)} %collective-permute-done.5.refs_2_, f32[2,4,160,256]{3,2,1,0:T(8,128)} %collective-permute-done.6.refs_3_, ...), custom_call_target="tpu_custom_call" | custom-call | flops 99999997952 | bytes 100000000 | tf_op jit(solution)/shard_map/pallas_call | solution.py:97
  156.3 5.1 %shard_map.203 = (f32[2,4,128,256]{3,2,1,0:T(8,128)}, f32[2,4,128,256]{3,2,1,0:T(8,128)}) custom-call(f32[4,4,128,256]{3,2,1,0:T(8,128)} %get-tuple-element.43.refs_0_, f32[4,4,128,256]{3,2,1,0:T(8,128)} %get-tuple-element.44.refs_1_, f32[4,4,256,256]{3,2,1,0:T(8,128)} %collective-permute-done.4.refs_2_, f32[4,640,256]{2,1,0:T(8,128)} %shard_map.202.refs_3_), custom_call_target="tpu_custom_call" | custom-call | flops 99999997952 | bytes 100000000 | tf_op jit(solution)/shard_map/pallas_call | solution.py:97
  161.4 3.3 %collective-permute-start.12 = (f32[2,4,128,256]{3,2,1,0:T(8,128)}, f32[2,4,128,256]{3,2,1,0:T(8,128)S(1)}, u32[]{:S(2)}, u32[]{:S(2)}) collective-permute-start(f32[2,4,128,256]{3,2,1,0:T(8,128)} %get-tuple-element.52), channel_id=1, source_target_pairs={{0,12},{1,13},{2,14},{3,15},{4,0},{5,1},{6,2},{7,3},{8,4},{9,5},{1... | collective-permute-start | bytes 3145736 | tf_op jit(solution)/shard_map/ppermute | solution.py:80
  164.8 2.5 shard_map.204
  167.3 3.2 %collective-permute-start.10 = (f32[2,112,256]{2,1,0:T(8,128)}, f32[2,112,256]{2,1,0:T(8,128)S(1)}, u32[]{:S(2)}, u32[]{:S(2)}) collective-permute-start(f32[2,112,256]{2,1,0:T(8,128)} %get-tuple-element.51), channel_id=1, source_target_pairs={{0,12},{1,13},{2,14},{3,15},{4,0},{5,1},{6,2},{7,3},{8,4},{9,5},{1... | collective-permute-start | bytes 688136 | tf_op jit(solution)/shard_map/ppermute | solution.py:80
  170.5 16.3 %collective-permute-done.12.refs_4_ = f32[2,4,128,256]{3,2,1,0:T(8,128)S(1)} collective-permute-done((f32[2,4,128,256]{3,2,1,0:T(8,128)}, f32[2,4,128,256]{3,2,1,0:T(8,128)S(1)}, u32[]{:S(2)}, u32[]{:S(2)}) %collective-permute-start.12) | collective-permute-done | bytes 1048608 | tf_op jit(solution)/shard_map/ppermute | solution.py:80
  186.8 3.3 %collective-permute-done.11.refs_3_ = f32[2,4,128,256]{3,2,1,0:T(8,128)S(1)} collective-permute-done((f32[2,4,128,256]{3,2,1,0:T(8,128)}, f32[2,4,128,256]{3,2,1,0:T(8,128)S(1)}, u32[]{:S(2)}, u32[]{:S(2)}) %collective-permute-start.11) | collective-permute-done | bytes 1048608 | tf_op jit(solution)/shard_map/ppermute | solution.py:80
  191.1 5.6 %shard_map.205 = (f32[4,128,256]{2,1,0:T(8,128)}, f32[4,128,256]{2,1,0:T(8,128)}) custom-call(f32[4,4,128,256]{3,2,1,0:T(8,128)} %get-tuple-element.43.refs_0_, f32[4,4,128,256]{3,2,1,0:T(8,128)} %get-tuple-element.44.refs_1_, f32[4,4,256,256]{3,2,1,0:T(8,128)} %collective-permute-done.4.refs_2_, f32[2,4,128,256]{3,2,1,0:T(8,128)} %copy-done.15, ...), custom_call_target="tpu_custom_call" | custom-call | flops 99999997952 | bytes 100000000 | tf_op jit(solution)/shard_map/pallas_call | solution.py:97
  200.1 2.8 %shard_map.206 = (f32[224,256]{1,0:T(8,128)}, f32[224,256]{1,0:T(8,128)}) custom-call(f32[8,224,256]{2,1,0:T(8,128)} %bitcast.37, f32[2,2,112,256]{3,2,1,0:T(8,128)} %collective-permute-done.2.refs_1_, f32[2,2,112,256]{3,2,1,0:T(8,128)} %collective-permute-done.3.refs_2_, f32[2,112,256]{2,1,0:T(8,128)} %copy-done.21, f32[2,112,256]{2,1,0:T(8,128)} %copy-done.20, ...), custom_call_target="tpu_custom_call" | custom-call | flops 99999997952 | bytes 100000000 | tf_op jit(solution)/shard_map/pallas_call | solution.py:97
  202.9 3.2 %collective-permute-done.15.refs_6_ = f32[4,128,256]{2,1,0:T(8,128)S(1)} collective-permute-done((f32[4,128,256]{2,1,0:T(8,128)}, f32[4,128,256]{2,1,0:T(8,128)S(1)}, u32[]{:S(2)}, u32[]{:S(2)}) %collective-permute-start.15) | collective-permute-done | bytes 524320 | tf_op jit(solution)/shard_map/ppermute | solution.py:80
  206.1 2.4 collective-permute-done.14.refs_5_
  209.3 5.5 %shard_map.207.refs_1_ = f32[4,256,256]{2,1,0:T(8,128)} custom-call(f32[4,4,128,256]{3,2,1,0:T(8,128)} %get-tuple-element.43.refs_0_, f32[4,4,128,256]{3,2,1,0:T(8,128)} %get-tuple-element.44.refs_1_, f32[4,4,256,256]{3,2,1,0:T(8,128)} %collective-permute-done.4.refs_2_, f32[2,4,128,256]{3,2,1,0:T(8,128)} %copy-done.15, f32[2,4,128,256]{3,2,1,0:T(8,128)} %copy-done.14, ...), custom_call_target="tpu_custom_call" | custom-call | flops 99999997952 | bytes 100000000 | tf_op jit(solution)/shard_map/pallas_call | solution.py:97
  214.8 2.5 shard_map.208
  219.3 8.3 %collective-permute-done.17.refs_2_ = f32[2,2,112,256]{3,2,1,0:T(8,128)S(1)} collective-permute-done((f32[2,2,112,256]{3,2,1,0:T(8,128)}, f32[2,2,112,256]{3,2,1,0:T(8,128)S(1)}, u32[]{:S(2)}, u32[]{:S(2)}) %collective-permute-start.17) | collective-permute-done | bytes 458784 | tf_op jit(solution)/shard_map/ppermute | solution.py:80
  229.2 2.5 shard_map.209
  234.8 3.1 %collective-permute-done.19.refs_4_ = f32[2,112,256]{2,1,0:T(8,128)S(1)} collective-permute-done((f32[2,112,256]{2,1,0:T(8,128)}, f32[2,112,256]{2,1,0:T(8,128)S(1)}, u32[]{:S(2)}, u32[]{:S(2)}) %collective-permute-start.19) | collective-permute-done | bytes 229408 | tf_op jit(solution)/shard_map/ppermute | solution.py:80
  240.1 2.7 %shard_map.210 = (f32[224,256]{1,0:T(8,128)}, f32[224,256]{1,0:T(8,128)}) custom-call(f32[8,224,256]{2,1,0:T(8,128)} %bitcast.40, f32[2,2,112,256]{3,2,1,0:T(8,128)} %copy-done.19, f32[2,2,112,256]{3,2,1,0:T(8,128)} %copy-done.18, f32[2,112,256]{2,1,0:T(8,128)} %copy-done.23, f32[2,112,256]{2,1,0:T(8,128)} %copy-done.22, ...), custom_call_target="tpu_custom_call" | custom-call | flops 99999997952 | bytes 100000000 | tf_op jit(solution)/shard_map/pallas_call | solution.py:97
  243.9 5.2 %collective-permute-done.20 = f32[224,256]{1,0:T(8,128)S(1)} collective-permute-done((f32[224,256]{1,0:T(8,128)}, f32[224,256]{1,0:T(8,128)S(1)}, u32[]{:S(2)}, u32[]{:S(2)}) %collective-permute-start.20) | collective-permute-done | bytes 229408 | tf_op jit(solution)/shard_map/ppermute | solution.py:86
  (116 shorter events, 42.3 us)
Async XLA Ops:
  28.4 70.6 %all-reduce.2.cloned.1.call-start = ((), (), s32[]{:S(2)}) async-start(), calls=%async_computation.4 | async-start | bytes 2097152 | tf_op jit(solution)/shard_map/psum | solution.py:185
  29.2 77.9 %reduce-scatter.5.cloned.1.call-start = ((), (), s32[]{:S(2)}) async-start(), calls=%async_computation.5 | async-start | bytes 9175040 | tf_op jit(solution)/shard_map/reduce_scatter | solution.py:90
  29.7 185.0 %reduce-scatter.7.cloned.1.call-start = ((), (), s32[]{:S(2)}) async-start(), calls=%async_computation.6 | async-start | bytes 9175040 | tf_op jit(solution)/shard_map/reduce_scatter | solution.py:90
  38.5 54.3 %collective-permute-start.1 = (f32[2,4,160,256]{3,2,1,0:T(8,128)}, f32[2,4,160,256]{3,2,1,0:T(8,128)}, u32[]{:S(2)}, u32[]{:S(2)}) collective-permute-start(f32[2,4,160,256]{3,2,1,0:T(8,128)} %get-tuple-element.37), channel_id=1, source_target_pairs={{0,12},{1,13},{2,14},{3,15},{4,0},{5,1},{6,2},{7,3},{8,4},{9,5},{1... | collective-permute-start | bytes 3932168 | tf_op jit(solution)/shard_map/ppermute | solution.py:80
  41.6 51.2 %collective-permute-start = (f32[2,4,160,256]{3,2,1,0:T(8,128)}, f32[2,4,160,256]{3,2,1,0:T(8,128)}, u32[]{:S(2)}, u32[]{:S(2)}) collective-permute-start(f32[2,4,160,256]{3,2,1,0:T(8,128)} %get-tuple-element.33.refs_3_), channel_id=1, source_target_pairs={{0,4},{1,5},{2,6},{3,7},{4,8},{5,9},{6,10},{7,11},{8,12},{9,13},{1... | collective-permute-start | bytes 3932168 | tf_op jit(solution)/shard_map/ppermute | solution.py:80
  44.2 9.9 %copy-start.1 = (bf16[1024,224]{1,0:T(8,128)(2,1)S(1)}, bf16[1024,224]{1,0:T(8,128)(2,1)}, u32[]{:S(2)}) copy-start(bf16[1024,224]{1,0:T(8,128)(2,1)} %get-tuple-element.67) | copy-start | bytes 1376260
  52.2 104.0 %collective-permute-start.4 = (f32[4,4,256,256]{3,2,1,0:T(8,128)}, f32[4,4,256,256]{3,2,1,0:T(8,128)}, u32[]{:S(2)}, u32[]{:S(2)}) collective-permute-start(f32[4,4,256,256]{3,2,1,0:T(8,128)} %shard_map.195.refs_3_), channel_id=1, source_target_pairs={{0,16},{1,17},{2,18},{3,19},{4,20},{5,21},{6,22},{7,23},{8,24},{9,... | collective-permute-start | bytes 12582920 | tf_op jit(solution)/shard_map/ppermute | solution.py:86
  68.5 165.2 %reduce-scatter.9.cloned.1.call-start = ((), (), s32[]{:S(2)}) async-start(), calls=%async_computation.7 | async-start | bytes 3276800 | tf_op jit(solution)/shard_map/reduce_scatter | solution.py:90
  69.6 10.7 %copy-start.8 = (s32[4]{0:T(128)S(1)}, s32[4]{0:T(128)}, u32[]{:S(2)}) copy-start(s32[4]{0:T(128)} %constant.158.clone) | copy-start | bytes 52
  69.6 10.7 %copy-start.9 = (s32[4]{0:T(128)S(1)}, s32[4]{0:T(128)}, u32[]{:S(2)}) copy-start(s32[4]{0:T(128)} %constant.157.clone) | copy-start | bytes 52
  89.5 33.2 %collective-permute-start.5 = (f32[2,4,160,256]{3,2,1,0:T(8,128)}, f32[2,4,160,256]{3,2,1,0:T(8,128)}, u32[]{:S(2)}, u32[]{:S(2)}) collective-permute-start(f32[2,4,160,256]{3,2,1,0:T(8,128)} %get-tuple-element.46), channel_id=1, source_target_pairs={{0,4},{1,5},{2,6},{3,7},{4,8},{5,9},{6,10},{7,11},{8,12},{9,13},{1... | collective-permute-start | bytes 3932168 | tf_op jit(solution)/shard_map/ppermute | solution.py:80
  90.5 34.3 %collective-permute-start.6 = (f32[2,4,160,256]{3,2,1,0:T(8,128)}, f32[2,4,160,256]{3,2,1,0:T(8,128)}, u32[]{:S(2)}, u32[]{:S(2)}) collective-permute-start(f32[2,4,160,256]{3,2,1,0:T(8,128)} %get-tuple-element.47), channel_id=1, source_target_pairs={{0,12},{1,13},{2,14},{3,15},{4,0},{5,1},{6,2},{7,3},{8,4},{9,5},{1... | collective-permute-start | bytes 3932168 | tf_op jit(solution)/shard_map/ppermute | solution.py:80
  97.0 53.6 %collective-permute-start.8 = (f32[2,4,160,256]{3,2,1,0:T(8,128)}, f32[2,4,160,256]{3,2,1,0:T(8,128)}, u32[]{:S(2)}, u32[]{:S(2)}) collective-permute-start(f32[2,4,160,256]{3,2,1,0:T(8,128)} %get-tuple-element.48), channel_id=1, source_target_pairs={{0,12},{1,13},{2,14},{3,15},{4,0},{5,1},{6,2},{7,3},{8,4},{9,5},{1... | collective-permute-start | bytes 3932168 | tf_op jit(solution)/shard_map/ppermute | solution.py:80
  99.0 51.8 %collective-permute-start.7 = (f32[2,4,160,256]{3,2,1,0:T(8,128)}, f32[2,4,160,256]{3,2,1,0:T(8,128)}, u32[]{:S(2)}, u32[]{:S(2)}) collective-permute-start(f32[2,4,160,256]{3,2,1,0:T(8,128)} %get-tuple-element.38.refs_3_), channel_id=1, source_target_pairs={{0,4},{1,5},{2,6},{3,7},{4,8},{5,9},{6,10},{7,11},{8,12},{9,13},{1... | collective-permute-start | bytes 3932168 | tf_op jit(solution)/shard_map/ppermute | solution.py:80
  122.7 42.0 %collective-permute-start.3 = (f32[2,2,112,256]{3,2,1,0:T(8,128)}, f32[2,2,112,256]{3,2,1,0:T(8,128)}, u32[]{:S(2)}, u32[]{:S(2)}) collective-permute-start(f32[2,2,112,256]{3,2,1,0:T(8,128)} %get-tuple-element.42), channel_id=1, source_target_pairs={{0,12},{1,13},{2,14},{3,15},{4,0},{5,1},{6,2},{7,3},{8,4},{9,5},{1... | collective-permute-start | bytes 1376264 | tf_op jit(solution)/shard_map/ppermute | solution.py:80
  124.8 40.0 %collective-permute-start.2 = (f32[2,2,112,256]{3,2,1,0:T(8,128)}, f32[2,2,112,256]{3,2,1,0:T(8,128)}, u32[]{:S(2)}, u32[]{:S(2)}) collective-permute-start(f32[2,2,112,256]{3,2,1,0:T(8,128)} %get-tuple-element.41.refs_6_), channel_id=1, source_target_pairs={{0,4},{1,5},{2,6},{3,7},{4,8},{5,9},{6,10},{7,11},{8,12},{9,13},{1... | collective-permute-start | bytes 1376264 | tf_op jit(solution)/shard_map/ppermute | solution.py:80
  156.2 93.9 %reduce-scatter.11.cloned.1.call-start = ((), (), s32[]{:S(2)}) async-start(), calls=%async_computation.8 | async-start | bytes 1310720 | tf_op jit(solution)/shard_map/reduce_scatter | solution.py:90
  161.4 25.4 %collective-permute-start.12 = (f32[2,4,128,256]{3,2,1,0:T(8,128)}, f32[2,4,128,256]{3,2,1,0:T(8,128)S(1)}, u32[]{:S(2)}, u32[]{:S(2)}) collective-permute-start(f32[2,4,128,256]{3,2,1,0:T(8,128)} %get-tuple-element.52), channel_id=1, source_target_pairs={{0,12},{1,13},{2,14},{3,15},{4,0},{5,1},{6,2},{7,3},{8,4},{9,5},{1... | collective-permute-start | bytes 3145736 | tf_op jit(solution)/shard_map/ppermute | solution.py:80
  164.7 25.4 %collective-permute-start.11 = (f32[2,4,128,256]{3,2,1,0:T(8,128)}, f32[2,4,128,256]{3,2,1,0:T(8,128)S(1)}, u32[]{:S(2)}, u32[]{:S(2)}) collective-permute-start(f32[2,4,128,256]{3,2,1,0:T(8,128)} %get-tuple-element.49.refs_3_), channel_id=1, source_target_pairs={{0,4},{1,5},{2,6},{3,7},{4,8},{5,9},{6,10},{7,11},{8,12},{9,13},{1... | collective-permute-start | bytes 3145736 | tf_op jit(solution)/shard_map/ppermute | solution.py:80
  167.3 31.4 %collective-permute-start.10 = (f32[2,112,256]{2,1,0:T(8,128)}, f32[2,112,256]{2,1,0:T(8,128)S(1)}, u32[]{:S(2)}, u32[]{:S(2)}) collective-permute-start(f32[2,112,256]{2,1,0:T(8,128)} %get-tuple-element.51), channel_id=1, source_target_pairs={{0,12},{1,13},{2,14},{3,15},{4,0},{5,1},{6,2},{7,3},{8,4},{9,5},{1... | collective-permute-start | bytes 688136 | tf_op jit(solution)/shard_map/ppermute | solution.py:80
  170.5 28.2 %collective-permute-start.9 = (f32[2,112,256]{2,1,0:T(8,128)}, f32[2,112,256]{2,1,0:T(8,128)S(1)}, u32[]{:S(2)}, u32[]{:S(2)}) collective-permute-start(f32[2,112,256]{2,1,0:T(8,128)} %get-tuple-element.50.refs_5_), channel_id=1, source_target_pairs={{0,4},{1,5},{2,6},{3,7},{4,8},{5,9},{6,10},{7,11},{8,12},{9,13},{1... | collective-permute-start | bytes 688136 | tf_op jit(solution)/shard_map/ppermute | solution.py:80
  196.7 9.4 %collective-permute-start.15 = (f32[4,128,256]{2,1,0:T(8,128)}, f32[4,128,256]{2,1,0:T(8,128)S(1)}, u32[]{:S(2)}, u32[]{:S(2)}) collective-permute-start(f32[4,128,256]{2,1,0:T(8,128)} %get-tuple-element.56), channel_id=1, source_target_pairs={{0,12},{1,13},{2,14},{3,15},{4,0},{5,1},{6,2},{7,3},{8,4},{9,5},{1... | collective-permute-start | bytes 1572872 | tf_op jit(solution)/shard_map/ppermute | solution.py:80
  197.9 10.6 %collective-permute-start.14 = (f32[4,128,256]{2,1,0:T(8,128)}, f32[4,128,256]{2,1,0:T(8,128)S(1)}, u32[]{:S(2)}, u32[]{:S(2)}) collective-permute-start(f32[4,128,256]{2,1,0:T(8,128)} %get-tuple-element.53.refs_5_), channel_id=1, source_target_pairs={{0,4},{1,5},{2,6},{3,7},{4,8},{5,9},{6,10},{7,11},{8,12},{9,13},{1... | collective-permute-start | bytes 1572872 | tf_op jit(solution)/shard_map/ppermute | solution.py:80
  217.2 10.4 %collective-permute-start.17 = (f32[2,2,112,256]{3,2,1,0:T(8,128)}, f32[2,2,112,256]{3,2,1,0:T(8,128)S(1)}, u32[]{:S(2)}, u32[]{:S(2)}) collective-permute-start(f32[2,2,112,256]{3,2,1,0:T(8,128)} %get-tuple-element.58), channel_id=1, source_target_pairs={{0,12},{1,13},{2,14},{3,15},{4,0},{5,1},{6,2},{7,3},{8,4},{9,5},{1... | collective-permute-start | bytes 1376264 | tf_op jit(solution)/shard_map/ppermute | solution.py:80
  217.5 10.7 %collective-permute-start.16 = (f32[2,2,112,256]{3,2,1,0:T(8,128)}, f32[2,2,112,256]{3,2,1,0:T(8,128)S(1)}, u32[]{:S(2)}, u32[]{:S(2)}) collective-permute-start(f32[2,2,112,256]{3,2,1,0:T(8,128)} %get-tuple-element.57.refs_3_), channel_id=1, source_target_pairs={{0,4},{1,5},{2,6},{3,7},{4,8},{5,9},{6,10},{7,11},{8,12},{9,13},{1... | collective-permute-start | bytes 1376264 | tf_op jit(solution)/shard_map/ppermute | solution.py:80
  219.3 23.6 %collective-permute-start.13 = (f32[224,256]{1,0:T(8,128)}, f32[224,256]{1,0:T(8,128)}, u32[]{:S(2)}, u32[]{:S(2)}) collective-permute-start(f32[224,256]{1,0:T(8,128)} %get-tuple-element.55), channel_id=1, source_target_pairs={{0,16},{1,17},{2,18},{3,19},{4,20},{5,21},{6,22},{7,23},{8,24},{9,... | collective-permute-start | bytes 688136 | tf_op jit(solution)/shard_map/ppermute | solution.py:86
  231.7 6.2 %collective-permute-start.19 = (f32[2,112,256]{2,1,0:T(8,128)}, f32[2,112,256]{2,1,0:T(8,128)S(1)}, u32[]{:S(2)}, u32[]{:S(2)}) collective-permute-start(f32[2,112,256]{2,1,0:T(8,128)} %get-tuple-element.60), channel_id=1, source_target_pairs={{0,12},{1,13},{2,14},{3,15},{4,0},{5,1},{6,2},{7,3},{8,4},{9,5},{1... | collective-permute-start | bytes 688136 | tf_op jit(solution)/shard_map/ppermute | solution.py:80
  232.0 7.4 %collective-permute-start.18 = (f32[2,112,256]{2,1,0:T(8,128)}, f32[2,112,256]{2,1,0:T(8,128)S(1)}, u32[]{:S(2)}, u32[]{:S(2)}) collective-permute-start(f32[2,112,256]{2,1,0:T(8,128)} %get-tuple-element.59.refs_5_), channel_id=1, source_target_pairs={{0,4},{1,5},{2,6},{3,7},{4,8},{5,9},{6,10},{7,11},{8,12},{9,13},{1... | collective-permute-start | bytes 688136 | tf_op jit(solution)/shard_map/ppermute | solution.py:80
  234.7 8.2 %copy-start.7 = (f32[224,256]{1,0:T(8,128)S(1)}, f32[224,256]{1,0:T(8,128)}, u32[]{:S(2)}) copy-start(f32[224,256]{1,0:T(8,128)} %get-tuple-element.54.refs_7_) | copy-start | bytes 688132
  234.7 15.3 %collective-permute-start.21 = (f32[320,256]{1,0:T(8,128)S(1)}, f32[320,256]{1,0:T(8,128)S(1)}, u32[]{:S(2)}, u32[]{:S(2)}) collective-permute-start(f32[320,256]{1,0:T(8,128)S(1)} %slice_bitcast_fusion), channel_id=1, source_target_pairs={{0,16},{1,17},{2,18},{3,19},{4,20},{5,21},{6,22},{7,23},{8,24},{9,... | collective-permute-start | bytes 983048 | tf_op jit(solution)/shard_map/ppermute | solution.py:86
  242.8 7.2 %copy-start.5 = (f32[1,640,256]{2,1,0:T(8,128)S(1)}, f32[1,640,256]{2,1,0:T(8,128)}, u32[]{:S(2)}) copy-start(f32[1,640,256]{2,1,0:T(8,128)} %reduce-scatter.9.cloned.1.call-done) | copy-start | bytes 1966084
  242.8 6.2 %collective-permute-start.20 = (f32[224,256]{1,0:T(8,128)}, f32[224,256]{1,0:T(8,128)S(1)}, u32[]{:S(2)}, u32[]{:S(2)}) collective-permute-start(f32[224,256]{1,0:T(8,128)} %get-tuple-element.62), channel_id=1, source_target_pairs={{0,16},{1,17},{2,18},{3,19},{4,20},{5,21},{6,22},{7,23},{8,24},{9,... | collective-permute-start | bytes 688136 | tf_op jit(solution)/shard_map/ppermute | solution.py:86
  (19 other events, 26.3 us)
Sparse Core Ops, SparseCore 0:
  32.3 56.3 all-reduce.1
Sparse Core Ops, SparseCore 1:
  32.2 74.8 reduce-scatter.4
  109.5 72.1 reduce-scatter.6
  184.1 33.5 reduce-scatter.8
  220.2 23.2 reduce-scatter.10

commit v3 on v0

v3 whole, which is shorter than its diff:
```python
import jax
import jax.numpy as jnp
from jax import lax
from jax.experimental import pallas as pl
from jax.experimental.pallas import tpu as pltpu
from jax.sharding import PartitionSpec as P

WIDTH = 256
ROW = 4
STRIP = ROW * WIDTH
STRIPS = 8
A = 416
B = 352
C = 256
X_RINGS = [[16 * z + 4 * y + x for x in range(4)] for z in range(2) for y in range(4)]
COST = pl.CostEstimate(flops=10**10, bytes_accessed=10**7, transcendentals=0)
MIB = 1024 * 1024


def store_blocks(value, out, swapped):
    for x in range(ROW):
        piece = value[:, x * WIDTH : (x + 1) * WIDTH]
        if swapped:
            out[x, 0] = piece
        else:
            out[0, x] = piece


def first_products(inputs, cotangent, place):
    depth, columns = cotangent.shape
    halves = 2
    part = depth // halves

    def body(table, *refs):
        xs, k, out, strips, turned = refs[:halves], *refs[halves:]
        step = pl.program_id(0)

        @pl.when(step == 0)
        def _():
            turned[...] = k[...].T

        value = jnp.dot(turned[:A, :part], xs[0][...], preferred_element_type=jnp.float32)
        value += jnp.dot(turned[:A, part:], xs[1][...], preferred_element_type=jnp.float32)
        store_blocks(value, out, True)
        for s in range(halves):
            strips[step, s * part : (s + 1) * part, :] = xs[s][...]

    at = jnp.arange(STRIPS)
    table = 4 * ((place[0] + at // 4) % 2) + (place[1] + at % 4) % 4
    out, strips, turned = pl.pallas_call(
        body,
        grid_spec=pltpu.PrefetchScalarGridSpec(
            num_scalar_prefetch=1,
            grid=(STRIPS,),
            in_specs=[pl.BlockSpec((part, STRIP), lambda i, table, s=s: (s, table[i])) for s in range(halves)]
            + [pl.BlockSpec((depth, columns), lambda i, table: (0, 0), pipeline_mode=pl.Buffered(1))],
            out_specs=[
                pl.BlockSpec((ROW, 1, A, WIDTH), lambda i, table: (0, i, 0, 0)),
                pl.BlockSpec(memory_space=pltpu.VMEM),
                pl.BlockSpec(memory_space=pltpu.VMEM),
            ],
        ),
        out_shape=[
            jax.ShapeDtypeStruct((ROW, STRIPS, A, WIDTH), jnp.float32),
            pltpu.VMEM((STRIPS, depth, STRIP), inputs.dtype),
            pltpu.VMEM((columns, depth), cotangent.dtype),
        ],
        compiler_params=pltpu.CompilerParams(dimension_semantics=("arbitrary",), vmem_limit_bytes=40 * MIB),
        cost_estimate=COST,
    )(table.astype(jnp.int32), *[inputs] * halves, cotangent)
    return out, pltpu.with_memory_space_constraint(strips, pltpu.VMEM), pltpu.with_memory_space_constraint(
        turned, pltpu.VMEM
    )


def products(strips, turned, count, strip_of, wanted, after):
    def body(x, k, *refs):
        outs = refs[len(after) :]
        step = pl.program_id(0)
        for (low, height, first, number), out in zip(wanted, outs):

            def emit(low=low, height=height, out=out):
                value = jnp.dot(
                    k[low : low + height, :], x[strip_of(step)], preferred_element_type=jnp.float32
                )
                store_blocks(value, out, False)

            if number == count:
                emit()
            else:
                pl.when((step >= first) & (step < first + number))(emit)

    def out_spec(low, height, first, number):
        return pl.BlockSpec(
            (1, ROW, height, WIDTH), lambda i: (jnp.clip(i - first, 0, number - 1), 0, 0, 0)
        )

    return pl.pallas_call(
        body,
        grid=(count,),
        in_specs=[pl.BlockSpec(memory_space=pltpu.VMEM)] * 2 + [pl.BlockSpec(memory_space=pl.ANY)] * len(after),
        out_specs=[out_spec(*w) for w in wanted],
        out_shape=[jax.ShapeDtypeStruct((n, ROW, height, WIDTH), jnp.float32) for _, height, _, n in wanted],
        compiler_params=pltpu.CompilerParams(dimension_semantics=("arbitrary",), vmem_limit_bytes=40 * MIB),
        cost_estimate=COST,
    )(strips, turned, *after)


def combine(body, pieces, shapes, after=()):
    pieces = [p if isinstance(p, tuple) else (p, p.shape, (0,) * p.ndim) for p in pieces]

    def kernel(*refs):
        body(*refs[: len(pieces)], *refs[len(pieces) + len(after) :])

    return pl.pallas_call(
        kernel,
        grid=(1,),
        in_specs=[pl.BlockSpec(block, lambda i, at=at: at) for _, block, at in pieces]
        + [pl.BlockSpec(memory_space=pl.ANY)] * len(after),
        out_specs=[pl.BlockSpec(s, lambda i, at=(0,) * len(s): at) for s in shapes],
        out_shape=[jax.ShapeDtypeStruct(s, jnp.float32) for s in shapes],
        compiler_params=pltpu.CompilerParams(vmem_limit_bytes=60 * MIB),
        cost_estimate=COST,
    )(*[p[0] for p in pieces], *after)


def along_y(array, step):
    return lax.ppermute(
        array, "fsdp", [(f, f // 16 * 16 + (f // 4 + step) % 4 * 4 + f % 4) for f in range(32)]
    )


def along_z(array):
    return lax.ppermute(array, "fsdp", [(f, (f + 16) % 32) for f in range(32)])


def over_x(array):
    return lax.psum_scatter(array, "fsdp", scatter_dimension=0, axis_index_groups=X_RINGS, tiled=True)[0]


def reduce_y(terms, outer, rows, home):
    shape = (outer, rows, WIDTH)
    count = len(terms(0, 0))

    def total(refs):
        value = refs[0][...].reshape(shape)
        for ref in refs[1:]:
            value = value + ref[...].reshape(shape)
        return value

    def first(*refs):
        *groups, up, down = [refs[i * count : (i + 1) * count] for i in range(4)] + list(refs[4 * count :])
        up[0], up[1], down[0], down[1] = [total(g) for g in groups]

    after = yield
    pieces = terms(2, 0) + terms(1, 1) + terms(2, 1) + terms(3, 0)
    up, down = combine(first, pieces, [(2,) + shape] * 2, after)
    up_in, down_in = along_y(up, 1), along_y(down, -1)
    after = yield [up]

    def got(array, n):
        return (array, (1,) + shape, (n, 0, 0, 0))

    def second(*refs):
        refs[-2][...] = total(refs[: count + 1])
        refs[-1][...] = total(refs[count + 1 : -2])

    up, down = combine(
        second, terms(1, 0) + [got(up_in, 0)] + terms(3, 1) + [got(down_in, 0)], [shape] * 2, after
    )
    up_last, down_last = along_y(up, 1), along_y(down, -1)
    after = yield [up]
    shapes, write = home

    def third(*refs):
        n = count + 2
        write(total(refs[:n]), total(refs[n : 2 * n]), *refs[2 * n :])

    pieces = terms(0, 0) + [got(down_in, 1), up_last] + terms(0, 1) + [got(up_in, 1), down_last]
    out = combine(third, pieces, shapes, after)
    yield out


def local(params, momentum, local_params, exps, inputs, cotangent):
    groups = lax.axis_size("rep")
    group = lax.axis_index("rep")
    me = lax.axis_index("fsdp")

    a, strips, turned = first_products(inputs, cotangent, (me // 16, me // 4 % 4))
    a_x = over_x(a).reshape(2, 4, A, WIDTH)
    half = B // 2
    b_low, b_high, c_low = A, A + half, A + B
    b_far = products(
        strips, turned, 2, lambda i: 2 + 4 * i, [(b_low, half, 0, 2), (b_high, half, 0, 2)], [a]
    )
    b_up1, b_down1 = along_y(b_far[0], 1), along_y(b_far[1], -1)
    (c_far,) = products(strips, turned, 4, lambda i: 4 + i, [(c_low, C, 0, 4)], b_far[:1])
    c_z = along_z(c_far)
    b_near = products(
        strips,
        turned,
        4,
        lambda i: 1 + 4 * lax.rem(i, 2) + 2 * (i // 2),
        [(low, half, first, 2) for first in (0, 2) for low in (b_low, b_high)],
        [c_far],
    )
    b_up2, b_down2 = along_y(b_near[1], 1), along_y(b_near[2], -1)
    *b_own, c_near = products(
        strips,
        turned,
        5,
        lambda i: jnp.where(i == 0, 4, i - 1),
        [(b_low, half, 0, 2), (b_high, half, 0, 2), (c_low, C, 1, 4)],
        b_near[:1],
    )

    picked = jnp.sum(jnp.where(jnp.arange(groups) == group, exps, 0))
    scale_up = jnp.full((8, 128), jnp.left_shift(1, picked).astype(jnp.float32))

    def copy(scale, out):
        out[...] = scale[...]

    (scale_late,) = combine(copy, [scale_up], [scale_up.shape], [c_near])
    scale = scale_late[0, 0]
    delta = params - local_params[0].astype(jnp.float32)
    coded = jnp.clip(delta * scale, -448.0, 448.0).astype(jnp.bfloat16)
    total = lax.psum(coded.astype(jnp.float32) / scale, "rep")

    def b_third(near_up, near_down, got_up, got_down, up, down):
        up[...] = near_up[...] + got_up[...]
        down[...] = near_down[...] + got_down[...]

    b_last = combine(b_third, [b_near[0], b_near[3], b_up1, b_down1], [(2, ROW, half, WIDTH)] * 2, [scale_late])
    b_up3, b_down3 = along_y(b_last[0], 1), along_y(b_last[1], -1)

    def b_home(own0, own1, up2, down2, up3, down3, out):
        for z in range(2):
            for x in range(ROW):
                low = B * z
                out[x, low : low + half, :] = own0[1 - z, x] + down2[z, x] + up3[z, x]
                out[x, low + half : low + B, :] = own1[1 - z, x] + up2[z, x] + down3[z, x]

    (b_sum,) = combine(b_home, [*b_own, b_up2, b_down2, b_up3, b_down3], [(ROW, 2 * B, WIDTH)])
    b_x = over_x(b_sum)

    def nesterov(weights, moment, total, new_weights, fresh):
        outer_grad = total[...] / groups
        fresh[...] = 0.9 * moment[...] + outer_grad
        new_weights[...] = weights[...] - 0.7 * (outer_grad + 0.9 * fresh[...])

    def a_terms(dy, h):
        return [(a_x, (2, 1, A // 2, WIDTH), (0, dy, h, 0))]

    def a_home(low, high, keep, cross):
        keep[: A // 2, :], keep[A // 2 :, :] = low[0], high[0]
        cross[: A // 2, :], cross[A // 2 :, :] = low[1], high[1]

    def c_terms(dy, h):
        block = (1, ROW, C // 2, WIDTH)
        return [(c_near, block, (dy, 0, h, 0)), (c_z, block, (dy, 0, h, 0))]

    def c_home(low, high, out):
        out[:, : C // 2, :], out[:, C // 2 :, :] = low, high

    ring_a = reduce_y(a_terms, 2, A // 2, ([(A, WIDTH)] * 2, a_home))
    ring_c = reduce_y(c_terms, ROW, C // 2, ([(ROW, C, WIDTH)], c_home))
    next(ring_a), next(ring_c)
    done = ring_c.send([b_sum])
    done = ring_a.send(done)
    new_params, new_momentum = combine(nesterov, [params, momentum, total], [params.shape] * 2, done)
    done = ring_c.send([new_params])
    done = ring_a.send(done)
    (c_sum,) = ring_c.send(done)
    c_own = over_x(c_sum)
    a_keep, a_cross = ring_a.send([c_sum])
    a_in = along_z(a_cross)
    b_in = along_z(b_x[B:])

    def assemble(keep_a, got_a, keep_b, got_b, own_c, out):
        value = jnp.concatenate([keep_a[...] + got_a[...], keep_b[...] + got_b[...], own_c[...]], axis=0)
        out[0] = value.T

    (kv_grad,) = combine(
        assemble, [a_keep, a_in, (b_x, (B, WIDTH), (0, 0)), b_in, c_own], [(1, WIDTH, A + B + C)]
    )
    return (new_params, new_momentum, kv_grad)


def solution(mesh):
    in_specs = (
        P("fsdp", None),
        P("fsdp", None),
        P("rep", "fsdp", None),
        P(),
        P(("rep", "fsdp"), None),
        P(("rep", "fsdp"), None),
    )
    out_specs = (P("fsdp", None), P("fsdp", None), P("rep", "fsdp", None))
    return jax.shard_map(local, mesh=mesh, in_specs=in_specs, out_specs=out_specs, check_vma=False)
```

time: 421 us -> 264 us (0.63)
  waiting for transfers between devices: 369 us -> 125 us
  Pallas kernels: 0 us -> 71.8 us
  matrix products: 27.1 us -> 0 us
  starting transfers between devices: 0.08 us -> 24.1 us
  local copies, waits for them, and re-layouts: 0.01 us -> 23.7 us
  other arithmetic: 7.28 us -> 2.96 us
    psum x1, waiting for transfers between devices: 369 us -> 0.01 us  [local(): total = lax.psum(coded.astype(jnp.float32) / scale, 'rep')]
    ppermute x0 -> x17, waiting for transfers between devices: none -> 125 us  [the longest x14 101 us: along_y(): lax.ppermute(array, 'fsdp', [(f, f // 16 * 16 + (f // 4 + step) % 4 * 4 +...]
    pallas_call x0 -> x16, Pallas kernels: none -> 71.8 us  [the longest x11 35.2 us: combine(): pl.pallas_call(kernel, grid=(1,), in_specs=[pl.BlockSpec(block, lambda i,...]
    dot_general x1 -> x0, matrix products: 27.1 us -> none  [local(): lax.dot_general(inputs, key_cotangent, (((0,), (0,)), ((), ())), preferre...]
    ppermute x0 -> x17, starting transfers between devices: none -> 23.9 us  [the longest x14 19.9 us: along_y(): lax.ppermute(array, 'fsdp', [(f, f // 16 * 16 + (f // 4 + step) % 4 * 4 +...]
    unnamed x4 -> x36, local copies, waits for them, and re-layouts: 0.01 us -> 20.9 us
  transfers between devices with their start and end apart: 2 -> 21, of which waited for: 1 -> 14; matrix products, arithmetic and copies ran while one was open for 7% -> 2% of each run, Pallas kernels for 0% -> 20%
where the time goes in v3:
time: 264 us
  waiting for transfers between devices  125 us (47%)
  Pallas kernels  71.8 us (27%)
  starting transfers between devices  24.1 us (9%)
  local copies, waits for them, and re-layouts  23.7 us (9%)
  between operations  16 us (6%)
  other arithmetic  2.96 us (1%)
    ppermute x14, waiting for transfers between devices, along_y(): lax.ppermute(array, 'fsdp', [(f, f // 16 * 16 + (f // 4 + step) % 4 * 4 +...  101 us
    pallas_call x11, Pallas kernels, combine(): pl.pallas_call(kernel, grid=(1,), in_specs=[pl.BlockSpec(block, lambda i,...  35.2 us
    ppermute x3, waiting for transfers between devices, along_z(): return lax.ppermute(array, 'fsdp', [(f, (f + 16) % 32) for f in range(32)])  24.6 us
    unnamed x36, local copies, waits for them, and re-layouts  20.9 us
    ppermute x14, starting transfers between devices, along_y(): lax.ppermute(array, 'fsdp', [(f, f // 16 * 16 + (f // 4 + step) % 4 * 4 +...  19.9 us
    pallas_call x4, Pallas kernels, products(): pl.pallas_call(body, grid=(count,), in_specs=[pl.BlockSpec(memory_space=p...  19 us
    pallas_call x1, Pallas kernels, first_products(): pl.pallas_call(body, grid_spec=pltpu.PrefetchScalarGridSpec(num_scalar_pr...  17.6 us
  transfers between devices with their start and end apart: 21, of which 14 were waited for; matrix products, arithmetic and copies ran while one was open for 2% of the time, Pallas kernels for 20%

profile of v3, /device:TPU:0, one launch (start us, length us, event | category | flops | bytes accessed | tf_op | source)
XLA Modules:
  0.0 263.7 jit_solution(15983719288864520527)
XLA Ops:
  8.6 17.6 %shard_map.85 = (f32[4,8,416,256]{3,2,1,0:T(8,128)}, bf16[8,1024,1024]{2,1,0:T(8,128)(2,1)S(1)}, bf16[1024,1024]{1,0:T(8,128)(2,1)S(1)}) custom-call(s32[8]{0:T(128)} %fusion.4.table, bf16[1024,8192]{1,0:T(8,128)(2,1)} %refs_1_.2, bf16[1024,8192]{1,0:T(8,128)(2,1)} %refs_1_.2, bf16[1024,1024]{1,0:T(8,128)(2,1)} %refs_2_.1), custom_call_target="tpu_custom_call" | custom-call | flops 10000000000 | bytes 10000000 | tf_op jit(solution)/shard_map/pallas_call | solution.py:50
  26.2 5.7 %copy-done = bf16[8,1024,1024]{2,1,0:T(8,128)(2,1)} copy-done((bf16[8,1024,1024]{2,1,0:T(8,128)(2,1)}, bf16[8,1024,1024]{2,1,0:T(8,128)(2,1)S(1)}, u32[]{:S(2)}) %copy-start) | copy-done | bytes 16777240
  32.0 5.8 %copy-done.1 = bf16[8,1024,1024]{2,1,0:T(8,128)(2,1)S(1)} copy-done((bf16[8,1024,1024]{2,1,0:T(8,128)(2,1)S(1)}, bf16[8,1024,1024]{2,1,0:T(8,128)(2,1)}, u32[]{:S(2)}) %copy-start.1) | copy-done | bytes 16777240
  37.8 2.8 %shard_map.86 = (f32[2,4,176,256]{3,2,1,0:T(8,128)}, f32[2,4,176,256]{3,2,1,0:T(8,128)}) custom-call(bf16[8,1024,1024]{2,1,0:T(8,128)(2,1)S(1)} %copy-done.1, bf16[1024,1024]{1,0:T(8,128)(2,1)S(1)} %get-tuple-element.30.k, f32[4,8,416,256]{3,2,1,0:T(8,128)} %get-tuple-element.31.refs_0_), custom_call_target="tpu_custom_call" | custom-call | flops 10000000000 | bytes 10000000 | tf_op jit(solution)/shard_map/pallas_call | solution.py:98
  40.6 3.1 %collective-permute-start.4 = (f32[2,4,176,256]{3,2,1,0:T(8,128)}, f32[2,4,176,256]{3,2,1,0:T(8,128)}, u32[]{:S(2)}, u32[]{:S(2)}) collective-permute-start(f32[2,4,176,256]{3,2,1,0:T(8,128)} %get-tuple-element.40), channel_id=1, source_target_pairs={{0,12},{1,13},{2,14},{3,15},{4,0},{5,1},{6,2},{7,3},{8,4},{9,5},{1... | collective-permute-start | bytes 4325384 | tf_op jit(solution)/shard_map/ppermute | solution.py:128
  43.7 4.1 %shard_map.87.refs_0_ = f32[4,4,256,256]{3,2,1,0:T(8,128)} custom-call(bf16[8,1024,1024]{2,1,0:T(8,128)(2,1)S(1)} %copy-done.1, bf16[1024,1024]{1,0:T(8,128)(2,1)S(1)} %get-tuple-element.30.k, f32[2,4,176,256]{3,2,1,0:T(8,128)} %get-tuple-element.32.refs_0_), custom_call_target="tpu_custom_call" | custom-call | flops 10000000000 | bytes 10000000 | tf_op jit(solution)/shard_map/pallas_call | solution.py:98
  49.7 5.5 %shard_map.88 = (f32[2,4,176,256]{3,2,1,0:T(8,128)}, f32[2,4,176,256]{3,2,1,0:T(8,128)}, f32[2,4,176,256]{3,2,1,0:T(8,128)}, f32[2,4,176,256]{3,2,1,0:T(8,128)}) custom-call(bf16[8,1024,1024]{2,1,0:T(8,128)(2,1)S(1)} %copy-done.1, bf16[1024,1024]{1,0:T(8,128)(2,1)S(1)} %get-tuple-element.30.k, f32[4,4,256,256]{3,2,1,0:T(8,128)} %shard_map.87.refs_0_), custom_call_target="tpu_custom_call" | custom-call | flops 10000000000 | bytes 10000000 | tf_op jit(solution)/shard_map/pallas_call | solution.py:98
  59.8 5.9 %copy-done.2 = bf16[8,1024,1024]{2,1,0:T(8,128)(2,1)S(1)} copy-done((bf16[8,1024,1024]{2,1,0:T(8,128)(2,1)S(1)}, bf16[8,1024,1024]{2,1,0:T(8,128)(2,1)}, u32[]{:S(2)}) %copy-start.2) | copy-done | bytes 16777240
  65.7 6.6 %shard_map.89 = (f32[2,4,176,256]{3,2,1,0:T(8,128)}, f32[2,4,176,256]{3,2,1,0:T(8,128)}, f32[4,4,256,256]{3,2,1,0:T(8,128)}) custom-call(bf16[8,1024,1024]{2,1,0:T(8,128)(2,1)S(1)} %copy-done.2, bf16[1024,1024]{1,0:T(8,128)(2,1)S(1)} %get-tuple-element.30.k, f32[2,4,176,256]{3,2,1,0:T(8,128)} %get-tuple-element.33.refs_0_), custom_call_target="tpu_custom_call" | custom-call | flops 10000000000 | bytes 10000000 | tf_op jit(solution)/shard_map/pallas_call | solution.py:98
  76.0 3.7 %collective-permute-done.3.refs_2_ = f32[2,4,176,256]{3,2,1,0:T(8,128)} collective-permute-done((f32[2,4,176,256]{3,2,1,0:T(8,128)}, f32[2,4,176,256]{3,2,1,0:T(8,128)}, u32[]{:S(2)}, u32[]{:S(2)}) %collective-permute-start.3) | collective-permute-done | bytes 1441824 | tf_op jit(solution)/shard_map/ppermute | solution.py:128
  79.8 4.7 %shard_map.91 = (f32[2,4,176,256]{3,2,1,0:T(8,128)}, f32[2,4,176,256]{3,2,1,0:T(8,128)}) custom-call(f32[2,4,176,256]{3,2,1,0:T(8,128)} %get-tuple-element.33.refs_0_, f32[2,4,176,256]{3,2,1,0:T(8,128)} %get-tuple-element.39.refs_1_, f32[2,4,176,256]{3,2,1,0:T(8,128)} %collective-permute-done.3.refs_2_, f32[2,4,176,256]{3,2,1,0:T(8,128)} %collective-permute-done.4.refs_3_, ...), custom_call_target="tpu_custom_call" | custom-call | flops 10000000000 | bytes 10000000 | tf_op jit(solution)/shard_map/pallas_call | solution.py:115
  84.4 3.2 %collective-permute-start.6 = (f32[2,4,176,256]{3,2,1,0:T(8,128)}, f32[2,4,176,256]{3,2,1,0:T(8,128)}, u32[]{:S(2)}, u32[]{:S(2)}) collective-permute-start(f32[2,4,176,256]{3,2,1,0:T(8,128)} %get-tuple-element.42), channel_id=1, source_target_pairs={{0,12},{1,13},{2,14},{3,15},{4,0},{5,1},{6,2},{7,3},{8,4},{9,5},{1... | collective-permute-start | bytes 4325384 | tf_op jit(solution)/shard_map/ppermute | solution.py:128
  90.7 19.8 %collective-permute-done.1.refs_2_ = f32[2,4,176,256]{3,2,1,0:T(8,128)S(1)} collective-permute-done((f32[2,4,176,256]{3,2,1,0:T(8,128)}, f32[2,4,176,256]{3,2,1,0:T(8,128)S(1)}, u32[]{:S(2)}, u32[]{:S(2)}) %collective-permute-start.1) | collective-permute-done | bytes 1441824 | tf_op jit(solution)/shard_map/ppermute | solution.py:128
  110.6 29.5 %collective-permute-done.5.refs_4_ = f32[2,4,176,256]{3,2,1,0:T(8,128)} collective-permute-done((f32[2,4,176,256]{3,2,1,0:T(8,128)}, f32[2,4,176,256]{3,2,1,0:T(8,128)}, u32[]{:S(2)}, u32[]{:S(2)}) %collective-permute-start.5) | collective-permute-done | bytes 1441824 | tf_op jit(solution)/shard_map/ppermute | solution.py:128
  140.1 5.5 %shard_map.92.refs_8_ = f32[4,704,256]{2,1,0:T(8,128)} custom-call(f32[2,4,176,256]{3,2,1,0:T(8,128)} %get-tuple-element.35.refs_0_, f32[2,4,176,256]{3,2,1,0:T(8,128)} %get-tuple-element.36.refs_1_, f32[2,4,176,256]{3,2,1,0:T(8,128)} %copy-done.5, f32[2,4,176,256]{3,2,1,0:T(8,128)} %collective-permute-done.2.refs_3_, ...), custom_call_target="tpu_custom_call" | custom-call | flops 10000000000 | bytes 10000000 | tf_op jit(solution)/shard_map/pallas_call | solution.py:115
  145.7 11.5 %collective-permute-done.refs_1_.refs_3_.refs_5_.refs_7_.refs_4_ = f32[4,4,256,256]{3,2,1,0:T(8,128)} collective-permute-done((f32[4,4,256,256]{3,2,1,0:T(8,128)}, f32[4,4,256,256]{3,2,1,0:T(8,128)}, u32[]{:S(2)}, u32[]{:S(2)}) %collective-permute-start) | collective-permute-done | bytes 4194336 | tf_op jit(solution)/shard_map/ppermute | solution.py:134
  157.2 3.6 %shard_map.93 = (f32[2,4,128,256]{3,2,1,0:T(8,128)}, f32[2,4,128,256]{3,2,1,0:T(8,128)}) custom-call(f32[4,4,256,256]{3,2,1,0:T(8,128)} %get-tuple-element.34.refs_1_.refs_0_.refs_2_.refs_4_.refs_6_.refs_3_, f32[4,4,256,256]{3,2,1,0:T(8,128)} %collective-permute-done.refs_1_.refs_3_.refs_5_.refs_7_.refs_4_, ...), custom_call_target="tpu_custom_call" | custom-call | flops 10000000000 | bytes 10000000 | tf_op jit(solution)/shard_map/pallas_call | solution.py:115
  160.8 2.9 %collective-permute-start.10 = (f32[2,4,128,256]{3,2,1,0:T(8,128)}, f32[2,4,128,256]{3,2,1,0:T(8,128)S(1)}, u32[]{:S(2)}, u32[]{:S(2)}) collective-permute-start(f32[2,4,128,256]{3,2,1,0:T(8,128)} %get-tuple-element.48), channel_id=1, source_target_pairs={{0,12},{1,13},{2,14},{3,15},{4,0},{5,1},{6,2},{7,3},{8,4},{9,5},{1... | collective-permute-start | bytes 3145736 | tf_op jit(solution)/shard_map/ppermute | solution.py:128
  166.4 3.2 %collective-permute-start.7 = (f32[2,2,208,256]{3,2,1,0:T(8,128)}, f32[2,2,208,256]{3,2,1,0:T(8,128)S(1)}, u32[]{:S(2)}, u32[]{:S(2)}) collective-permute-start(f32[2,2,208,256]{3,2,1,0:T(8,128)} %get-tuple-element.47), channel_id=1, source_target_pairs={{0,12},{1,13},{2,14},{3,15},{4,0},{5,1},{6,2},{7,3},{8,4},{9,5},{1... | collective-permute-start | bytes 2555912 | tf_op jit(solution)/shard_map/ppermute | solution.py:128
  169.6 3.4 %shard_map.95 = (f32[256,1024]{1,0:T(8,128)}, f32[256,1024]{1,0:T(8,128)}) custom-call(f32[256,1024]{1,0:T(8,128)} %refs_0_.3, f32[256,1024]{1,0:T(8,128)} %refs_1_.3, f32[256,1024]{1,0:T(8,128)} %all-reduce.2.cloned.1.call-done.refs_2_, f32[2,2,208,256]{3,2,1,0:T(8,128)} %get-tuple-element.44.refs_3_), custom_call_target="tpu_custom_call" | custom-call | flops 10000000000 | bytes 10000000 | tf_op jit(solution)/shard_map/pallas_call | solution.py:115
  173.1 14.6 %collective-permute-done.10.refs_5_.refs_2_ = f32[2,4,128,256]{3,2,1,0:T(8,128)S(1)} collective-permute-done((f32[2,4,128,256]{3,2,1,0:T(8,128)}, f32[2,4,128,256]{3,2,1,0:T(8,128)S(1)}, u32[]{:S(2)}, u32[]{:S(2)}) %collective-permute-start.10) | collective-permute-done | bytes 1048608 | tf_op jit(solution)/shard_map/ppermute | solution.py:128
  187.7 3.6 %collective-permute-done.9.refs_2_.refs_6_ = f32[2,4,128,256]{3,2,1,0:T(8,128)S(1)} collective-permute-done((f32[2,4,128,256]{3,2,1,0:T(8,128)}, f32[2,4,128,256]{3,2,1,0:T(8,128)S(1)}, u32[]{:S(2)}, u32[]{:S(2)}) %collective-permute-start.9) | collective-permute-done | bytes 1048608 | tf_op jit(solution)/shard_map/ppermute | solution.py:128
  192.2 2.9 %shard_map.96 = (f32[4,128,256]{2,1,0:T(8,128)}, f32[4,128,256]{2,1,0:T(8,128)}) custom-call(f32[4,4,256,256]{3,2,1,0:T(8,128)} %get-tuple-element.34.refs_1_.refs_0_.refs_2_.refs_4_.refs_6_.refs_3_, f32[4,4,256,256]{3,2,1,0:T(8,128)} %collective-permute-done.refs_1_.refs_3_.refs_5_.refs_7_.refs_4_, f32[2,4,128,256]{3,2,1,0:T(8,128)} %copy-done.7, ...), custom_call_target="tpu_custom_call" | custom-call | flops 10000000000 | bytes 10000000 | tf_op jit(solution)/shard_map/pallas_call | solution.py:115
  197.2 8.8 %collective-permute-done.7.refs_3_.refs_1_ = f32[2,2,208,256]{3,2,1,0:T(8,128)S(1)} collective-permute-done((f32[2,2,208,256]{3,2,1,0:T(8,128)}, f32[2,2,208,256]{3,2,1,0:T(8,128)S(1)}, u32[]{:S(2)}, u32[]{:S(2)}) %collective-permute-start.7) | collective-permute-done | bytes 852000 | tf_op jit(solution)/shard_map/ppermute | solution.py:128
  206.0 3.7 %collective-permute-done.8.refs_1_.refs_4_ = f32[2,2,208,256]{3,2,1,0:T(8,128)} collective-permute-done((f32[2,2,208,256]{3,2,1,0:T(8,128)}, f32[2,2,208,256]{3,2,1,0:T(8,128)}, u32[]{:S(2)}, u32[]{:S(2)}) %collective-permute-start.8) | collective-permute-done | bytes 852000 | tf_op jit(solution)/shard_map/ppermute | solution.py:128
  212.0 2.8 %collective-permute-done.14.refs_7_ = f32[4,128,256]{2,1,0:T(8,128)S(1)} collective-permute-done((f32[4,128,256]{2,1,0:T(8,128)}, f32[4,128,256]{2,1,0:T(8,128)S(1)}, u32[]{:S(2)}, u32[]{:S(2)}) %collective-permute-start.14) | collective-permute-done | bytes 524320 | tf_op jit(solution)/shard_map/ppermute | solution.py:128
  214.8 3.3 %collective-permute-done.13.refs_3_ = f32[4,128,256]{2,1,0:T(8,128)S(1)} collective-permute-done((f32[4,128,256]{2,1,0:T(8,128)}, f32[4,128,256]{2,1,0:T(8,128)S(1)}, u32[]{:S(2)}, u32[]{:S(2)}) %collective-permute-start.13) | collective-permute-done | bytes 524320 | tf_op jit(solution)/shard_map/ppermute | solution.py:128
  218.9 3.4 %shard_map.98.refs_6_ = f32[4,256,256]{2,1,0:T(8,128)} custom-call(f32[4,4,256,256]{3,2,1,0:T(8,128)} %get-tuple-element.34.refs_1_.refs_0_.refs_2_.refs_4_.refs_6_.refs_3_, f32[4,4,256,256]{3,2,1,0:T(8,128)} %collective-permute-done.refs_1_.refs_3_.refs_5_.refs_7_.refs_4_, f32[2,4,128,256]{3,2,1,0:T(8,128)} %copy-done.6, f32[4,128,256]{2,1,0:T(8,128)} %copy-done.10, ...), custom_call_target="tpu_custom_call" | custom-call | flops 10000000000 | bytes 10000000 | tf_op jit(solution)/shard_map/pallas_call | solution.py:115
  224.4 7.1 %collective-permute-done.12.refs_5_ = f32[2,208,256]{2,1,0:T(8,128)S(1)} collective-permute-done((f32[2,208,256]{2,1,0:T(8,128)S(1)}, f32[2,208,256]{2,1,0:T(8,128)S(1)}, u32[]{:S(2)}, u32[]{:S(2)}) %collective-permute-start.12) | collective-permute-done | bytes 426016 | tf_op jit(solution)/shard_map/ppermute | solution.py:128
  234.0 2.7 %shard_map.99 = (f32[416,256]{1,0:T(8,128)}, f32[416,256]{1,0:T(8,128)}) custom-call(f32[2,4,416,256]{3,2,1,0:T(8,128)} %bitcast.16, f32[2,2,208,256]{3,2,1,0:T(8,128)} %copy-done.8, f32[2,208,256]{2,1,0:T(8,128)} %copy-done.15, f32[2,4,416,256]{3,2,1,0:T(8,128)} %bitcast.17, f32[2,2,208,256]{3,2,1,0:T(8,128)} %collective-permute-done.8.refs_1_.refs_4_, ...), custom_call_target="tpu_custom_call" | custom-call | flops 10000000000 | bytes 10000000 | tf_op jit(solution)/shard_map/pallas_call | solution.py:115
  239.8 13.1 %collective-permute-done.16.refs_3_ = f32[352,256]{1,0:T(8,128)S(1)} collective-permute-done((f32[352,256]{1,0:T(8,128)S(1)}, f32[352,256]{1,0:T(8,128)S(1)}, u32[]{:S(2)}, u32[]{:S(2)}) %collective-permute-start.16) | collective-permute-done | bytes 360480 | tf_op jit(solution)/shard_map/ppermute | solution.py:134
  253.8 2.7 %shard_map.100 = f32[1,256,1024]{2,1,0:T(8,128)} custom-call(f32[416,256]{1,0:T(8,128)} %get-tuple-element.53.refs_0_, f32[416,256]{1,0:T(8,128)} %copy-done.13, f32[704,256]{1,0:T(8,128)} %bitcast.9, f32[352,256]{1,0:T(8,128)} %copy-done.16, f32[256,256]{1,0:T(8,128)} %bitcast.18), custom_call_target="tpu_custom_call" | custom-call | flops 10000000000 | bytes 10000000 | tf_op jit(solution)/shard_map/pallas_call | solution.py:115
  (72 shorter events, 30.7 us)
Async XLA Ops:
  8.0 155.8 %reduce-scatter.4.cloned.1.call-start = ((), (), s32[]{:S(2)}) async-start(), calls=%async_computation.4 | async-start | bytes 17039360 | tf_op jit(solution)/shard_map/reduce_scatter | solution.py:138
  26.2 5.7 %copy-start = (bf16[8,1024,1024]{2,1,0:T(8,128)(2,1)}, bf16[8,1024,1024]{2,1,0:T(8,128)(2,1)S(1)}, u32[]{:S(2)}) copy-start(bf16[8,1024,1024]{2,1,0:T(8,128)(2,1)S(1)} %get-tuple-element.29.x) | copy-start | bytes 50331652
  32.0 137.7 %all-reduce.2.cloned.1.call-start = ((), (), s32[]{:S(2)}) async-start(), calls=%async_computation.3 | async-start | bytes 2097152 | tf_op jit(solution)/shard_map/psum | solution.py:227
  32.0 5.8 %copy-start.1 = (bf16[8,1024,1024]{2,1,0:T(8,128)(2,1)S(1)}, bf16[8,1024,1024]{2,1,0:T(8,128)(2,1)}, u32[]{:S(2)}) copy-start(bf16[8,1024,1024]{2,1,0:T(8,128)(2,1)} %copy-done) | copy-start | bytes 50331652
  40.6 35.4 %collective-permute-start.4 = (f32[2,4,176,256]{3,2,1,0:T(8,128)}, f32[2,4,176,256]{3,2,1,0:T(8,128)}, u32[]{:S(2)}, u32[]{:S(2)}) collective-permute-start(f32[2,4,176,256]{3,2,1,0:T(8,128)} %get-tuple-element.40), channel_id=1, source_target_pairs={{0,12},{1,13},{2,14},{3,15},{4,0},{5,1},{6,2},{7,3},{8,4},{9,5},{1... | collective-permute-start | bytes 4325384 | tf_op jit(solution)/shard_map/ppermute | solution.py:128
  43.7 36.0 %collective-permute-start.3 = (f32[2,4,176,256]{3,2,1,0:T(8,128)}, f32[2,4,176,256]{3,2,1,0:T(8,128)}, u32[]{:S(2)}, u32[]{:S(2)}) collective-permute-start(f32[2,4,176,256]{3,2,1,0:T(8,128)} %get-tuple-element.32.refs_0_), channel_id=1, source_target_pairs={{0,4},{1,5},{2,6},{3,7},{4,8},{5,9},{6,10},{7,11},{8,12},{9,13},{1... | collective-permute-start | bytes 4325384 | tf_op jit(solution)/shard_map/ppermute | solution.py:128
  47.8 10.7 %copy-start.17 = (s32[4]{0:T(128)S(1)}, s32[4]{0:T(128)}, u32[]{:S(2)}) copy-start(s32[4]{0:T(128)} %param.9) | copy-start | bytes 52
  47.8 109.4 %collective-permute-start = (f32[4,4,256,256]{3,2,1,0:T(8,128)}, f32[4,4,256,256]{3,2,1,0:T(8,128)}, u32[]{:S(2)}, u32[]{:S(2)}) collective-permute-start(f32[4,4,256,256]{3,2,1,0:T(8,128)} %shard_map.87.refs_0_), channel_id=1, source_target_pairs={{0,16},{1,17},{2,18},{3,19},{4,20},{5,21},{6,22},{7,23},{8,24},{9,... | collective-permute-start | bytes 12582920 | tf_op jit(solution)/shard_map/ppermute | solution.py:134
  55.3 55.3 %collective-permute-start.1 = (f32[2,4,176,256]{3,2,1,0:T(8,128)}, f32[2,4,176,256]{3,2,1,0:T(8,128)S(1)}, u32[]{:S(2)}, u32[]{:S(2)}) collective-permute-start(f32[2,4,176,256]{3,2,1,0:T(8,128)} %get-tuple-element.37), channel_id=1, source_target_pairs={{0,4},{1,5},{2,6},{3,7},{4,8},{5,9},{6,10},{7,11},{8,12},{9,13},{1... | collective-permute-start | bytes 4325384 | tf_op jit(solution)/shard_map/ppermute | solution.py:128
  55.9 54.7 %collective-permute-start.2 = (f32[2,4,176,256]{3,2,1,0:T(8,128)}, f32[2,4,176,256]{3,2,1,0:T(8,128)}, u32[]{:S(2)}, u32[]{:S(2)}) collective-permute-start(f32[2,4,176,256]{3,2,1,0:T(8,128)} %get-tuple-element.38), channel_id=1, source_target_pairs={{0,12},{1,13},{2,14},{3,15},{4,0},{5,1},{6,2},{7,3},{8,4},{9,5},{1... | collective-permute-start | bytes 4325384 | tf_op jit(solution)/shard_map/ppermute | solution.py:128
  59.8 5.9 %copy-start.2 = (bf16[8,1024,1024]{2,1,0:T(8,128)(2,1)S(1)}, bf16[8,1024,1024]{2,1,0:T(8,128)(2,1)}, u32[]{:S(2)}) copy-start(bf16[8,1024,1024]{2,1,0:T(8,128)(2,1)} %copy-done) | copy-start | bytes 50331652
  79.8 9.1 %copy-start.3 = (f32[256,1024]{1,0:T(8,128)S(1)}, f32[256,1024]{1,0:T(8,128)}, u32[]{:S(2)}) copy-start(f32[256,1024]{1,0:T(8,128)} %refs_0_.3) | copy-start | bytes 3145732
  79.8 9.1 %copy-start.4 = (bf16[1,256,1024]{2,1,0:T(8,128)(2,1)S(1)}, bf16[1,256,1024]{2,1,0:T(8,128)(2,1)}, u32[]{:S(2)}) copy-start(bf16[1,256,1024]{2,1,0:T(8,128)(2,1)} %param.8) | copy-start | bytes 1572868
  84.4 55.7 %collective-permute-start.5 = (f32[2,4,176,256]{3,2,1,0:T(8,128)}, f32[2,4,176,256]{3,2,1,0:T(8,128)}, u32[]{:S(2)}, u32[]{:S(2)}) collective-permute-start(f32[2,4,176,256]{3,2,1,0:T(8,128)} %get-tuple-element.41), channel_id=1, source_target_pairs={{0,4},{1,5},{2,6},{3,7},{4,8},{5,9},{6,10},{7,11},{8,12},{9,13},{1... | collective-permute-start | bytes 4325384 | tf_op jit(solution)/shard_map/ppermute | solution.py:128
  84.4 55.7 %collective-permute-start.6 = (f32[2,4,176,256]{3,2,1,0:T(8,128)}, f32[2,4,176,256]{3,2,1,0:T(8,128)}, u32[]{:S(2)}, u32[]{:S(2)}) collective-permute-start(f32[2,4,176,256]{3,2,1,0:T(8,128)} %get-tuple-element.42), channel_id=1, source_target_pairs={{0,12},{1,13},{2,14},{3,15},{4,0},{5,1},{6,2},{7,3},{8,4},{9,5},{1... | collective-permute-start | bytes 4325384 | tf_op jit(solution)/shard_map/ppermute | solution.py:128
  90.7 147.4 %reduce-scatter.6.cloned.1.call-start = ((), (), s32[]{:S(2)}) async-start(), calls=%async_computation.5 | async-start | bytes 3604480 | tf_op jit(solution)/shard_map/reduce_scatter | solution.py:138
  110.5 29.6 %copy-start.5 = (f32[2,4,176,256]{3,2,1,0:T(8,128)}, f32[2,4,176,256]{3,2,1,0:T(8,128)S(1)}, u32[]{:S(2)}) copy-start(f32[2,4,176,256]{3,2,1,0:T(8,128)S(1)} %collective-permute-done.1.refs_2_) | copy-start | bytes 4325380
  145.7 107.3 %reduce-scatter.8.cloned.1.call-start = ((), (), s32[]{:S(2)}) async-start(), calls=%async_computation.6 | async-start | bytes 1310720 | tf_op jit(solution)/shard_map/reduce_scatter | solution.py:138
  160.8 26.9 %collective-permute-start.10 = (f32[2,4,128,256]{3,2,1,0:T(8,128)}, f32[2,4,128,256]{3,2,1,0:T(8,128)S(1)}, u32[]{:S(2)}, u32[]{:S(2)}) collective-permute-start(f32[2,4,128,256]{3,2,1,0:T(8,128)} %get-tuple-element.48), channel_id=1, source_target_pairs={{0,12},{1,13},{2,14},{3,15},{4,0},{5,1},{6,2},{7,3},{8,4},{9,5},{1... | collective-permute-start | bytes 3145736 | tf_op jit(solution)/shard_map/ppermute | solution.py:128
  163.8 27.5 %collective-permute-start.9 = (f32[2,4,128,256]{3,2,1,0:T(8,128)}, f32[2,4,128,256]{3,2,1,0:T(8,128)S(1)}, u32[]{:S(2)}, u32[]{:S(2)}) collective-permute-start(f32[2,4,128,256]{3,2,1,0:T(8,128)} %get-tuple-element.43.refs_4_), channel_id=1, source_target_pairs={{0,4},{1,5},{2,6},{3,7},{4,8},{5,9},{6,10},{7,11},{8,12},{9,13},{1... | collective-permute-start | bytes 3145736 | tf_op jit(solution)/shard_map/ppermute | solution.py:128
  166.4 39.5 %collective-permute-start.7 = (f32[2,2,208,256]{3,2,1,0:T(8,128)}, f32[2,2,208,256]{3,2,1,0:T(8,128)S(1)}, u32[]{:S(2)}, u32[]{:S(2)}) collective-permute-start(f32[2,2,208,256]{3,2,1,0:T(8,128)} %get-tuple-element.47), channel_id=1, source_target_pairs={{0,12},{1,13},{2,14},{3,15},{4,0},{5,1},{6,2},{7,3},{8,4},{9,5},{1... | collective-permute-start | bytes 2555912 | tf_op jit(solution)/shard_map/ppermute | solution.py:128
  169.6 40.0 %collective-permute-start.8 = (f32[2,2,208,256]{3,2,1,0:T(8,128)}, f32[2,2,208,256]{3,2,1,0:T(8,128)}, u32[]{:S(2)}, u32[]{:S(2)}) collective-permute-start(f32[2,2,208,256]{3,2,1,0:T(8,128)} %get-tuple-element.44.refs_3_), channel_id=1, source_target_pairs={{0,4},{1,5},{2,6},{3,7},{4,8},{5,9},{6,10},{7,11},{8,12},{9,13},{1... | collective-permute-start | bytes 2555912 | tf_op jit(solution)/shard_map/ppermute | solution.py:128
  187.7 3.6 %copy-start.6 = (f32[2,4,128,256]{3,2,1,0:T(8,128)}, f32[2,4,128,256]{3,2,1,0:T(8,128)S(1)}, u32[]{:S(2)}) copy-start(f32[2,4,128,256]{3,2,1,0:T(8,128)S(1)} %collective-permute-done.10.refs_5_.refs_2_) | copy-start | bytes 3145732
  195.1 19.7 %collective-permute-start.14 = (f32[4,128,256]{2,1,0:T(8,128)}, f32[4,128,256]{2,1,0:T(8,128)S(1)}, u32[]{:S(2)}, u32[]{:S(2)}) collective-permute-start(f32[4,128,256]{2,1,0:T(8,128)} %get-tuple-element.52), channel_id=1, source_target_pairs={{0,12},{1,13},{2,14},{3,15},{4,0},{5,1},{6,2},{7,3},{8,4},{9,5},{1... | collective-permute-start | bytes 1572872 | tf_op jit(solution)/shard_map/ppermute | solution.py:128
  195.5 22.6 %collective-permute-start.13 = (f32[4,128,256]{2,1,0:T(8,128)}, f32[4,128,256]{2,1,0:T(8,128)S(1)}, u32[]{:S(2)}, u32[]{:S(2)}) collective-permute-start(f32[4,128,256]{2,1,0:T(8,128)} %get-tuple-element.49.refs_4_), channel_id=1, source_target_pairs={{0,4},{1,5},{2,6},{3,7},{4,8},{5,9},{6,10},{7,11},{8,12},{9,13},{1... | collective-permute-start | bytes 1572872 | tf_op jit(solution)/shard_map/ppermute | solution.py:128
  205.9 3.7 %copy-start.8 = (f32[2,2,208,256]{3,2,1,0:T(8,128)}, f32[2,2,208,256]{3,2,1,0:T(8,128)S(1)}, u32[]{:S(2)}) copy-start(f32[2,2,208,256]{3,2,1,0:T(8,128)S(1)} %collective-permute-done.7.refs_3_.refs_1_) | copy-start | bytes 2555908
  218.9 3.4 %copy-start.12 = (f32[2,208,256]{2,1,0:T(8,128)S(1)}, f32[2,208,256]{2,1,0:T(8,128)}, u32[]{:S(2)}) copy-start(f32[2,208,256]{2,1,0:T(8,128)} %get-tuple-element.51) | copy-start | bytes 1277956
  218.9 4.0 %copy-start.11 = (f32[2,208,256]{2,1,0:T(8,128)S(1)}, f32[2,208,256]{2,1,0:T(8,128)}, u32[]{:S(2)}) copy-start(f32[2,208,256]{2,1,0:T(8,128)} %get-tuple-element.50.refs_8_) | copy-start | bytes 1277956
  222.3 9.2 %collective-permute-start.12 = (f32[2,208,256]{2,1,0:T(8,128)S(1)}, f32[2,208,256]{2,1,0:T(8,128)S(1)}, u32[]{:S(2)}, u32[]{:S(2)}) collective-permute-start(f32[2,208,256]{2,1,0:T(8,128)S(1)} %copy-done.12), channel_id=1, source_target_pairs={{0,12},{1,13},{2,14},{3,15},{4,0},{5,1},{6,2},{7,3},{8,4},{9,5},{1... | collective-permute-start | bytes 1277960 | tf_op jit(solution)/shard_map/ppermute | solution.py:128
  222.9 10.4 %collective-permute-start.11 = (f32[2,208,256]{2,1,0:T(8,128)S(1)}, f32[2,208,256]{2,1,0:T(8,128)S(1)}, u32[]{:S(2)}, u32[]{:S(2)}) collective-permute-start(f32[2,208,256]{2,1,0:T(8,128)S(1)} %copy-done.11), channel_id=1, source_target_pairs={{0,4},{1,5},{2,6},{3,7},{4,8},{5,9},{6,10},{7,11},{8,12},{9,13},{1... | collective-permute-start | bytes 1277960 | tf_op jit(solution)/shard_map/ppermute | solution.py:128
  236.7 16.2 %collective-permute-start.15 = (f32[416,256]{1,0:T(8,128)}, f32[416,256]{1,0:T(8,128)S(1)}, u32[]{:S(2)}, u32[]{:S(2)}) collective-permute-start(f32[416,256]{1,0:T(8,128)} %get-tuple-element.54), channel_id=1, source_target_pairs={{0,16},{1,17},{2,18},{3,19},{4,20},{5,21},{6,22},{7,23},{8,24},{9,... | collective-permute-start | bytes 1277960 | tf_op jit(solution)/shard_map/ppermute | solution.py:134
  239.1 13.8 %collective-permute-start.16 = (f32[352,256]{1,0:T(8,128)S(1)}, f32[352,256]{1,0:T(8,128)S(1)}, u32[]{:S(2)}, u32[]{:S(2)}) collective-permute-start(f32[352,256]{1,0:T(8,128)S(1)} %slice_bitcast_fusion), channel_id=1, source_target_pairs={{0,16},{1,17},{2,18},{3,19},{4,20},{5,21},{6,22},{7,23},{8,24},{9,... | collective-permute-start | bytes 1081352 | tf_op jit(solution)/shard_map/ppermute | solution.py:134
  (7 other events, 9.2 us)
Sparse Core Ops, SparseCore 0:
  32.1 125.4 reduce-scatter.3
  160.1 35.8 reduce-scatter.5
  222.4 22.7 reduce-scatter.7
Sparse Core Ops, SparseCore 1:
  90.8 58.9 all-reduce.1

commit v4 on v0

v4 whole, which is shorter than its diff:
```python
import jax
import jax.numpy as jnp
from jax import lax
from jax.experimental import pallas as pl
from jax.experimental.pallas import tpu as pltpu
from jax.sharding import PartitionSpec as P

WIDTH = 256
ROW = 4
STRIP = ROW * WIDTH
STRIPS = 8
A = 416
B = 352
C = 256
X_RINGS = [[16 * z + 4 * y + x for x in range(4)] for z in range(2) for y in range(4)]
LONG = pl.CostEstimate(flops=5 * 10**10, bytes_accessed=1000, transcendentals=0)
SHORT = pl.CostEstimate(flops=5 * 10**9, bytes_accessed=1000, transcendentals=0)
MIB = 1024 * 1024


def far_products(inputs, cotangent, table, wanted):
    depth, columns = cotangent.shape

    def body(table, x, k, *refs):
        *outs, strips, turned = refs
        step = pl.program_id(0)

        @pl.when(step == 0)
        def _():
            turned[...] = k[...].T

        for (low, height), out in zip(wanted, outs):
            value = jnp.dot(turned[low : low + height, :], x[...], preferred_element_type=jnp.float32)
            for place in range(ROW):
                out[0, (place - table[STRIPS]) & (ROW - 1)] = value[:, place * WIDTH : (place + 1) * WIDTH]
        strips[step] = x[...]

    *outs, strips, turned = pl.pallas_call(
        body,
        grid_spec=pltpu.PrefetchScalarGridSpec(
            num_scalar_prefetch=1,
            grid=(2,),
            in_specs=[
                pl.BlockSpec((depth, STRIP), lambda i, table: (0, table[2 + 4 * i])),
                pl.BlockSpec((depth, columns), lambda i, table: (0, 0), pipeline_mode=pl.Buffered(1)),
            ],
            out_specs=[pl.BlockSpec((1, ROW, height, WIDTH), lambda i, table: (i, 0, 0, 0)) for _, height in wanted]
            + [pl.BlockSpec(memory_space=pltpu.VMEM)] * 2,
        ),
        out_shape=[jax.ShapeDtypeStruct((2, ROW, height, WIDTH), jnp.float32) for _, height in wanted]
        + [pltpu.VMEM((2, depth, STRIP), inputs.dtype), pltpu.VMEM((columns, depth), cotangent.dtype)],
        compiler_params=pltpu.CompilerParams(dimension_semantics=("arbitrary",), vmem_limit_bytes=56 * MIB),
        cost_estimate=LONG,
    )(table, inputs, cotangent)
    return (
        outs,
        pltpu.with_memory_space_constraint(strips, pltpu.VMEM),
        pltpu.with_memory_space_constraint(turned, pltpu.VMEM),
    )


def all_products(inputs, strips, turned, table, low, height, after):
    depth = inputs.shape[0]

    def order(i):
        rest = i - 2 + (i >= 4).astype(jnp.int32) + (i >= 7).astype(jnp.int32)
        return jnp.where(i < 2, 2 + 4 * i, rest)

    def body(table, x, held, k, *refs):
        out = refs[-1]
        step = pl.program_id(0)

        def emit(block):
            value = jnp.dot(k[low : low + height, :], block, preferred_element_type=jnp.float32)
            for place in range(ROW):
                out[place, 0] = value[:, place * WIDTH : (place + 1) * WIDTH]

        pl.when(step < 2)(lambda: emit(held[jnp.minimum(step, 1)]))
        pl.when(step >= 2)(lambda: emit(x[...]))

    return pl.pallas_call(
        body,
        grid_spec=pltpu.PrefetchScalarGridSpec(
            num_scalar_prefetch=1,
            grid=(STRIPS,),
            in_specs=[pl.BlockSpec((depth, STRIP), lambda i, table: (0, table[order(jnp.maximum(i, 2))]))]
            + [pl.BlockSpec(memory_space=pltpu.VMEM)] * 2
            + [pl.BlockSpec(memory_space=pl.ANY)] * len(after),
            out_specs=pl.BlockSpec((ROW, 1, height, WIDTH), lambda i, table: (0, order(i), 0, 0)),
        ),
        out_shape=jax.ShapeDtypeStruct((ROW, STRIPS, height, WIDTH), jnp.float32),
        compiler_params=pltpu.CompilerParams(dimension_semantics=("arbitrary",), vmem_limit_bytes=56 * MIB),
        cost_estimate=LONG,
    )(table, inputs, strips, turned, *after)


def products(inputs, turned, table, count, strip_of, wanted, after):
    depth = inputs.shape[0]

    def body(table, x, k, *refs):
        outs = refs[len(after) :]
        step = pl.program_id(0)
        for (low, height, first, number, _), out in zip(wanted, outs):

            def emit(low=low, height=height, out=out):
                value = jnp.dot(k[low : low + height, :], x[...], preferred_element_type=jnp.float32)
                for place in range(ROW):
                    out[0, (place - table[STRIPS]) & (ROW - 1)] = value[:, place * WIDTH : (place + 1) * WIDTH]

            if number == count:
                emit()
            else:
                pl.when((step >= first) & (step < first + number))(emit)

    def out_spec(low, height, first, number, order):
        def at(i, table):
            n = jnp.clip(i - first, 0, number - 1)
            return (n if order > 0 else number - 1 - n, 0, 0, 0)

        return pl.BlockSpec((1, ROW, height, WIDTH), at)

    return pl.pallas_call(
        body,
        grid_spec=pltpu.PrefetchScalarGridSpec(
            num_scalar_prefetch=1,
            grid=(count,),
            in_specs=[
                pl.BlockSpec((depth, STRIP), lambda i, table: (0, table[strip_of(i)])),
                pl.BlockSpec(memory_space=pltpu.VMEM),
            ]
            + [pl.BlockSpec(memory_space=pl.ANY)] * len(after),
            out_specs=[out_spec(*w) for w in wanted],
        ),
        out_shape=[jax.ShapeDtypeStruct((w[3], ROW, w[1], WIDTH), jnp.float32) for w in wanted],
        compiler_params=pltpu.CompilerParams(dimension_semantics=("arbitrary",), vmem_limit_bytes=60 * MIB),
        cost_estimate=LONG,
    )(table, inputs, turned, *after)


def combine(body, pieces, shapes, after=()):
    pieces = [p if isinstance(p, tuple) else (p, p.shape, (0,) * p.ndim) for p in pieces]

    def kernel(*refs):
        body(*refs[: len(pieces)], *refs[len(pieces) + len(after) :])

    return pl.pallas_call(
        kernel,
        grid=(1,),
        in_specs=[pl.BlockSpec(block, lambda i, at=at: at) for _, block, at in pieces]
        + [pl.BlockSpec(memory_space=pl.ANY)] * len(after),
        out_specs=[pl.BlockSpec(s, lambda i, at=(0,) * len(s): at) for s in shapes],
        out_shape=[jax.ShapeDtypeStruct(s, jnp.float32) for s in shapes],
        compiler_params=pltpu.CompilerParams(vmem_limit_bytes=60 * MIB),
        cost_estimate=SHORT,
    )(*[p[0] for p in pieces], *after)


def along(axis, array, step):
    stride = 1 if axis == "x" else 4
    pairs = [(f, f + ((f // stride + step) % 4 - f // stride % 4) * stride) for f in range(32)]
    return lax.ppermute(array, "fsdp", pairs)


def along_z(array):
    return lax.ppermute(array, "fsdp", [(f, (f + 16) % 32) for f in range(32)])


def over_x(array):
    return lax.psum_scatter(array, "fsdp", scatter_dimension=0, axis_index_groups=X_RINGS, tiled=True)[0]


def reduce_ring(axis, terms, outer, rows):
    shape = (outer, rows, WIDTH)
    count = len(terms(0, 0))

    def total(refs):
        value = refs[0][...].reshape(shape)
        for ref in refs[1:]:
            value = value + ref[...].reshape(shape)
        return value

    def first(*refs):
        up, down = refs[4 * count :]
        up[0], up[1], down[0], down[1] = [total(refs[i * count : (i + 1) * count]) for i in range(4)]

    after = yield
    pieces = terms(2, 0) + terms(1, 1) + terms(2, 1) + terms(3, 0)
    up, down = combine(first, pieces, [(2,) + shape] * 2, after)
    up_in, down_in = along(axis, up, 1), along(axis, down, -1)
    after = yield [up]

    def got(array):
        return [(array, (1,) + shape, (0, 0, 0, 0))]

    def second(*refs):
        up, down = refs[-2:]
        up[...], down[...] = total(refs[: count + 1]), total(refs[count + 1 : -2])

    pieces = terms(1, 0) + got(up_in) + terms(3, 1) + got(down_in)
    up, down = combine(second, pieces, [shape] * 2, after)
    up_last, down_last = along(axis, up, 1), along(axis, down, -1)
    yield [up], lambda half: [(down_in, 1), (up_last, None)] if half == 0 else [(up_in, 1), (down_last, None)]


def settle(low, high, write, shapes, after):
    def body(*refs):
        sums = []
        for group, pieces in ((refs[: len(low)], low), (refs[len(low) : len(low) + len(high)], high)):
            shape = [n for n in pieces[-1][1]]
            value = group[0][...].reshape(shape)
            for ref in group[1:]:
                value = value + ref[...].reshape(shape)
            sums.append(value)
        write(*sums, *refs[len(low) + len(high) :])

    return combine(body, low + high, shapes, after)


def local(params, momentum, local_params, exps, inputs, cotangent):
    groups = lax.axis_size("rep")
    group = lax.axis_index("rep")
    me = lax.axis_index("fsdp")
    at = jnp.arange(STRIPS + 1)
    table = 4 * ((me // 16 + at // 4) % 2) + (me // 4 + at) % 4
    table = jnp.where(at == STRIPS, me % 4, table).astype(jnp.int32)

    half = B // 2
    b_low, b_high, c_low = A, A + half, A + B
    b_far, strips, turned = far_products(inputs, cotangent, table, [(b_low, half), (b_high, half)])
    b_up1, b_down1 = along("y", b_far[0], 1), along("y", b_far[1], -1)
    a = all_products(inputs, strips, turned, table, 0, A, b_far[:1])
    a_x = over_x(a).reshape(2, 4, A, WIDTH)
    (c_far,) = products(inputs, turned, table, 4, lambda i: 4 + i, [(c_low, C, 0, 4, 1)], [a])
    c_z = along_z(c_far)
    b_near = products(
        inputs,
        turned,
        table,
        4,
        lambda i: 1 + 4 * lax.rem(i, 2) + 2 * (i // 2),
        [(low, half, first, 2, 1) for first in (0, 2) for low in (b_low, b_high)],
        [c_far],
    )
    b_up2, b_down2 = along("y", b_near[1], 1), along("y", b_near[2], -1)
    *b_own, c_near = products(
        inputs,
        turned,
        table,
        5,
        lambda i: jnp.where(i == 0, 4, i - 1),
        [(b_low, half, 0, 2, -1), (b_high, half, 0, 2, -1), (c_low, C, 1, 4, 1)],
        b_near[:1],
    )

    def b_third(near_up, near_down, got_up, got_down, up, down):
        up[...] = near_up[...] + got_up[...]
        down[...] = near_down[...] + got_down[...]

    b_last = combine(b_third, [b_near[0], b_near[3], b_up1, b_down1], [(2, ROW, half, WIDTH)] * 2, [c_near])
    b_up3, b_down3 = along("y", b_last[0], 1), along("y", b_last[1], -1)

    def b_terms(dx, h):
        arrays = (b_own[0], b_down2, b_up3) if h == 0 else (b_own[1], b_up2, b_down3)
        return [(array, (2, 1, half, WIDTH), (0, dx, 0, 0)) for array in arrays]

    def c_terms(dy, h):
        block = (1, ROW, C // 2, WIDTH)
        return [(c_near, block, (dy, 0, h, 0)), (c_z, block, (dy, 0, h, 0))]

    def a_terms(dy, h):
        return [(a_x, (2, 1, A // 2, WIDTH), (0, dy, h, 0))]

    def whole(arrived):
        return [
            (array, array.shape, (0,) * 3) if n is None else (array, (1,) + array.shape[1:], (n, 0, 0, 0))
            for array, n in arrived
        ]

    ring_b = reduce_ring("x", b_terms, 2, half)
    ring_c = reduce_ring("y", c_terms, ROW, C // 2)
    ring_a = reduce_ring("y", a_terms, 2, A // 2)
    next(ring_b), next(ring_c), next(ring_a)
    done = ring_b.send(b_last[:1])
    done = ring_c.send(done)

    picked = jnp.sum(jnp.where(jnp.arange(groups) == group, exps, 0))
    scale_up = jnp.full((8, 128), jnp.left_shift(1, picked).astype(jnp.float32))

    def copy(scale, out):
        out[...] = scale[...]

    done = combine(copy, [scale_up], [scale_up.shape], done)
    scale = done[0][0, 0]
    delta = params - local_params[0].astype(jnp.float32)
    coded = jnp.clip(delta * scale, -448.0, 448.0).astype(jnp.bfloat16)
    total = lax.psum(coded.astype(jnp.float32) / scale, "rep")

    done, b_got = ring_b.send(done)
    done, c_got = ring_c.send(done)
    done = ring_a.send(done)

    def c_x_terms(dx, h):
        block = (1, 1, C // 2, WIDTH)
        terms = [(c_near, block, (0, dx, h, 0)), (c_z, block, (0, dx, h, 0))]
        for array, n in c_got(h):
            terms.append((array, block[1:], (dx, 0, 0)) if n is None else (array, block, (n, dx, 0, 0)))
        return terms

    def keep_and_cross(low, high, keep, cross):
        rows = low.shape[1]
        keep[:rows, :], keep[rows:, :] = low[0], high[0]
        cross[:rows, :], cross[rows:, :] = low[1], high[1]

    b_keep, b_cross = settle(
        b_terms(0, 0) + whole(b_got(0)), b_terms(0, 1) + whole(b_got(1)), keep_and_cross, [(B, WIDTH)] * 2, done
    )
    b_in = along_z(b_cross)
    ring_cx = reduce_ring("x", c_x_terms, 1, C // 2)
    next(ring_cx)
    done = ring_cx.send([b_keep])
    done, cx_got = ring_cx.send(done)
    done, a_got = ring_a.send(done)

    def c_home(low, high, out):
        out[: C // 2, :], out[C // 2 :, :] = low[0], high[0]

    (c_own,) = settle(
        c_x_terms(0, 0) + whole(cx_got(0)), c_x_terms(0, 1) + whole(cx_got(1)), c_home, [(C, WIDTH)], done
    )
    a_keep, a_cross = settle(
        a_terms(0, 0) + whole(a_got(0)), a_terms(0, 1) + whole(a_got(1)), keep_and_cross, [(A, WIDTH)] * 2, [c_own]
    )
    a_in = along_z(a_cross)

    def nesterov(weights, moment, total, new_weights, fresh):
        outer_grad = total[...] / groups
        fresh[...] = 0.9 * moment[...] + outer_grad
        new_weights[...] = weights[...] - 0.7 * (outer_grad + 0.9 * fresh[...])

    new_params, new_momentum = combine(nesterov, [params, momentum, total], [params.shape] * 2, [a_keep])

    def assemble(keep_a, got_a, keep_b, got_b, own_c, out):
        value = jnp.concatenate([keep_a[...] + got_a[...], keep_b[...] + got_b[...], own_c[...]], axis=0)
        out[0] = value.T

    (kv_grad,) = combine(
        assemble, [a_keep, a_in, b_keep, b_in, c_own], [(1, WIDTH, A + B + C)], [new_params]
    )
    return (new_params, new_momentum, kv_grad)


def solution(mesh):
    in_specs = (
        P("fsdp", None),
        P("fsdp", None),
        P("rep", "fsdp", None),
        P(),
        P(("rep", "fsdp"), None),
        P(("rep", "fsdp"), None),
    )
    out_specs = (P("fsdp", None), P("fsdp", None), P("rep", "fsdp", None))
    return jax.shard_map(local, mesh=mesh, in_specs=in_specs, out_specs=out_specs, check_vma=False)
```

time: 421 us -> 273 us (0.65)
  waiting for transfers between devices: 369 us -> 113 us
  Pallas kernels: 0 us -> 92.3 us
  starting transfers between devices: 0.08 us -> 33.2 us
  matrix products: 27.1 us -> 0 us
  local copies, waits for them, and re-layouts: 0.01 us -> 13.1 us
  other arithmetic: 7.28 us -> 2.98 us
    psum x1, waiting for transfers between devices: 369 us -> 17.8 us  [local(): total = lax.psum(coded.astype(jnp.float32) / scale, 'rep')]
    ppermute x0 -> x25, waiting for transfers between devices: none -> 95 us  [the longest x22 95 us: along(): return lax.ppermute(array, 'fsdp', pairs)]
    pallas_call x0 -> x20, Pallas kernels: none -> 92.3 us  [the longest x15 42.3 us: combine(): pl.pallas_call(kernel, grid=(1,), in_specs=[pl.BlockSpec(block, lambda i,...]
    ppermute x0 -> x25, starting transfers between devices: none -> 33.1 us  [the longest x22 28.4 us: along(): return lax.ppermute(array, 'fsdp', pairs)]
    dot_general x1 -> x0, matrix products: 27.1 us -> none  [local(): lax.dot_general(inputs, key_cotangent, (((0,), (0,)), ((), ())), preferre...]
    unnamed x4 -> x48, local copies, waits for them, and re-layouts: 0.01 us -> 11.4 us
  transfers between devices with their start and end apart: 2 -> 27, of which waited for: 1 -> 13; matrix products, arithmetic and copies ran while one was open for 7% -> 2% of each run, Pallas kernels for 0% -> 25%
where the time goes in v4:
time: 273 us; the launch traced here: 271 us
  waiting for transfers between devices  113 us (41%)
  Pallas kernels  92.3 us (34%)
  starting transfers between devices  33.2 us (12%)
  between operations  16.2 us (6%)
  local copies, waits for them, and re-layouts  13.1 us (5%)
  other arithmetic  2.98 us (1%)
    ppermute x22, waiting for transfers between devices, along(): return lax.ppermute(array, 'fsdp', pairs)  95 us
    pallas_call x15, Pallas kernels, combine(): pl.pallas_call(kernel, grid=(1,), in_specs=[pl.BlockSpec(block, lambda i,...  42.3 us
    ppermute x22, starting transfers between devices, along(): return lax.ppermute(array, 'fsdp', pairs)  28.4 us
    pallas_call x3, Pallas kernels, products(): pl.pallas_call(body, grid_spec=pltpu.PrefetchScalarGridSpec(num_scalar_pr...  27.1 us
    psum x1, waiting for transfers between devices, local(): total = lax.psum(coded.astype(jnp.float32) / scale, 'rep')  17.8 us
    pallas_call x1, Pallas kernels, all_products(): pl.pallas_call(body, grid_spec=pltpu.PrefetchScalarGridSpec(num_scalar_pr...  16.3 us
    unnamed x48, local copies, waits for them, and re-layouts  11.4 us
    pallas_call x1, Pallas kernels, far_products(): pl.pallas_call(body, grid_spec=pltpu.PrefetchScalarGridSpec(num_scalar_pr...  6.68 us
  transfers between devices with their start and end apart: 27, of which 13 were waited for; matrix products, arithmetic and copies ran while one was open for 2% of the time, Pallas kernels for 25%

profile of v4, /device:TPU:0, one launch (start us, length us, event | category | flops | bytes accessed | tf_op | source)
XLA Modules:
  0.0 270.7 jit_solution(369578599091176770)
XLA Ops:
  8.6 6.7 %shard_map.85 = (f32[2,4,176,256]{3,2,1,0:T(8,128)}, f32[2,4,176,256]{3,2,1,0:T(8,128)}, bf16[2,1024,1024]{2,1,0:T(8,128)(2,1)S(1)}, bf16[1024,1024]{1,0:T(8,128)(2,1)S(1)}) custom-call(s32[9]{0:T(128)} %compare_select_fusion.4.table, bf16[1024,8192]{1,0:T(8,128)(2,1)} %x.9, bf16[1024,1024]{1,0:T(8,128)(2,1)} %k.1), custom_call_target="tpu_custom_call" | custom-call | flops 49999998976 | bytes 1000 | tf_op jit(solution)/shard_map/pallas_call | solution.py:38
  15.3 16.3 %shard_map.86.refs_0_ = f32[4,8,416,256]{3,2,1,0:T(8,128)} custom-call(s32[9]{0:T(128)} %compare_select_fusion.4.table, bf16[1024,8192]{1,0:T(8,128)(2,1)} %x.9, bf16[2,1024,1024]{2,1,0:T(8,128)(2,1)S(1)} %get-tuple-element.39.held, bf16[1024,1024]{1,0:T(8,128)(2,1)S(1)} %get-tuple-element.38.k, f32[2,4,176,256]{3,2,1,0:T(8,128)} %get-tuple-element.40.refs_0_), custom_call_target="tpu_custom_call" | custom-call | flops 49999998976 | bytes 1000 | tf_op jit(solution)/shard_map/pallas_call | solution.py:81
  36.3 7.8 %shard_map.87.refs_0_ = f32[4,4,256,256]{3,2,1,0:T(8,128)} custom-call(s32[9]{0:T(128)} %compare_select_fusion.4.table, bf16[1024,8192]{1,0:T(8,128)(2,1)} %x.9, bf16[1024,1024]{1,0:T(8,128)(2,1)S(1)} %copy-done.1, f32[4,8,416,256]{3,2,1,0:T(8,128)} %shard_map.86.refs_0_), custom_call_target="tpu_custom_call" | custom-call | flops 49999998976 | bytes 1000 | tf_op jit(solution)/shard_map/pallas_call | solution.py:122
  46.0 8.8 %shard_map.88 = (f32[2,4,176,256]{3,2,1,0:T(8,128)}, f32[2,4,176,256]{3,2,1,0:T(8,128)}, f32[2,4,176,256]{3,2,1,0:T(8,128)}, f32[2,4,176,256]{3,2,1,0:T(8,128)}) custom-call(s32[9]{0:T(128)} %compare_select_fusion.4.table, bf16[1024,8192]{1,0:T(8,128)(2,1)} %x.9, bf16[1024,1024]{1,0:T(8,128)(2,1)S(1)} %copy-done.1, f32[4,4,256,256]{3,2,1,0:T(8,128)} %shard_map.87.refs_0_), custom_call_target="tpu_custom_call" | custom-call | flops 49999998976 | bytes 1000 | tf_op jit(solution)/shard_map/pallas_call | solution.py:122
  56.9 10.5 %shard_map.89 = (f32[2,4,176,256]{3,2,1,0:T(8,128)}, f32[2,4,176,256]{3,2,1,0:T(8,128)}, f32[4,4,256,256]{3,2,1,0:T(8,128)}) custom-call(s32[9]{0:T(128)} %compare_select_fusion.4.table, bf16[1024,8192]{1,0:T(8,128)(2,1)} %x.9, bf16[1024,1024]{1,0:T(8,128)(2,1)S(1)} %copy-done.1, f32[2,4,176,256]{3,2,1,0:T(8,128)} %get-tuple-element.41.refs_0_), custom_call_target="tpu_custom_call" | custom-call | flops 49999998976 | bytes 1000 | tf_op jit(solution)/shard_map/pallas_call | solution.py:122
  69.5 4.4 %shard_map.90 = (f32[2,4,176,256]{3,2,1,0:T(8,128)}, f32[2,4,176,256]{3,2,1,0:T(8,128)}) custom-call(f32[2,4,176,256]{3,2,1,0:T(8,128)} %get-tuple-element.41.refs_0_, f32[2,4,176,256]{3,2,1,0:T(8,128)} %get-tuple-element.45.refs_1_, f32[2,4,176,256]{3,2,1,0:T(8,128)} %collective-permute-done.2.refs_2_, f32[2,4,176,256]{3,2,1,0:T(8,128)} %collective-permute-done.3.refs_3_, ...), custom_call_target="tpu_custom_call" | custom-call | flops 5000000000 | bytes 1000 | tf_op jit(solution)/shard_map/pallas_call | solution.py:146
  73.9 2.8 %collective-permute-start.6 = (f32[2,4,176,256]{3,2,1,0:T(8,128)}, f32[2,4,176,256]{3,2,1,0:T(8,128)S(1)}, u32[]{:S(2)}, u32[]{:S(2)}) collective-permute-start(f32[2,4,176,256]{3,2,1,0:T(8,128)} %get-tuple-element.50), channel_id=1, source_target_pairs={{0,12},{1,13},{2,14},{3,15},{4,0},{5,1},{6,2},{7,3},{8,4},{9,5},{1... | collective-permute-start | bytes 4325384 | tf_op jit(solution)/shard_map/ppermute | solution.py:161
  76.7 23.6 %collective-permute-done.1.refs_1_.refs_10_ = f32[2,4,176,256]{3,2,1,0:T(8,128)S(1)} collective-permute-done((f32[2,4,176,256]{3,2,1,0:T(8,128)}, f32[2,4,176,256]{3,2,1,0:T(8,128)S(1)}, u32[]{:S(2)}, u32[]{:S(2)}) %collective-permute-start.1) | collective-permute-done | bytes 1441824 | tf_op jit(solution)/shard_map/ppermute | solution.py:161
  100.3 29.4 %collective-permute-done.6.refs_5_.refs_8_.refs_6_.refs_7_ = f32[2,4,176,256]{3,2,1,0:T(8,128)S(1)} collective-permute-done((f32[2,4,176,256]{3,2,1,0:T(8,128)}, f32[2,4,176,256]{3,2,1,0:T(8,128)S(1)}, u32[]{:S(2)}, u32[]{:S(2)}) %collective-permute-start.6) | collective-permute-done | bytes 1441824 | tf_op jit(solution)/shard_map/ppermute | solution.py:161
  130.9 3.5 %shard_map.91 = (f32[2,2,176,256]{3,2,1,0:T(8,128)}, f32[2,2,176,256]{3,2,1,0:T(8,128)}) custom-call(f32[2,4,176,256]{3,2,1,0:T(8,128)} %get-tuple-element.43.refs_0_.refs_9_, f32[2,4,176,256]{3,2,1,0:T(8,128)} %copy-done.6, f32[2,4,176,256]{3,2,1,0:T(8,128)} %collective-permute-done.4.refs_2_.refs_11_, ...), custom_call_target="tpu_custom_call" | custom-call | flops 5000000000 | bytes 1000 | tf_op jit(solution)/shard_map/pallas_call | solution.py:146
  134.4 2.8 %collective-permute-start.10 = (f32[2,2,176,256]{3,2,1,0:T(8,128)}, f32[2,2,176,256]{3,2,1,0:T(8,128)S(1)}, u32[]{:S(2)}, u32[]{:S(2)}) collective-permute-start(f32[2,2,176,256]{3,2,1,0:T(8,128)} %get-tuple-element.54), channel_id=1, source_target_pairs={{0,3},{1,0},{2,1},{3,2},{4,7},{5,4},{6,5},{7,6},{8,11},{9,8},{10,9... | collective-permute-start | bytes 2162696 | tf_op jit(solution)/shard_map/ppermute | solution.py:161
  137.2 3.6 %shard_map.92 = (f32[2,4,128,256]{3,2,1,0:T(8,128)}, f32[2,4,128,256]{3,2,1,0:T(8,128)}) custom-call(f32[4,4,256,256]{3,2,1,0:T(8,128)} %get-tuple-element.42.refs_4_.refs_0_.refs_2_.refs_6_.refs_3_.refs_8_.refs_12_.refs_5_, f32[4,4,256,256]{3,2,1,0:T(8,128)} %collective-permute-done.refs_1_.refs_3_.refs_5_.refs_7_.refs_4_.refs_9_.refs_13_.refs_6_, ...), custom_call_target="tpu_custom_call" | custom-call | flops 5000000000 | bytes 1000 | tf_op jit(solution)/shard_map/pallas_call | solution.py:146
  140.8 3.0 %collective-permute-start.8 = (f32[2,4,128,256]{3,2,1,0:T(8,128)}, f32[2,4,128,256]{3,2,1,0:T(8,128)S(1)}, u32[]{:S(2)}, u32[]{:S(2)}) collective-permute-start(f32[2,4,128,256]{3,2,1,0:T(8,128)} %get-tuple-element.53), channel_id=1, source_target_pairs={{0,12},{1,13},{2,14},{3,15},{4,0},{5,1},{6,2},{7,3},{8,4},{9,5},{1... | collective-permute-start | bytes 3145736 | tf_op jit(solution)/shard_map/ppermute | solution.py:161
  148.1 20.6 %collective-permute-done.10.refs_7_.refs_3_ = f32[2,2,176,256]{3,2,1,0:T(8,128)S(1)} collective-permute-done((f32[2,2,176,256]{3,2,1,0:T(8,128)}, f32[2,2,176,256]{3,2,1,0:T(8,128)S(1)}, u32[]{:S(2)}, u32[]{:S(2)}) %collective-permute-start.10) | collective-permute-done | bytes 720928 | tf_op jit(solution)/shard_map/ppermute | solution.py:161
  168.7 3.5 %collective-permute-done.9.refs_3_.refs_8_ = f32[2,2,176,256]{3,2,1,0:T(8,128)S(1)} collective-permute-done((f32[2,2,176,256]{3,2,1,0:T(8,128)}, f32[2,2,176,256]{3,2,1,0:T(8,128)S(1)}, u32[]{:S(2)}, u32[]{:S(2)}) %collective-permute-start.9) | collective-permute-done | bytes 720928 | tf_op jit(solution)/shard_map/ppermute | solution.py:161
  173.1 2.8 %shard_map.94 = (f32[2,176,256]{2,1,0:T(8,128)}, f32[2,176,256]{2,1,0:T(8,128)}) custom-call(f32[2,4,176,256]{3,2,1,0:T(8,128)} %get-tuple-element.43.refs_0_.refs_9_, f32[2,4,176,256]{3,2,1,0:T(8,128)} %copy-done.6, f32[2,4,176,256]{3,2,1,0:T(8,128)} %collective-permute-done.4.refs_2_.refs_11_, f32[2,2,176,256]{3,2,1,0:T(8,128)} %copy-done.16, ...), custom_call_target="tpu_custom_call" | custom-call | flops 5000000000 | bytes 1000 | tf_op jit(solution)/shard_map/pallas_call | solution.py:146
  179.8 2.9 %shard_map.95 = (f32[4,128,256]{2,1,0:T(8,128)}, f32[4,128,256]{2,1,0:T(8,128)}) custom-call(f32[4,4,256,256]{3,2,1,0:T(8,128)} %get-tuple-element.42.refs_4_.refs_0_.refs_2_.refs_6_.refs_3_.refs_8_.refs_12_.refs_5_, f32[4,4,256,256]{3,2,1,0:T(8,128)} %collective-permute-done.refs_1_.refs_3_.refs_5_.refs_7_.refs_4_.refs_9_.refs_13_.refs_6_, ...), custom_call_target="tpu_custom_call" | custom-call | flops 5000000000 | bytes 1000 | tf_op jit(solution)/shard_map/pallas_call | solution.py:146
  182.7 2.8 %collective-permute-start.14 = (f32[4,128,256]{2,1,0:T(8,128)}, f32[4,128,256]{2,1,0:T(8,128)S(1)}, u32[]{:S(2)}, u32[]{:S(2)}) collective-permute-start(f32[4,128,256]{2,1,0:T(8,128)} %get-tuple-element.59), channel_id=1, source_target_pairs={{0,12},{1,13},{2,14},{3,15},{4,0},{5,1},{6,2},{7,3},{8,4},{9,5},{1... | collective-permute-start | bytes 1572872 | tf_op jit(solution)/shard_map/ppermute | solution.py:161
  185.5 2.8 %shard_map.96 = (f32[2,2,208,256]{3,2,1,0:T(8,128)}, f32[2,2,208,256]{3,2,1,0:T(8,128)}) custom-call(f32[2,4,416,256]{3,2,1,0:T(8,128)} %bitcast.5, f32[2,4,416,256]{3,2,1,0:T(8,128)} %bitcast.6, f32[2,4,416,256]{3,2,1,0:T(8,128)} %bitcast.7, f32[2,4,416,256]{3,2,1,0:T(8,128)} %bitcast.8, f32[4,128,256]{2,1,0:T(8,128)} %get-tuple-element.56.refs_4_), custom_call_target="tpu_custom_call" | custom-call | flops 5000000000 | bytes 1000 | tf_op jit(solution)/shard_map/pallas_call | solution.py:146
  188.2 3.2 %collective-permute-start.11 = (f32[2,2,208,256]{3,2,1,0:T(8,128)}, f32[2,2,208,256]{3,2,1,0:T(8,128)S(1)}, u32[]{:S(2)}, u32[]{:S(2)}) collective-permute-start(f32[2,2,208,256]{3,2,1,0:T(8,128)} %get-tuple-element.57), channel_id=1, source_target_pairs={{0,12},{1,13},{2,14},{3,15},{4,0},{5,1},{6,2},{7,3},{8,4},{9,5},{1... | collective-permute-start | bytes 2555912 | tf_op jit(solution)/shard_map/ppermute | solution.py:161
  192.2 2.9 %shard_map.97 = (f32[352,256]{1,0:T(8,128)}, f32[352,256]{1,0:T(8,128)}) custom-call(f32[2,4,176,256]{3,2,1,0:T(8,128)} %get-tuple-element.43.refs_0_.refs_9_, f32[2,4,176,256]{3,2,1,0:T(8,128)} %copy-done.6, f32[2,4,176,256]{3,2,1,0:T(8,128)} %collective-permute-done.4.refs_2_.refs_11_, f32[2,2,176,256]{3,2,1,0:T(8,128)} %copy-done.15, ...), custom_call_target="tpu_custom_call" | custom-call | flops 5000000000 | bytes 1000 | tf_op jit(solution)/shard_map/pallas_call | solution.py:146
  195.1 3.0 %collective-permute-done.14.refs_7_.refs_11_.refs_8_.refs_9_ = f32[4,128,256]{2,1,0:T(8,128)S(1)} collective-permute-done((f32[4,128,256]{2,1,0:T(8,128)}, f32[4,128,256]{2,1,0:T(8,128)S(1)}, u32[]{:S(2)}, u32[]{:S(2)}) %collective-permute-start.14) | collective-permute-done | bytes 524320 | tf_op jit(solution)/shard_map/ppermute | solution.py:161
  198.2 3.6 %collective-permute-done.13.refs_3_.refs_15_ = f32[4,128,256]{2,1,0:T(8,128)S(1)} collective-permute-done((f32[4,128,256]{2,1,0:T(8,128)}, f32[4,128,256]{2,1,0:T(8,128)S(1)}, u32[]{:S(2)}, u32[]{:S(2)}) %collective-permute-start.13) | collective-permute-done | bytes 524320 | tf_op jit(solution)/shard_map/ppermute | solution.py:161
  202.5 2.6 shard_map.98
  205.1 2.5 collective-permute-start.18
  212.2 3.9 %collective-permute-done.17.refs_4_.refs_10_ = f32[2,1,128,256]{3,2,1,0:T(8,128)S(1)} collective-permute-done((f32[2,1,128,256]{3,2,1,0:T(8,128)}, f32[2,1,128,256]{3,2,1,0:T(8,128)S(1)}, u32[]{:S(2)}, u32[]{:S(2)}) %collective-permute-start.17) | collective-permute-done | bytes 262176 | tf_op jit(solution)/shard_map/ppermute | solution.py:161
  222.0 2.4 shard_map.100
  229.9 2.8 %collective-permute-done.20.refs_5_ = f32[2,208,256]{2,1,0:T(8,128)S(1)} collective-permute-done((f32[2,208,256]{2,1,0:T(8,128)}, f32[2,208,256]{2,1,0:T(8,128)S(1)}, u32[]{:S(2)}, u32[]{:S(2)}) %collective-permute-start.20) | collective-permute-done | bytes 426016 | tf_op jit(solution)/shard_map/ppermute | solution.py:161
  234.7 2.7 shard_map.102
  238.4 17.8 %all-reduce.2.cloned.1.call-done.refs_2_ = f32[256,1024]{1,0:T(8,128)} async-done(((f32[256,1024]{1,0:T(8,128)}), f32[256,1024]{1,0:T(8,128)}) %all-reduce.2.cloned.1.call-update) | async-done | bytes 1048592 | tf_op jit(solution)/shard_map/psum | solution.py:296
  256.2 3.4 %shard_map.103 = (f32[256,1024]{1,0:T(8,128)}, f32[256,1024]{1,0:T(8,128)}) custom-call(f32[256,1024]{1,0:T(8,128)} %refs_0_.1, f32[256,1024]{1,0:T(8,128)} %refs_1_.1, f32[256,1024]{1,0:T(8,128)} %all-reduce.2.cloned.1.call-done.refs_2_, f32[416,256]{1,0:T(8,128)} %get-tuple-element.68.refs_3_.refs_0_), custom_call_target="tpu_custom_call" | custom-call | flops 5000000000 | bytes 1000 | tf_op jit(solution)/shard_map/pallas_call | solution.py:146
  260.5 2.7 %shard_map.104 = f32[1,256,1024]{2,1,0:T(8,128)} custom-call(f32[416,256]{1,0:T(8,128)} %get-tuple-element.68.refs_3_.refs_0_, f32[416,256]{1,0:T(8,128)} %copy-done.19, f32[352,256]{1,0:T(8,128)} %get-tuple-element.61.refs_16_.refs_2_, f32[352,256]{1,0:T(8,128)} %copy-done.21, f32[256,256]{1,0:T(8,128)} %shard_map.101.refs_6_.refs_4_, ...), custom_call_target="tpu_custom_call" | custom-call | flops 5000000000 | bytes 1000 | tf_op jit(solution)/shard_map/pallas_call | solution.py:146
  (97 shorter events, 42.6 us)
Async XLA Ops:
  8.0 177.5 %reduce-scatter.2.cloned.1.call-start = ((), (), s32[]{:S(2)}) async-start(), calls=%async_computation.2 | async-start | bytes 17039360 | tf_op jit(solution)/shard_map/reduce_scatter | solution.py:169
  32.9 223.3 %all-reduce.2.cloned.1.call-start = ((), (), s32[]{:S(2)}) async-start(), calls=%async_computation.1 | async-start | bytes 2097152 | tf_op jit(solution)/shard_map/psum | solution.py:296
  33.0 36.6 %collective-permute-start.2 = (f32[2,4,176,256]{3,2,1,0:T(8,128)}, f32[2,4,176,256]{3,2,1,0:T(8,128)}, u32[]{:S(2)}, u32[]{:S(2)}) collective-permute-start(f32[2,4,176,256]{3,2,1,0:T(8,128)} %get-tuple-element.40.refs_0_), channel_id=1, source_target_pairs={{0,4},{1,5},{2,6},{3,7},{4,8},{5,9},{6,10},{7,11},{8,12},{9,13},{1... | collective-permute-start | bytes 4325384 | tf_op jit(solution)/shard_map/ppermute | solution.py:161
  34.7 34.8 %collective-permute-start.3 = (f32[2,4,176,256]{3,2,1,0:T(8,128)}, f32[2,4,176,256]{3,2,1,0:T(8,128)}, u32[]{:S(2)}, u32[]{:S(2)}) collective-permute-start(f32[2,4,176,256]{3,2,1,0:T(8,128)} %get-tuple-element.46), channel_id=1, source_target_pairs={{0,12},{1,13},{2,14},{3,15},{4,0},{5,1},{6,2},{7,3},{8,4},{9,5},{1... | collective-permute-start | bytes 4325384 | tf_op jit(solution)/shard_map/ppermute | solution.py:161
  44.0 93.1 %collective-permute-start = (f32[4,4,256,256]{3,2,1,0:T(8,128)}, f32[4,4,256,256]{3,2,1,0:T(8,128)}, u32[]{:S(2)}, u32[]{:S(2)}) collective-permute-start(f32[4,4,256,256]{3,2,1,0:T(8,128)} %shard_map.87.refs_0_), channel_id=1, source_target_pairs={{0,16},{1,17},{2,18},{3,19},{4,20},{5,21},{6,22},{7,23},{8,24},{9,... | collective-permute-start | bytes 12582920 | tf_op jit(solution)/shard_map/ppermute | solution.py:165
  54.9 45.4 %collective-permute-start.1 = (f32[2,4,176,256]{3,2,1,0:T(8,128)}, f32[2,4,176,256]{3,2,1,0:T(8,128)S(1)}, u32[]{:S(2)}, u32[]{:S(2)}) collective-permute-start(f32[2,4,176,256]{3,2,1,0:T(8,128)} %get-tuple-element.44), channel_id=1, source_target_pairs={{0,12},{1,13},{2,14},{3,15},{4,0},{5,1},{6,2},{7,3},{8,4},{9,5},{1... | collective-permute-start | bytes 4325384 | tf_op jit(solution)/shard_map/ppermute | solution.py:161
  56.8 43.6 %collective-permute-start.5 = (f32[2,4,176,256]{3,2,1,0:T(8,128)}, f32[2,4,176,256]{3,2,1,0:T(8,128)}, u32[]{:S(2)}, u32[]{:S(2)}) collective-permute-start(f32[2,4,176,256]{3,2,1,0:T(8,128)} %get-tuple-element.49), channel_id=1, source_target_pairs={{0,4},{1,5},{2,6},{3,7},{4,8},{5,9},{6,10},{7,11},{8,12},{9,13},{1... | collective-permute-start | bytes 4325384 | tf_op jit(solution)/shard_map/ppermute | solution.py:161
  73.9 55.8 %collective-permute-start.6 = (f32[2,4,176,256]{3,2,1,0:T(8,128)}, f32[2,4,176,256]{3,2,1,0:T(8,128)S(1)}, u32[]{:S(2)}, u32[]{:S(2)}) collective-permute-start(f32[2,4,176,256]{3,2,1,0:T(8,128)} %get-tuple-element.50), channel_id=1, source_target_pairs={{0,12},{1,13},{2,14},{3,15},{4,0},{5,1},{6,2},{7,3},{8,4},{9,5},{1... | collective-permute-start | bytes 4325384 | tf_op jit(solution)/shard_map/ppermute | solution.py:161
  76.7 53.1 %collective-permute-start.4 = (f32[2,4,176,256]{3,2,1,0:T(8,128)}, f32[2,4,176,256]{3,2,1,0:T(8,128)}, u32[]{:S(2)}, u32[]{:S(2)}) collective-permute-start(f32[2,4,176,256]{3,2,1,0:T(8,128)} %get-tuple-element.47.refs_12_), channel_id=1, source_target_pairs={{0,4},{1,5},{2,6},{3,7},{4,8},{5,9},{6,10},{7,11},{8,12},{9,13},{1... | collective-permute-start | bytes 4325384 | tf_op jit(solution)/shard_map/ppermute | solution.py:161
  100.3 29.5 %copy-start.6 = (f32[2,4,176,256]{3,2,1,0:T(8,128)}, f32[2,4,176,256]{3,2,1,0:T(8,128)S(1)}, u32[]{:S(2)}) copy-start(f32[2,4,176,256]{3,2,1,0:T(8,128)S(1)} %collective-permute-done.1.refs_1_.refs_10_) | copy-start | bytes 4325380
  134.4 34.3 %collective-permute-start.10 = (f32[2,2,176,256]{3,2,1,0:T(8,128)}, f32[2,2,176,256]{3,2,1,0:T(8,128)S(1)}, u32[]{:S(2)}, u32[]{:S(2)}) collective-permute-start(f32[2,2,176,256]{3,2,1,0:T(8,128)} %get-tuple-element.54), channel_id=1, source_target_pairs={{0,3},{1,0},{2,1},{3,2},{4,7},{5,4},{6,5},{7,6},{8,11},{9,8},{10,9... | collective-permute-start | bytes 2162696 | tf_op jit(solution)/shard_map/ppermute | solution.py:161
  137.2 6.6 %copy-start.23 = (s32[4]{0:T(128)S(1)}, s32[4]{0:T(128)}, u32[]{:S(2)}) copy-start(s32[4]{0:T(128)} %param.9) | copy-start | bytes 52
  137.2 35.0 %collective-permute-start.9 = (f32[2,2,176,256]{3,2,1,0:T(8,128)}, f32[2,2,176,256]{3,2,1,0:T(8,128)S(1)}, u32[]{:S(2)}, u32[]{:S(2)}) collective-permute-start(f32[2,2,176,256]{3,2,1,0:T(8,128)} %get-tuple-element.51.refs_8_), channel_id=1, source_target_pairs={{0,1},{1,2},{2,3},{3,0},{4,5},{5,6},{6,7},{7,4},{8,9},{9,10},{10,1... | collective-permute-start | bytes 2162696 | tf_op jit(solution)/shard_map/ppermute | solution.py:161
  140.8 37.1 %collective-permute-start.8 = (f32[2,4,128,256]{3,2,1,0:T(8,128)}, f32[2,4,128,256]{3,2,1,0:T(8,128)S(1)}, u32[]{:S(2)}, u32[]{:S(2)}) collective-permute-start(f32[2,4,128,256]{3,2,1,0:T(8,128)} %get-tuple-element.53), channel_id=1, source_target_pairs={{0,12},{1,13},{2,14},{3,15},{4,0},{5,1},{6,2},{7,3},{8,4},{9,5},{1... | collective-permute-start | bytes 3145736 | tf_op jit(solution)/shard_map/ppermute | solution.py:161
  143.7 34.1 %collective-permute-start.7 = (f32[2,4,128,256]{3,2,1,0:T(8,128)}, f32[2,4,128,256]{3,2,1,0:T(8,128)S(1)}, u32[]{:S(2)}, u32[]{:S(2)}) collective-permute-start(f32[2,4,128,256]{3,2,1,0:T(8,128)} %get-tuple-element.52.refs_1_), channel_id=1, source_target_pairs={{0,4},{1,5},{2,6},{3,7},{4,8},{5,9},{6,10},{7,11},{8,12},{9,13},{1... | collective-permute-start | bytes 3145736 | tf_op jit(solution)/shard_map/ppermute | solution.py:161
  175.8 15.6 %collective-permute-start.16 = (f32[2,176,256]{2,1,0:T(8,128)}, f32[2,176,256]{2,1,0:T(8,128)S(1)}, u32[]{:S(2)}, u32[]{:S(2)}) collective-permute-start(f32[2,176,256]{2,1,0:T(8,128)} %get-tuple-element.60), channel_id=1, source_target_pairs={{0,3},{1,0},{2,1},{3,2},{4,7},{5,4},{6,5},{7,6},{8,11},{9,8},{10,9... | collective-permute-start | bytes 1081352 | tf_op jit(solution)/shard_map/ppermute | solution.py:161
  176.8 14.7 %collective-permute-start.15 = (f32[2,176,256]{2,1,0:T(8,128)}, f32[2,176,256]{2,1,0:T(8,128)}, u32[]{:S(2)}, u32[]{:S(2)}) collective-permute-start(f32[2,176,256]{2,1,0:T(8,128)} %get-tuple-element.55.refs_6_), channel_id=1, source_target_pairs={{0,1},{1,2},{2,3},{3,0},{4,5},{5,6},{6,7},{7,4},{8,9},{9,10},{10,1... | collective-permute-start | bytes 1081352 | tf_op jit(solution)/shard_map/ppermute | solution.py:161
  182.7 15.5 %collective-permute-start.14 = (f32[4,128,256]{2,1,0:T(8,128)}, f32[4,128,256]{2,1,0:T(8,128)S(1)}, u32[]{:S(2)}, u32[]{:S(2)}) collective-permute-start(f32[4,128,256]{2,1,0:T(8,128)} %get-tuple-element.59), channel_id=1, source_target_pairs={{0,12},{1,13},{2,14},{3,15},{4,0},{5,1},{6,2},{7,3},{8,4},{9,5},{1... | collective-permute-start | bytes 1572872 | tf_op jit(solution)/shard_map/ppermute | solution.py:161
  185.5 16.3 %collective-permute-start.13 = (f32[4,128,256]{2,1,0:T(8,128)}, f32[4,128,256]{2,1,0:T(8,128)S(1)}, u32[]{:S(2)}, u32[]{:S(2)}) collective-permute-start(f32[4,128,256]{2,1,0:T(8,128)} %get-tuple-element.56.refs_4_), channel_id=1, source_target_pairs={{0,4},{1,5},{2,6},{3,7},{4,8},{5,9},{6,10},{7,11},{8,12},{9,13},{1... | collective-permute-start | bytes 1572872 | tf_op jit(solution)/shard_map/ppermute | solution.py:161
  188.2 32.8 %collective-permute-start.11 = (f32[2,2,208,256]{3,2,1,0:T(8,128)}, f32[2,2,208,256]{3,2,1,0:T(8,128)S(1)}, u32[]{:S(2)}, u32[]{:S(2)}) collective-permute-start(f32[2,2,208,256]{3,2,1,0:T(8,128)} %get-tuple-element.57), channel_id=1, source_target_pairs={{0,12},{1,13},{2,14},{3,15},{4,0},{5,1},{6,2},{7,3},{8,4},{9,5},{1... | collective-permute-start | bytes 2555912 | tf_op jit(solution)/shard_map/ppermute | solution.py:161
  191.5 29.5 %collective-permute-start.12 = (f32[2,2,208,256]{3,2,1,0:T(8,128)}, f32[2,2,208,256]{3,2,1,0:T(8,128)}, u32[]{:S(2)}, u32[]{:S(2)}) collective-permute-start(f32[2,2,208,256]{3,2,1,0:T(8,128)} %get-tuple-element.58.refs_10_), channel_id=1, source_target_pairs={{0,4},{1,5},{2,6},{3,7},{4,8},{5,9},{6,10},{7,11},{8,12},{9,13},{1... | collective-permute-start | bytes 2555912 | tf_op jit(solution)/shard_map/ppermute | solution.py:161
  202.5 5.0 %copy-start.10 = (f32[256,1024]{1,0:T(8,128)S(1)}, f32[256,1024]{1,0:T(8,128)}, u32[]{:S(2)}) copy-start(f32[256,1024]{1,0:T(8,128)} %refs_0_.1) | copy-start | bytes 3145732
  202.5 5.0 %copy-start.11 = (bf16[1,256,1024]{2,1,0:T(8,128)(2,1)S(1)}, bf16[1,256,1024]{2,1,0:T(8,128)(2,1)}, u32[]{:S(2)}) copy-start(bf16[1,256,1024]{2,1,0:T(8,128)(2,1)} %param.8) | copy-start | bytes 1572868
  205.1 7.1 %collective-permute-start.18 = (f32[2,1,128,256]{3,2,1,0:T(8,128)}, f32[2,1,128,256]{3,2,1,0:T(8,128)S(1)}, u32[]{:S(2)}, u32[]{:S(2)}) collective-permute-start(f32[2,1,128,256]{3,2,1,0:T(8,128)} %get-tuple-element.63), channel_id=1, source_target_pairs={{0,3},{1,0},{2,1},{3,2},{4,7},{5,4},{6,5},{7,6},{8,11},{9,8},{10,9... | collective-permute-start | bytes 786440 | tf_op jit(solution)/shard_map/ppermute | solution.py:161
  207.6 8.5 %collective-permute-start.17 = (f32[2,1,128,256]{3,2,1,0:T(8,128)}, f32[2,1,128,256]{3,2,1,0:T(8,128)S(1)}, u32[]{:S(2)}, u32[]{:S(2)}) collective-permute-start(f32[2,1,128,256]{3,2,1,0:T(8,128)} %get-tuple-element.62.refs_10_), channel_id=1, source_target_pairs={{0,1},{1,2},{2,3},{3,0},{4,5},{5,6},{6,7},{7,4},{8,9},{9,10},{10,1... | collective-permute-start | bytes 786440 | tf_op jit(solution)/shard_map/ppermute | solution.py:161
  209.4 50.2 %collective-permute-start.24 = (f32[352,256]{1,0:T(8,128)S(1)}, f32[352,256]{1,0:T(8,128)S(1)}, u32[]{:S(2)}, u32[]{:S(2)}) collective-permute-start(f32[352,256]{1,0:T(8,128)S(1)} %copy-done.20), channel_id=1, source_target_pairs={{0,16},{1,17},{2,18},{3,19},{4,20},{5,21},{6,22},{7,23},{8,24},{9,... | collective-permute-start | bytes 1081352 | tf_op jit(solution)/shard_map/ppermute | solution.py:165
  212.2 3.9 %copy-start.8 = (f32[2,1,128,256]{3,2,1,0:T(8,128)}, f32[2,1,128,256]{3,2,1,0:T(8,128)S(1)}, u32[]{:S(2)}) copy-start(f32[2,1,128,256]{3,2,1,0:T(8,128)S(1)} %collective-permute-done.18.refs_9_.refs_4_) | copy-start | bytes 786436
  219.0 7.5 %collective-permute-start.22 = (f32[1,128,256]{2,1,0:T(8,128)}, f32[1,128,256]{2,1,0:T(8,128)S(1)}, u32[]{:S(2)}, u32[]{:S(2)}) collective-permute-start(f32[1,128,256]{2,1,0:T(8,128)} %get-tuple-element.67), channel_id=1, source_target_pairs={{0,3},{1,0},{2,1},{3,2},{4,7},{5,4},{6,5},{7,6},{8,11},{9,8},{10,9... | collective-permute-start | bytes 393224 | tf_op jit(solution)/shard_map/ppermute | solution.py:161
  219.3 7.1 %collective-permute-start.21 = (f32[1,128,256]{2,1,0:T(8,128)}, f32[1,128,256]{2,1,0:T(8,128)S(1)}, u32[]{:S(2)}, u32[]{:S(2)}) collective-permute-start(f32[1,128,256]{2,1,0:T(8,128)} %get-tuple-element.64.refs_4_), channel_id=1, source_target_pairs={{0,1},{1,2},{2,3},{3,0},{4,5},{5,6},{6,7},{7,4},{8,9},{9,10},{10,1... | collective-permute-start | bytes 393224 | tf_op jit(solution)/shard_map/ppermute | solution.py:161
  224.4 8.3 %collective-permute-start.20 = (f32[2,208,256]{2,1,0:T(8,128)}, f32[2,208,256]{2,1,0:T(8,128)S(1)}, u32[]{:S(2)}, u32[]{:S(2)}) collective-permute-start(f32[2,208,256]{2,1,0:T(8,128)} %get-tuple-element.66), channel_id=1, source_target_pairs={{0,12},{1,13},{2,14},{3,15},{4,0},{5,1},{6,2},{7,3},{8,4},{9,5},{1... | collective-permute-start | bytes 1277960 | tf_op jit(solution)/shard_map/ppermute | solution.py:161
  224.4 9.5 %collective-permute-start.19 = (f32[2,208,256]{2,1,0:T(8,128)}, f32[2,208,256]{2,1,0:T(8,128)S(1)}, u32[]{:S(2)}, u32[]{:S(2)}) collective-permute-start(f32[2,208,256]{2,1,0:T(8,128)} %get-tuple-element.65.refs_12_), channel_id=1, source_target_pairs={{0,4},{1,5},{2,6},{3,7},{4,8},{5,9},{6,10},{7,11},{8,12},{9,13},{1... | collective-permute-start | bytes 1277960 | tf_op jit(solution)/shard_map/ppermute | solution.py:161
  237.4 22.3 %collective-permute-start.23 = (f32[416,256]{1,0:T(8,128)}, f32[416,256]{1,0:T(8,128)S(1)}, u32[]{:S(2)}, u32[]{:S(2)}) collective-permute-start(f32[416,256]{1,0:T(8,128)} %get-tuple-element.71), channel_id=1, source_target_pairs={{0,16},{1,17},{2,18},{3,19},{4,20},{5,21},{6,22},{7,23},{8,24},{9,... | collective-permute-start | bytes 1277960 | tf_op jit(solution)/shard_map/ppermute | solution.py:165
  (19 other events, 25.7 us)
Sparse Core Ops, SparseCore 0:
  33.0 140.8 reduce-scatter.1
Sparse Core Ops, SparseCore 1:
  209.5 46.7 all-reduce.1

commit v5 on v4

--- a/solution.py
+++ b/solution.py
@@ -13,85 +13,91 @@
 B = 352
 C = 256
 X_RINGS = [[16 * z + 4 * y + x for x in range(4)] for z in range(2) for y in range(4)]
-LONG = pl.CostEstimate(flops=5 * 10**10, bytes_accessed=1000, transcendentals=0)
-SHORT = pl.CostEstimate(flops=5 * 10**9, bytes_accessed=1000, transcendentals=0)
+LONG = pl.CostEstimate(flops=2 * 10**10, bytes_accessed=1000, transcendentals=0)
+SHORT = pl.CostEstimate(flops=4 * 10**9, bytes_accessed=1000, transcendentals=0)
 MIB = 1024 * 1024
 
 
-def far_products(inputs, cotangent, table, wanted):
+def all_products(inputs, cotangent, table, height):
     depth, columns = cotangent.shape
 
-    def body(table, x, k, *refs):
-        *outs, strips, turned = refs
+    def body(table, x, k, out, turned):
         step = pl.program_id(0)
 
         @pl.when(step == 0)
         def _():
             turned[...] = k[...].T
 
-        for (low, height), out in zip(wanted, outs):
-            value = jnp.dot(turned[low : low + height, :], x[...], preferred_element_type=jnp.float32)
-            for place in range(ROW):
-                out[0, (place - table[STRIPS]) & (ROW - 1)] = value[:, place * WIDTH : (place + 1) * WIDTH]
-        strips[step] = x[...]
-
-    *outs, strips, turned = pl.pallas_call(
+        value = jnp.dot(turned[:height, :], x[...], preferred_element_type=jnp.float32)
+        for place in range(ROW):
+            out[place, 0] = value[:, place * WIDTH : (place + 1) * WIDTH]
+
+    out, turned = pl.pallas_call(
         body,
         grid_spec=pltpu.PrefetchScalarGridSpec(
             num_scalar_prefetch=1,
-            grid=(2,),
+            grid=(STRIPS,),
             in_specs=[
-                pl.BlockSpec((depth, STRIP), lambda i, table: (0, table[2 + 4 * i])),
+                pl.BlockSpec((depth, STRIP), lambda i, table: (0, table[i])),
                 pl.BlockSpec((depth, columns), lambda i, table: (0, 0), pipeline_mode=pl.Buffered(1)),
             ],
-            out_specs=[pl.BlockSpec((1, ROW, height, WIDTH), lambda i, table: (i, 0, 0, 0)) for _, height in wanted]
-            + [pl.BlockSpec(memory_space=pltpu.VMEM)] * 2,
+            out_specs=[
+                pl.BlockSpec((ROW, 1, height, WIDTH), lambda i, table: (0, i, 0, 0)),
+                pl.BlockSpec(memory_space=pltpu.VMEM),
+            ],
         ),
-        out_shape=[jax.ShapeDtypeStruct((2, ROW, height, WIDTH), jnp.float32) for _, height in wanted]
-        + [pltpu.VMEM((2, depth, STRIP), inputs.dtype), pltpu.VMEM((columns, depth), cotangent.dtype)],
-        compiler_params=pltpu.CompilerParams(dimension_semantics=("arbitrary",), vmem_limit_bytes=56 * MIB),
+        out_shape=[
+            jax.ShapeDtypeStruct((ROW, STRIPS, height, WIDTH), jnp.float32),
+            pltpu.VMEM((columns, depth), cotangent.dtype),
+        ],
+        compiler_params=pltpu.CompilerParams(dimension_semantics=("arbitrary",), vmem_limit_bytes=60 * MIB),
         cost_estimate=LONG,
     )(table, inputs, cotangent)
-    return (
-        outs,
-        pltpu.with_memory_space_constraint(strips, pltpu.VMEM),
-        pltpu.with_memory_space_constraint(turned, pltpu.VMEM),
-    )
-
-
-def all_products(inputs, strips, turned, table, low, height, after):
+    return out, pltpu.with_memory_space_constraint(turned, pltpu.VMEM)
+
+
+def crossing_products(inputs, turned, table, low, half, after):
     depth = inputs.shape[0]
 
-    def order(i):
-        rest = i - 2 + (i >= 4).astype(jnp.int32) + (i >= 7).astype(jnp.int32)
-        return jnp.where(i < 2, 2 + 4 * i, rest)
-
-    def body(table, x, held, k, *refs):
-        out = refs[-1]
+    def body(table, x, k, *refs):
+        soon, late = refs[-2:]
         step = pl.program_id(0)
 
-        def emit(block):
-            value = jnp.dot(k[low : low + height, :], block, preferred_element_type=jnp.float32)
+        def emit(h, out, n):
+            value = jnp.dot(k[low + h * half : low + (h + 1) * half, :], x[...], preferred_element_type=jnp.float32)
             for place in range(ROW):
-                out[place, 0] = value[:, place * WIDTH : (place + 1) * WIDTH]
-
-        pl.when(step < 2)(lambda: emit(held[jnp.minimum(step, 1)]))
-        pl.when(step >= 2)(lambda: emit(x[...]))
-
+                out[n, (place - table[STRIPS]) & (ROW - 1)] = value[:, place * WIDTH : (place + 1) * WIDTH]
+
+        for at, first, second in ((0, soon, soon), (1, late, soon), (2, soon, late), (3, late, late)):
+
+            @pl.when(step == at)
+            def _(at=at, first=first, second=second):
+                emit(0, first, 1 if at == 2 else 0)
+                emit(1, second, 0 if at == 1 else 1)
+
+    block = (2, ROW, half, WIDTH)
     return pl.pallas_call(
         body,
         grid_spec=pltpu.PrefetchScalarGridSpec(
             num_scalar_prefetch=1,
-            grid=(STRIPS,),
-            in_specs=[pl.BlockSpec((depth, STRIP), lambda i, table: (0, table[order(jnp.maximum(i, 2))]))]
-            + [pl.BlockSpec(memory_space=pltpu.VMEM)] * 2
+            grid=(4,),
+            in_specs=[
+                pl.BlockSpec(
+                    (depth, STRIP),
+                    lambda i, table: (0, table[4 + jnp.where(i == 0, 2, jnp.where(i == 3, 0, 2 * i - 1))]),
+                ),
+                pl.BlockSpec(memory_space=pltpu.VMEM),
+            ]
             + [pl.BlockSpec(memory_space=pl.ANY)] * len(after),
-            out_specs=pl.BlockSpec((ROW, 1, height, WIDTH), lambda i, table: (0, order(i), 0, 0)),
+            out_specs=[
+                pl.BlockSpec(block, lambda i, table: (jnp.minimum(i, 1), 0, 0, 0)),
+                pl.BlockSpec(block, lambda i, table: (i // 3, 0, 0, 0)),
+            ],
         ),
-        out_shape=jax.ShapeDtypeStruct((ROW, STRIPS, height, WIDTH), jnp.float32),
-        compiler_params=pltpu.CompilerParams(dimension_semantics=("arbitrary",), vmem_limit_bytes=56 * MIB),
+        out_shape=[jax.ShapeDtypeStruct((4, ROW, half, WIDTH), jnp.float32)] * 2,
+        compiler_params=pltpu.CompilerParams(dimension_semantics=("arbitrary",), vmem_limit_bytes=60 * MIB),
         cost_estimate=LONG,
-    )(table, inputs, strips, turned, *after)
+    )(table, inputs, turned, *after)
 
 
 def products(inputs, turned, table, count, strip_of, wanted, after):
@@ -224,14 +230,29 @@
     table = 4 * ((me // 16 + at // 4) % 2) + (me // 4 + at) % 4
     table = jnp.where(at == STRIPS, me % 4, table).astype(jnp.int32)
 
+    picked = jnp.sum(jnp.where(jnp.arange(groups) == group, exps, 0))
+    scale_up = jnp.left_shift(1, picked).astype(jnp.float32)
+    delta = params - local_params[0].astype(jnp.float32)
+    coded = jnp.clip(delta * scale_up, -448.0, 448.0).astype(jnp.bfloat16)
+    total = lax.psum(coded.astype(jnp.float32) / scale_up, "rep")
+
     half = B // 2
     b_low, b_high, c_low = A, A + half, A + B
-    b_far, strips, turned = far_products(inputs, cotangent, table, [(b_low, half), (b_high, half)])
+    a, turned = all_products(inputs, cotangent, table, A)
+    a_x = over_x(a).reshape(2, 4, A, WIDTH)
+    b_far = products(
+        inputs,
+        turned,
+        table,
+        2,
+        lambda i: 2 + 4 * i,
+        [(b_low, half, 0, 2, 1), (b_high, half, 0, 2, 1)],
+        [a],
+    )
     b_up1, b_down1 = along("y", b_far[0], 1), along("y", b_far[1], -1)
-    a = all_products(inputs, strips, turned, table, 0, A, b_far[:1])
-    a_x = over_x(a).reshape(2, 4, A, WIDTH)
-    (c_far,) = products(inputs, turned, table, 4, lambda i: 4 + i, [(c_low, C, 0, 4, 1)], [a])
-    c_z = along_z(c_far)
+    c_far = crossing_products(inputs, turned, table, c_low, C // 2, b_far[:1])
+    c_soon, c_late = along_z(c_far[0]), along_z(c_far[1])
+    c_places = {(2, 0): 0, (2, 1): 1, (1, 1): 2, (3, 0): 3, (1, 0): 4, (3, 1): 5, (0, 0): 6, (0, 1): 7}
     b_near = products(
         inputs,
         turned,
@@ -239,7 +260,7 @@
         4,
         lambda i: 1 + 4 * lax.rem(i, 2) + 2 * (i // 2),
         [(low, half, first, 2, 1) for first in (0, 2) for low in (b_low, b_high)],
-        [c_far],
+        c_far[:1],
     )
     b_up2, b_down2 = along("y", b_near[1], 1), along("y", b_near[2], -1)
     *b_own, c_near = products(
@@ -265,7 +286,8 @@
 
     def c_terms(dy, h):
         block = (1, ROW, C // 2, WIDTH)
-        return [(c_near, block, (dy, 0, h, 0)), (c_z, block, (dy, 0, h, 0))]
+        place = c_places[dy, h]
+        return [(c_near, block, (dy, 0, h, 0)), ((c_soon, c_late)[place // 4], block, (place % 4, 0, 0, 0))]
 
     def a_terms(dy, h):
         return [(a_x, (2, 1, A // 2, WIDTH), (0, dy, h, 0))]
@@ -276,32 +298,26 @@
             for array, n in arrived
         ]
 
+    def nesterov(weights, moment, total, new_weights, fresh):
+        outer_grad = total[...] / groups
+        fresh[...] = 0.9 * moment[...] + outer_grad
+        new_weights[...] = weights[...] - 0.7 * (outer_grad + 0.9 * fresh[...])
+
+    new_params, new_momentum = combine(nesterov, [params, momentum, total], [params.shape] * 2, b_last[:1])
+
     ring_b = reduce_ring("x", b_terms, 2, half)
     ring_c = reduce_ring("y", c_terms, ROW, C // 2)
     ring_a = reduce_ring("y", a_terms, 2, A // 2)
     next(ring_b), next(ring_c), next(ring_a)
-    done = ring_b.send(b_last[:1])
-    done = ring_c.send(done)
-
-    picked = jnp.sum(jnp.where(jnp.arange(groups) == group, exps, 0))
-    scale_up = jnp.full((8, 128), jnp.left_shift(1, picked).astype(jnp.float32))
-
-    def copy(scale, out):
-        out[...] = scale[...]
-
-    done = combine(copy, [scale_up], [scale_up.shape], done)
-    scale = done[0][0, 0]
-    delta = params - local_params[0].astype(jnp.float32)
-    coded = jnp.clip(delta * scale, -448.0, 448.0).astype(jnp.bfloat16)
-    total = lax.psum(coded.astype(jnp.float32) / scale, "rep")
-
-    done, b_got = ring_b.send(done)
+    done = ring_c.send([new_params])
+    done = ring_b.send(done)
     done, c_got = ring_c.send(done)
     done = ring_a.send(done)
+    done, b_got = ring_b.send(done)
 
     def c_x_terms(dx, h):
         block = (1, 1, C // 2, WIDTH)
-        terms = [(c_near, block, (0, dx, h, 0)), (c_z, block, (0, dx, h, 0))]
+        terms = [(c_near, block, (0, dx, h, 0)), (c_late, block, (2 + h, dx, 0, 0))]
         for array, n in c_got(h):
             terms.append((array, block[1:], (dx, 0, 0)) if n is None else (array, block, (n, dx, 0, 0)))
         return terms
@@ -311,14 +327,14 @@
         keep[:rows, :], keep[rows:, :] = low[0], high[0]
         cross[:rows, :], cross[rows:, :] = low[1], high[1]
 
+    ring_cx = reduce_ring("x", c_x_terms, 1, C // 2)
+    next(ring_cx)
+    done = ring_cx.send(done)
     b_keep, b_cross = settle(
         b_terms(0, 0) + whole(b_got(0)), b_terms(0, 1) + whole(b_got(1)), keep_and_cross, [(B, WIDTH)] * 2, done
     )
     b_in = along_z(b_cross)
-    ring_cx = reduce_ring("x", c_x_terms, 1, C // 2)
-    next(ring_cx)
-    done = ring_cx.send([b_keep])
-    done, cx_got = ring_cx.send(done)
+    done, cx_got = ring_cx.send([b_keep])
     done, a_got = ring_a.send(done)
 
     def c_home(low, high, out):
@@ -328,23 +344,16 @@
         c_x_terms(0, 0) + whole(cx_got(0)), c_x_terms(0, 1) + whole(cx_got(1)), c_home, [(C, WIDTH)], done
     )
     a_keep, a_cross = settle(
-        a_terms(0, 0) + whole(a_got(0)), a_terms(0, 1) + whole(a_got(1)), keep_and_cross, [(A, WIDTH)] * 2, [c_own]
+        a_terms(0, 0) + whole(a_got(0)), a_terms(0, 1) + whole(a_got(1)), keep_and_cross, [(A, WIDTH)] * 2, [c_own, b_in]
     )
     a_in = along_z(a_cross)
-
-    def nesterov(weights, moment, total, new_weights, fresh):
-        outer_grad = total[...] / groups
-        fresh[...] = 0.9 * moment[...] + outer_grad
-        new_weights[...] = weights[...] - 0.7 * (outer_grad + 0.9 * fresh[...])
-
-    new_params, new_momentum = combine(nesterov, [params, momentum, total], [params.shape] * 2, [a_keep])
 
     def assemble(keep_a, got_a, keep_b, got_b, own_c, out):
         value = jnp.concatenate([keep_a[...] + got_a[...], keep_b[...] + got_b[...], own_c[...]], axis=0)
         out[0] = value.T
 
     (kv_grad,) = combine(
-        assemble, [a_keep, a_in, b_keep, b_in, c_own], [(1, WIDTH, A + B + C)], [new_params]
+        assemble, [a_keep, a_in, b_keep, b_in, c_own], [(1, WIDTH, A + B + C)]
     )
     return (new_params, new_momentum, kv_grad)
 

time: 273 us -> 238 us (0.87)
  waiting for transfers between devices: 113 us -> 78.2 us
  starting transfers between devices: 33.2 us -> 37.7 us
  local copies, waits for them, and re-layouts: 13.1 us -> 8.98 us
    ppermute x22, waiting for transfers between devices: 95 us -> 44.6 us  [along(): return lax.ppermute(array, 'fsdp', pairs)]
    ppermute x3 -> x4, waiting for transfers between devices: 0.01 us -> 32.3 us  [along_z(): return lax.ppermute(array, 'fsdp', [(f, (f + 16) % 32) for f in range(32)])]
    psum x1, waiting for transfers between devices: 17.8 us -> 0.01 us  [local(): total = lax.psum(coded.astype(jnp.float32) / scale_up, 'rep')]
    unnamed x48 -> x36, local copies, waits for them, and re-layouts: 11.4 us -> 8.98 us
    ppermute x3 -> x4, starting transfers between devices: 4.74 us -> 7.08 us  [along_z(): return lax.ppermute(array, 'fsdp', [(f, (f + 16) % 32) for f in range(32)])]
    pallas_call x15 -> x14, Pallas kernels: 42.3 us -> 40.6 us  [combine(): pl.pallas_call(kernel, grid=(1,), in_specs=[pl.BlockSpec(block, lambda i,...]
  transfers between devices with their start and end apart: 27 -> 28, of which waited for: 13 -> 13; matrix products, arithmetic and copies ran while one was open for 2% -> 0% of each run, Pallas kernels for 25% -> 36%
where the time goes in v5:
time: 238 us; the launch traced here: 237 us
  Pallas kernels  91.6 us (38%)
  waiting for transfers between devices  78.2 us (33%)
  starting transfers between devices  37.7 us (16%)
  between operations  16.2 us (7%)
  local copies, waits for them, and re-layouts  8.98 us (4%)
  other arithmetic  4.36 us (2%)
    ppermute x22, waiting for transfers between devices, along(): return lax.ppermute(array, 'fsdp', pairs)  44.6 us
    pallas_call x14, Pallas kernels, combine(): pl.pallas_call(kernel, grid=(1,), in_specs=[pl.BlockSpec(block, lambda i,...  40.6 us
    ppermute x4, waiting for transfers between devices, along_z(): return lax.ppermute(array, 'fsdp', [(f, (f + 16) % 32) for f in range(32)])  32.3 us
    ppermute x22, starting transfers between devices, along(): return lax.ppermute(array, 'fsdp', pairs)  30.5 us
    pallas_call x3, Pallas kernels, products(): pl.pallas_call(body, grid_spec=pltpu.PrefetchScalarGridSpec(num_scalar_pr...  24.5 us
    pallas_call x1, Pallas kernels, all_products(): pl.pallas_call(body, grid_spec=pltpu.PrefetchScalarGridSpec(num_scalar_pr...  18 us
    unnamed x36, local copies, waits for them, and re-layouts  8.98 us
    pallas_call x1, Pallas kernels, crossing_products(): pl.pallas_call(body, grid_spec=pltpu.PrefetchScalarGridSpec(num_scalar_pr...  8.41 us
  transfers between devices with their start and end apart: 28, of which 13 were waited for; matrix products, arithmetic and copies ran while one was open for 0% of the time, Pallas kernels for 36%

profile of v5, /device:TPU:0, one launch (start us, length us, event | category | flops | bytes accessed | tf_op | source)
XLA Modules:
  0.0 237.0 jit_solution(4899996971518743590)
XLA Ops:
  10.0 2.5 %convert_divide_fusion = f32[256,1024]{1,0:T(8,128)} fusion(f32[256,1024]{1,0:T(8,128)} %refs_0_.1, bf16[1,256,1024]{2,1,0:T(8,128)(2,1)} %param.8, f32[]{:T(128)S(6)} %convert_element_type.17), kind=kLoop, calls=%fused_computation.4 | loop fusion | flops 1835008 | bytes 2621444 | tf_op jit(solution)/shard_map/div | solution.py:237
  13.2 18.0 %shard_map.85 = (f32[4,8,416,256]{3,2,1,0:T(8,128)}, bf16[1024,1024]{1,0:T(8,128)(2,1)S(1)}) custom-call(s32[9]{0:T(128)} %compare_select_fusion.4.table, bf16[1024,8192]{1,0:T(8,128)(2,1)} %x.9, bf16[1024,1024]{1,0:T(8,128)(2,1)} %k.1), custom_call_target="tpu_custom_call" | custom-call | flops 20000000000 | bytes 1000 | tf_op jit(solution)/shard_map/pallas_call | solution.py:35
  31.2 5.1 %shard_map.86 = (f32[2,4,176,256]{3,2,1,0:T(8,128)}, f32[2,4,176,256]{3,2,1,0:T(8,128)}) custom-call(s32[9]{0:T(128)} %compare_select_fusion.4.table, bf16[1024,8192]{1,0:T(8,128)(2,1)} %x.9, bf16[1024,1024]{1,0:T(8,128)(2,1)S(1)} %get-tuple-element.40.k, f32[4,8,416,256]{3,2,1,0:T(8,128)} %get-tuple-element.41.refs_0_), custom_call_target="tpu_custom_call" | custom-call | flops 20000000000 | bytes 1000 | tf_op jit(solution)/shard_map/pallas_call | solution.py:128
  36.3 3.1 %collective-permute-start.1 = (f32[2,4,176,256]{3,2,1,0:T(8,128)}, f32[2,4,176,256]{3,2,1,0:T(8,128)}, u32[]{:S(2)}, u32[]{:S(2)}) collective-permute-start(f32[2,4,176,256]{3,2,1,0:T(8,128)} %get-tuple-element.46), channel_id=1, source_target_pairs={{0,12},{1,13},{2,14},{3,15},{4,0},{5,1},{6,2},{7,3},{8,4},{9,5},{1... | collective-permute-start | bytes 4325384 | tf_op jit(solution)/shard_map/ppermute | solution.py:167
  39.4 8.4 %shard_map.87 = (f32[4,4,128,256]{3,2,1,0:T(8,128)}, f32[4,4,128,256]{3,2,1,0:T(8,128)}) custom-call(s32[9]{0:T(128)} %compare_select_fusion.4.table, bf16[1024,8192]{1,0:T(8,128)(2,1)} %x.9, bf16[1024,1024]{1,0:T(8,128)(2,1)S(1)} %get-tuple-element.40.k, f32[2,4,176,256]{3,2,1,0:T(8,128)} %get-tuple-element.42.refs_0_), custom_call_target="tpu_custom_call" | custom-call | flops 20000000000 | bytes 1000 | tf_op jit(solution)/shard_map/pallas_call | solution.py:79
  49.9 8.9 %shard_map.88 = (f32[2,4,176,256]{3,2,1,0:T(8,128)}, f32[2,4,176,256]{3,2,1,0:T(8,128)}, f32[2,4,176,256]{3,2,1,0:T(8,128)}, f32[2,4,176,256]{3,2,1,0:T(8,128)}) custom-call(s32[9]{0:T(128)} %compare_select_fusion.4.table, bf16[1024,8192]{1,0:T(8,128)(2,1)} %x.9, bf16[1024,1024]{1,0:T(8,128)(2,1)S(1)} %get-tuple-element.40.k, ...), custom_call_target="tpu_custom_call" | custom-call | flops 20000000000 | bytes 1000 | tf_op jit(solution)/shard_map/pallas_call | solution.py:128
  58.8 3.3 %collective-permute-start.6 = (f32[2,4,176,256]{3,2,1,0:T(8,128)}, f32[2,4,176,256]{3,2,1,0:T(8,128)S(1)}, u32[]{:S(2)}, u32[]{:S(2)}) collective-permute-start(f32[2,4,176,256]{3,2,1,0:T(8,128)} %get-tuple-element.55), channel_id=1, source_target_pairs={{0,12},{1,13},{2,14},{3,15},{4,0},{5,1},{6,2},{7,3},{8,4},{9,5},{1... | collective-permute-start | bytes 4325384 | tf_op jit(solution)/shard_map/ppermute | solution.py:167
  62.1 10.5 %shard_map.89 = (f32[2,4,176,256]{3,2,1,0:T(8,128)}, f32[2,4,176,256]{3,2,1,0:T(8,128)}, f32[4,4,256,256]{3,2,1,0:T(8,128)}) custom-call(s32[9]{0:T(128)} %compare_select_fusion.4.table, bf16[1024,8192]{1,0:T(8,128)(2,1)} %x.9, bf16[1024,1024]{1,0:T(8,128)(2,1)S(1)} %get-tuple-element.40.k, f32[2,4,176,256]{3,2,1,0:T(8,128)} %get-tuple-element.44.refs_0_), custom_call_target="tpu_custom_call" | custom-call | flops 20000000000 | bytes 1000 | tf_op jit(solution)/shard_map/pallas_call | solution.py:128
  75.5 4.4 %shard_map.90 = (f32[2,4,176,256]{3,2,1,0:T(8,128)}, f32[2,4,176,256]{3,2,1,0:T(8,128)}) custom-call(f32[2,4,176,256]{3,2,1,0:T(8,128)} %get-tuple-element.44.refs_0_, f32[2,4,176,256]{3,2,1,0:T(8,128)} %get-tuple-element.45.refs_1_, f32[2,4,176,256]{3,2,1,0:T(8,128)} %collective-permute-done.refs_2_, f32[2,4,176,256]{3,2,1,0:T(8,128)} %collective-permute-done.1.refs_3_, ...), custom_call_target="tpu_custom_call" | custom-call | flops 4000000000 | bytes 1000 | tf_op jit(solution)/shard_map/pallas_call | solution.py:152
  82.1 20.9 %collective-permute-done.3.refs_1_.refs_3_.refs_5_.refs_7_ = f32[4,4,128,256]{3,2,1,0:T(8,128)} collective-permute-done((f32[4,4,128,256]{3,2,1,0:T(8,128)}, f32[4,4,128,256]{3,2,1,0:T(8,128)}, u32[]{:S(2)}, u32[]{:S(2)}) %collective-permute-start.3) | collective-permute-done | bytes 2097184 | tf_op jit(solution)/shard_map/ppermute | solution.py:171
  104.5 3.4 %shard_map.91 = (f32[256,1024]{1,0:T(8,128)}, f32[256,1024]{1,0:T(8,128)}) custom-call(f32[256,1024]{1,0:T(8,128)} %refs_0_.1, f32[256,1024]{1,0:T(8,128)} %refs_1_.1, f32[256,1024]{1,0:T(8,128)} %all-reduce.2.cloned.1.call-done.refs_2_, f32[2,4,176,256]{3,2,1,0:T(8,128)} %get-tuple-element.48.refs_3_), custom_call_target="tpu_custom_call" | custom-call | flops 4000000000 | bytes 1000 | tf_op jit(solution)/shard_map/pallas_call | solution.py:152
  107.9 3.6 %shard_map.92 = (f32[2,4,128,256]{3,2,1,0:T(8,128)}, f32[2,4,128,256]{3,2,1,0:T(8,128)}) custom-call(f32[4,4,256,256]{3,2,1,0:T(8,128)} %get-tuple-element.47.refs_4_.refs_0_.refs_2_.refs_6_.refs_3_.refs_8_.refs_12_.refs_5_, f32[4,4,128,256]{3,2,1,0:T(8,128)} %collective-permute-done.3.refs_1_.refs_3_.refs_5_.refs_7_, ...), custom_call_target="tpu_custom_call" | custom-call | flops 4000000000 | bytes 1000 | tf_op jit(solution)/shard_map/pallas_call | solution.py:152
  114.7 18.8 %collective-permute-done.9.refs_5_.refs_8_.refs_6_.refs_7_ = f32[2,4,176,256]{3,2,1,0:T(8,128)} collective-permute-done((f32[2,4,176,256]{3,2,1,0:T(8,128)}, f32[2,4,176,256]{3,2,1,0:T(8,128)}, u32[]{:S(2)}, u32[]{:S(2)}) %collective-permute-start.9) | collective-permute-done | bytes 1441824 | tf_op jit(solution)/shard_map/ppermute | solution.py:167
  133.5 5.6 %collective-permute-done.7.refs_2_.refs_11_ = f32[2,4,176,256]{3,2,1,0:T(8,128)} collective-permute-done((f32[2,4,176,256]{3,2,1,0:T(8,128)}, f32[2,4,176,256]{3,2,1,0:T(8,128)}, u32[]{:S(2)}, u32[]{:S(2)}) %collective-permute-start.7) | collective-permute-done | bytes 1441824 | tf_op jit(solution)/shard_map/ppermute | solution.py:167
  139.1 3.4 %shard_map.93 = (f32[2,2,176,256]{3,2,1,0:T(8,128)}, f32[2,2,176,256]{3,2,1,0:T(8,128)}) custom-call(f32[2,4,176,256]{3,2,1,0:T(8,128)} %get-tuple-element.54.refs_0_.refs_9_, f32[2,4,176,256]{3,2,1,0:T(8,128)} %copy-done.4, f32[2,4,176,256]{3,2,1,0:T(8,128)} %collective-permute-done.7.refs_2_.refs_11_, ...), custom_call_target="tpu_custom_call" | custom-call | flops 4000000000 | bytes 1000 | tf_op jit(solution)/shard_map/pallas_call | solution.py:152
  142.5 2.6 %collective-permute-start.15 = (f32[2,2,176,256]{3,2,1,0:T(8,128)}, f32[2,2,176,256]{3,2,1,0:T(8,128)}, u32[]{:S(2)}, u32[]{:S(2)}) collective-permute-start(f32[2,2,176,256]{3,2,1,0:T(8,128)} %get-tuple-element.64), channel_id=1, source_target_pairs={{0,3},{1,0},{2,1},{3,2},{4,7},{5,4},{6,5},{7,6},{8,11},{9,8},{10,9... | collective-permute-start | bytes 2162696 | tf_op jit(solution)/shard_map/ppermute | solution.py:167
  145.1 2.5 %collective-permute-done.2.refs_1_.refs_4_.refs_5_.refs_9_.refs_13_.refs_6_.refs_7_ = f32[4,4,128,256]{3,2,1,0:T(8,128)S(1)} collective-permute-done((f32[4,4,128,256]{3,2,1,0:T(8,128)}, f32[4,4,128,256]{3,2,1,0:T(8,128)S(1)}, u32[]{:S(2)}, u32[]{:S(2)}) %collective-permute-start.2) | collective-permute-done | bytes 2097184 | tf_op jit(solution)/shard_map/ppermute | solution.py:171
  147.6 7.3 %collective-permute-done.5.refs_5_.refs_2_.refs_14_ = f32[2,4,128,256]{3,2,1,0:T(8,128)S(1)} collective-permute-done((f32[2,4,128,256]{3,2,1,0:T(8,128)}, f32[2,4,128,256]{3,2,1,0:T(8,128)S(1)}, u32[]{:S(2)}, u32[]{:S(2)}) %collective-permute-start.5) | collective-permute-done | bytes 1048608 | tf_op jit(solution)/shard_map/ppermute | solution.py:167
  154.8 5.2 %collective-permute-done.4.refs_2_.refs_6_.refs_10_.refs_7_.refs_8_ = f32[2,4,128,256]{3,2,1,0:T(8,128)} collective-permute-done((f32[2,4,128,256]{3,2,1,0:T(8,128)}, f32[2,4,128,256]{3,2,1,0:T(8,128)}, u32[]{:S(2)}, u32[]{:S(2)}) %collective-permute-start.4) | collective-permute-done | bytes 1048608 | tf_op jit(solution)/shard_map/ppermute | solution.py:167
  160.0 3.0 %shard_map.94 = (f32[4,128,256]{2,1,0:T(8,128)}, f32[4,128,256]{2,1,0:T(8,128)}) custom-call(f32[4,4,256,256]{3,2,1,0:T(8,128)} %get-tuple-element.47.refs_4_.refs_0_.refs_2_.refs_6_.refs_3_.refs_8_.refs_12_.refs_5_, f32[4,4,128,256]{3,2,1,0:T(8,128)} %copy-done, f32[2,4,128,256]{3,2,1,0:T(8,128)} %collective-permute-done.4.refs_2_.refs_6_.refs_10_.refs_7_.refs_8_, ...), custom_call_target="tpu_custom_call" | custom-call | flops 4000000000 | bytes 1000 | tf_op jit(solution)/shard_map/pallas_call | solution.py:152
  166.1 2.7 %shard_map.95 = (f32[2,2,208,256]{3,2,1,0:T(8,128)}, f32[2,2,208,256]{3,2,1,0:T(8,128)}) custom-call(f32[2,4,416,256]{3,2,1,0:T(8,128)} %bitcast.4, f32[2,4,416,256]{3,2,1,0:T(8,128)} %bitcast.5, f32[2,4,416,256]{3,2,1,0:T(8,128)} %bitcast.6, f32[2,4,416,256]{3,2,1,0:T(8,128)} %bitcast.7, f32[4,128,256]{2,1,0:T(8,128)} %get-tuple-element.60.refs_4_), custom_call_target="tpu_custom_call" | custom-call | flops 4000000000 | bytes 1000 | tf_op jit(solution)/shard_map/pallas_call | solution.py:152
  168.8 3.0 %collective-permute-start.11 = (f32[2,2,208,256]{3,2,1,0:T(8,128)}, f32[2,2,208,256]{3,2,1,0:T(8,128)S(1)}, u32[]{:S(2)}, u32[]{:S(2)}) collective-permute-start(f32[2,2,208,256]{3,2,1,0:T(8,128)} %get-tuple-element.62.refs_8_), channel_id=1, source_target_pairs={{0,4},{1,5},{2,6},{3,7},{4,8},{5,9},{6,10},{7,11},{8,12},{9,13},{1... | collective-permute-start | bytes 2555912 | tf_op jit(solution)/shard_map/ppermute | solution.py:167
  171.8 2.7 %shard_map.96 = (f32[2,176,256]{2,1,0:T(8,128)}, f32[2,176,256]{2,1,0:T(8,128)}) custom-call(f32[2,4,176,256]{3,2,1,0:T(8,128)} %get-tuple-element.54.refs_0_.refs_9_, f32[2,4,176,256]{3,2,1,0:T(8,128)} %copy-done.4, f32[2,4,176,256]{3,2,1,0:T(8,128)} %collective-permute-done.7.refs_2_.refs_11_, f32[2,2,176,256]{3,2,1,0:T(8,128)} %collective-permute-done.14.refs_3_.refs_8_, ...), custom_call_target="tpu_custom_call" | custom-call | flops 4000000000 | bytes 1000 | tf_op jit(solution)/shard_map/pallas_call | solution.py:152
  178.2 2.4 %collective-permute-done.12.refs_3_.refs_15_ = f32[4,128,256]{2,1,0:T(8,128)S(1)} collective-permute-done((f32[4,128,256]{2,1,0:T(8,128)}, f32[4,128,256]{2,1,0:T(8,128)S(1)}, u32[]{:S(2)}, u32[]{:S(2)}) %collective-permute-start.12) | collective-permute-done | bytes 524320 | tf_op jit(solution)/shard_map/ppermute | solution.py:167
  183.9 2.7 %collective-permute-start.17 = (f32[2,1,128,256]{3,2,1,0:T(8,128)}, f32[2,1,128,256]{3,2,1,0:T(8,128)S(1)}, u32[]{:S(2)}, u32[]{:S(2)}) collective-permute-start(f32[2,1,128,256]{3,2,1,0:T(8,128)} %get-tuple-element.67), channel_id=1, source_target_pairs={{0,3},{1,0},{2,1},{3,2},{4,7},{5,4},{6,5},{7,6},{8,11},{9,8},{10,9... | collective-permute-start | bytes 786440 | tf_op jit(solution)/shard_map/ppermute | solution.py:167
  188.1 2.9 %shard_map.98 = (f32[352,256]{1,0:T(8,128)}, f32[352,256]{1,0:T(8,128)}) custom-call(f32[2,4,176,256]{3,2,1,0:T(8,128)} %get-tuple-element.54.refs_0_.refs_9_, f32[2,4,176,256]{3,2,1,0:T(8,128)} %copy-done.4, f32[2,4,176,256]{3,2,1,0:T(8,128)} %collective-permute-done.7.refs_2_.refs_11_, f32[2,2,176,256]{3,2,1,0:T(8,128)} %collective-permute-done.15.refs_7_.refs_3_, ...), custom_call_target="tpu_custom_call" | custom-call | flops 4000000000 | bytes 1000 | tf_op jit(solution)/shard_map/pallas_call | solution.py:152
  191.1 3.4 %collective-permute-done.16.refs_4_.refs_10_ = f32[2,1,128,256]{3,2,1,0:T(8,128)S(1)} collective-permute-done((f32[2,1,128,256]{3,2,1,0:T(8,128)}, f32[2,1,128,256]{3,2,1,0:T(8,128)S(1)}, u32[]{:S(2)}, u32[]{:S(2)}) %collective-permute-start.16) | collective-permute-done | bytes 262176 | tf_op jit(solution)/shard_map/ppermute | solution.py:167
  210.3 2.6 %collective-permute-done.24.refs_7_.refs_3_ = f32[352,256]{1,0:T(8,128)S(1)} collective-permute-done((f32[352,256]{1,0:T(8,128)S(1)}, f32[352,256]{1,0:T(8,128)S(1)}, u32[]{:S(2)}, u32[]{:S(2)}) %collective-permute-start.24) | collective-permute-done | bytes 360480 | tf_op jit(solution)/shard_map/ppermute | solution.py:171
  214.6 2.6 %shard_map.102 = (f32[416,256]{1,0:T(8,128)}, f32[416,256]{1,0:T(8,128)}) custom-call(f32[2,4,416,256]{3,2,1,0:T(8,128)} %bitcast.10, f32[2,2,208,256]{3,2,1,0:T(8,128)} %copy-done.10, f32[2,208,256]{2,1,0:T(8,128)} %copy-done.12, f32[2,4,416,256]{3,2,1,0:T(8,128)} %bitcast.11, f32[2,2,208,256]{3,2,1,0:T(8,128)} %copy-done.9, f32[2,208,256]{2,1,0:T(8,128)} %copy-done.11, ...), custom_call_target="tpu_custom_call" | custom-call | flops 4000000000 | bytes 1000 | tf_op jit(solution)/shard_map/pallas_call | solution.py:152
  217.3 2.5 %collective-permute-start.25 = (f32[416,256]{1,0:T(8,128)}, f32[416,256]{1,0:T(8,128)S(1)}, u32[]{:S(2)}, u32[]{:S(2)}) collective-permute-start(f32[416,256]{1,0:T(8,128)} %get-tuple-element.76), channel_id=1, source_target_pairs={{0,16},{1,17},{2,18},{3,19},{4,20},{5,21},{6,22},{7,23},{8,24},{9,... | collective-permute-start | bytes 1277960 | tf_op jit(solution)/shard_map/ppermute | solution.py:171
  219.7 6.3 %collective-permute-done.25.refs_1_ = f32[416,256]{1,0:T(8,128)S(1)} collective-permute-done((f32[416,256]{1,0:T(8,128)}, f32[416,256]{1,0:T(8,128)S(1)}, u32[]{:S(2)}, u32[]{:S(2)}) %collective-permute-start.25) | collective-permute-done | bytes 426016 | tf_op jit(solution)/shard_map/ppermute | solution.py:171
  226.8 2.7 %shard_map.103 = f32[1,256,1024]{2,1,0:T(8,128)} custom-call(f32[416,256]{1,0:T(8,128)} %get-tuple-element.75.refs_0_, f32[416,256]{1,0:T(8,128)} %copy-done.13, f32[352,256]{1,0:T(8,128)} %get-tuple-element.69.refs_10_.refs_2_, f32[352,256]{1,0:T(8,128)} %copy-done.15, f32[256,256]{1,0:T(8,128)} %shard_map.101.refs_6_.refs_4_), custom_call_target="tpu_custom_call" | custom-call | flops 4000000000 | bytes 1000 | tf_op jit(solution)/shard_map/pallas_call | solution.py:152
  (84 shorter events, 43.6 us)
Async XLA Ops:
  8.0 96.5 %all-reduce.2.cloned.1.call-start = ((), (), s32[]{:S(2)}) async-start(), calls=%async_computation.1 | async-start | bytes 2097152 | tf_op jit(solution)/shard_map/psum | solution.py:237
  12.6 153.6 %reduce-scatter.2.cloned.1.call-start = ((), (), s32[]{:S(2)}) async-start(), calls=%async_computation.2 | async-start | bytes 17039360 | tf_op jit(solution)/shard_map/reduce_scatter | solution.py:175
  36.3 36.3 %collective-permute-start.1 = (f32[2,4,176,256]{3,2,1,0:T(8,128)}, f32[2,4,176,256]{3,2,1,0:T(8,128)}, u32[]{:S(2)}, u32[]{:S(2)}) collective-permute-start(f32[2,4,176,256]{3,2,1,0:T(8,128)} %get-tuple-element.46), channel_id=1, source_target_pairs={{0,12},{1,13},{2,14},{3,15},{4,0},{5,1},{6,2},{7,3},{8,4},{9,5},{1... | collective-permute-start | bytes 4325384 | tf_op jit(solution)/shard_map/ppermute | solution.py:167
  39.4 36.1 %collective-permute-start = (f32[2,4,176,256]{3,2,1,0:T(8,128)}, f32[2,4,176,256]{3,2,1,0:T(8,128)}, u32[]{:S(2)}, u32[]{:S(2)}) collective-permute-start(f32[2,4,176,256]{3,2,1,0:T(8,128)} %get-tuple-element.42.refs_0_), channel_id=1, source_target_pairs={{0,4},{1,5},{2,6},{3,7},{4,8},{5,9},{6,10},{7,11},{8,12},{9,13},{1... | collective-permute-start | bytes 4325384 | tf_op jit(solution)/shard_map/ppermute | solution.py:167
  47.9 55.2 %collective-permute-start.3 = (f32[4,4,128,256]{3,2,1,0:T(8,128)}, f32[4,4,128,256]{3,2,1,0:T(8,128)}, u32[]{:S(2)}, u32[]{:S(2)}) collective-permute-start(f32[4,4,128,256]{3,2,1,0:T(8,128)} %get-tuple-element.43.refs_0_), channel_id=1, source_target_pairs={{0,16},{1,17},{2,18},{3,19},{4,20},{5,21},{6,22},{7,23},{8,24},{9,... | collective-permute-start | bytes 6291464 | tf_op jit(solution)/shard_map/ppermute | solution.py:171
  58.8 52.7 %collective-permute-start.6 = (f32[2,4,176,256]{3,2,1,0:T(8,128)}, f32[2,4,176,256]{3,2,1,0:T(8,128)S(1)}, u32[]{:S(2)}, u32[]{:S(2)}) collective-permute-start(f32[2,4,176,256]{3,2,1,0:T(8,128)} %get-tuple-element.55), channel_id=1, source_target_pairs={{0,12},{1,13},{2,14},{3,15},{4,0},{5,1},{6,2},{7,3},{8,4},{9,5},{1... | collective-permute-start | bytes 4325384 | tf_op jit(solution)/shard_map/ppermute | solution.py:167
  62.1 52.4 %collective-permute-start.8 = (f32[2,4,176,256]{3,2,1,0:T(8,128)}, f32[2,4,176,256]{3,2,1,0:T(8,128)}, u32[]{:S(2)}, u32[]{:S(2)}) collective-permute-start(f32[2,4,176,256]{3,2,1,0:T(8,128)} %get-tuple-element.57), channel_id=1, source_target_pairs={{0,4},{1,5},{2,6},{3,7},{4,8},{5,9},{6,10},{7,11},{8,12},{9,13},{1... | collective-permute-start | bytes 4325384 | tf_op jit(solution)/shard_map/ppermute | solution.py:167
  72.7 74.9 %collective-permute-start.2 = (f32[4,4,128,256]{3,2,1,0:T(8,128)}, f32[4,4,128,256]{3,2,1,0:T(8,128)S(1)}, u32[]{:S(2)}, u32[]{:S(2)}) collective-permute-start(f32[4,4,128,256]{3,2,1,0:T(8,128)} %get-tuple-element.51), channel_id=1, source_target_pairs={{0,16},{1,17},{2,18},{3,19},{4,20},{5,21},{6,22},{7,23},{8,24},{9,... | collective-permute-start | bytes 6291464 | tf_op jit(solution)/shard_map/ppermute | solution.py:171
  79.9 53.7 %collective-permute-start.9 = (f32[2,4,176,256]{3,2,1,0:T(8,128)}, f32[2,4,176,256]{3,2,1,0:T(8,128)}, u32[]{:S(2)}, u32[]{:S(2)}) collective-permute-start(f32[2,4,176,256]{3,2,1,0:T(8,128)} %get-tuple-element.58), channel_id=1, source_target_pairs={{0,12},{1,13},{2,14},{3,15},{4,0},{5,1},{6,2},{7,3},{8,4},{9,5},{1... | collective-permute-start | bytes 4325384 | tf_op jit(solution)/shard_map/ppermute | solution.py:167
  103.1 36.0 %collective-permute-start.7 = (f32[2,4,176,256]{3,2,1,0:T(8,128)}, f32[2,4,176,256]{3,2,1,0:T(8,128)}, u32[]{:S(2)}, u32[]{:S(2)}) collective-permute-start(f32[2,4,176,256]{3,2,1,0:T(8,128)} %get-tuple-element.48.refs_3_), channel_id=1, source_target_pairs={{0,4},{1,5},{2,6},{3,7},{4,8},{5,9},{6,10},{7,11},{8,12},{9,13},{1... | collective-permute-start | bytes 4325384 | tf_op jit(solution)/shard_map/ppermute | solution.py:167
  112.7 42.1 %collective-permute-start.5 = (f32[2,4,128,256]{3,2,1,0:T(8,128)}, f32[2,4,128,256]{3,2,1,0:T(8,128)S(1)}, u32[]{:S(2)}, u32[]{:S(2)}) collective-permute-start(f32[2,4,128,256]{3,2,1,0:T(8,128)} %get-tuple-element.53), channel_id=1, source_target_pairs={{0,12},{1,13},{2,14},{3,15},{4,0},{5,1},{6,2},{7,3},{8,4},{9,5},{1... | collective-permute-start | bytes 3145736 | tf_op jit(solution)/shard_map/ppermute | solution.py:167
  114.6 45.4 %collective-permute-start.4 = (f32[2,4,128,256]{3,2,1,0:T(8,128)}, f32[2,4,128,256]{3,2,1,0:T(8,128)}, u32[]{:S(2)}, u32[]{:S(2)}) collective-permute-start(f32[2,4,128,256]{3,2,1,0:T(8,128)} %get-tuple-element.52.refs_12_), channel_id=1, source_target_pairs={{0,4},{1,5},{2,6},{3,7},{4,8},{5,9},{6,10},{7,11},{8,12},{9,13},{1... | collective-permute-start | bytes 3145736 | tf_op jit(solution)/shard_map/ppermute | solution.py:167
  142.5 29.3 %collective-permute-start.15 = (f32[2,2,176,256]{3,2,1,0:T(8,128)}, f32[2,2,176,256]{3,2,1,0:T(8,128)}, u32[]{:S(2)}, u32[]{:S(2)}) collective-permute-start(f32[2,2,176,256]{3,2,1,0:T(8,128)} %get-tuple-element.64), channel_id=1, source_target_pairs={{0,3},{1,0},{2,1},{3,2},{4,7},{5,4},{6,5},{7,6},{8,11},{9,8},{10,9... | collective-permute-start | bytes 2162696 | tf_op jit(solution)/shard_map/ppermute | solution.py:167
  145.1 26.7 %collective-permute-start.14 = (f32[2,2,176,256]{3,2,1,0:T(8,128)}, f32[2,2,176,256]{3,2,1,0:T(8,128)}, u32[]{:S(2)}, u32[]{:S(2)}) collective-permute-start(f32[2,2,176,256]{3,2,1,0:T(8,128)} %get-tuple-element.59.refs_6_), channel_id=1, source_target_pairs={{0,1},{1,2},{2,3},{3,0},{4,5},{5,6},{6,7},{7,4},{8,9},{9,10},{10,1... | collective-permute-start | bytes 2162696 | tf_op jit(solution)/shard_map/ppermute | solution.py:167
  147.6 12.4 %copy-start = (f32[4,4,128,256]{3,2,1,0:T(8,128)}, f32[4,4,128,256]{3,2,1,0:T(8,128)S(1)}, u32[]{:S(2)}) copy-start(f32[4,4,128,256]{3,2,1,0:T(8,128)S(1)} %collective-permute-done.2.refs_1_.refs_4_.refs_5_.refs_9_.refs_13_.refs_6_.refs_7_) | copy-start | bytes 6291460
  154.8 5.2 %copy-start.1 = (f32[2,4,128,256]{3,2,1,0:T(8,128)}, f32[2,4,128,256]{3,2,1,0:T(8,128)S(1)}, u32[]{:S(2)}) copy-start(f32[2,4,128,256]{3,2,1,0:T(8,128)S(1)} %collective-permute-done.5.refs_5_.refs_2_.refs_14_) | copy-start | bytes 3145732
  162.9 13.6 %collective-permute-start.13 = (f32[4,128,256]{2,1,0:T(8,128)}, f32[4,128,256]{2,1,0:T(8,128)S(1)}, u32[]{:S(2)}, u32[]{:S(2)}) collective-permute-start(f32[4,128,256]{2,1,0:T(8,128)} %get-tuple-element.63), channel_id=1, source_target_pairs={{0,12},{1,13},{2,14},{3,15},{4,0},{5,1},{6,2},{7,3},{8,4},{9,5},{1... | collective-permute-start | bytes 1572872 | tf_op jit(solution)/shard_map/ppermute | solution.py:167
  164.4 16.3 %collective-permute-start.12 = (f32[4,128,256]{2,1,0:T(8,128)}, f32[4,128,256]{2,1,0:T(8,128)S(1)}, u32[]{:S(2)}, u32[]{:S(2)}) collective-permute-start(f32[4,128,256]{2,1,0:T(8,128)} %get-tuple-element.60.refs_4_), channel_id=1, source_target_pairs={{0,4},{1,5},{2,6},{3,7},{4,8},{5,9},{6,10},{7,11},{8,12},{9,13},{1... | collective-permute-start | bytes 1572872 | tf_op jit(solution)/shard_map/ppermute | solution.py:167
  168.8 30.5 %collective-permute-start.11 = (f32[2,2,208,256]{3,2,1,0:T(8,128)}, f32[2,2,208,256]{3,2,1,0:T(8,128)S(1)}, u32[]{:S(2)}, u32[]{:S(2)}) collective-permute-start(f32[2,2,208,256]{3,2,1,0:T(8,128)} %get-tuple-element.62.refs_8_), channel_id=1, source_target_pairs={{0,4},{1,5},{2,6},{3,7},{4,8},{5,9},{6,10},{7,11},{8,12},{9,13},{1... | collective-permute-start | bytes 2555912 | tf_op jit(solution)/shard_map/ppermute | solution.py:167
  174.5 12.1 %collective-permute-start.19 = (f32[2,176,256]{2,1,0:T(8,128)}, f32[2,176,256]{2,1,0:T(8,128)S(1)}, u32[]{:S(2)}, u32[]{:S(2)}) collective-permute-start(f32[2,176,256]{2,1,0:T(8,128)} %get-tuple-element.68), channel_id=1, source_target_pairs={{0,3},{1,0},{2,1},{3,2},{4,7},{5,4},{6,5},{7,6},{8,11},{9,8},{10,9... | collective-permute-start | bytes 1081352 | tf_op jit(solution)/shard_map/ppermute | solution.py:167
  175.3 11.7 %collective-permute-start.18 = (f32[2,176,256]{2,1,0:T(8,128)}, f32[2,176,256]{2,1,0:T(8,128)S(1)}, u32[]{:S(2)}, u32[]{:S(2)}) collective-permute-start(f32[2,176,256]{2,1,0:T(8,128)} %get-tuple-element.65.refs_16_), channel_id=1, source_target_pairs={{0,1},{1,2},{2,3},{3,0},{4,5},{5,6},{6,7},{7,4},{8,9},{9,10},{10,1... | collective-permute-start | bytes 1081352 | tf_op jit(solution)/shard_map/ppermute | solution.py:167
  176.6 4.1 %copy-start.2 = (f32[4,128,256]{2,1,0:T(8,128)}, f32[4,128,256]{2,1,0:T(8,128)S(1)}, u32[]{:S(2)}) copy-start(f32[4,128,256]{2,1,0:T(8,128)S(1)} %collective-permute-done.13.refs_7_.refs_11_.refs_8_.refs_9_) | copy-start | bytes 1572868
  176.6 22.7 %collective-permute-start.10 = (f32[2,2,208,256]{3,2,1,0:T(8,128)}, f32[2,2,208,256]{3,2,1,0:T(8,128)S(1)}, u32[]{:S(2)}, u32[]{:S(2)}) collective-permute-start(f32[2,2,208,256]{3,2,1,0:T(8,128)} %get-tuple-element.61), channel_id=1, source_target_pairs={{0,12},{1,13},{2,14},{3,15},{4,0},{5,1},{6,2},{7,3},{8,4},{9,5},{1... | collective-permute-start | bytes 2555912 | tf_op jit(solution)/shard_map/ppermute | solution.py:167
  183.9 7.1 %collective-permute-start.17 = (f32[2,1,128,256]{3,2,1,0:T(8,128)}, f32[2,1,128,256]{3,2,1,0:T(8,128)S(1)}, u32[]{:S(2)}, u32[]{:S(2)}) collective-permute-start(f32[2,1,128,256]{3,2,1,0:T(8,128)} %get-tuple-element.67), channel_id=1, source_target_pairs={{0,3},{1,0},{2,1},{3,2},{4,7},{5,4},{6,5},{7,6},{8,11},{9,8},{10,9... | collective-permute-start | bytes 786440 | tf_op jit(solution)/shard_map/ppermute | solution.py:167
  186.6 7.8 %collective-permute-start.16 = (f32[2,1,128,256]{3,2,1,0:T(8,128)}, f32[2,1,128,256]{3,2,1,0:T(8,128)S(1)}, u32[]{:S(2)}, u32[]{:S(2)}) collective-permute-start(f32[2,1,128,256]{3,2,1,0:T(8,128)} %get-tuple-element.66.refs_10_), channel_id=1, source_target_pairs={{0,1},{1,2},{2,3},{3,0},{4,5},{5,6},{6,7},{7,4},{8,9},{9,10},{10,1... | collective-permute-start | bytes 786440 | tf_op jit(solution)/shard_map/ppermute | solution.py:167
  197.3 9.5 %collective-permute-start.23 = (f32[1,128,256]{2,1,0:T(8,128)}, f32[1,128,256]{2,1,0:T(8,128)S(1)}, u32[]{:S(2)}, u32[]{:S(2)}) collective-permute-start(f32[1,128,256]{2,1,0:T(8,128)} %get-tuple-element.73), channel_id=1, source_target_pairs={{0,3},{1,0},{2,1},{3,2},{4,7},{5,4},{6,5},{7,6},{8,11},{9,8},{10,9... | collective-permute-start | bytes 393224 | tf_op jit(solution)/shard_map/ppermute | solution.py:167
  197.3 8.2 %copy-start.14 = (f32[352,256]{1,0:T(8,128)S(1)}, f32[352,256]{1,0:T(8,128)}, u32[]{:S(2)}) copy-start(f32[352,256]{1,0:T(8,128)} %get-tuple-element.74) | copy-start | bytes 1081348
  197.3 9.5 %collective-permute-start.22 = (f32[1,128,256]{2,1,0:T(8,128)}, f32[1,128,256]{2,1,0:T(8,128)S(1)}, u32[]{:S(2)}, u32[]{:S(2)}) collective-permute-start(f32[1,128,256]{2,1,0:T(8,128)} %get-tuple-element.70.refs_4_), channel_id=1, source_target_pairs={{0,1},{1,2},{2,3},{3,0},{4,5},{5,6},{6,7},{7,4},{8,9},{9,10},{10,1... | collective-permute-start | bytes 393224 | tf_op jit(solution)/shard_map/ppermute | solution.py:167
  203.5 9.5 %collective-permute-start.21 = (f32[2,208,256]{2,1,0:T(8,128)}, f32[2,208,256]{2,1,0:T(8,128)S(1)}, u32[]{:S(2)}, u32[]{:S(2)}) collective-permute-start(f32[2,208,256]{2,1,0:T(8,128)} %get-tuple-element.72), channel_id=1, source_target_pairs={{0,12},{1,13},{2,14},{3,15},{4,0},{5,1},{6,2},{7,3},{8,4},{9,5},{1... | collective-permute-start | bytes 1277960 | tf_op jit(solution)/shard_map/ppermute | solution.py:167
  203.8 9.5 %collective-permute-start.20 = (f32[2,208,256]{2,1,0:T(8,128)}, f32[2,208,256]{2,1,0:T(8,128)S(1)}, u32[]{:S(2)}, u32[]{:S(2)}) collective-permute-start(f32[2,208,256]{2,1,0:T(8,128)} %get-tuple-element.71.refs_12_), channel_id=1, source_target_pairs={{0,4},{1,5},{2,6},{3,7},{4,8},{5,9},{6,10},{7,11},{8,12},{9,13},{1... | collective-permute-start | bytes 1277960 | tf_op jit(solution)/shard_map/ppermute | solution.py:167
  205.5 7.4 %collective-permute-start.24 = (f32[352,256]{1,0:T(8,128)S(1)}, f32[352,256]{1,0:T(8,128)S(1)}, u32[]{:S(2)}, u32[]{:S(2)}) collective-permute-start(f32[352,256]{1,0:T(8,128)S(1)} %copy-done.14), channel_id=1, source_target_pairs={{0,16},{1,17},{2,18},{3,19},{4,20},{5,21},{6,22},{7,23},{8,24},{9,... | collective-permute-start | bytes 1081352 | tf_op jit(solution)/shard_map/ppermute | solution.py:171
  217.3 8.8 %collective-permute-start.25 = (f32[416,256]{1,0:T(8,128)}, f32[416,256]{1,0:T(8,128)S(1)}, u32[]{:S(2)}, u32[]{:S(2)}) collective-permute-start(f32[416,256]{1,0:T(8,128)} %get-tuple-element.76), channel_id=1, source_target_pairs={{0,16},{1,17},{2,18},{3,19},{4,20},{5,21},{6,22},{7,23},{8,24},{9,... | collective-permute-start | bytes 1277960 | tf_op jit(solution)/shard_map/ppermute | solution.py:171
  (14 other events, 13.9 us)
Sparse Core Ops, SparseCore 0:
  12.7 51.8 all-reduce.1
Sparse Core Ops, SparseCore 1:
  31.3 134.8 reduce-scatter.1

commit v6 on v5

--- a/solution.py
+++ b/solution.py
@@ -9,9 +9,9 @@
 ROW = 4
 STRIP = ROW * WIDTH
 STRIPS = 8
-A = 416
-B = 352
-C = 256
+A = 384
+B = 320
+C = 320
 X_RINGS = [[16 * z + 4 * y + x for x in range(4)] for z in range(2) for y in range(4)]
 LONG = pl.CostEstimate(flops=2 * 10**10, bytes_accessed=1000, transcendentals=0)
 SHORT = pl.CostEstimate(flops=4 * 10**9, bytes_accessed=1000, transcendentals=0)
@@ -60,7 +60,7 @@
     depth = inputs.shape[0]
 
     def body(table, x, k, *refs):
-        soon, late = refs[-2:]
+        soon, later, last = refs[-3:]
         step = pl.program_id(0)
 
         def emit(h, out, n):
@@ -68,7 +68,7 @@
             for place in range(ROW):
                 out[n, (place - table[STRIPS]) & (ROW - 1)] = value[:, place * WIDTH : (place + 1) * WIDTH]
 
-        for at, first, second in ((0, soon, soon), (1, late, soon), (2, soon, late), (3, late, late)):
+        for at, first, second in ((0, soon, soon), (1, later, soon), (2, soon, later), (3, last, last)):
 
             @pl.when(step == at)
             def _(at=at, first=first, second=second):
@@ -91,10 +91,11 @@
             + [pl.BlockSpec(memory_space=pl.ANY)] * len(after),
             out_specs=[
                 pl.BlockSpec(block, lambda i, table: (jnp.minimum(i, 1), 0, 0, 0)),
-                pl.BlockSpec(block, lambda i, table: (i // 3, 0, 0, 0)),
+                pl.BlockSpec(block, lambda i, table: (0, 0, 0, 0)),
+                pl.BlockSpec(block, lambda i, table: (0, 0, 0, 0)),
             ],
         ),
-        out_shape=[jax.ShapeDtypeStruct((4, ROW, half, WIDTH), jnp.float32)] * 2,
+        out_shape=[jax.ShapeDtypeStruct((n, ROW, half, WIDTH), jnp.float32) for n in (4, 2, 2)],
         compiler_params=pltpu.CompilerParams(dimension_semantics=("arbitrary",), vmem_limit_bytes=60 * MIB),
         cost_estimate=LONG,
     )(table, inputs, turned, *after)
@@ -251,8 +252,9 @@
     )
     b_up1, b_down1 = along("y", b_far[0], 1), along("y", b_far[1], -1)
     c_far = crossing_products(inputs, turned, table, c_low, C // 2, b_far[:1])
-    c_soon, c_late = along_z(c_far[0]), along_z(c_far[1])
-    c_places = {(2, 0): 0, (2, 1): 1, (1, 1): 2, (3, 0): 3, (1, 0): 4, (3, 1): 5, (0, 0): 6, (0, 1): 7}
+    c_z = [along_z(array) for array in c_far]
+    c_places = {(2, 0): (0, 0), (2, 1): (0, 1), (1, 1): (0, 2), (3, 0): (0, 3)}
+    c_places |= {(1, 0): (1, 0), (3, 1): (1, 1), (0, 0): (2, 0), (0, 1): (2, 1)}
     b_near = products(
         inputs,
         turned,
@@ -286,8 +288,8 @@
 
     def c_terms(dy, h):
         block = (1, ROW, C // 2, WIDTH)
-        place = c_places[dy, h]
-        return [(c_near, block, (dy, 0, h, 0)), ((c_soon, c_late)[place // 4], block, (place % 4, 0, 0, 0))]
+        array, n = c_places[dy, h]
+        return [(c_near, block, (dy, 0, h, 0)), (c_z[array], block, (n, 0, 0, 0))]
 
     def a_terms(dy, h):
         return [(a_x, (2, 1, A // 2, WIDTH), (0, dy, h, 0))]
@@ -317,7 +319,7 @@
 
     def c_x_terms(dx, h):
         block = (1, 1, C // 2, WIDTH)
-        terms = [(c_near, block, (0, dx, h, 0)), (c_late, block, (2 + h, dx, 0, 0))]
+        terms = [(c_near, block, (0, dx, h, 0)), (c_z[2], block, (h, dx, 0, 0))]
         for array, n in c_got(h):
             terms.append((array, block[1:], (dx, 0, 0)) if n is None else (array, block, (n, dx, 0, 0)))
         return terms

time: 238 us -> 235 us (0.987)
  waiting for transfers between devices: 78.2 us -> 70.7 us
  starting transfers between devices: 37.7 us -> 40.9 us
    ppermute x22, waiting for transfers between devices: 44.6 us -> 16.9 us  [along(): return lax.ppermute(array, 'fsdp', pairs)]
    ppermute x4 -> x5, waiting for transfers between devices: 32.3 us -> 53.7 us  [along_z(): return lax.ppermute(array, 'fsdp', [(f, (f + 16) % 32) for f in range(32)])]
    ppermute x4 -> x5, starting transfers between devices: 7.08 us -> 8.41 us  [along_z(): return lax.ppermute(array, 'fsdp', [(f, (f + 16) % 32) for f in range(32)])]
    unnamed x36 -> x34, local copies, waits for them, and re-layouts: 8.98 us -> 9.21 us
  transfers between devices with their start and end apart: 28 -> 29, of which waited for: 13 -> 13; matrix products, arithmetic and copies ran while one was open for 0% -> 0% of each run, Pallas kernels for 36% -> 37%
where the time goes in v6:
time: 235 us; the launch traced here: 234 us
  Pallas kernels  92.4 us (39%)
  waiting for transfers between devices  70.7 us (30%)
  starting transfers between devices  40.9 us (17%)
  between operations  16.2 us (7%)
  local copies, waits for them, and re-layouts  9.21 us (4%)
  other arithmetic  4.36 us (2%)
    ppermute x5, waiting for transfers between devices, along_z(): return lax.ppermute(array, 'fsdp', [(f, (f + 16) % 32) for f in range(32)])  53.7 us
    pallas_call x14, Pallas kernels, combine(): pl.pallas_call(kernel, grid=(1,), in_specs=[pl.BlockSpec(block, lambda i,...  41.1 us
    ppermute x22, starting transfers between devices, along(): return lax.ppermute(array, 'fsdp', pairs)  32.4 us
    pallas_call x3, Pallas kernels, products(): pl.pallas_call(body, grid_spec=pltpu.PrefetchScalarGridSpec(num_scalar_pr...  24.3 us
    pallas_call x1, Pallas kernels, all_products(): pl.pallas_call(body, grid_spec=pltpu.PrefetchScalarGridSpec(num_scalar_pr...  17.7 us
    ppermute x22, waiting for transfers between devices, along(): return lax.ppermute(array, 'fsdp', pairs)  16.9 us
    pallas_call x1, Pallas kernels, crossing_products(): pl.pallas_call(body, grid_spec=pltpu.PrefetchScalarGridSpec(num_scalar_pr...  9.3 us
    unnamed x34, local copies, waits for them, and re-layouts  9.21 us
  transfers between devices with their start and end apart: 29, of which 13 were waited for; matrix products, arithmetic and copies ran while one was open for 0% of the time, Pallas kernels for 37%

profile of v6, /device:TPU:0, one launch (start us, length us, event | category | flops | bytes accessed | tf_op | source)
XLA Modules:
  0.0 233.8 jit_solution(10061140091141565538)
XLA Ops:
  10.0 2.5 %convert_divide_fusion = f32[256,1024]{1,0:T(8,128)} fusion(f32[256,1024]{1,0:T(8,128)} %refs_0_.1, bf16[1,256,1024]{2,1,0:T(8,128)(2,1)} %param.8, f32[]{:T(128)S(6)} %convert_element_type.17), kind=kLoop, calls=%fused_computation.4 | loop fusion | flops 1835008 | bytes 2621444 | tf_op jit(solution)/shard_map/div | solution.py:238
  13.2 17.7 %shard_map.85 = (f32[4,8,384,256]{3,2,1,0:T(8,128)}, bf16[1024,1024]{1,0:T(8,128)(2,1)S(1)}) custom-call(s32[9]{0:T(128)} %compare_select_fusion.4.table, bf16[1024,8192]{1,0:T(8,128)(2,1)} %x.9, bf16[1024,1024]{1,0:T(8,128)(2,1)} %k.1), custom_call_target="tpu_custom_call" | custom-call | flops 20000000000 | bytes 1000 | tf_op jit(solution)/shard_map/pallas_call | solution.py:35
  30.9 4.9 %shard_map.86 = (f32[2,4,160,256]{3,2,1,0:T(8,128)}, f32[2,4,160,256]{3,2,1,0:T(8,128)}) custom-call(s32[9]{0:T(128)} %compare_select_fusion.4.table, bf16[1024,8192]{1,0:T(8,128)(2,1)} %x.9, bf16[1024,1024]{1,0:T(8,128)(2,1)S(1)} %get-tuple-element.41.k, f32[4,8,384,256]{3,2,1,0:T(8,128)} %get-tuple-element.42.refs_0_), custom_call_target="tpu_custom_call" | custom-call | flops 20000000000 | bytes 1000 | tf_op jit(solution)/shard_map/pallas_call | solution.py:129
  35.8 3.1 %collective-permute-start.1 = (f32[2,4,160,256]{3,2,1,0:T(8,128)}, f32[2,4,160,256]{3,2,1,0:T(8,128)}, u32[]{:S(2)}, u32[]{:S(2)}) collective-permute-start(f32[2,4,160,256]{3,2,1,0:T(8,128)} %get-tuple-element.47), channel_id=1, source_target_pairs={{0,12},{1,13},{2,14},{3,15},{4,0},{5,1},{6,2},{7,3},{8,4},{9,5},{1... | collective-permute-start | bytes 3932168 | tf_op jit(solution)/shard_map/ppermute | solution.py:168
  38.9 9.3 %shard_map.87 = (f32[4,4,160,256]{3,2,1,0:T(8,128)}, f32[2,4,160,256]{3,2,1,0:T(8,128)}, f32[2,4,160,256]{3,2,1,0:T(8,128)}) custom-call(s32[9]{0:T(128)} %compare_select_fusion.4.table, bf16[1024,8192]{1,0:T(8,128)(2,1)} %x.9, bf16[1024,1024]{1,0:T(8,128)(2,1)S(1)} %get-tuple-element.41.k, f32[2,4,160,256]{3,2,1,0:T(8,128)} %get-tuple-element.43.refs_0_), custom_call_target="tpu_custom_call" | custom-call | flops 20000000000 | bytes 1000 | tf_op jit(solution)/shard_map/pallas_call | solution.py:79
  50.2 8.7 %shard_map.88 = (f32[2,4,160,256]{3,2,1,0:T(8,128)}, f32[2,4,160,256]{3,2,1,0:T(8,128)}, f32[2,4,160,256]{3,2,1,0:T(8,128)}, f32[2,4,160,256]{3,2,1,0:T(8,128)}) custom-call(s32[9]{0:T(128)} %compare_select_fusion.4.table, bf16[1024,8192]{1,0:T(8,128)(2,1)} %x.9, bf16[1024,1024]{1,0:T(8,128)(2,1)S(1)} %get-tuple-element.41.k, ...), custom_call_target="tpu_custom_call" | custom-call | flops 20000000000 | bytes 1000 | tf_op jit(solution)/shard_map/pallas_call | solution.py:129
  58.8 3.1 %collective-permute-start.6 = (f32[2,4,160,256]{3,2,1,0:T(8,128)}, f32[2,4,160,256]{3,2,1,0:T(8,128)S(1)}, u32[]{:S(2)}, u32[]{:S(2)}) collective-permute-start(f32[2,4,160,256]{3,2,1,0:T(8,128)} %get-tuple-element.56), channel_id=1, source_target_pairs={{0,12},{1,13},{2,14},{3,15},{4,0},{5,1},{6,2},{7,3},{8,4},{9,5},{1... | collective-permute-start | bytes 3932168 | tf_op jit(solution)/shard_map/ppermute | solution.py:168
  61.9 10.7 %shard_map.89 = (f32[2,4,160,256]{3,2,1,0:T(8,128)}, f32[2,4,160,256]{3,2,1,0:T(8,128)}, f32[4,4,320,256]{3,2,1,0:T(8,128)}) custom-call(s32[9]{0:T(128)} %compare_select_fusion.4.table, bf16[1024,8192]{1,0:T(8,128)(2,1)} %x.9, bf16[1024,1024]{1,0:T(8,128)(2,1)S(1)} %get-tuple-element.41.k, f32[2,4,160,256]{3,2,1,0:T(8,128)} %get-tuple-element.45.refs_0_), custom_call_target="tpu_custom_call" | custom-call | flops 20000000000 | bytes 1000 | tf_op jit(solution)/shard_map/pallas_call | solution.py:129
  72.6 4.1 %shard_map.90 = (f32[2,4,160,256]{3,2,1,0:T(8,128)}, f32[2,4,160,256]{3,2,1,0:T(8,128)}) custom-call(f32[2,4,160,256]{3,2,1,0:T(8,128)} %get-tuple-element.45.refs_0_, f32[2,4,160,256]{3,2,1,0:T(8,128)} %get-tuple-element.46.refs_1_, f32[2,4,160,256]{3,2,1,0:T(8,128)} %collective-permute-done.refs_2_, f32[2,4,160,256]{3,2,1,0:T(8,128)} %collective-permute-done.1.refs_3_, ...), custom_call_target="tpu_custom_call" | custom-call | flops 4000000000 | bytes 1000 | tf_op jit(solution)/shard_map/pallas_call | solution.py:153
  76.8 3.3 %collective-permute-start.9 = (f32[2,4,160,256]{3,2,1,0:T(8,128)}, f32[2,4,160,256]{3,2,1,0:T(8,128)S(1)}, u32[]{:S(2)}, u32[]{:S(2)}) collective-permute-start(f32[2,4,160,256]{3,2,1,0:T(8,128)} %get-tuple-element.59), channel_id=1, source_target_pairs={{0,12},{1,13},{2,14},{3,15},{4,0},{5,1},{6,2},{7,3},{8,4},{9,5},{1... | collective-permute-start | bytes 3932168 | tf_op jit(solution)/shard_map/ppermute | solution.py:168
  80.0 3.4 %shard_map.91 = (f32[256,1024]{1,0:T(8,128)}, f32[256,1024]{1,0:T(8,128)}) custom-call(f32[256,1024]{1,0:T(8,128)} %refs_0_.1, f32[256,1024]{1,0:T(8,128)} %refs_1_.1, f32[256,1024]{1,0:T(8,128)} %all-reduce.2.cloned.1.call-done.refs_2_, f32[2,4,160,256]{3,2,1,0:T(8,128)} %get-tuple-element.49.refs_3_), custom_call_target="tpu_custom_call" | custom-call | flops 4000000000 | bytes 1000 | tf_op jit(solution)/shard_map/pallas_call | solution.py:153
  83.4 30.6 %collective-permute-done.3.refs_1_.refs_3_.refs_5_.refs_7_ = f32[4,4,160,256]{3,2,1,0:T(8,128)} collective-permute-done((f32[4,4,160,256]{3,2,1,0:T(8,128)}, f32[4,4,160,256]{3,2,1,0:T(8,128)}, u32[]{:S(2)}, u32[]{:S(2)}) %collective-permute-start.3) | collective-permute-done | bytes 2621472 | tf_op jit(solution)/shard_map/ppermute | solution.py:172
  114.5 4.2 %shard_map.92 = (f32[2,4,160,256]{3,2,1,0:T(8,128)}, f32[2,4,160,256]{3,2,1,0:T(8,128)}) custom-call(f32[4,4,320,256]{3,2,1,0:T(8,128)} %get-tuple-element.48.refs_4_.refs_0_.refs_2_.refs_6_.refs_3_.refs_8_.refs_12_.refs_5_, f32[4,4,160,256]{3,2,1,0:T(8,128)} %collective-permute-done.3.refs_1_.refs_3_.refs_5_.refs_7_, ...), custom_call_target="tpu_custom_call" | custom-call | flops 4000000000 | bytes 1000 | tf_op jit(solution)/shard_map/pallas_call | solution.py:153
  119.8 2.9 %collective-permute-start.5 = (f32[2,4,160,256]{3,2,1,0:T(8,128)}, f32[2,4,160,256]{3,2,1,0:T(8,128)S(1)}, u32[]{:S(2)}, u32[]{:S(2)}) collective-permute-start(f32[2,4,160,256]{3,2,1,0:T(8,128)} %get-tuple-element.54), channel_id=1, source_target_pairs={{0,12},{1,13},{2,14},{3,15},{4,0},{5,1},{6,2},{7,3},{8,4},{9,5},{1... | collective-permute-start | bytes 3932168 | tf_op jit(solution)/shard_map/ppermute | solution.py:168
  127.9 3.2 %shard_map.93 = (f32[2,2,160,256]{3,2,1,0:T(8,128)}, f32[2,2,160,256]{3,2,1,0:T(8,128)}) custom-call(f32[2,4,160,256]{3,2,1,0:T(8,128)} %get-tuple-element.55.refs_0_.refs_9_, f32[2,4,160,256]{3,2,1,0:T(8,128)} %copy-done.4, f32[2,4,160,256]{3,2,1,0:T(8,128)} %collective-permute-done.7.refs_2_.refs_11_, ...), custom_call_target="tpu_custom_call" | custom-call | flops 4000000000 | bytes 1000 | tf_op jit(solution)/shard_map/pallas_call | solution.py:153
  131.2 2.8 %collective-permute-start.16 = (f32[2,2,160,256]{3,2,1,0:T(8,128)}, f32[2,2,160,256]{3,2,1,0:T(8,128)S(1)}, u32[]{:S(2)}, u32[]{:S(2)}) collective-permute-start(f32[2,2,160,256]{3,2,1,0:T(8,128)} %get-tuple-element.66), channel_id=1, source_target_pairs={{0,3},{1,0},{2,1},{3,2},{4,7},{5,4},{6,5},{7,6},{8,11},{9,8},{10,9... | collective-permute-start | bytes 1966088 | tf_op jit(solution)/shard_map/ppermute | solution.py:168
  133.9 12.1 %collective-permute-done.2.refs_1_.refs_4_ = f32[2,4,160,256]{3,2,1,0:T(8,128)} collective-permute-done((f32[2,4,160,256]{3,2,1,0:T(8,128)}, f32[2,4,160,256]{3,2,1,0:T(8,128)}, u32[]{:S(2)}, u32[]{:S(2)}) %collective-permute-start.2) | collective-permute-done | bytes 1310752 | tf_op jit(solution)/shard_map/ppermute | solution.py:172
  147.5 4.1 %collective-permute-done.5.refs_5_.refs_2_.refs_14_ = f32[2,4,160,256]{3,2,1,0:T(8,128)S(1)} collective-permute-done((f32[2,4,160,256]{3,2,1,0:T(8,128)}, f32[2,4,160,256]{3,2,1,0:T(8,128)S(1)}, u32[]{:S(2)}, u32[]{:S(2)}) %collective-permute-start.5) | collective-permute-done | bytes 1310752 | tf_op jit(solution)/shard_map/ppermute | solution.py:168
  151.5 3.4 %collective-permute-done.4.refs_2_.refs_6_.refs_10_.refs_7_.refs_8_ = f32[2,4,160,256]{3,2,1,0:T(8,128)} collective-permute-done((f32[2,4,160,256]{3,2,1,0:T(8,128)}, f32[2,4,160,256]{3,2,1,0:T(8,128)}, u32[]{:S(2)}, u32[]{:S(2)}) %collective-permute-start.4) | collective-permute-done | bytes 1310752 | tf_op jit(solution)/shard_map/ppermute | solution.py:168
  155.0 3.2 %shard_map.94 = (f32[4,160,256]{2,1,0:T(8,128)}, f32[4,160,256]{2,1,0:T(8,128)}) custom-call(f32[4,4,320,256]{3,2,1,0:T(8,128)} %get-tuple-element.48.refs_4_.refs_0_.refs_2_.refs_6_.refs_3_.refs_8_.refs_12_.refs_5_, f32[2,4,160,256]{3,2,1,0:T(8,128)} %collective-permute-done.2.refs_1_.refs_4_, ...), custom_call_target="tpu_custom_call" | custom-call | flops 4000000000 | bytes 1000 | tf_op jit(solution)/shard_map/pallas_call | solution.py:153
  160.2 2.6 %shard_map.95 = (f32[2,2,192,256]{3,2,1,0:T(8,128)}, f32[2,2,192,256]{3,2,1,0:T(8,128)}) custom-call(f32[2,4,384,256]{3,2,1,0:T(8,128)} %bitcast.4, f32[2,4,384,256]{3,2,1,0:T(8,128)} %bitcast.5, f32[2,4,384,256]{3,2,1,0:T(8,128)} %bitcast.6, f32[2,4,384,256]{3,2,1,0:T(8,128)} %bitcast.7, f32[4,160,256]{2,1,0:T(8,128)} %get-tuple-element.61.refs_4_), custom_call_target="tpu_custom_call" | custom-call | flops 4000000000 | bytes 1000 | tf_op jit(solution)/shard_map/pallas_call | solution.py:153
  164.8 2.6 %shard_map.96 = (f32[2,160,256]{2,1,0:T(8,128)}, f32[2,160,256]{2,1,0:T(8,128)}) custom-call(f32[2,4,160,256]{3,2,1,0:T(8,128)} %get-tuple-element.55.refs_0_.refs_9_, f32[2,4,160,256]{3,2,1,0:T(8,128)} %copy-done.4, f32[2,4,160,256]{3,2,1,0:T(8,128)} %collective-permute-done.7.refs_2_.refs_11_, f32[2,2,160,256]{3,2,1,0:T(8,128)} %collective-permute-done.15.refs_3_.refs_8_, ...), custom_call_target="tpu_custom_call" | custom-call | flops 4000000000 | bytes 1000 | tf_op jit(solution)/shard_map/pallas_call | solution.py:153
  169.0 3.6 %collective-permute-done.12.refs_1_.refs_5_.refs_9_.refs_13_.refs_6_.refs_7_ = f32[2,4,160,256]{3,2,1,0:T(8,128)S(1)} collective-permute-done((f32[2,4,160,256]{3,2,1,0:T(8,128)}, f32[2,4,160,256]{3,2,1,0:T(8,128)S(1)}, u32[]{:S(2)}, u32[]{:S(2)}) %collective-permute-start.12) | collective-permute-done | bytes 1310752 | tf_op jit(solution)/shard_map/ppermute | solution.py:172
  174.1 2.8 %collective-permute-start.10 = (f32[2,2,192,256]{3,2,1,0:T(8,128)}, f32[2,2,192,256]{3,2,1,0:T(8,128)}, u32[]{:S(2)}, u32[]{:S(2)}) collective-permute-start(f32[2,2,192,256]{3,2,1,0:T(8,128)} %get-tuple-element.62), channel_id=1, source_target_pairs={{0,12},{1,13},{2,14},{3,15},{4,0},{5,1},{6,2},{7,3},{8,4},{9,5},{1... | collective-permute-start | bytes 2359304 | tf_op jit(solution)/shard_map/ppermute | solution.py:168
  179.4 2.7 %shard_map.97 = (f32[2,1,160,256]{3,2,1,0:T(8,128)}, f32[2,1,160,256]{3,2,1,0:T(8,128)}) custom-call(f32[4,4,320,256]{3,2,1,0:T(8,128)} %get-tuple-element.48.refs_4_.refs_0_.refs_2_.refs_6_.refs_3_.refs_8_.refs_12_.refs_5_, f32[2,4,160,256]{3,2,1,0:T(8,128)} %copy-done, f32[2,4,160,256]{3,2,1,0:T(8,128)} %copy-done.1, f32[4,160,256]{2,1,0:T(8,128)} %copy-done.3, ...), custom_call_target="tpu_custom_call" | custom-call | flops 4000000000 | bytes 1000 | tf_op jit(solution)/shard_map/pallas_call | solution.py:153
  182.0 2.8 %collective-permute-start.18 = (f32[2,1,160,256]{3,2,1,0:T(8,128)}, f32[2,1,160,256]{3,2,1,0:T(8,128)S(1)}, u32[]{:S(2)}, u32[]{:S(2)}) collective-permute-start(f32[2,1,160,256]{3,2,1,0:T(8,128)} %get-tuple-element.69), channel_id=1, source_target_pairs={{0,3},{1,0},{2,1},{3,2},{4,7},{5,4},{6,5},{7,6},{8,11},{9,8},{10,9... | collective-permute-start | bytes 983048 | tf_op jit(solution)/shard_map/ppermute | solution.py:168
  184.8 2.8 %shard_map.98 = (f32[320,256]{1,0:T(8,128)}, f32[320,256]{1,0:T(8,128)}) custom-call(f32[2,4,160,256]{3,2,1,0:T(8,128)} %get-tuple-element.55.refs_0_.refs_9_, f32[2,4,160,256]{3,2,1,0:T(8,128)} %copy-done.4, f32[2,4,160,256]{3,2,1,0:T(8,128)} %collective-permute-done.7.refs_2_.refs_11_, f32[2,2,160,256]{3,2,1,0:T(8,128)} %copy-done.11, ...), custom_call_target="tpu_custom_call" | custom-call | flops 4000000000 | bytes 1000 | tf_op jit(solution)/shard_map/pallas_call | solution.py:153
  189.7 3.6 %collective-permute-done.17.refs_4_.refs_10_ = f32[2,1,160,256]{3,2,1,0:T(8,128)S(1)} collective-permute-done((f32[2,1,160,256]{3,2,1,0:T(8,128)}, f32[2,1,160,256]{3,2,1,0:T(8,128)S(1)}, u32[]{:S(2)}, u32[]{:S(2)}) %collective-permute-start.17) | collective-permute-done | bytes 327712 | tf_op jit(solution)/shard_map/ppermute | solution.py:168
  206.9 2.4 %shard_map.101.refs_6_.refs_4_ = f32[320,256]{1,0:T(8,128)} custom-call(f32[4,4,320,256]{3,2,1,0:T(8,128)} %get-tuple-element.48.refs_4_.refs_0_.refs_2_.refs_6_.refs_3_.refs_8_.refs_12_.refs_5_, f32[2,4,160,256]{3,2,1,0:T(8,128)} %copy-done, f32[2,4,160,256]{3,2,1,0:T(8,128)} %copy-done.1, f32[4,160,256]{2,1,0:T(8,128)} %copy-done.3, ...), custom_call_target="tpu_custom_call" | custom-call | flops 4000000000 | bytes 1000 | tf_op jit(solution)/shard_map/pallas_call | solution.py:153
  212.3 2.5 %shard_map.102 = (f32[384,256]{1,0:T(8,128)}, f32[384,256]{1,0:T(8,128)}) custom-call(f32[2,4,384,256]{3,2,1,0:T(8,128)} %bitcast.10, f32[2,2,192,256]{3,2,1,0:T(8,128)} %collective-permute-done.10.refs_3_.refs_1_, f32[2,192,256]{2,1,0:T(8,128)} %copy-done.13, f32[2,4,384,256]{3,2,1,0:T(8,128)} %bitcast.11, f32[2,2,192,256]{3,2,1,0:T(8,128)} %copy-done.10, ...), custom_call_target="tpu_custom_call" | custom-call | flops 4000000000 | bytes 1000 | tf_op jit(solution)/shard_map/pallas_call | solution.py:153
  216.8 6.0 %collective-permute-done.26.refs_1_ = f32[384,256]{1,0:T(8,128)S(1)} collective-permute-done((f32[384,256]{1,0:T(8,128)}, f32[384,256]{1,0:T(8,128)S(1)}, u32[]{:S(2)}, u32[]{:S(2)}) %collective-permute-start.26) | collective-permute-done | bytes 393248 | tf_op jit(solution)/shard_map/ppermute | solution.py:172
  223.6 2.7 %shard_map.103 = f32[1,256,1024]{2,1,0:T(8,128)} custom-call(f32[384,256]{1,0:T(8,128)} %get-tuple-element.77.refs_0_, f32[384,256]{1,0:T(8,128)} %copy-done.14, f32[320,256]{1,0:T(8,128)} %get-tuple-element.71.refs_10_.refs_2_, f32[320,256]{1,0:T(8,128)} %copy-done.16, f32[320,256]{1,0:T(8,128)} %shard_map.101.refs_6_.refs_4_), custom_call_target="tpu_custom_call" | custom-call | flops 4000000000 | bytes 1000 | tf_op jit(solution)/shard_map/pallas_call | solution.py:153
  (84 shorter events, 43.2 us)
Async XLA Ops:
  8.0 72.0 %all-reduce.2.cloned.1.call-start = ((), (), s32[]{:S(2)}) async-start(), calls=%async_computation.1 | async-start | bytes 2097152 | tf_op jit(solution)/shard_map/psum | solution.py:238
  12.6 147.7 %reduce-scatter.2.cloned.1.call-start = ((), (), s32[]{:S(2)}) async-start(), calls=%async_computation.2 | async-start | bytes 15728640 | tf_op jit(solution)/shard_map/reduce_scatter | solution.py:176
  35.8 36.8 %collective-permute-start.1 = (f32[2,4,160,256]{3,2,1,0:T(8,128)}, f32[2,4,160,256]{3,2,1,0:T(8,128)}, u32[]{:S(2)}, u32[]{:S(2)}) collective-permute-start(f32[2,4,160,256]{3,2,1,0:T(8,128)} %get-tuple-element.47), channel_id=1, source_target_pairs={{0,12},{1,13},{2,14},{3,15},{4,0},{5,1},{6,2},{7,3},{8,4},{9,5},{1... | collective-permute-start | bytes 3932168 | tf_op jit(solution)/shard_map/ppermute | solution.py:168
  38.9 33.7 %collective-permute-start = (f32[2,4,160,256]{3,2,1,0:T(8,128)}, f32[2,4,160,256]{3,2,1,0:T(8,128)}, u32[]{:S(2)}, u32[]{:S(2)}) collective-permute-start(f32[2,4,160,256]{3,2,1,0:T(8,128)} %get-tuple-element.43.refs_0_), channel_id=1, source_target_pairs={{0,4},{1,5},{2,6},{3,7},{4,8},{5,9},{6,10},{7,11},{8,12},{9,13},{1... | collective-permute-start | bytes 3932168 | tf_op jit(solution)/shard_map/ppermute | solution.py:168
  48.2 65.7 %collective-permute-start.3 = (f32[4,4,160,256]{3,2,1,0:T(8,128)}, f32[4,4,160,256]{3,2,1,0:T(8,128)}, u32[]{:S(2)}, u32[]{:S(2)}) collective-permute-start(f32[4,4,160,256]{3,2,1,0:T(8,128)} %get-tuple-element.44.refs_0_), channel_id=1, source_target_pairs={{0,16},{1,17},{2,18},{3,19},{4,20},{5,21},{6,22},{7,23},{8,24},{9,... | collective-permute-start | bytes 7864328 | tf_op jit(solution)/shard_map/ppermute | solution.py:172
  58.8 59.8 %collective-permute-start.6 = (f32[2,4,160,256]{3,2,1,0:T(8,128)}, f32[2,4,160,256]{3,2,1,0:T(8,128)S(1)}, u32[]{:S(2)}, u32[]{:S(2)}) collective-permute-start(f32[2,4,160,256]{3,2,1,0:T(8,128)} %get-tuple-element.56), channel_id=1, source_target_pairs={{0,12},{1,13},{2,14},{3,15},{4,0},{5,1},{6,2},{7,3},{8,4},{9,5},{1... | collective-permute-start | bytes 3932168 | tf_op jit(solution)/shard_map/ppermute | solution.py:168
  61.9 60.8 %collective-permute-start.8 = (f32[2,4,160,256]{3,2,1,0:T(8,128)}, f32[2,4,160,256]{3,2,1,0:T(8,128)}, u32[]{:S(2)}, u32[]{:S(2)}) collective-permute-start(f32[2,4,160,256]{3,2,1,0:T(8,128)} %get-tuple-element.58), channel_id=1, source_target_pairs={{0,4},{1,5},{2,6},{3,7},{4,8},{5,9},{6,10},{7,11},{8,12},{9,13},{1... | collective-permute-start | bytes 3932168 | tf_op jit(solution)/shard_map/ppermute | solution.py:168
  76.8 47.8 %collective-permute-start.9 = (f32[2,4,160,256]{3,2,1,0:T(8,128)}, f32[2,4,160,256]{3,2,1,0:T(8,128)S(1)}, u32[]{:S(2)}, u32[]{:S(2)}) collective-permute-start(f32[2,4,160,256]{3,2,1,0:T(8,128)} %get-tuple-element.59), channel_id=1, source_target_pairs={{0,12},{1,13},{2,14},{3,15},{4,0},{5,1},{6,2},{7,3},{8,4},{9,5},{1... | collective-permute-start | bytes 3932168 | tf_op jit(solution)/shard_map/ppermute | solution.py:168
  80.0 47.9 %collective-permute-start.7 = (f32[2,4,160,256]{3,2,1,0:T(8,128)}, f32[2,4,160,256]{3,2,1,0:T(8,128)}, u32[]{:S(2)}, u32[]{:S(2)}) collective-permute-start(f32[2,4,160,256]{3,2,1,0:T(8,128)} %get-tuple-element.49.refs_3_), channel_id=1, source_target_pairs={{0,4},{1,5},{2,6},{3,7},{4,8},{5,9},{6,10},{7,11},{8,12},{9,13},{1... | collective-permute-start | bytes 3932168 | tf_op jit(solution)/shard_map/ppermute | solution.py:168
  114.0 32.0 %collective-permute-start.2 = (f32[2,4,160,256]{3,2,1,0:T(8,128)}, f32[2,4,160,256]{3,2,1,0:T(8,128)}, u32[]{:S(2)}, u32[]{:S(2)}) collective-permute-start(f32[2,4,160,256]{3,2,1,0:T(8,128)} %get-tuple-element.52), channel_id=1, source_target_pairs={{0,16},{1,17},{2,18},{3,19},{4,20},{5,21},{6,22},{7,23},{8,24},{9,... | collective-permute-start | bytes 3932168 | tf_op jit(solution)/shard_map/ppermute | solution.py:172
  119.8 31.7 %collective-permute-start.5 = (f32[2,4,160,256]{3,2,1,0:T(8,128)}, f32[2,4,160,256]{3,2,1,0:T(8,128)S(1)}, u32[]{:S(2)}, u32[]{:S(2)}) collective-permute-start(f32[2,4,160,256]{3,2,1,0:T(8,128)} %get-tuple-element.54), channel_id=1, source_target_pairs={{0,12},{1,13},{2,14},{3,15},{4,0},{5,1},{6,2},{7,3},{8,4},{9,5},{1... | collective-permute-start | bytes 3932168 | tf_op jit(solution)/shard_map/ppermute | solution.py:168
  122.7 32.3 %collective-permute-start.4 = (f32[2,4,160,256]{3,2,1,0:T(8,128)}, f32[2,4,160,256]{3,2,1,0:T(8,128)}, u32[]{:S(2)}, u32[]{:S(2)}) collective-permute-start(f32[2,4,160,256]{3,2,1,0:T(8,128)} %get-tuple-element.53.refs_12_), channel_id=1, source_target_pairs={{0,4},{1,5},{2,6},{3,7},{4,8},{5,9},{6,10},{7,11},{8,12},{9,13},{1... | collective-permute-start | bytes 3932168 | tf_op jit(solution)/shard_map/ppermute | solution.py:168
  125.6 47.0 %collective-permute-start.12 = (f32[2,4,160,256]{3,2,1,0:T(8,128)}, f32[2,4,160,256]{3,2,1,0:T(8,128)S(1)}, u32[]{:S(2)}, u32[]{:S(2)}) collective-permute-start(f32[2,4,160,256]{3,2,1,0:T(8,128)} %get-tuple-element.64), channel_id=1, source_target_pairs={{0,16},{1,17},{2,18},{3,19},{4,20},{5,21},{6,22},{7,23},{8,24},{9,... | collective-permute-start | bytes 3932168 | tf_op jit(solution)/shard_map/ppermute | solution.py:172
  131.2 31.6 %collective-permute-start.16 = (f32[2,2,160,256]{3,2,1,0:T(8,128)}, f32[2,2,160,256]{3,2,1,0:T(8,128)S(1)}, u32[]{:S(2)}, u32[]{:S(2)}) collective-permute-start(f32[2,2,160,256]{3,2,1,0:T(8,128)} %get-tuple-element.66), channel_id=1, source_target_pairs={{0,3},{1,0},{2,1},{3,2},{4,7},{5,4},{6,5},{7,6},{8,11},{9,8},{10,9... | collective-permute-start | bytes 1966088 | tf_op jit(solution)/shard_map/ppermute | solution.py:168
  146.0 18.8 %collective-permute-start.15 = (f32[2,2,160,256]{3,2,1,0:T(8,128)}, f32[2,2,160,256]{3,2,1,0:T(8,128)}, u32[]{:S(2)}, u32[]{:S(2)}) collective-permute-start(f32[2,2,160,256]{3,2,1,0:T(8,128)} %get-tuple-element.60.refs_6_), channel_id=1, source_target_pairs={{0,1},{1,2},{2,3},{3,0},{4,5},{5,6},{6,7},{7,4},{8,9},{9,10},{10,1... | collective-permute-start | bytes 1966088 | tf_op jit(solution)/shard_map/ppermute | solution.py:168
  158.2 16.0 %collective-permute-start.14 = (f32[4,160,256]{2,1,0:T(8,128)}, f32[4,160,256]{2,1,0:T(8,128)S(1)}, u32[]{:S(2)}, u32[]{:S(2)}) collective-permute-start(f32[4,160,256]{2,1,0:T(8,128)} %get-tuple-element.65), channel_id=1, source_target_pairs={{0,12},{1,13},{2,14},{3,15},{4,0},{5,1},{6,2},{7,3},{8,4},{9,5},{1... | collective-permute-start | bytes 1966088 | tf_op jit(solution)/shard_map/ppermute | solution.py:168
  159.4 19.1 %collective-permute-start.13 = (f32[4,160,256]{2,1,0:T(8,128)}, f32[4,160,256]{2,1,0:T(8,128)S(1)}, u32[]{:S(2)}, u32[]{:S(2)}) collective-permute-start(f32[4,160,256]{2,1,0:T(8,128)} %get-tuple-element.61.refs_4_), channel_id=1, source_target_pairs={{0,4},{1,5},{2,6},{3,7},{4,8},{5,9},{6,10},{7,11},{8,12},{9,13},{1... | collective-permute-start | bytes 1966088 | tf_op jit(solution)/shard_map/ppermute | solution.py:168
  163.6 34.7 %collective-permute-start.11 = (f32[2,2,192,256]{3,2,1,0:T(8,128)}, f32[2,2,192,256]{3,2,1,0:T(8,128)S(1)}, u32[]{:S(2)}, u32[]{:S(2)}) collective-permute-start(f32[2,2,192,256]{3,2,1,0:T(8,128)} %get-tuple-element.63.refs_8_), channel_id=1, source_target_pairs={{0,4},{1,5},{2,6},{3,7},{4,8},{5,9},{6,10},{7,11},{8,12},{9,13},{1... | collective-permute-start | bytes 2359304 | tf_op jit(solution)/shard_map/ppermute | solution.py:168
  167.4 17.4 %collective-permute-start.20 = (f32[2,160,256]{2,1,0:T(8,128)}, f32[2,160,256]{2,1,0:T(8,128)}, u32[]{:S(2)}, u32[]{:S(2)}) collective-permute-start(f32[2,160,256]{2,1,0:T(8,128)} %get-tuple-element.70), channel_id=1, source_target_pairs={{0,3},{1,0},{2,1},{3,2},{4,7},{5,4},{6,5},{7,6},{8,11},{9,8},{10,9... | collective-permute-start | bytes 983048 | tf_op jit(solution)/shard_map/ppermute | solution.py:168
  172.7 5.9 %copy-start = (f32[2,4,160,256]{3,2,1,0:T(8,128)}, f32[2,4,160,256]{3,2,1,0:T(8,128)S(1)}, u32[]{:S(2)}) copy-start(f32[2,4,160,256]{3,2,1,0:T(8,128)S(1)} %collective-permute-done.12.refs_1_.refs_5_.refs_9_.refs_13_.refs_6_.refs_7_) | copy-start | bytes 3932164
  172.7 12.2 %collective-permute-start.19 = (f32[2,160,256]{2,1,0:T(8,128)}, f32[2,160,256]{2,1,0:T(8,128)}, u32[]{:S(2)}, u32[]{:S(2)}) collective-permute-start(f32[2,160,256]{2,1,0:T(8,128)} %get-tuple-element.67.refs_16_), channel_id=1, source_target_pairs={{0,1},{1,2},{2,3},{3,0},{4,5},{5,6},{6,7},{7,4},{8,9},{9,10},{10,1... | collective-permute-start | bytes 983048 | tf_op jit(solution)/shard_map/ppermute | solution.py:168
  174.1 4.4 %copy-start.2 = (f32[4,160,256]{2,1,0:T(8,128)}, f32[4,160,256]{2,1,0:T(8,128)S(1)}, u32[]{:S(2)}) copy-start(f32[4,160,256]{2,1,0:T(8,128)S(1)} %collective-permute-done.14.refs_7_.refs_11_.refs_8_.refs_9_) | copy-start | bytes 1966084
  174.1 24.2 %collective-permute-start.10 = (f32[2,2,192,256]{3,2,1,0:T(8,128)}, f32[2,2,192,256]{3,2,1,0:T(8,128)}, u32[]{:S(2)}, u32[]{:S(2)}) collective-permute-start(f32[2,2,192,256]{3,2,1,0:T(8,128)} %get-tuple-element.62), channel_id=1, source_target_pairs={{0,12},{1,13},{2,14},{3,15},{4,0},{5,1},{6,2},{7,3},{8,4},{9,5},{1... | collective-permute-start | bytes 2359304 | tf_op jit(solution)/shard_map/ppermute | solution.py:168
  182.0 7.7 %collective-permute-start.18 = (f32[2,1,160,256]{3,2,1,0:T(8,128)}, f32[2,1,160,256]{3,2,1,0:T(8,128)S(1)}, u32[]{:S(2)}, u32[]{:S(2)}) collective-permute-start(f32[2,1,160,256]{3,2,1,0:T(8,128)} %get-tuple-element.69), channel_id=1, source_target_pairs={{0,3},{1,0},{2,1},{3,2},{4,7},{5,4},{6,5},{7,6},{8,11},{9,8},{10,9... | collective-permute-start | bytes 983048 | tf_op jit(solution)/shard_map/ppermute | solution.py:168
  184.8 8.5 %collective-permute-start.17 = (f32[2,1,160,256]{3,2,1,0:T(8,128)}, f32[2,1,160,256]{3,2,1,0:T(8,128)S(1)}, u32[]{:S(2)}, u32[]{:S(2)}) collective-permute-start(f32[2,1,160,256]{3,2,1,0:T(8,128)} %get-tuple-element.68.refs_10_), channel_id=1, source_target_pairs={{0,1},{1,2},{2,3},{3,0},{4,5},{5,6},{6,7},{7,4},{8,9},{9,10},{10,1... | collective-permute-start | bytes 983048 | tf_op jit(solution)/shard_map/ppermute | solution.py:168
  196.3 9.2 %collective-permute-start.24 = (f32[1,160,256]{2,1,0:T(8,128)}, f32[1,160,256]{2,1,0:T(8,128)S(1)}, u32[]{:S(2)}, u32[]{:S(2)}) collective-permute-start(f32[1,160,256]{2,1,0:T(8,128)} %get-tuple-element.75), channel_id=1, source_target_pairs={{0,3},{1,0},{2,1},{3,2},{4,7},{5,4},{6,5},{7,6},{8,11},{9,8},{10,9... | collective-permute-start | bytes 491528 | tf_op jit(solution)/shard_map/ppermute | solution.py:168
  196.5 7.1 %copy-start.15 = (f32[320,256]{1,0:T(8,128)S(1)}, f32[320,256]{1,0:T(8,128)}, u32[]{:S(2)}) copy-start(f32[320,256]{1,0:T(8,128)} %get-tuple-element.76) | copy-start | bytes 983044
  196.5 9.1 %collective-permute-start.23 = (f32[1,160,256]{2,1,0:T(8,128)}, f32[1,160,256]{2,1,0:T(8,128)S(1)}, u32[]{:S(2)}, u32[]{:S(2)}) collective-permute-start(f32[1,160,256]{2,1,0:T(8,128)} %get-tuple-element.72.refs_4_), channel_id=1, source_target_pairs={{0,1},{1,2},{2,3},{3,0},{4,5},{5,6},{6,7},{7,4},{8,9},{9,10},{10,1... | collective-permute-start | bytes 491528 | tf_op jit(solution)/shard_map/ppermute | solution.py:168
  201.6 9.1 %collective-permute-start.22 = (f32[2,192,256]{2,1,0:T(8,128)}, f32[2,192,256]{2,1,0:T(8,128)S(1)}, u32[]{:S(2)}, u32[]{:S(2)}) collective-permute-start(f32[2,192,256]{2,1,0:T(8,128)} %get-tuple-element.74), channel_id=1, source_target_pairs={{0,12},{1,13},{2,14},{3,15},{4,0},{5,1},{6,2},{7,3},{8,4},{9,5},{1... | collective-permute-start | bytes 1179656 | tf_op jit(solution)/shard_map/ppermute | solution.py:168
  201.6 9.2 %collective-permute-start.21 = (f32[2,192,256]{2,1,0:T(8,128)}, f32[2,192,256]{2,1,0:T(8,128)S(1)}, u32[]{:S(2)}, u32[]{:S(2)}) collective-permute-start(f32[2,192,256]{2,1,0:T(8,128)} %get-tuple-element.73.refs_12_), channel_id=1, source_target_pairs={{0,4},{1,5},{2,6},{3,7},{4,8},{5,9},{6,10},{7,11},{8,12},{9,13},{1... | collective-permute-start | bytes 1179656 | tf_op jit(solution)/shard_map/ppermute | solution.py:168
  203.6 7.1 %collective-permute-start.25 = (f32[320,256]{1,0:T(8,128)S(1)}, f32[320,256]{1,0:T(8,128)S(1)}, u32[]{:S(2)}, u32[]{:S(2)}) collective-permute-start(f32[320,256]{1,0:T(8,128)S(1)} %copy-done.15), channel_id=1, source_target_pairs={{0,16},{1,17},{2,18},{3,19},{4,20},{5,21},{6,22},{7,23},{8,24},{9,... | collective-permute-start | bytes 983048 | tf_op jit(solution)/shard_map/ppermute | solution.py:172
  214.9 8.0 %collective-permute-start.26 = (f32[384,256]{1,0:T(8,128)}, f32[384,256]{1,0:T(8,128)S(1)}, u32[]{:S(2)}, u32[]{:S(2)}) collective-permute-start(f32[384,256]{1,0:T(8,128)} %get-tuple-element.78), channel_id=1, source_target_pairs={{0,16},{1,17},{2,18},{3,19},{4,20},{5,21},{6,22},{7,23},{8,24},{9,... | collective-permute-start | bytes 1179656 | tf_op jit(solution)/shard_map/ppermute | solution.py:172
  (14 other events, 17.0 us)
Sparse Core Ops, SparseCore 0:
  12.7 51.6 all-reduce.1
Sparse Core Ops, SparseCore 1:
  31.0 128.3 reduce-scatter.1

commit v7 on v6

--- a/solution.py
+++ b/solution.py
@@ -66,7 +66,7 @@
         def emit(h, out, n):
             value = jnp.dot(k[low + h * half : low + (h + 1) * half, :], x[...], preferred_element_type=jnp.float32)
             for place in range(ROW):
-                out[n, (place - table[STRIPS]) & (ROW - 1)] = value[:, place * WIDTH : (place + 1) * WIDTH]
+                out[n, place] = value[:, place * WIDTH : (place + 1) * WIDTH]
 
         for at, first, second in ((0, soon, soon), (1, later, soon), (2, soon, later), (3, last, last)):
 
@@ -112,7 +112,7 @@
             def emit(low=low, height=height, out=out):
                 value = jnp.dot(k[low : low + height, :], x[...], preferred_element_type=jnp.float32)
                 for place in range(ROW):
-                    out[0, (place - table[STRIPS]) & (ROW - 1)] = value[:, place * WIDTH : (place + 1) * WIDTH]
+                    out[0, place] = value[:, place * WIDTH : (place + 1) * WIDTH]
 
             if number == count:
                 emit()
@@ -162,9 +162,8 @@
     )(*[p[0] for p in pieces], *after)
 
 
-def along(axis, array, step):
-    stride = 1 if axis == "x" else 4
-    pairs = [(f, f + ((f // stride + step) % 4 - f // stride % 4) * stride) for f in range(32)]
+def along_y(array, step):
+    pairs = [(f, f + ((f // 4 + step) % 4 - f // 4 % 4) * 4) for f in range(32)]
     return lax.ppermute(array, "fsdp", pairs)
 
 
@@ -176,7 +175,7 @@
     return lax.psum_scatter(array, "fsdp", scatter_dimension=0, axis_index_groups=X_RINGS, tiled=True)[0]
 
 
-def reduce_ring(axis, terms, outer, rows):
+def reduce_ring(terms, outer, rows):
     shape = (outer, rows, WIDTH)
     count = len(terms(0, 0))
 
@@ -193,7 +192,7 @@
     after = yield
     pieces = terms(2, 0) + terms(1, 1) + terms(2, 1) + terms(3, 0)
     up, down = combine(first, pieces, [(2,) + shape] * 2, after)
-    up_in, down_in = along(axis, up, 1), along(axis, down, -1)
+    up_in, down_in = along_y(up, 1), along_y(down, -1)
     after = yield [up]
 
     def got(array):
@@ -205,7 +204,7 @@
 
     pieces = terms(1, 0) + got(up_in) + terms(3, 1) + got(down_in)
     up, down = combine(second, pieces, [shape] * 2, after)
-    up_last, down_last = along(axis, up, 1), along(axis, down, -1)
+    up_last, down_last = along_y(up, 1), along_y(down, -1)
     yield [up], lambda half: [(down_in, 1), (up_last, None)] if half == 0 else [(up_in, 1), (down_last, None)]
 
 
@@ -227,9 +226,8 @@
     groups = lax.axis_size("rep")
     group = lax.axis_index("rep")
     me = lax.axis_index("fsdp")
-    at = jnp.arange(STRIPS + 1)
-    table = 4 * ((me // 16 + at // 4) % 2) + (me // 4 + at) % 4
-    table = jnp.where(at == STRIPS, me % 4, table).astype(jnp.int32)
+    at = jnp.arange(STRIPS)
+    table = (4 * ((me // 16 + at // 4) % 2) + (me // 4 + at) % 4).astype(jnp.int32)
 
     picked = jnp.sum(jnp.where(jnp.arange(groups) == group, exps, 0))
     scale_up = jnp.left_shift(1, picked).astype(jnp.float32)
@@ -250,7 +248,7 @@
         [(b_low, half, 0, 2, 1), (b_high, half, 0, 2, 1)],
         [a],
     )
-    b_up1, b_down1 = along("y", b_far[0], 1), along("y", b_far[1], -1)
+    b_up1, b_down1 = along_y(b_far[0], 1), along_y(b_far[1], -1)
     c_far = crossing_products(inputs, turned, table, c_low, C // 2, b_far[:1])
     c_z = [along_z(array) for array in c_far]
     c_places = {(2, 0): (0, 0), (2, 1): (0, 1), (1, 1): (0, 2), (3, 0): (0, 3)}
@@ -264,7 +262,7 @@
         [(low, half, first, 2, 1) for first in (0, 2) for low in (b_low, b_high)],
         c_far[:1],
     )
-    b_up2, b_down2 = along("y", b_near[1], 1), along("y", b_near[2], -1)
+    b_up2, b_down2 = along_y(b_near[1], 1), along_y(b_near[2], -1)
     *b_own, c_near = products(
         inputs,
         turned,
@@ -280,11 +278,14 @@
         down[...] = near_down[...] + got_down[...]
 
     b_last = combine(b_third, [b_near[0], b_near[3], b_up1, b_down1], [(2, ROW, half, WIDTH)] * 2, [c_near])
-    b_up3, b_down3 = along("y", b_last[0], 1), along("y", b_last[1], -1)
-
-    def b_terms(dx, h):
-        arrays = (b_own[0], b_down2, b_up3) if h == 0 else (b_own[1], b_up2, b_down3)
-        return [(array, (2, 1, half, WIDTH), (0, dx, 0, 0)) for array in arrays]
+    b_up3, b_down3 = along_y(b_last[0], 1), along_y(b_last[1], -1)
+
+    def b_home(own0, own1, up2, down2, up3, down3, out):
+        for z in range(2):
+            for x in range(ROW):
+                low = B * z
+                out[x, low : low + half, :] = own0[z, x] + down2[z, x] + up3[z, x]
+                out[x, low + half : low + B, :] = own1[z, x] + up2[z, x] + down3[z, x]
 
     def c_terms(dy, h):
         block = (1, ROW, C // 2, WIDTH)
@@ -307,46 +308,31 @@
 
     new_params, new_momentum = combine(nesterov, [params, momentum, total], [params.shape] * 2, b_last[:1])
 
-    ring_b = reduce_ring("x", b_terms, 2, half)
-    ring_c = reduce_ring("y", c_terms, ROW, C // 2)
-    ring_a = reduce_ring("y", a_terms, 2, A // 2)
-    next(ring_b), next(ring_c), next(ring_a)
+    ring_c = reduce_ring(c_terms, ROW, C // 2)
+    ring_a = reduce_ring(a_terms, 2, A // 2)
+    next(ring_c), next(ring_a)
     done = ring_c.send([new_params])
-    done = ring_b.send(done)
+    (b_sum,) = combine(b_home, [*b_own, b_up2, b_down2, b_up3, b_down3], [(ROW, 2 * B, WIDTH)], done)
+    b_x = over_x(b_sum)
+    b_in = along_z(b_x[B:])
+    done = ring_a.send([b_sum])
     done, c_got = ring_c.send(done)
-    done = ring_a.send(done)
-    done, b_got = ring_b.send(done)
-
-    def c_x_terms(dx, h):
-        block = (1, 1, C // 2, WIDTH)
-        terms = [(c_near, block, (0, dx, h, 0)), (c_z[2], block, (h, dx, 0, 0))]
-        for array, n in c_got(h):
-            terms.append((array, block[1:], (dx, 0, 0)) if n is None else (array, block, (n, dx, 0, 0)))
-        return terms
+    done, a_got = ring_a.send(done)
 
     def keep_and_cross(low, high, keep, cross):
         rows = low.shape[1]
         keep[:rows, :], keep[rows:, :] = low[0], high[0]
         cross[:rows, :], cross[rows:, :] = low[1], high[1]
 
-    ring_cx = reduce_ring("x", c_x_terms, 1, C // 2)
-    next(ring_cx)
-    done = ring_cx.send(done)
-    b_keep, b_cross = settle(
-        b_terms(0, 0) + whole(b_got(0)), b_terms(0, 1) + whole(b_got(1)), keep_and_cross, [(B, WIDTH)] * 2, done
-    )
-    b_in = along_z(b_cross)
-    done, cx_got = ring_cx.send([b_keep])
-    done, a_got = ring_a.send(done)
-
     def c_home(low, high, out):
-        out[: C // 2, :], out[C // 2 :, :] = low[0], high[0]
-
-    (c_own,) = settle(
-        c_x_terms(0, 0) + whole(cx_got(0)), c_x_terms(0, 1) + whole(cx_got(1)), c_home, [(C, WIDTH)], done
-    )
+        out[:, : C // 2, :], out[:, C // 2 :, :] = low, high
+
+    (c_sum,) = settle(
+        c_terms(0, 0) + whole(c_got(0)), c_terms(0, 1) + whole(c_got(1)), c_home, [(ROW, C, WIDTH)], done
+    )
+    c_own = over_x(c_sum)
     a_keep, a_cross = settle(
-        a_terms(0, 0) + whole(a_got(0)), a_terms(0, 1) + whole(a_got(1)), keep_and_cross, [(A, WIDTH)] * 2, [c_own, b_in]
+        a_terms(0, 0) + whole(a_got(0)), a_terms(0, 1) + whole(a_got(1)), keep_and_cross, [(A, WIDTH)] * 2, [c_sum, b_in]
     )
     a_in = along_z(a_cross)
 
@@ -355,7 +341,7 @@
         out[0] = value.T
 
     (kv_grad,) = combine(
-        assemble, [a_keep, a_in, b_keep, b_in, c_own], [(1, WIDTH, A + B + C)]
+        assemble, [a_keep, a_in, (b_x, (B, WIDTH), (0, 0)), b_in, c_own], [(1, WIDTH, A + B + C)]
     )
     return (new_params, new_momentum, kv_grad)
 

time: 235 us -> 238 us (1.013)
  waiting for transfers between devices: 70.7 us -> 101 us
  starting transfers between devices: 40.9 us -> 23.6 us
  Pallas kernels: 92.4 us -> 85.5 us
  local copies, waits for them, and re-layouts: 9.21 us -> 6.43 us
    ppermute x22 -> x14, waiting for transfers between devices: 16.9 us -> 30.9 us  [along_y(): return lax.ppermute(array, 'fsdp', pairs)]
    ppermute x22 -> x14, starting transfers between devices: 32.4 us -> 18.4 us  [along_y(): return lax.ppermute(array, 'fsdp', pairs)]
    reduce_scatter x1 -> x3, waiting for transfers between devices: 0.01 us -> 11.4 us  [over_x(): lax.psum_scatter(array, 'fsdp', scatter_dimension=0, axis_index_groups=X_...]
    pallas_call x14 -> x10, Pallas kernels: 41.1 us -> 34.3 us  [combine(): pl.pallas_call(kernel, grid=(1,), in_specs=[pl.BlockSpec(block, lambda i,...]
    ppermute x5, waiting for transfers between devices: 53.7 us -> 58.7 us  [along_z(): return lax.ppermute(array, 'fsdp', [(f, (f + 16) % 32) for f in range(32)])]
    unnamed x34 -> x26, local copies, waits for them, and re-layouts: 9.21 us -> 5.44 us
    ppermute x5, starting transfers between devices: 8.41 us -> 4.98 us  [along_z(): return lax.ppermute(array, 'fsdp', [(f, (f + 16) % 32) for f in range(32)])]
  transfers between devices with their start and end apart: 29 -> 23, of which waited for: 13 -> 14; matrix products, arithmetic and copies ran while one was open for 0% -> 1% of each run, Pallas kernels for 37% -> 35%
where the time goes in v7:
time: 238 us; the launch traced here: 237 us
  waiting for transfers between devices  101 us (42%)
  Pallas kernels  85.5 us (36%)
  starting transfers between devices  23.6 us (10%)
  between operations  16.4 us (7%)
  local copies, waits for them, and re-layouts  6.43 us (3%)
  other arithmetic  4.36 us (2%)
    ppermute x5, waiting for transfers between devices, along_z(): return lax.ppermute(array, 'fsdp', [(f, (f + 16) % 32) for f in range(32)])  58.7 us
    pallas_call x10, Pallas kernels, combine(): pl.pallas_call(kernel, grid=(1,), in_specs=[pl.BlockSpec(block, lambda i,...  34.3 us
    ppermute x14, waiting for transfers between devices, along_y(): return lax.ppermute(array, 'fsdp', pairs)  30.9 us
    pallas_call x3, Pallas kernels, products(): pl.pallas_call(body, grid_spec=pltpu.PrefetchScalarGridSpec(num_scalar_pr...  24.2 us
    ppermute x14, starting transfers between devices, along_y(): return lax.ppermute(array, 'fsdp', pairs)  18.4 us
    pallas_call x1, Pallas kernels, all_products(): pl.pallas_call(body, grid_spec=pltpu.PrefetchScalarGridSpec(num_scalar_pr...  17.7 us
    reduce_scatter x3, waiting for transfers between devices, over_x(): lax.psum_scatter(array, 'fsdp', scatter_dimension=0, axis_index_groups=X_...  11.4 us
    pallas_call x1, Pallas kernels, crossing_products(): pl.pallas_call(body, grid_spec=pltpu.PrefetchScalarGridSpec(num_scalar_pr...  9.3 us
  transfers between devices with their start and end apart: 23, of which 14 were waited for; matrix products, arithmetic and copies ran while one was open for 1% of the time, Pallas kernels for 35%

profile of v7, /device:TPU:0, one launch (start us, length us, event | category | flops | bytes accessed | tf_op | source)
XLA Modules:
  0.0 237.4 jit_solution(8283114293105007463)
XLA Ops:
  10.0 2.5 %convert_divide_fusion = f32[256,1024]{1,0:T(8,128)} fusion(f32[256,1024]{1,0:T(8,128)} %refs_0_.1, bf16[1,256,1024]{2,1,0:T(8,128)(2,1)} %param.8, f32[]{:T(128)S(6)} %convert_element_type.17), kind=kLoop, calls=%fused_computation.4 | loop fusion | flops 1835008 | bytes 2621444 | tf_op jit(solution)/shard_map/div | solution.py:236
  13.2 17.7 %shard_map.85 = (f32[4,8,384,256]{3,2,1,0:T(8,128)}, bf16[1024,1024]{1,0:T(8,128)(2,1)S(1)}) custom-call(s32[8]{0:T(128)} %fusion.3.table, bf16[1024,8192]{1,0:T(8,128)(2,1)} %x.9, bf16[1024,1024]{1,0:T(8,128)(2,1)} %k.1), custom_call_target="tpu_custom_call" | custom-call | flops 20000000000 | bytes 1000 | tf_op jit(solution)/shard_map/pallas_call | solution.py:35
  30.9 4.9 %shard_map.86 = (f32[2,4,160,256]{3,2,1,0:T(8,128)}, f32[2,4,160,256]{3,2,1,0:T(8,128)}) custom-call(s32[8]{0:T(128)} %fusion.3.table, bf16[1024,8192]{1,0:T(8,128)(2,1)} %x.9, bf16[1024,1024]{1,0:T(8,128)(2,1)S(1)} %get-tuple-element.31.k, f32[4,8,384,256]{3,2,1,0:T(8,128)} %get-tuple-element.32.refs_0_), custom_call_target="tpu_custom_call" | custom-call | flops 20000000000 | bytes 1000 | tf_op jit(solution)/shard_map/pallas_call | solution.py:129
  35.8 3.1 %collective-permute-start.1 = (f32[2,4,160,256]{3,2,1,0:T(8,128)}, f32[2,4,160,256]{3,2,1,0:T(8,128)}, u32[]{:S(2)}, u32[]{:S(2)}) collective-permute-start(f32[2,4,160,256]{3,2,1,0:T(8,128)} %get-tuple-element.37), channel_id=1, source_target_pairs={{0,12},{1,13},{2,14},{3,15},{4,0},{5,1},{6,2},{7,3},{8,4},{9,5},{1... | collective-permute-start | bytes 3932168 | tf_op jit(solution)/shard_map/ppermute | solution.py:167
  39.0 9.3 %shard_map.87 = (f32[4,4,160,256]{3,2,1,0:T(8,128)}, f32[2,4,160,256]{3,2,1,0:T(8,128)}, f32[2,4,160,256]{3,2,1,0:T(8,128)}) custom-call(s32[8]{0:T(128)} %fusion.3.table, bf16[1024,8192]{1,0:T(8,128)(2,1)} %x.9, bf16[1024,1024]{1,0:T(8,128)(2,1)S(1)} %get-tuple-element.31.k, f32[2,4,160,256]{3,2,1,0:T(8,128)} %get-tuple-element.33.refs_0_), custom_call_target="tpu_custom_call" | custom-call | flops 20000000000 | bytes 1000 | tf_op jit(solution)/shard_map/pallas_call | solution.py:79
  50.2 8.7 %shard_map.88 = (f32[2,4,160,256]{3,2,1,0:T(8,128)}, f32[2,4,160,256]{3,2,1,0:T(8,128)}, f32[2,4,160,256]{3,2,1,0:T(8,128)}, f32[2,4,160,256]{3,2,1,0:T(8,128)}) custom-call(s32[8]{0:T(128)} %fusion.3.table, bf16[1024,8192]{1,0:T(8,128)(2,1)} %x.9, bf16[1024,1024]{1,0:T(8,128)(2,1)S(1)} %get-tuple-element.31.k, f32[4,4,160,256]{3,2,1,0:T(8,128)} %get-tuple-element.34.refs_0_), custom_call_target="tpu_custom_call" | custom-call | flops 20000000000 | bytes 1000 | tf_op jit(solution)/shard_map/pallas_call | solution.py:129
  59.6 2.5 %collective-permute-start.3 = (f32[2,4,160,256]{3,2,1,0:T(8,128)}, f32[2,4,160,256]{3,2,1,0:T(8,128)}, u32[]{:S(2)}, u32[]{:S(2)}) collective-permute-start(f32[2,4,160,256]{3,2,1,0:T(8,128)} %get-tuple-element.45), channel_id=1, source_target_pairs={{0,12},{1,13},{2,14},{3,15},{4,0},{5,1},{6,2},{7,3},{8,4},{9,5},{1... | collective-permute-start | bytes 3932168 | tf_op jit(solution)/shard_map/ppermute | solution.py:167
  62.1 10.7 %shard_map.89 = (f32[2,4,160,256]{3,2,1,0:T(8,128)}, f32[2,4,160,256]{3,2,1,0:T(8,128)}, f32[4,4,320,256]{3,2,1,0:T(8,128)}) custom-call(s32[8]{0:T(128)} %fusion.3.table, bf16[1024,8192]{1,0:T(8,128)(2,1)} %x.9, bf16[1024,1024]{1,0:T(8,128)(2,1)S(1)} %get-tuple-element.31.k, f32[2,4,160,256]{3,2,1,0:T(8,128)} %get-tuple-element.35.refs_0_), custom_call_target="tpu_custom_call" | custom-call | flops 20000000000 | bytes 1000 | tf_op jit(solution)/shard_map/pallas_call | solution.py:129
  72.7 4.2 %shard_map.90 = (f32[2,4,160,256]{3,2,1,0:T(8,128)}, f32[2,4,160,256]{3,2,1,0:T(8,128)}) custom-call(f32[2,4,160,256]{3,2,1,0:T(8,128)} %get-tuple-element.35.refs_0_, f32[2,4,160,256]{3,2,1,0:T(8,128)} %get-tuple-element.36.refs_1_, f32[2,4,160,256]{3,2,1,0:T(8,128)} %collective-permute-done.refs_2_, f32[2,4,160,256]{3,2,1,0:T(8,128)} %collective-permute-done.1.refs_3_, ...), custom_call_target="tpu_custom_call" | custom-call | flops 4000000000 | bytes 1000 | tf_op jit(solution)/shard_map/pallas_call | solution.py:153
  79.0 3.4 %shard_map.91 = (f32[256,1024]{1,0:T(8,128)}, f32[256,1024]{1,0:T(8,128)}) custom-call(f32[256,1024]{1,0:T(8,128)} %refs_0_.1, f32[256,1024]{1,0:T(8,128)} %refs_1_.1, f32[256,1024]{1,0:T(8,128)} %all-reduce.2.cloned.1.call-done.refs_2_, f32[2,4,160,256]{3,2,1,0:T(8,128)} %get-tuple-element.39.refs_3_), custom_call_target="tpu_custom_call" | custom-call | flops 4000000000 | bytes 1000 | tf_op jit(solution)/shard_map/pallas_call | solution.py:153
  82.4 31.6 %collective-permute-done.6.refs_1_.refs_3_.refs_5_.refs_7_ = f32[4,4,160,256]{3,2,1,0:T(8,128)} collective-permute-done((f32[4,4,160,256]{3,2,1,0:T(8,128)}, f32[4,4,160,256]{3,2,1,0:T(8,128)}, u32[]{:S(2)}, u32[]{:S(2)}) %collective-permute-start.6) | collective-permute-done | bytes 2621472 | tf_op jit(solution)/shard_map/ppermute | solution.py:171
  114.0 4.2 %shard_map.92 = (f32[2,4,160,256]{3,2,1,0:T(8,128)}, f32[2,4,160,256]{3,2,1,0:T(8,128)}) custom-call(f32[4,4,320,256]{3,2,1,0:T(8,128)} %get-tuple-element.38.refs_4_.refs_0_.refs_2_.refs_6_.refs_3_, f32[4,4,160,256]{3,2,1,0:T(8,128)} %collective-permute-done.6.refs_1_.refs_3_.refs_5_.refs_7_, ...), custom_call_target="tpu_custom_call" | custom-call | flops 4000000000 | bytes 1000 | tf_op jit(solution)/shard_map/pallas_call | solution.py:153
  118.2 5.2 %collective-permute-done.5.refs_5_ = f32[2,4,160,256]{3,2,1,0:T(8,128)S(1)} collective-permute-done((f32[2,4,160,256]{3,2,1,0:T(8,128)}, f32[2,4,160,256]{3,2,1,0:T(8,128)S(1)}, u32[]{:S(2)}, u32[]{:S(2)}) %collective-permute-start.5) | collective-permute-done | bytes 1310752 | tf_op jit(solution)/shard_map/ppermute | solution.py:167
  123.5 3.4 %collective-permute-done.4.refs_4_ = f32[2,4,160,256]{3,2,1,0:T(8,128)} collective-permute-done((f32[2,4,160,256]{3,2,1,0:T(8,128)}, f32[2,4,160,256]{3,2,1,0:T(8,128)}, u32[]{:S(2)}, u32[]{:S(2)}) %collective-permute-start.4) | collective-permute-done | bytes 1310752 | tf_op jit(solution)/shard_map/ppermute | solution.py:167
  126.9 5.3 %shard_map.93.refs_4_ = f32[4,640,256]{2,1,0:T(8,128)} custom-call(f32[2,4,160,256]{3,2,1,0:T(8,128)} %get-tuple-element.42.refs_0_, f32[2,4,160,256]{3,2,1,0:T(8,128)} %get-tuple-element.43.refs_1_, f32[2,4,160,256]{3,2,1,0:T(8,128)} %copy-done.5, f32[2,4,160,256]{3,2,1,0:T(8,128)} %collective-permute-done.3.refs_3_, ...), custom_call_target="tpu_custom_call" | custom-call | flops 4000000000 | bytes 1000 | tf_op jit(solution)/shard_map/pallas_call | solution.py:153
  132.3 2.2 collective-permute-start.9
  136.6 11.4 %reduce-scatter.4.cloned.1.call-done = f32[1,8,384,256]{3,2,1,0:T(8,128)} async-done(((f32[4,8,384,256]{3,2,1,0:T(8,128)}), f32[1,8,384,256]{3,2,1,0:T(8,128)}) %reduce-scatter.4.cloned.1.call-update) | async-done | bytes 3145744 | tf_op jit(solution)/shard_map/reduce_scatter | solution.py:175
  148.0 2.6 %shard_map.94 = (f32[2,2,192,256]{3,2,1,0:T(8,128)}, f32[2,2,192,256]{3,2,1,0:T(8,128)}) custom-call(f32[2,4,384,256]{3,2,1,0:T(8,128)} %bitcast.8, f32[2,4,384,256]{3,2,1,0:T(8,128)} %bitcast.9, f32[2,4,384,256]{3,2,1,0:T(8,128)} %bitcast.10, f32[2,4,384,256]{3,2,1,0:T(8,128)} %bitcast.11, f32[4,640,256]{2,1,0:T(8,128)} %shard_map.93.refs_4_), custom_call_target="tpu_custom_call" | custom-call | flops 4000000000 | bytes 1000 | tf_op jit(solution)/shard_map/pallas_call | solution.py:153
  150.5 2.8 %collective-permute-start.7 = (f32[2,2,192,256]{3,2,1,0:T(8,128)}, f32[2,2,192,256]{3,2,1,0:T(8,128)S(1)}, u32[]{:S(2)}, u32[]{:S(2)}) collective-permute-start(f32[2,2,192,256]{3,2,1,0:T(8,128)} %get-tuple-element.48), channel_id=1, source_target_pairs={{0,12},{1,13},{2,14},{3,15},{4,0},{5,1},{6,2},{7,3},{8,4},{9,5},{1... | collective-permute-start | bytes 2359304 | tf_op jit(solution)/shard_map/ppermute | solution.py:167
  153.3 11.2 %collective-permute-done.9.refs_1_.refs_4_ = f32[2,4,160,256]{3,2,1,0:T(8,128)} collective-permute-done((f32[2,4,160,256]{3,2,1,0:T(8,128)}, f32[2,4,160,256]{3,2,1,0:T(8,128)}, u32[]{:S(2)}, u32[]{:S(2)}) %collective-permute-start.9) | collective-permute-done | bytes 1310752 | tf_op jit(solution)/shard_map/ppermute | solution.py:171
  169.3 3.3 %shard_map.95 = (f32[4,160,256]{2,1,0:T(8,128)}, f32[4,160,256]{2,1,0:T(8,128)}) custom-call(f32[4,4,320,256]{3,2,1,0:T(8,128)} %get-tuple-element.38.refs_4_.refs_0_.refs_2_.refs_6_.refs_3_, f32[2,4,160,256]{3,2,1,0:T(8,128)} %collective-permute-done.9.refs_1_.refs_4_, f32[2,4,160,256]{3,2,1,0:T(8,128)} %copy-done.1, ...), custom_call_target="tpu_custom_call" | custom-call | flops 4000000000 | bytes 1000 | tf_op jit(solution)/shard_map/pallas_call | solution.py:153
  174.7 8.5 %collective-permute-done.7.refs_3_.refs_1_ = f32[2,2,192,256]{3,2,1,0:T(8,128)S(1)} collective-permute-done((f32[2,2,192,256]{3,2,1,0:T(8,128)}, f32[2,2,192,256]{3,2,1,0:T(8,128)S(1)}, u32[]{:S(2)}, u32[]{:S(2)}) %collective-permute-start.7) | collective-permute-done | bytes 786464 | tf_op jit(solution)/shard_map/ppermute | solution.py:167
  183.2 3.4 %collective-permute-done.8.refs_1_.refs_4_ = f32[2,2,192,256]{3,2,1,0:T(8,128)} collective-permute-done((f32[2,2,192,256]{3,2,1,0:T(8,128)}, f32[2,2,192,256]{3,2,1,0:T(8,128)}, u32[]{:S(2)}, u32[]{:S(2)}) %collective-permute-start.8) | collective-permute-done | bytes 786464 | tf_op jit(solution)/shard_map/ppermute | solution.py:167
  186.6 2.3 shard_map.96
  190.4 4.2 %collective-permute-done.16.refs_7_ = f32[4,160,256]{2,1,0:T(8,128)S(1)} collective-permute-done((f32[4,160,256]{2,1,0:T(8,128)}, f32[4,160,256]{2,1,0:T(8,128)S(1)}, u32[]{:S(2)}, u32[]{:S(2)}) %collective-permute-start.16) | collective-permute-done | bytes 655392 | tf_op jit(solution)/shard_map/ppermute | solution.py:167
  194.6 2.6 %collective-permute-done.15.refs_3_ = f32[4,160,256]{2,1,0:T(8,128)S(1)} collective-permute-done((f32[4,160,256]{2,1,0:T(8,128)}, f32[4,160,256]{2,1,0:T(8,128)S(1)}, u32[]{:S(2)}, u32[]{:S(2)}) %collective-permute-start.15) | collective-permute-done | bytes 655392 | tf_op jit(solution)/shard_map/ppermute | solution.py:167
  198.0 3.8 %shard_map.97.refs_6_ = f32[4,320,256]{2,1,0:T(8,128)} custom-call(f32[4,4,320,256]{3,2,1,0:T(8,128)} %get-tuple-element.38.refs_4_.refs_0_.refs_2_.refs_6_.refs_3_, f32[2,4,160,256]{3,2,1,0:T(8,128)} %collective-permute-done.14.refs_1_.refs_5_, f32[2,4,160,256]{3,2,1,0:T(8,128)} %copy-done, f32[4,160,256]{2,1,0:T(8,128)} %copy-done.3, ...), custom_call_target="tpu_custom_call" | custom-call | flops 4000000000 | bytes 1000 | tf_op jit(solution)/shard_map/pallas_call | solution.py:153
  202.9 3.1 %collective-permute-start.13 = (f32[2,192,256]{2,1,0:T(8,128)S(1)}, f32[2,192,256]{2,1,0:T(8,128)S(1)}, u32[]{:S(2)}, u32[]{:S(2)}) collective-permute-start(f32[2,192,256]{2,1,0:T(8,128)S(1)} %copy-done.8), channel_id=1, source_target_pairs={{0,12},{1,13},{2,14},{3,15},{4,0},{5,1},{6,2},{7,3},{8,4},{9,5},{1... | collective-permute-start | bytes 1179656 | tf_op jit(solution)/shard_map/ppermute | solution.py:167
  207.4 6.7 %collective-permute-done.17.refs_7_.refs_3_ = f32[320,256]{1,0:T(8,128)S(1)} collective-permute-done((f32[320,256]{1,0:T(8,128)S(1)}, f32[320,256]{1,0:T(8,128)S(1)}, u32[]{:S(2)}, u32[]{:S(2)}) %collective-permute-start.17) | collective-permute-done | bytes 327712 | tf_op jit(solution)/shard_map/ppermute | solution.py:171
  215.8 2.6 %shard_map.98 = (f32[384,256]{1,0:T(8,128)}, f32[384,256]{1,0:T(8,128)}) custom-call(f32[2,4,384,256]{3,2,1,0:T(8,128)} %bitcast.14, f32[2,2,192,256]{3,2,1,0:T(8,128)} %copy-done.7, f32[2,192,256]{2,1,0:T(8,128)} %copy-done.9, f32[2,4,384,256]{3,2,1,0:T(8,128)} %bitcast.15, f32[2,2,192,256]{3,2,1,0:T(8,128)} %collective-permute-done.8.refs_1_.refs_4_, ...), custom_call_target="tpu_custom_call" | custom-call | flops 4000000000 | bytes 1000 | tf_op jit(solution)/shard_map/pallas_call | solution.py:153
  218.7 7.6 %collective-permute-done.18.refs_1_ = f32[384,256]{1,0:T(8,128)S(1)} collective-permute-done((f32[384,256]{1,0:T(8,128)}, f32[384,256]{1,0:T(8,128)S(1)}, u32[]{:S(2)}, u32[]{:S(2)}) %collective-permute-start.18) | collective-permute-done | bytes 393248 | tf_op jit(solution)/shard_map/ppermute | solution.py:171
  227.1 2.7 %shard_map.99 = f32[1,256,1024]{2,1,0:T(8,128)} custom-call(f32[384,256]{1,0:T(8,128)} %get-tuple-element.57.refs_0_, f32[384,256]{1,0:T(8,128)} %copy-done.11, f32[640,256]{1,0:T(8,128)} %bitcast.16, f32[320,256]{1,0:T(8,128)} %copy-done.12, f32[320,256]{1,0:T(8,128)} %bitcast.17), custom_call_target="tpu_custom_call" | custom-call | flops 4000000000 | bytes 1000 | tf_op jit(solution)/shard_map/pallas_call | solution.py:153
  (63 shorter events, 23.4 us)
Async XLA Ops:
  8.0 71.0 %all-reduce.2.cloned.1.call-start = ((), (), s32[]{:S(2)}) async-start(), calls=%async_computation.3 | async-start | bytes 2097152 | tf_op jit(solution)/shard_map/psum | solution.py:236
  12.6 135.4 %reduce-scatter.4.cloned.1.call-start = ((), (), s32[]{:S(2)}) async-start(), calls=%async_computation.4 | async-start | bytes 15728640 | tf_op jit(solution)/shard_map/reduce_scatter | solution.py:175
  30.9 175.1 %reduce-scatter.6.cloned.1.call-start = ((), (), s32[]{:S(2)}) async-start(), calls=%async_computation.5 | async-start | bytes 3276800 | tf_op jit(solution)/shard_map/reduce_scatter | solution.py:175
  35.8 36.9 %collective-permute-start.1 = (f32[2,4,160,256]{3,2,1,0:T(8,128)}, f32[2,4,160,256]{3,2,1,0:T(8,128)}, u32[]{:S(2)}, u32[]{:S(2)}) collective-permute-start(f32[2,4,160,256]{3,2,1,0:T(8,128)} %get-tuple-element.37), channel_id=1, source_target_pairs={{0,12},{1,13},{2,14},{3,15},{4,0},{5,1},{6,2},{7,3},{8,4},{9,5},{1... | collective-permute-start | bytes 3932168 | tf_op jit(solution)/shard_map/ppermute | solution.py:167
  39.0 33.8 %collective-permute-start = (f32[2,4,160,256]{3,2,1,0:T(8,128)}, f32[2,4,160,256]{3,2,1,0:T(8,128)}, u32[]{:S(2)}, u32[]{:S(2)}) collective-permute-start(f32[2,4,160,256]{3,2,1,0:T(8,128)} %get-tuple-element.33.refs_0_), channel_id=1, source_target_pairs={{0,4},{1,5},{2,6},{3,7},{4,8},{5,9},{6,10},{7,11},{8,12},{9,13},{1... | collective-permute-start | bytes 3932168 | tf_op jit(solution)/shard_map/ppermute | solution.py:167
  48.3 65.7 %collective-permute-start.6 = (f32[4,4,160,256]{3,2,1,0:T(8,128)}, f32[4,4,160,256]{3,2,1,0:T(8,128)}, u32[]{:S(2)}, u32[]{:S(2)}) collective-permute-start(f32[4,4,160,256]{3,2,1,0:T(8,128)} %get-tuple-element.34.refs_0_), channel_id=1, source_target_pairs={{0,16},{1,17},{2,18},{3,19},{4,20},{5,21},{6,22},{7,23},{8,24},{9,... | collective-permute-start | bytes 7864328 | tf_op jit(solution)/shard_map/ppermute | solution.py:171
  58.8 59.4 %collective-permute-start.2 = (f32[2,4,160,256]{3,2,1,0:T(8,128)}, f32[2,4,160,256]{3,2,1,0:T(8,128)S(1)}, u32[]{:S(2)}, u32[]{:S(2)}) collective-permute-start(f32[2,4,160,256]{3,2,1,0:T(8,128)} %get-tuple-element.44), channel_id=1, source_target_pairs={{0,4},{1,5},{2,6},{3,7},{4,8},{5,9},{6,10},{7,11},{8,12},{9,13},{1... | collective-permute-start | bytes 3932168 | tf_op jit(solution)/shard_map/ppermute | solution.py:167
  59.6 58.6 %collective-permute-start.3 = (f32[2,4,160,256]{3,2,1,0:T(8,128)}, f32[2,4,160,256]{3,2,1,0:T(8,128)}, u32[]{:S(2)}, u32[]{:S(2)}) collective-permute-start(f32[2,4,160,256]{3,2,1,0:T(8,128)} %get-tuple-element.45), channel_id=1, source_target_pairs={{0,12},{1,13},{2,14},{3,15},{4,0},{5,1},{6,2},{7,3},{8,4},{9,5},{1... | collective-permute-start | bytes 3932168 | tf_op jit(solution)/shard_map/ppermute | solution.py:167
  76.9 46.6 %collective-permute-start.5 = (f32[2,4,160,256]{3,2,1,0:T(8,128)}, f32[2,4,160,256]{3,2,1,0:T(8,128)S(1)}, u32[]{:S(2)}, u32[]{:S(2)}) collective-permute-start(f32[2,4,160,256]{3,2,1,0:T(8,128)} %get-tuple-element.46), channel_id=1, source_target_pairs={{0,12},{1,13},{2,14},{3,15},{4,0},{5,1},{6,2},{7,3},{8,4},{9,5},{1... | collective-permute-start | bytes 3932168 | tf_op jit(solution)/shard_map/ppermute | solution.py:167
  79.0 47.9 %collective-permute-start.4 = (f32[2,4,160,256]{3,2,1,0:T(8,128)}, f32[2,4,160,256]{3,2,1,0:T(8,128)}, u32[]{:S(2)}, u32[]{:S(2)}) collective-permute-start(f32[2,4,160,256]{3,2,1,0:T(8,128)} %get-tuple-element.39.refs_3_), channel_id=1, source_target_pairs={{0,4},{1,5},{2,6},{3,7},{4,8},{5,9},{6,10},{7,11},{8,12},{9,13},{1... | collective-permute-start | bytes 3932168 | tf_op jit(solution)/shard_map/ppermute | solution.py:167
  118.2 8.7 %copy-start.5 = (f32[2,4,160,256]{3,2,1,0:T(8,128)}, f32[2,4,160,256]{3,2,1,0:T(8,128)S(1)}, u32[]{:S(2)}) copy-start(f32[2,4,160,256]{3,2,1,0:T(8,128)S(1)} %collective-permute-done.2.refs_2_) | copy-start | bytes 3932164
  123.5 3.4 %copy-start.6 = (f32[2,4,160,256]{3,2,1,0:T(8,128)}, f32[2,4,160,256]{3,2,1,0:T(8,128)S(1)}, u32[]{:S(2)}) copy-start(f32[2,4,160,256]{3,2,1,0:T(8,128)S(1)} %collective-permute-done.5.refs_5_) | copy-start | bytes 3932164
  132.2 94.2 %reduce-scatter.8.cloned.1.call-start = ((), (), s32[]{:S(2)}) async-start(), calls=%async_computation.6 | async-start | bytes 1638400 | tf_op jit(solution)/shard_map/reduce_scatter | solution.py:175
  132.3 32.3 %collective-permute-start.9 = (f32[2,4,160,256]{3,2,1,0:T(8,128)}, f32[2,4,160,256]{3,2,1,0:T(8,128)}, u32[]{:S(2)}, u32[]{:S(2)}) collective-permute-start(f32[2,4,160,256]{3,2,1,0:T(8,128)} %get-tuple-element.50), channel_id=1, source_target_pairs={{0,16},{1,17},{2,18},{3,19},{4,20},{5,21},{6,22},{7,23},{8,24},{9,... | collective-permute-start | bytes 3932168 | tf_op jit(solution)/shard_map/ppermute | solution.py:171
  134.4 31.9 %collective-permute-start.11 = (f32[2,4,160,256]{3,2,1,0:T(8,128)}, f32[2,4,160,256]{3,2,1,0:T(8,128)S(1)}, u32[]{:S(2)}, u32[]{:S(2)}) collective-permute-start(f32[2,4,160,256]{3,2,1,0:T(8,128)} %get-tuple-element.51), channel_id=1, source_target_pairs={{0,12},{1,13},{2,14},{3,15},{4,0},{5,1},{6,2},{7,3},{8,4},{9,5},{1... | collective-permute-start | bytes 3932168 | tf_op jit(solution)/shard_map/ppermute | solution.py:167
  135.7 32.5 %collective-permute-start.10 = (f32[2,4,160,256]{3,2,1,0:T(8,128)}, f32[2,4,160,256]{3,2,1,0:T(8,128)S(1)}, u32[]{:S(2)}, u32[]{:S(2)}) collective-permute-start(f32[2,4,160,256]{3,2,1,0:T(8,128)} %get-tuple-element.47.refs_6_), channel_id=1, source_target_pairs={{0,4},{1,5},{2,6},{3,7},{4,8},{5,9},{6,10},{7,11},{8,12},{9,13},{1... | collective-permute-start | bytes 3932168 | tf_op jit(solution)/shard_map/ppermute | solution.py:167
  136.4 53.9 %collective-permute-start.14 = (f32[2,4,160,256]{3,2,1,0:T(8,128)}, f32[2,4,160,256]{3,2,1,0:T(8,128)}, u32[]{:S(2)}, u32[]{:S(2)}) collective-permute-start(f32[2,4,160,256]{3,2,1,0:T(8,128)} %get-tuple-element.55), channel_id=1, source_target_pairs={{0,16},{1,17},{2,18},{3,19},{4,20},{5,21},{6,22},{7,23},{8,24},{9,... | collective-permute-start | bytes 3932168 | tf_op jit(solution)/shard_map/ppermute | solution.py:171
  150.5 32.7 %collective-permute-start.7 = (f32[2,2,192,256]{3,2,1,0:T(8,128)}, f32[2,2,192,256]{3,2,1,0:T(8,128)S(1)}, u32[]{:S(2)}, u32[]{:S(2)}) collective-permute-start(f32[2,2,192,256]{3,2,1,0:T(8,128)} %get-tuple-element.48), channel_id=1, source_target_pairs={{0,12},{1,13},{2,14},{3,15},{4,0},{5,1},{6,2},{7,3},{8,4},{9,5},{1... | collective-permute-start | bytes 2359304 | tf_op jit(solution)/shard_map/ppermute | solution.py:167
  164.5 22.0 %collective-permute-start.8 = (f32[2,2,192,256]{3,2,1,0:T(8,128)}, f32[2,2,192,256]{3,2,1,0:T(8,128)}, u32[]{:S(2)}, u32[]{:S(2)}) collective-permute-start(f32[2,2,192,256]{3,2,1,0:T(8,128)} %get-tuple-element.49.refs_6_), channel_id=1, source_target_pairs={{0,4},{1,5},{2,6},{3,7},{4,8},{5,9},{6,10},{7,11},{8,12},{9,13},{1... | collective-permute-start | bytes 2359304 | tf_op jit(solution)/shard_map/ppermute | solution.py:167
  166.3 1.9 copy-start
  168.2 1.1 copy-start.1
  172.6 21.9 %collective-permute-start.16 = (f32[4,160,256]{2,1,0:T(8,128)}, f32[4,160,256]{2,1,0:T(8,128)S(1)}, u32[]{:S(2)}, u32[]{:S(2)}) collective-permute-start(f32[4,160,256]{2,1,0:T(8,128)} %get-tuple-element.56), channel_id=1, source_target_pairs={{0,12},{1,13},{2,14},{3,15},{4,0},{5,1},{6,2},{7,3},{8,4},{9,5},{1... | collective-permute-start | bytes 1966088 | tf_op jit(solution)/shard_map/ppermute | solution.py:167
  174.4 22.8 %collective-permute-start.15 = (f32[4,160,256]{2,1,0:T(8,128)}, f32[4,160,256]{2,1,0:T(8,128)S(1)}, u32[]{:S(2)}, u32[]{:S(2)}) collective-permute-start(f32[4,160,256]{2,1,0:T(8,128)} %get-tuple-element.52.refs_4_), channel_id=1, source_target_pairs={{0,4},{1,5},{2,6},{3,7},{4,8},{5,9},{6,10},{7,11},{8,12},{9,13},{1... | collective-permute-start | bytes 1966088 | tf_op jit(solution)/shard_map/ppermute | solution.py:167
  183.2 3.4 %copy-start.7 = (f32[2,2,192,256]{3,2,1,0:T(8,128)}, f32[2,2,192,256]{3,2,1,0:T(8,128)S(1)}, u32[]{:S(2)}) copy-start(f32[2,2,192,256]{3,2,1,0:T(8,128)S(1)} %collective-permute-done.7.refs_3_.refs_1_) | copy-start | bytes 2359300
  194.6 2.6 %copy-start.2 = (f32[4,160,256]{2,1,0:T(8,128)}, f32[4,160,256]{2,1,0:T(8,128)S(1)}, u32[]{:S(2)}) copy-start(f32[4,160,256]{2,1,0:T(8,128)S(1)} %collective-permute-done.16.refs_7_) | copy-start | bytes 1966084
  201.7 1.0 copy-start.4
  201.7 1.1 copy-start.8
  202.7 11.4 %collective-permute-start.12 = (f32[2,192,256]{2,1,0:T(8,128)S(1)}, f32[2,192,256]{2,1,0:T(8,128)S(1)}, u32[]{:S(2)}, u32[]{:S(2)}) collective-permute-start(f32[2,192,256]{2,1,0:T(8,128)S(1)} %copy-done.4), channel_id=1, source_target_pairs={{0,4},{1,5},{2,6},{3,7},{4,8},{5,9},{6,10},{7,11},{8,12},{9,13},{1... | collective-permute-start | bytes 1179656 | tf_op jit(solution)/shard_map/ppermute | solution.py:167
  202.9 11.3 %collective-permute-start.13 = (f32[2,192,256]{2,1,0:T(8,128)S(1)}, f32[2,192,256]{2,1,0:T(8,128)S(1)}, u32[]{:S(2)}, u32[]{:S(2)}) collective-permute-start(f32[2,192,256]{2,1,0:T(8,128)S(1)} %copy-done.8), channel_id=1, source_target_pairs={{0,12},{1,13},{2,14},{3,15},{4,0},{5,1},{6,2},{7,3},{8,4},{9,5},{1... | collective-permute-start | bytes 1179656 | tf_op jit(solution)/shard_map/ppermute | solution.py:167
  207.0 7.2 %collective-permute-start.17 = (f32[320,256]{1,0:T(8,128)S(1)}, f32[320,256]{1,0:T(8,128)S(1)}, u32[]{:S(2)}, u32[]{:S(2)}) collective-permute-start(f32[320,256]{1,0:T(8,128)S(1)} %slice_bitcast_fusion), channel_id=1, source_target_pairs={{0,16},{1,17},{2,18},{3,19},{4,20},{5,21},{6,22},{7,23},{8,24},{9,... | collective-permute-start | bytes 983048 | tf_op jit(solution)/shard_map/ppermute | solution.py:171
  214.1 0.9 copy-start.10
  218.4 8.0 %collective-permute-start.18 = (f32[384,256]{1,0:T(8,128)}, f32[384,256]{1,0:T(8,128)S(1)}, u32[]{:S(2)}, u32[]{:S(2)}) collective-permute-start(f32[384,256]{1,0:T(8,128)} %get-tuple-element.58), channel_id=1, source_target_pairs={{0,16},{1,17},{2,18},{3,19},{4,20},{5,21},{6,22},{7,23},{8,24},{9,... | collective-permute-start | bytes 1179656 | tf_op jit(solution)/shard_map/ppermute | solution.py:171
  (4 other events, 3.1 us)
Sparse Core Ops, SparseCore 0:
  12.7 51.5 all-reduce.1
Sparse Core Ops, SparseCore 1:
  30.9 117.0 reduce-scatter.3
  150.4 33.5 reduce-scatter.5
  201.8 24.0 reduce-scatter.7

commit v8 on v7

--- a/solution.py
+++ b/solution.py
@@ -14,7 +14,7 @@
 C = 320
 X_RINGS = [[16 * z + 4 * y + x for x in range(4)] for z in range(2) for y in range(4)]
 LONG = pl.CostEstimate(flops=2 * 10**10, bytes_accessed=1000, transcendentals=0)
-SHORT = pl.CostEstimate(flops=4 * 10**9, bytes_accessed=1000, transcendentals=0)
+SHORT = pl.CostEstimate(flops=6 * 10**9, bytes_accessed=1000, transcendentals=0)
 MIB = 1024 * 1024
 
 

time: 238 us -> 239 us (level)
    unnamed x26 -> x28, local copies, waits for them, and re-layouts: 5.44 us -> 5.55 us
where the time goes in v8:
time: 239 us; the launch traced here: 238 us
  waiting for transfers between devices  101 us (42%)
  Pallas kernels  85.7 us (36%)
  starting transfers between devices  24.8 us (10%)
  between operations  16.4 us (7%)
  local copies, waits for them, and re-layouts  6.55 us (3%)
  other arithmetic  4.36 us (2%)
    ppermute x5, waiting for transfers between devices, along_z(): return lax.ppermute(array, 'fsdp', [(f, (f + 16) % 32) for f in range(32)])  58.6 us
    pallas_call x10, Pallas kernels, combine(): pl.pallas_call(kernel, grid=(1,), in_specs=[pl.BlockSpec(block, lambda i,...  34.5 us
    ppermute x14, waiting for transfers between devices, along_y(): return lax.ppermute(array, 'fsdp', pairs)  31.3 us
    pallas_call x3, Pallas kernels, products(): pl.pallas_call(body, grid_spec=pltpu.PrefetchScalarGridSpec(num_scalar_pr...  24.2 us
    ppermute x14, starting transfers between devices, along_y(): return lax.ppermute(array, 'fsdp', pairs)  18.4 us
    pallas_call x1, Pallas kernels, all_products(): pl.pallas_call(body, grid_spec=pltpu.PrefetchScalarGridSpec(num_scalar_pr...  17.7 us
    reduce_scatter x3, waiting for transfers between devices, over_x(): lax.psum_scatter(array, 'fsdp', scatter_dimension=0, axis_index_groups=X_...  10.5 us
    pallas_call x1, Pallas kernels, crossing_products(): pl.pallas_call(body, grid_spec=pltpu.PrefetchScalarGridSpec(num_scalar_pr...  9.32 us
  transfers between devices with their start and end apart: 23, of which 14 were waited for; matrix products, arithmetic and copies ran while one was open for 1% of the time, Pallas kernels for 35%

profile of v8, /device:TPU:0, one launch (start us, length us, event | category | flops | bytes accessed | tf_op | source)
XLA Modules:
  0.0 238.3 jit_solution(3335354498202768155)
XLA Ops:
  10.0 2.5 %convert_divide_fusion = f32[256,1024]{1,0:T(8,128)} fusion(f32[256,1024]{1,0:T(8,128)} %refs_0_.1, bf16[1,256,1024]{2,1,0:T(8,128)(2,1)} %param.8, f32[]{:T(128)S(6)} %convert_element_type.17), kind=kLoop, calls=%fused_computation.4 | loop fusion | flops 1835008 | bytes 2621444 | tf_op jit(solution)/shard_map/div | solution.py:236
  13.2 17.7 %shard_map.85 = (f32[4,8,384,256]{3,2,1,0:T(8,128)}, bf16[1024,1024]{1,0:T(8,128)(2,1)S(1)}) custom-call(s32[8]{0:T(128)} %fusion.3.table, bf16[1024,8192]{1,0:T(8,128)(2,1)} %x.9, bf16[1024,1024]{1,0:T(8,128)(2,1)} %k.1), custom_call_target="tpu_custom_call" | custom-call | flops 20000000000 | bytes 1000 | tf_op jit(solution)/shard_map/pallas_call | solution.py:35
  30.9 4.9 %shard_map.86 = (f32[2,4,160,256]{3,2,1,0:T(8,128)}, f32[2,4,160,256]{3,2,1,0:T(8,128)}) custom-call(s32[8]{0:T(128)} %fusion.3.table, bf16[1024,8192]{1,0:T(8,128)(2,1)} %x.9, bf16[1024,1024]{1,0:T(8,128)(2,1)S(1)} %get-tuple-element.31.k, f32[4,8,384,256]{3,2,1,0:T(8,128)} %get-tuple-element.32.refs_0_), custom_call_target="tpu_custom_call" | custom-call | flops 20000000000 | bytes 1000 | tf_op jit(solution)/shard_map/pallas_call | solution.py:129
  35.9 3.1 %collective-permute-start.1 = (f32[2,4,160,256]{3,2,1,0:T(8,128)}, f32[2,4,160,256]{3,2,1,0:T(8,128)}, u32[]{:S(2)}, u32[]{:S(2)}) collective-permute-start(f32[2,4,160,256]{3,2,1,0:T(8,128)} %get-tuple-element.37), channel_id=1, source_target_pairs={{0,12},{1,13},{2,14},{3,15},{4,0},{5,1},{6,2},{7,3},{8,4},{9,5},{1... | collective-permute-start | bytes 3932168 | tf_op jit(solution)/shard_map/ppermute | solution.py:167
  39.0 9.3 %shard_map.87 = (f32[4,4,160,256]{3,2,1,0:T(8,128)}, f32[2,4,160,256]{3,2,1,0:T(8,128)}, f32[2,4,160,256]{3,2,1,0:T(8,128)}) custom-call(s32[8]{0:T(128)} %fusion.3.table, bf16[1024,8192]{1,0:T(8,128)(2,1)} %x.9, bf16[1024,1024]{1,0:T(8,128)(2,1)S(1)} %get-tuple-element.31.k, f32[2,4,160,256]{3,2,1,0:T(8,128)} %get-tuple-element.33.refs_0_), custom_call_target="tpu_custom_call" | custom-call | flops 20000000000 | bytes 1000 | tf_op jit(solution)/shard_map/pallas_call | solution.py:79
  50.2 8.6 %shard_map.88 = (f32[2,4,160,256]{3,2,1,0:T(8,128)}, f32[2,4,160,256]{3,2,1,0:T(8,128)}, f32[2,4,160,256]{3,2,1,0:T(8,128)}, f32[2,4,160,256]{3,2,1,0:T(8,128)}) custom-call(s32[8]{0:T(128)} %fusion.3.table, bf16[1024,8192]{1,0:T(8,128)(2,1)} %x.9, bf16[1024,1024]{1,0:T(8,128)(2,1)S(1)} %get-tuple-element.31.k, f32[4,4,160,256]{3,2,1,0:T(8,128)} %get-tuple-element.34.refs_0_), custom_call_target="tpu_custom_call" | custom-call | flops 20000000000 | bytes 1000 | tf_op jit(solution)/shard_map/pallas_call | solution.py:129
  59.6 2.5 %collective-permute-start.3 = (f32[2,4,160,256]{3,2,1,0:T(8,128)}, f32[2,4,160,256]{3,2,1,0:T(8,128)}, u32[]{:S(2)}, u32[]{:S(2)}) collective-permute-start(f32[2,4,160,256]{3,2,1,0:T(8,128)} %get-tuple-element.45), channel_id=1, source_target_pairs={{0,12},{1,13},{2,14},{3,15},{4,0},{5,1},{6,2},{7,3},{8,4},{9,5},{1... | collective-permute-start | bytes 3932168 | tf_op jit(solution)/shard_map/ppermute | solution.py:167
  62.1 10.7 %shard_map.89 = (f32[2,4,160,256]{3,2,1,0:T(8,128)}, f32[2,4,160,256]{3,2,1,0:T(8,128)}, f32[4,4,320,256]{3,2,1,0:T(8,128)}) custom-call(s32[8]{0:T(128)} %fusion.3.table, bf16[1024,8192]{1,0:T(8,128)(2,1)} %x.9, bf16[1024,1024]{1,0:T(8,128)(2,1)S(1)} %get-tuple-element.31.k, f32[2,4,160,256]{3,2,1,0:T(8,128)} %get-tuple-element.35.refs_0_), custom_call_target="tpu_custom_call" | custom-call | flops 20000000000 | bytes 1000 | tf_op jit(solution)/shard_map/pallas_call | solution.py:129
  72.7 4.2 %shard_map.90 = (f32[2,4,160,256]{3,2,1,0:T(8,128)}, f32[2,4,160,256]{3,2,1,0:T(8,128)}) custom-call(f32[2,4,160,256]{3,2,1,0:T(8,128)} %get-tuple-element.35.refs_0_, f32[2,4,160,256]{3,2,1,0:T(8,128)} %get-tuple-element.36.refs_1_, f32[2,4,160,256]{3,2,1,0:T(8,128)} %collective-permute-done.refs_2_, f32[2,4,160,256]{3,2,1,0:T(8,128)} %collective-permute-done.1.refs_3_, ...), custom_call_target="tpu_custom_call" | custom-call | flops 6000000000 | bytes 1000 | tf_op jit(solution)/shard_map/pallas_call | solution.py:153
  79.0 3.4 %shard_map.91 = (f32[256,1024]{1,0:T(8,128)}, f32[256,1024]{1,0:T(8,128)}) custom-call(f32[256,1024]{1,0:T(8,128)} %refs_0_.1, f32[256,1024]{1,0:T(8,128)} %refs_1_.1, f32[256,1024]{1,0:T(8,128)} %all-reduce.2.cloned.1.call-done.refs_2_, f32[2,4,160,256]{3,2,1,0:T(8,128)} %get-tuple-element.39.refs_3_), custom_call_target="tpu_custom_call" | custom-call | flops 6000000000 | bytes 1000 | tf_op jit(solution)/shard_map/pallas_call | solution.py:153
  82.4 31.7 %collective-permute-done.6.refs_1_.refs_3_.refs_5_.refs_7_ = f32[4,4,160,256]{3,2,1,0:T(8,128)} collective-permute-done((f32[4,4,160,256]{3,2,1,0:T(8,128)}, f32[4,4,160,256]{3,2,1,0:T(8,128)}, u32[]{:S(2)}, u32[]{:S(2)}) %collective-permute-start.6) | collective-permute-done | bytes 2621472 | tf_op jit(solution)/shard_map/ppermute | solution.py:171
  114.0 4.2 %shard_map.92 = (f32[2,4,160,256]{3,2,1,0:T(8,128)}, f32[2,4,160,256]{3,2,1,0:T(8,128)}) custom-call(f32[4,4,320,256]{3,2,1,0:T(8,128)} %get-tuple-element.38.refs_4_.refs_0_.refs_2_.refs_6_.refs_3_, f32[4,4,160,256]{3,2,1,0:T(8,128)} %collective-permute-done.6.refs_1_.refs_3_.refs_5_.refs_7_, ...), custom_call_target="tpu_custom_call" | custom-call | flops 6000000000 | bytes 1000 | tf_op jit(solution)/shard_map/pallas_call | solution.py:153
  118.3 5.2 %collective-permute-done.5.refs_5_ = f32[2,4,160,256]{3,2,1,0:T(8,128)S(1)} collective-permute-done((f32[2,4,160,256]{3,2,1,0:T(8,128)}, f32[2,4,160,256]{3,2,1,0:T(8,128)S(1)}, u32[]{:S(2)}, u32[]{:S(2)}) %collective-permute-start.5) | collective-permute-done | bytes 1310752 | tf_op jit(solution)/shard_map/ppermute | solution.py:167
  123.5 3.4 %collective-permute-done.4.refs_4_ = f32[2,4,160,256]{3,2,1,0:T(8,128)} collective-permute-done((f32[2,4,160,256]{3,2,1,0:T(8,128)}, f32[2,4,160,256]{3,2,1,0:T(8,128)}, u32[]{:S(2)}, u32[]{:S(2)}) %collective-permute-start.4) | collective-permute-done | bytes 1310752 | tf_op jit(solution)/shard_map/ppermute | solution.py:167
  126.9 5.3 %shard_map.93.refs_4_ = f32[4,640,256]{2,1,0:T(8,128)} custom-call(f32[2,4,160,256]{3,2,1,0:T(8,128)} %get-tuple-element.42.refs_0_, f32[2,4,160,256]{3,2,1,0:T(8,128)} %get-tuple-element.43.refs_1_, f32[2,4,160,256]{3,2,1,0:T(8,128)} %copy-done.3, f32[2,4,160,256]{3,2,1,0:T(8,128)} %collective-permute-done.3.refs_3_, ...), custom_call_target="tpu_custom_call" | custom-call | flops 6000000000 | bytes 1000 | tf_op jit(solution)/shard_map/pallas_call | solution.py:153
  137.5 10.5 %reduce-scatter.4.cloned.1.call-done = f32[1,8,384,256]{3,2,1,0:T(8,128)} async-done(((f32[4,8,384,256]{3,2,1,0:T(8,128)}), f32[1,8,384,256]{3,2,1,0:T(8,128)}) %reduce-scatter.4.cloned.1.call-update) | async-done | bytes 3145744 | tf_op jit(solution)/shard_map/reduce_scatter | solution.py:175
  148.0 2.6 %shard_map.94 = (f32[2,2,192,256]{3,2,1,0:T(8,128)}, f32[2,2,192,256]{3,2,1,0:T(8,128)}) custom-call(f32[2,4,384,256]{3,2,1,0:T(8,128)} %bitcast.9, f32[2,4,384,256]{3,2,1,0:T(8,128)} %bitcast.10, f32[2,4,384,256]{3,2,1,0:T(8,128)} %bitcast.11, f32[2,4,384,256]{3,2,1,0:T(8,128)} %bitcast.12, f32[4,640,256]{2,1,0:T(8,128)} %shard_map.93.refs_4_), custom_call_target="tpu_custom_call" | custom-call | flops 6000000000 | bytes 1000 | tf_op jit(solution)/shard_map/pallas_call | solution.py:153
  150.7 2.8 %collective-permute-start.7 = (f32[2,2,192,256]{3,2,1,0:T(8,128)}, f32[2,2,192,256]{3,2,1,0:T(8,128)}, u32[]{:S(2)}, u32[]{:S(2)}) collective-permute-start(f32[2,2,192,256]{3,2,1,0:T(8,128)} %get-tuple-element.48), channel_id=1, source_target_pairs={{0,12},{1,13},{2,14},{3,15},{4,0},{5,1},{6,2},{7,3},{8,4},{9,5},{1... | collective-permute-start | bytes 2359304 | tf_op jit(solution)/shard_map/ppermute | solution.py:167
  153.5 9.7 %collective-permute-done.9.refs_1_.refs_4_ = f32[2,4,160,256]{3,2,1,0:T(8,128)} collective-permute-done((f32[2,4,160,256]{3,2,1,0:T(8,128)S(1)}, f32[2,4,160,256]{3,2,1,0:T(8,128)}, u32[]{:S(2)}, u32[]{:S(2)}) %collective-permute-start.9) | collective-permute-done | bytes 1310752 | tf_op jit(solution)/shard_map/ppermute | solution.py:171
  164.9 2.6 %collective-permute-done.11.refs_5_.refs_2_ = f32[2,4,160,256]{3,2,1,0:T(8,128)} collective-permute-done((f32[2,4,160,256]{3,2,1,0:T(8,128)}, f32[2,4,160,256]{3,2,1,0:T(8,128)}, u32[]{:S(2)}, u32[]{:S(2)}) %collective-permute-start.11) | collective-permute-done | bytes 1310752 | tf_op jit(solution)/shard_map/ppermute | solution.py:167
  167.5 2.3 collective-permute-done.10.refs_2_.refs_6_
  169.8 3.3 %shard_map.95 = (f32[4,160,256]{2,1,0:T(8,128)}, f32[4,160,256]{2,1,0:T(8,128)}) custom-call(f32[4,4,320,256]{3,2,1,0:T(8,128)} %get-tuple-element.38.refs_4_.refs_0_.refs_2_.refs_6_.refs_3_, f32[2,4,160,256]{3,2,1,0:T(8,128)} %collective-permute-done.9.refs_1_.refs_4_, f32[2,4,160,256]{3,2,1,0:T(8,128)} %collective-permute-done.10.refs_2_.refs_6_, ...), custom_call_target="tpu_custom_call" | custom-call | flops 6000000000 | bytes 1000 | tf_op jit(solution)/shard_map/pallas_call | solution.py:153
  175.2 9.2 %collective-permute-done.7.refs_3_.refs_1_ = f32[2,2,192,256]{3,2,1,0:T(8,128)} collective-permute-done((f32[2,2,192,256]{3,2,1,0:T(8,128)}, f32[2,2,192,256]{3,2,1,0:T(8,128)}, u32[]{:S(2)}, u32[]{:S(2)}) %collective-permute-start.7) | collective-permute-done | bytes 786464 | tf_op jit(solution)/shard_map/ppermute | solution.py:167
  189.0 2.7 %collective-permute-done.14.refs_1_.refs_5_ = f32[2,4,160,256]{3,2,1,0:T(8,128)S(1)} collective-permute-done((f32[2,4,160,256]{3,2,1,0:T(8,128)S(1)}, f32[2,4,160,256]{3,2,1,0:T(8,128)S(1)}, u32[]{:S(2)}, u32[]{:S(2)}) %collective-permute-start.14) | collective-permute-done | bytes 1310752 | tf_op jit(solution)/shard_map/ppermute | solution.py:171
  191.7 3.9 %collective-permute-done.16.refs_7_ = f32[4,160,256]{2,1,0:T(8,128)S(1)} collective-permute-done((f32[4,160,256]{2,1,0:T(8,128)}, f32[4,160,256]{2,1,0:T(8,128)S(1)}, u32[]{:S(2)}, u32[]{:S(2)}) %collective-permute-start.16) | collective-permute-done | bytes 655392 | tf_op jit(solution)/shard_map/ppermute | solution.py:167
  195.6 2.4 %collective-permute-done.15.refs_3_ = f32[4,160,256]{2,1,0:T(8,128)S(1)} collective-permute-done((f32[4,160,256]{2,1,0:T(8,128)}, f32[4,160,256]{2,1,0:T(8,128)S(1)}, u32[]{:S(2)}, u32[]{:S(2)}) %collective-permute-start.15) | collective-permute-done | bytes 655392 | tf_op jit(solution)/shard_map/ppermute | solution.py:167
  198.8 3.8 %shard_map.97.refs_6_ = f32[4,320,256]{2,1,0:T(8,128)} custom-call(f32[4,4,320,256]{3,2,1,0:T(8,128)} %get-tuple-element.38.refs_4_.refs_0_.refs_2_.refs_6_.refs_3_, f32[2,4,160,256]{3,2,1,0:T(8,128)} %copy-done.4, f32[2,4,160,256]{3,2,1,0:T(8,128)} %collective-permute-done.11.refs_5_.refs_2_, f32[4,160,256]{2,1,0:T(8,128)} %copy-done.7, ...), custom_call_target="tpu_custom_call" | custom-call | flops 6000000000 | bytes 1000 | tf_op jit(solution)/shard_map/pallas_call | solution.py:153
  203.8 3.1 %collective-permute-start.13 = (f32[2,192,256]{2,1,0:T(8,128)S(1)}, f32[2,192,256]{2,1,0:T(8,128)S(1)}, u32[]{:S(2)}, u32[]{:S(2)}) collective-permute-start(f32[2,192,256]{2,1,0:T(8,128)S(1)} %copy-done.9), channel_id=1, source_target_pairs={{0,12},{1,13},{2,14},{3,15},{4,0},{5,1},{6,2},{7,3},{8,4},{9,5},{1... | collective-permute-start | bytes 1179656 | tf_op jit(solution)/shard_map/ppermute | solution.py:167
  208.3 6.8 %collective-permute-done.17.refs_7_.refs_3_ = f32[320,256]{1,0:T(8,128)S(1)} collective-permute-done((f32[320,256]{1,0:T(8,128)S(1)}, f32[320,256]{1,0:T(8,128)S(1)}, u32[]{:S(2)}, u32[]{:S(2)}) %collective-permute-start.17) | collective-permute-done | bytes 327712 | tf_op jit(solution)/shard_map/ppermute | solution.py:171
  216.7 2.6 %shard_map.98 = (f32[384,256]{1,0:T(8,128)}, f32[384,256]{1,0:T(8,128)}) custom-call(f32[2,4,384,256]{3,2,1,0:T(8,128)} %bitcast.15, f32[2,2,192,256]{3,2,1,0:T(8,128)} %collective-permute-done.7.refs_3_.refs_1_, f32[2,192,256]{2,1,0:T(8,128)} %copy-done.10, f32[2,4,384,256]{3,2,1,0:T(8,128)} %bitcast.16, ...), custom_call_target="tpu_custom_call" | custom-call | flops 6000000000 | bytes 1000 | tf_op jit(solution)/shard_map/pallas_call | solution.py:153
  219.5 7.7 %collective-permute-done.18.refs_1_ = f32[384,256]{1,0:T(8,128)S(1)} collective-permute-done((f32[384,256]{1,0:T(8,128)}, f32[384,256]{1,0:T(8,128)S(1)}, u32[]{:S(2)}, u32[]{:S(2)}) %collective-permute-start.18) | collective-permute-done | bytes 393248 | tf_op jit(solution)/shard_map/ppermute | solution.py:171
  228.0 2.7 %shard_map.99 = f32[1,256,1024]{2,1,0:T(8,128)} custom-call(f32[384,256]{1,0:T(8,128)} %get-tuple-element.57.refs_0_, f32[384,256]{1,0:T(8,128)} %copy-done.12, f32[640,256]{1,0:T(8,128)} %bitcast.8, f32[320,256]{1,0:T(8,128)} %copy-done.13, f32[320,256]{1,0:T(8,128)} %bitcast.17), custom_call_target="tpu_custom_call" | custom-call | flops 6000000000 | bytes 1000 | tf_op jit(solution)/shard_map/pallas_call | solution.py:153
  (65 shorter events, 26.3 us)
Async XLA Ops:
  8.0 71.0 %all-reduce.2.cloned.1.call-start = ((), (), s32[]{:S(2)}) async-start(), calls=%async_computation.3 | async-start | bytes 2097152 | tf_op jit(solution)/shard_map/psum | solution.py:236
  12.6 135.5 %reduce-scatter.4.cloned.1.call-start = ((), (), s32[]{:S(2)}) async-start(), calls=%async_computation.4 | async-start | bytes 15728640 | tf_op jit(solution)/shard_map/reduce_scatter | solution.py:175
  30.9 176.0 %reduce-scatter.6.cloned.1.call-start = ((), (), s32[]{:S(2)}) async-start(), calls=%async_computation.5 | async-start | bytes 3276800 | tf_op jit(solution)/shard_map/reduce_scatter | solution.py:175
  35.9 36.9 %collective-permute-start.1 = (f32[2,4,160,256]{3,2,1,0:T(8,128)}, f32[2,4,160,256]{3,2,1,0:T(8,128)}, u32[]{:S(2)}, u32[]{:S(2)}) collective-permute-start(f32[2,4,160,256]{3,2,1,0:T(8,128)} %get-tuple-element.37), channel_id=1, source_target_pairs={{0,12},{1,13},{2,14},{3,15},{4,0},{5,1},{6,2},{7,3},{8,4},{9,5},{1... | collective-permute-start | bytes 3932168 | tf_op jit(solution)/shard_map/ppermute | solution.py:167
  39.0 33.7 %collective-permute-start = (f32[2,4,160,256]{3,2,1,0:T(8,128)}, f32[2,4,160,256]{3,2,1,0:T(8,128)}, u32[]{:S(2)}, u32[]{:S(2)}) collective-permute-start(f32[2,4,160,256]{3,2,1,0:T(8,128)} %get-tuple-element.33.refs_0_), channel_id=1, source_target_pairs={{0,4},{1,5},{2,6},{3,7},{4,8},{5,9},{6,10},{7,11},{8,12},{9,13},{1... | collective-permute-start | bytes 3932168 | tf_op jit(solution)/shard_map/ppermute | solution.py:167
  48.3 65.7 %collective-permute-start.6 = (f32[4,4,160,256]{3,2,1,0:T(8,128)}, f32[4,4,160,256]{3,2,1,0:T(8,128)}, u32[]{:S(2)}, u32[]{:S(2)}) collective-permute-start(f32[4,4,160,256]{3,2,1,0:T(8,128)} %get-tuple-element.34.refs_0_), channel_id=1, source_target_pairs={{0,16},{1,17},{2,18},{3,19},{4,20},{5,21},{6,22},{7,23},{8,24},{9,... | collective-permute-start | bytes 7864328 | tf_op jit(solution)/shard_map/ppermute | solution.py:171
  58.8 59.4 %collective-permute-start.2 = (f32[2,4,160,256]{3,2,1,0:T(8,128)}, f32[2,4,160,256]{3,2,1,0:T(8,128)S(1)}, u32[]{:S(2)}, u32[]{:S(2)}) collective-permute-start(f32[2,4,160,256]{3,2,1,0:T(8,128)} %get-tuple-element.44), channel_id=1, source_target_pairs={{0,4},{1,5},{2,6},{3,7},{4,8},{5,9},{6,10},{7,11},{8,12},{9,13},{1... | collective-permute-start | bytes 3932168 | tf_op jit(solution)/shard_map/ppermute | solution.py:167
  59.6 58.7 %collective-permute-start.3 = (f32[2,4,160,256]{3,2,1,0:T(8,128)}, f32[2,4,160,256]{3,2,1,0:T(8,128)}, u32[]{:S(2)}, u32[]{:S(2)}) collective-permute-start(f32[2,4,160,256]{3,2,1,0:T(8,128)} %get-tuple-element.45), channel_id=1, source_target_pairs={{0,12},{1,13},{2,14},{3,15},{4,0},{5,1},{6,2},{7,3},{8,4},{9,5},{1... | collective-permute-start | bytes 3932168 | tf_op jit(solution)/shard_map/ppermute | solution.py:167
  76.9 46.6 %collective-permute-start.5 = (f32[2,4,160,256]{3,2,1,0:T(8,128)}, f32[2,4,160,256]{3,2,1,0:T(8,128)S(1)}, u32[]{:S(2)}, u32[]{:S(2)}) collective-permute-start(f32[2,4,160,256]{3,2,1,0:T(8,128)} %get-tuple-element.46), channel_id=1, source_target_pairs={{0,12},{1,13},{2,14},{3,15},{4,0},{5,1},{6,2},{7,3},{8,4},{9,5},{1... | collective-permute-start | bytes 3932168 | tf_op jit(solution)/shard_map/ppermute | solution.py:167
  79.0 47.9 %collective-permute-start.4 = (f32[2,4,160,256]{3,2,1,0:T(8,128)}, f32[2,4,160,256]{3,2,1,0:T(8,128)}, u32[]{:S(2)}, u32[]{:S(2)}) collective-permute-start(f32[2,4,160,256]{3,2,1,0:T(8,128)} %get-tuple-element.39.refs_3_), channel_id=1, source_target_pairs={{0,4},{1,5},{2,6},{3,7},{4,8},{5,9},{6,10},{7,11},{8,12},{9,13},{1... | collective-permute-start | bytes 3932168 | tf_op jit(solution)/shard_map/ppermute | solution.py:167
  118.3 8.6 %copy-start.3 = (f32[2,4,160,256]{3,2,1,0:T(8,128)}, f32[2,4,160,256]{3,2,1,0:T(8,128)S(1)}, u32[]{:S(2)}) copy-start(f32[2,4,160,256]{3,2,1,0:T(8,128)S(1)} %collective-permute-done.2.refs_2_) | copy-start | bytes 3932164
  123.5 3.4 %copy-start.5 = (f32[2,4,160,256]{3,2,1,0:T(8,128)}, f32[2,4,160,256]{3,2,1,0:T(8,128)S(1)}, u32[]{:S(2)}) copy-start(f32[2,4,160,256]{3,2,1,0:T(8,128)S(1)} %collective-permute-done.5.refs_5_) | copy-start | bytes 3932164
  132.2 1.3 copy-start.1
  132.2 4.6 %copy-start.2 = (f32[2,4,160,256]{3,2,1,0:T(8,128)S(1)}, f32[2,4,160,256]{3,2,1,0:T(8,128)}, u32[]{:S(2)}) copy-start(f32[2,4,160,256]{3,2,1,0:T(8,128)} %get-tuple-element.47.refs_6_) | copy-start | bytes 3932164
  132.3 95.0 %reduce-scatter.8.cloned.1.call-start = ((), (), s32[]{:S(2)}) async-start(), calls=%async_computation.6 | async-start | bytes 1638400 | tf_op jit(solution)/shard_map/reduce_scatter | solution.py:175
  133.5 29.6 %collective-permute-start.9 = (f32[2,4,160,256]{3,2,1,0:T(8,128)S(1)}, f32[2,4,160,256]{3,2,1,0:T(8,128)}, u32[]{:S(2)}, u32[]{:S(2)}) collective-permute-start(f32[2,4,160,256]{3,2,1,0:T(8,128)S(1)} %copy-done.1), channel_id=1, source_target_pairs={{0,16},{1,17},{2,18},{3,19},{4,20},{5,21},{6,22},{7,23},{8,24},{9,... | collective-permute-start | bytes 3932168 | tf_op jit(solution)/shard_map/ppermute | solution.py:171
  135.5 32.0 %collective-permute-start.11 = (f32[2,4,160,256]{3,2,1,0:T(8,128)}, f32[2,4,160,256]{3,2,1,0:T(8,128)}, u32[]{:S(2)}, u32[]{:S(2)}) collective-permute-start(f32[2,4,160,256]{3,2,1,0:T(8,128)} %get-tuple-element.51), channel_id=1, source_target_pairs={{0,12},{1,13},{2,14},{3,15},{4,0},{5,1},{6,2},{7,3},{8,4},{9,5},{1... | collective-permute-start | bytes 3932168 | tf_op jit(solution)/shard_map/ppermute | solution.py:167
  136.8 33.0 %collective-permute-start.10 = (f32[2,4,160,256]{3,2,1,0:T(8,128)S(1)}, f32[2,4,160,256]{3,2,1,0:T(8,128)}, u32[]{:S(2)}, u32[]{:S(2)}) collective-permute-start(f32[2,4,160,256]{3,2,1,0:T(8,128)S(1)} %copy-done.2), channel_id=1, source_target_pairs={{0,4},{1,5},{2,6},{3,7},{4,8},{5,9},{6,10},{7,11},{8,12},{9,13},{1... | collective-permute-start | bytes 3932168 | tf_op jit(solution)/shard_map/ppermute | solution.py:167
  148.0 15.1 %copy-start = (f32[2,4,160,256]{3,2,1,0:T(8,128)S(1)}, f32[2,4,160,256]{3,2,1,0:T(8,128)}, u32[]{:S(2)}) copy-start(f32[2,4,160,256]{3,2,1,0:T(8,128)} %get-tuple-element.55) | copy-start | bytes 3932164
  150.7 33.7 %collective-permute-start.7 = (f32[2,2,192,256]{3,2,1,0:T(8,128)}, f32[2,2,192,256]{3,2,1,0:T(8,128)}, u32[]{:S(2)}, u32[]{:S(2)}) collective-permute-start(f32[2,2,192,256]{3,2,1,0:T(8,128)} %get-tuple-element.48), channel_id=1, source_target_pairs={{0,12},{1,13},{2,14},{3,15},{4,0},{5,1},{6,2},{7,3},{8,4},{9,5},{1... | collective-permute-start | bytes 2359304 | tf_op jit(solution)/shard_map/ppermute | solution.py:167
  153.5 33.2 %collective-permute-start.8 = (f32[2,2,192,256]{3,2,1,0:T(8,128)}, f32[2,2,192,256]{3,2,1,0:T(8,128)}, u32[]{:S(2)}, u32[]{:S(2)}) collective-permute-start(f32[2,2,192,256]{3,2,1,0:T(8,128)} %get-tuple-element.49.refs_6_), channel_id=1, source_target_pairs={{0,4},{1,5},{2,6},{3,7},{4,8},{5,9},{6,10},{7,11},{8,12},{9,13},{1... | collective-permute-start | bytes 2359304 | tf_op jit(solution)/shard_map/ppermute | solution.py:167
  163.1 28.6 %collective-permute-start.14 = (f32[2,4,160,256]{3,2,1,0:T(8,128)S(1)}, f32[2,4,160,256]{3,2,1,0:T(8,128)S(1)}, u32[]{:S(2)}, u32[]{:S(2)}) collective-permute-start(f32[2,4,160,256]{3,2,1,0:T(8,128)S(1)} %copy-done), channel_id=1, source_target_pairs={{0,16},{1,17},{2,18},{3,19},{4,20},{5,21},{6,22},{7,23},{8,24},{9,... | collective-permute-start | bytes 3932168 | tf_op jit(solution)/shard_map/ppermute | solution.py:171
  173.2 22.4 %collective-permute-start.16 = (f32[4,160,256]{2,1,0:T(8,128)}, f32[4,160,256]{2,1,0:T(8,128)S(1)}, u32[]{:S(2)}, u32[]{:S(2)}) collective-permute-start(f32[4,160,256]{2,1,0:T(8,128)} %get-tuple-element.56), channel_id=1, source_target_pairs={{0,12},{1,13},{2,14},{3,15},{4,0},{5,1},{6,2},{7,3},{8,4},{9,5},{1... | collective-permute-start | bytes 1966088 | tf_op jit(solution)/shard_map/ppermute | solution.py:167
  173.4 24.6 %collective-permute-start.15 = (f32[4,160,256]{2,1,0:T(8,128)}, f32[4,160,256]{2,1,0:T(8,128)S(1)}, u32[]{:S(2)}, u32[]{:S(2)}) collective-permute-start(f32[4,160,256]{2,1,0:T(8,128)} %get-tuple-element.52.refs_4_), channel_id=1, source_target_pairs={{0,4},{1,5},{2,6},{3,7},{4,8},{5,9},{6,10},{7,11},{8,12},{9,13},{1... | collective-permute-start | bytes 1966088 | tf_op jit(solution)/shard_map/ppermute | solution.py:167
  191.7 6.3 %copy-start.4 = (f32[2,4,160,256]{3,2,1,0:T(8,128)}, f32[2,4,160,256]{3,2,1,0:T(8,128)S(1)}, u32[]{:S(2)}) copy-start(f32[2,4,160,256]{3,2,1,0:T(8,128)S(1)} %collective-permute-done.14.refs_1_.refs_5_) | copy-start | bytes 3932164
  195.6 2.4 %copy-start.6 = (f32[4,160,256]{2,1,0:T(8,128)}, f32[4,160,256]{2,1,0:T(8,128)S(1)}, u32[]{:S(2)}) copy-start(f32[4,160,256]{2,1,0:T(8,128)S(1)} %collective-permute-done.16.refs_7_) | copy-start | bytes 1966084
  202.7 1.0 copy-start.8
  202.7 1.1 copy-start.9
  203.7 11.4 %collective-permute-start.12 = (f32[2,192,256]{2,1,0:T(8,128)S(1)}, f32[2,192,256]{2,1,0:T(8,128)S(1)}, u32[]{:S(2)}, u32[]{:S(2)}) collective-permute-start(f32[2,192,256]{2,1,0:T(8,128)S(1)} %copy-done.8), channel_id=1, source_target_pairs={{0,4},{1,5},{2,6},{3,7},{4,8},{5,9},{6,10},{7,11},{8,12},{9,13},{1... | collective-permute-start | bytes 1179656 | tf_op jit(solution)/shard_map/ppermute | solution.py:167
  203.8 11.3 %collective-permute-start.13 = (f32[2,192,256]{2,1,0:T(8,128)S(1)}, f32[2,192,256]{2,1,0:T(8,128)S(1)}, u32[]{:S(2)}, u32[]{:S(2)}) collective-permute-start(f32[2,192,256]{2,1,0:T(8,128)S(1)} %copy-done.9), channel_id=1, source_target_pairs={{0,12},{1,13},{2,14},{3,15},{4,0},{5,1},{6,2},{7,3},{8,4},{9,5},{1... | collective-permute-start | bytes 1179656 | tf_op jit(solution)/shard_map/ppermute | solution.py:167
  207.9 7.2 %collective-permute-start.17 = (f32[320,256]{1,0:T(8,128)S(1)}, f32[320,256]{1,0:T(8,128)S(1)}, u32[]{:S(2)}, u32[]{:S(2)}) collective-permute-start(f32[320,256]{1,0:T(8,128)S(1)} %slice_bitcast_fusion), channel_id=1, source_target_pairs={{0,16},{1,17},{2,18},{3,19},{4,20},{5,21},{6,22},{7,23},{8,24},{9,... | collective-permute-start | bytes 983048 | tf_op jit(solution)/shard_map/ppermute | solution.py:171
  219.3 8.0 %collective-permute-start.18 = (f32[384,256]{1,0:T(8,128)}, f32[384,256]{1,0:T(8,128)S(1)}, u32[]{:S(2)}, u32[]{:S(2)}) collective-permute-start(f32[384,256]{1,0:T(8,128)} %get-tuple-element.58), channel_id=1, source_target_pairs={{0,16},{1,17},{2,18},{3,19},{4,20},{5,21},{6,22},{7,23},{8,24},{9,... | collective-permute-start | bytes 1179656 | tf_op jit(solution)/shard_map/ppermute | solution.py:171
  (5 other events, 4.0 us)
Sparse Core Ops, SparseCore 0:
  12.7 51.6 all-reduce.1
Sparse Core Ops, SparseCore 1:
  31.0 117.0 reduce-scatter.3
  150.4 33.5 reduce-scatter.5
  202.8 24.1 reduce-scatter.7

commit v9 on v6

--- a/solution.py
+++ b/solution.py
@@ -66,7 +66,7 @@
         def emit(h, out, n):
             value = jnp.dot(k[low + h * half : low + (h + 1) * half, :], x[...], preferred_element_type=jnp.float32)
             for place in range(ROW):
-                out[n, (place - table[STRIPS]) & (ROW - 1)] = value[:, place * WIDTH : (place + 1) * WIDTH]
+                out[n, place] = value[:, place * WIDTH : (place + 1) * WIDTH]
 
         for at, first, second in ((0, soon, soon), (1, later, soon), (2, soon, later), (3, last, last)):
 
@@ -107,19 +107,19 @@
     def body(table, x, k, *refs):
         outs = refs[len(after) :]
         step = pl.program_id(0)
-        for (low, height, first, number, _), out in zip(wanted, outs):
-
-            def emit(low=low, height=height, out=out):
+        for (low, height, first, number, _, turn), out in zip(wanted, outs):
+
+            def emit(low=low, height=height, turn=turn, out=out):
                 value = jnp.dot(k[low : low + height, :], x[...], preferred_element_type=jnp.float32)
                 for place in range(ROW):
-                    out[0, (place - table[STRIPS]) & (ROW - 1)] = value[:, place * WIDTH : (place + 1) * WIDTH]
+                    out[0, (place - turn * table[STRIPS]) & (ROW - 1)] = value[:, place * WIDTH : (place + 1) * WIDTH]
 
             if number == count:
                 emit()
             else:
                 pl.when((step >= first) & (step < first + number))(emit)
 
-    def out_spec(low, height, first, number, order):
+    def out_spec(low, height, first, number, order, turn):
         def at(i, table):
             n = jnp.clip(i - first, 0, number - 1)
             return (n if order > 0 else number - 1 - n, 0, 0, 0)
@@ -247,7 +247,7 @@
         table,
         2,
         lambda i: 2 + 4 * i,
-        [(b_low, half, 0, 2, 1), (b_high, half, 0, 2, 1)],
+        [(b_low, half, 0, 2, 1, 1), (b_high, half, 0, 2, 1, 1)],
         [a],
     )
     b_up1, b_down1 = along("y", b_far[0], 1), along("y", b_far[1], -1)
@@ -261,7 +261,7 @@
         table,
         4,
         lambda i: 1 + 4 * lax.rem(i, 2) + 2 * (i // 2),
-        [(low, half, first, 2, 1) for first in (0, 2) for low in (b_low, b_high)],
+        [(low, half, first, 2, 1, 1) for first in (0, 2) for low in (b_low, b_high)],
         c_far[:1],
     )
     b_up2, b_down2 = along("y", b_near[1], 1), along("y", b_near[2], -1)
@@ -271,7 +271,7 @@
         table,
         5,
         lambda i: jnp.where(i == 0, 4, i - 1),
-        [(b_low, half, 0, 2, -1), (b_high, half, 0, 2, -1), (c_low, C, 1, 4, 1)],
+        [(b_low, half, 0, 2, -1, 1), (b_high, half, 0, 2, -1, 1), (c_low, C, 1, 4, 1, 0)],
         b_near[:1],
     )
 
@@ -317,36 +317,26 @@
     done = ring_a.send(done)
     done, b_got = ring_b.send(done)
 
-    def c_x_terms(dx, h):
-        block = (1, 1, C // 2, WIDTH)
-        terms = [(c_near, block, (0, dx, h, 0)), (c_z[2], block, (h, dx, 0, 0))]
-        for array, n in c_got(h):
-            terms.append((array, block[1:], (dx, 0, 0)) if n is None else (array, block, (n, dx, 0, 0)))
-        return terms
-
     def keep_and_cross(low, high, keep, cross):
         rows = low.shape[1]
         keep[:rows, :], keep[rows:, :] = low[0], high[0]
         cross[:rows, :], cross[rows:, :] = low[1], high[1]
 
-    ring_cx = reduce_ring("x", c_x_terms, 1, C // 2)
-    next(ring_cx)
-    done = ring_cx.send(done)
+    def c_home(low, high, out):
+        out[:, : C // 2, :], out[:, C // 2 :, :] = low, high
+
+    (c_sum,) = settle(
+        c_terms(0, 0) + whole(c_got(0)), c_terms(0, 1) + whole(c_got(1)), c_home, [(ROW, C, WIDTH)], done
+    )
+    c_own = over_x(c_sum)
     b_keep, b_cross = settle(
-        b_terms(0, 0) + whole(b_got(0)), b_terms(0, 1) + whole(b_got(1)), keep_and_cross, [(B, WIDTH)] * 2, done
+        b_terms(0, 0) + whole(b_got(0)), b_terms(0, 1) + whole(b_got(1)), keep_and_cross, [(B, WIDTH)] * 2, [c_sum]
     )
     b_in = along_z(b_cross)
-    done, cx_got = ring_cx.send([b_keep])
-    done, a_got = ring_a.send(done)
-
-    def c_home(low, high, out):
-        out[: C // 2, :], out[C // 2 :, :] = low[0], high[0]
-
-    (c_own,) = settle(
-        c_x_terms(0, 0) + whole(cx_got(0)), c_x_terms(0, 1) + whole(cx_got(1)), c_home, [(C, WIDTH)], done
-    )
+    done, a_got = ring_a.send([b_keep])
+
     a_keep, a_cross = settle(
-        a_terms(0, 0) + whole(a_got(0)), a_terms(0, 1) + whole(a_got(1)), keep_and_cross, [(A, WIDTH)] * 2, [c_own, b_in]
+        a_terms(0, 0) + whole(a_got(0)), a_terms(0, 1) + whole(a_got(1)), keep_and_cross, [(A, WIDTH)] * 2, done + [b_in]
     )
     a_in = along_z(a_cross)
 

time: 235 us -> 239 us (1.017)
  waiting for transfers between devices: 70.7 us -> 87.8 us
  starting transfers between devices: 40.9 us -> 33.9 us
  local copies, waits for them, and re-layouts: 9.21 us -> 4.58 us
  Pallas kernels: 92.4 us -> 89.1 us
    ppermute x22 -> x18, waiting for transfers between devices: 16.9 us -> 27.8 us  [along(): return lax.ppermute(array, 'fsdp', pairs)]
    ppermute x22 -> x18, starting transfers between devices: 32.4 us -> 25.4 us  [along(): return lax.ppermute(array, 'fsdp', pairs)]
    ppermute x5, waiting for transfers between devices: 53.7 us -> 60 us  [along_z(): return lax.ppermute(array, 'fsdp', [(f, (f + 16) % 32) for f in range(32)])]
    unnamed x34 -> x36, local copies, waits for them, and re-layouts: 9.21 us -> 4.58 us
    pallas_call x14 -> x12, Pallas kernels: 41.1 us -> 37.7 us  [combine(): pl.pallas_call(kernel, grid=(1,), in_specs=[pl.BlockSpec(block, lambda i,...]
  transfers between devices with their start and end apart: 29 -> 26, of which waited for: 13 -> 15; matrix products, arithmetic and copies ran while one was open for 0% -> 0% of each run, Pallas kernels for 37% -> 35%
where the time goes in v9:
time: 239 us; the launch traced here: 236 us
  Pallas kernels  89.1 us (37%)
  waiting for transfers between devices  87.8 us (37%)
  starting transfers between devices  33.9 us (14%)
  between operations  16.2 us (7%)
  local copies, waits for them, and re-layouts  4.58 us (2%)
  other arithmetic  4.36 us (2%)
    ppermute x5, waiting for transfers between devices, along_z(): return lax.ppermute(array, 'fsdp', [(f, (f + 16) % 32) for f in range(32)])  60 us
    pallas_call x12, Pallas kernels, combine(): pl.pallas_call(kernel, grid=(1,), in_specs=[pl.BlockSpec(block, lambda i,...  37.7 us
    ppermute x18, waiting for transfers between devices, along(): return lax.ppermute(array, 'fsdp', pairs)  27.8 us
    ppermute x18, starting transfers between devices, along(): return lax.ppermute(array, 'fsdp', pairs)  25.4 us
    pallas_call x3, Pallas kernels, products(): pl.pallas_call(body, grid_spec=pltpu.PrefetchScalarGridSpec(num_scalar_pr...  24.3 us
    pallas_call x1, Pallas kernels, all_products(): pl.pallas_call(body, grid_spec=pltpu.PrefetchScalarGridSpec(num_scalar_pr...  17.7 us
    pallas_call x1, Pallas kernels, crossing_products(): pl.pallas_call(body, grid_spec=pltpu.PrefetchScalarGridSpec(num_scalar_pr...  9.34 us
    ppermute x5, starting transfers between devices, along_z(): return lax.ppermute(array, 'fsdp', [(f, (f + 16) % 32) for f in range(32)])  8.32 us
  transfers between devices with their start and end apart: 26, of which 15 were waited for; matrix products, arithmetic and copies ran while one was open for 0% of the time, Pallas kernels for 35%

profile of v9, /device:TPU:0, one launch (start us, length us, event | category | flops | bytes accessed | tf_op | source)
XLA Modules:
  0.0 236.0 jit_solution(15326504625596421741)
XLA Ops:
  10.0 2.5 %convert_divide_fusion = f32[256,1024]{1,0:T(8,128)} fusion(f32[256,1024]{1,0:T(8,128)} %refs_0_.1, bf16[1,256,1024]{2,1,0:T(8,128)(2,1)} %param.8, f32[]{:T(128)S(6)} %convert_element_type.17), kind=kLoop, calls=%fused_computation.4 | loop fusion | flops 1835008 | bytes 2621444 | tf_op jit(solution)/shard_map/div | solution.py:238
  13.2 17.7 %shard_map.85 = (f32[4,8,384,256]{3,2,1,0:T(8,128)}, bf16[1024,1024]{1,0:T(8,128)(2,1)S(1)}) custom-call(s32[9]{0:T(128)} %compare_select_fusion.4.table, bf16[1024,8192]{1,0:T(8,128)(2,1)} %x.9, bf16[1024,1024]{1,0:T(8,128)(2,1)} %k.1), custom_call_target="tpu_custom_call" | custom-call | flops 20000000000 | bytes 1000 | tf_op jit(solution)/shard_map/pallas_call | solution.py:35
  31.0 4.9 %shard_map.86 = (f32[2,4,160,256]{3,2,1,0:T(8,128)}, f32[2,4,160,256]{3,2,1,0:T(8,128)}) custom-call(s32[9]{0:T(128)} %compare_select_fusion.4.table, bf16[1024,8192]{1,0:T(8,128)(2,1)} %x.9, bf16[1024,1024]{1,0:T(8,128)(2,1)S(1)} %get-tuple-element.37.k, f32[4,8,384,256]{3,2,1,0:T(8,128)} %get-tuple-element.38.refs_0_), custom_call_target="tpu_custom_call" | custom-call | flops 20000000000 | bytes 1000 | tf_op jit(solution)/shard_map/pallas_call | solution.py:129
  35.9 3.1 %collective-permute-start.1 = (f32[2,4,160,256]{3,2,1,0:T(8,128)}, f32[2,4,160,256]{3,2,1,0:T(8,128)}, u32[]{:S(2)}, u32[]{:S(2)}) collective-permute-start(f32[2,4,160,256]{3,2,1,0:T(8,128)} %get-tuple-element.43), channel_id=1, source_target_pairs={{0,12},{1,13},{2,14},{3,15},{4,0},{5,1},{6,2},{7,3},{8,4},{9,5},{1... | collective-permute-start | bytes 3932168 | tf_op jit(solution)/shard_map/ppermute | solution.py:168
  39.0 9.3 %shard_map.87 = (f32[4,4,160,256]{3,2,1,0:T(8,128)}, f32[2,4,160,256]{3,2,1,0:T(8,128)}, f32[2,4,160,256]{3,2,1,0:T(8,128)}) custom-call(s32[9]{0:T(128)} %compare_select_fusion.4.table, bf16[1024,8192]{1,0:T(8,128)(2,1)} %x.9, bf16[1024,1024]{1,0:T(8,128)(2,1)S(1)} %get-tuple-element.37.k, f32[2,4,160,256]{3,2,1,0:T(8,128)} %get-tuple-element.39.refs_0_), custom_call_target="tpu_custom_call" | custom-call | flops 20000000000 | bytes 1000 | tf_op jit(solution)/shard_map/pallas_call | solution.py:79
  50.2 8.6 %shard_map.88 = (f32[2,4,160,256]{3,2,1,0:T(8,128)}, f32[2,4,160,256]{3,2,1,0:T(8,128)}, f32[2,4,160,256]{3,2,1,0:T(8,128)}, f32[2,4,160,256]{3,2,1,0:T(8,128)}) custom-call(s32[9]{0:T(128)} %compare_select_fusion.4.table, bf16[1024,8192]{1,0:T(8,128)(2,1)} %x.9, bf16[1024,1024]{1,0:T(8,128)(2,1)S(1)} %get-tuple-element.37.k, ...), custom_call_target="tpu_custom_call" | custom-call | flops 20000000000 | bytes 1000 | tf_op jit(solution)/shard_map/pallas_call | solution.py:129
  58.9 3.1 %collective-permute-start.6 = (f32[2,4,160,256]{3,2,1,0:T(8,128)}, f32[2,4,160,256]{3,2,1,0:T(8,128)S(1)}, u32[]{:S(2)}, u32[]{:S(2)}) collective-permute-start(f32[2,4,160,256]{3,2,1,0:T(8,128)} %get-tuple-element.52), channel_id=1, source_target_pairs={{0,12},{1,13},{2,14},{3,15},{4,0},{5,1},{6,2},{7,3},{8,4},{9,5},{1... | collective-permute-start | bytes 3932168 | tf_op jit(solution)/shard_map/ppermute | solution.py:168
  62.0 10.7 %shard_map.89 = (f32[2,4,160,256]{3,2,1,0:T(8,128)}, f32[2,4,160,256]{3,2,1,0:T(8,128)}, f32[4,4,320,256]{3,2,1,0:T(8,128)}) custom-call(s32[9]{0:T(128)} %compare_select_fusion.4.table, bf16[1024,8192]{1,0:T(8,128)(2,1)} %x.9, bf16[1024,1024]{1,0:T(8,128)(2,1)S(1)} %get-tuple-element.37.k, f32[2,4,160,256]{3,2,1,0:T(8,128)} %get-tuple-element.41.refs_0_), custom_call_target="tpu_custom_call" | custom-call | flops 20000000000 | bytes 1000 | tf_op jit(solution)/shard_map/pallas_call | solution.py:129
  72.7 4.1 %shard_map.90 = (f32[2,4,160,256]{3,2,1,0:T(8,128)}, f32[2,4,160,256]{3,2,1,0:T(8,128)}) custom-call(f32[2,4,160,256]{3,2,1,0:T(8,128)} %get-tuple-element.41.refs_0_, f32[2,4,160,256]{3,2,1,0:T(8,128)} %get-tuple-element.42.refs_1_, f32[2,4,160,256]{3,2,1,0:T(8,128)} %collective-permute-done.refs_2_, f32[2,4,160,256]{3,2,1,0:T(8,128)} %collective-permute-done.1.refs_3_, ...), custom_call_target="tpu_custom_call" | custom-call | flops 4000000000 | bytes 1000 | tf_op jit(solution)/shard_map/pallas_call | solution.py:153
  76.9 3.3 %collective-permute-start.9 = (f32[2,4,160,256]{3,2,1,0:T(8,128)}, f32[2,4,160,256]{3,2,1,0:T(8,128)S(1)}, u32[]{:S(2)}, u32[]{:S(2)}) collective-permute-start(f32[2,4,160,256]{3,2,1,0:T(8,128)} %get-tuple-element.55), channel_id=1, source_target_pairs={{0,12},{1,13},{2,14},{3,15},{4,0},{5,1},{6,2},{7,3},{8,4},{9,5},{1... | collective-permute-start | bytes 3932168 | tf_op jit(solution)/shard_map/ppermute | solution.py:168
  80.1 3.4 %shard_map.91 = (f32[256,1024]{1,0:T(8,128)}, f32[256,1024]{1,0:T(8,128)}) custom-call(f32[256,1024]{1,0:T(8,128)} %refs_0_.1, f32[256,1024]{1,0:T(8,128)} %refs_1_.1, f32[256,1024]{1,0:T(8,128)} %all-reduce.2.cloned.1.call-done.refs_2_, f32[2,4,160,256]{3,2,1,0:T(8,128)} %get-tuple-element.45.refs_3_), custom_call_target="tpu_custom_call" | custom-call | flops 4000000000 | bytes 1000 | tf_op jit(solution)/shard_map/pallas_call | solution.py:153
  83.5 30.5 %collective-permute-done.3.refs_1_.refs_3_.refs_5_.refs_7_ = f32[4,4,160,256]{3,2,1,0:T(8,128)} collective-permute-done((f32[4,4,160,256]{3,2,1,0:T(8,128)}, f32[4,4,160,256]{3,2,1,0:T(8,128)}, u32[]{:S(2)}, u32[]{:S(2)}) %collective-permute-start.3) | collective-permute-done | bytes 2621472 | tf_op jit(solution)/shard_map/ppermute | solution.py:172
  114.5 4.2 %shard_map.92 = (f32[2,4,160,256]{3,2,1,0:T(8,128)}, f32[2,4,160,256]{3,2,1,0:T(8,128)}) custom-call(f32[4,4,320,256]{3,2,1,0:T(8,128)} %get-tuple-element.44.refs_4_.refs_0_.refs_2_.refs_6_.refs_3_, f32[4,4,160,256]{3,2,1,0:T(8,128)} %collective-permute-done.3.refs_1_.refs_3_.refs_5_.refs_7_, ...), custom_call_target="tpu_custom_call" | custom-call | flops 4000000000 | bytes 1000 | tf_op jit(solution)/shard_map/pallas_call | solution.py:153
  118.7 3.1 %collective-permute-start.5 = (f32[2,4,160,256]{3,2,1,0:T(8,128)}, f32[2,4,160,256]{3,2,1,0:T(8,128)}, u32[]{:S(2)}, u32[]{:S(2)}) collective-permute-start(f32[2,4,160,256]{3,2,1,0:T(8,128)} %get-tuple-element.50), channel_id=1, source_target_pairs={{0,12},{1,13},{2,14},{3,15},{4,0},{5,1},{6,2},{7,3},{8,4},{9,5},{1... | collective-permute-start | bytes 3932168 | tf_op jit(solution)/shard_map/ppermute | solution.py:168
  121.8 2.9 %collective-permute-done.9.refs_5_.refs_8_.refs_6_.refs_7_ = f32[2,4,160,256]{3,2,1,0:T(8,128)S(1)} collective-permute-done((f32[2,4,160,256]{3,2,1,0:T(8,128)}, f32[2,4,160,256]{3,2,1,0:T(8,128)S(1)}, u32[]{:S(2)}, u32[]{:S(2)}) %collective-permute-start.9) | collective-permute-done | bytes 1310752 | tf_op jit(solution)/shard_map/ppermute | solution.py:168
  128.4 3.2 %shard_map.93 = (f32[2,2,160,256]{3,2,1,0:T(8,128)}, f32[2,2,160,256]{3,2,1,0:T(8,128)}) custom-call(f32[2,4,160,256]{3,2,1,0:T(8,128)} %get-tuple-element.51.refs_0_.refs_9_, f32[2,4,160,256]{3,2,1,0:T(8,128)} %copy-done, f32[2,4,160,256]{3,2,1,0:T(8,128)} %collective-permute-done.7.refs_2_.refs_11_, ...), custom_call_target="tpu_custom_call" | custom-call | flops 4000000000 | bytes 1000 | tf_op jit(solution)/shard_map/pallas_call | solution.py:153
  131.7 2.7 %collective-permute-start.12 = (f32[2,2,160,256]{3,2,1,0:T(8,128)}, f32[2,2,160,256]{3,2,1,0:T(8,128)S(1)}, u32[]{:S(2)}, u32[]{:S(2)}) collective-permute-start(f32[2,2,160,256]{3,2,1,0:T(8,128)} %get-tuple-element.60), channel_id=1, source_target_pairs={{0,3},{1,0},{2,1},{3,2},{4,7},{5,4},{6,5},{7,6},{8,11},{9,8},{10,9... | collective-permute-start | bytes 1966088 | tf_op jit(solution)/shard_map/ppermute | solution.py:168
  134.4 11.6 %collective-permute-done.2.refs_1_.refs_4_ = f32[2,4,160,256]{3,2,1,0:T(8,128)} collective-permute-done((f32[2,4,160,256]{3,2,1,0:T(8,128)}, f32[2,4,160,256]{3,2,1,0:T(8,128)}, u32[]{:S(2)}, u32[]{:S(2)}) %collective-permute-start.2) | collective-permute-done | bytes 1310752 | tf_op jit(solution)/shard_map/ppermute | solution.py:172
  147.5 4.1 %collective-permute-done.5.refs_5_.refs_2_ = f32[2,4,160,256]{3,2,1,0:T(8,128)} collective-permute-done((f32[2,4,160,256]{3,2,1,0:T(8,128)}, f32[2,4,160,256]{3,2,1,0:T(8,128)}, u32[]{:S(2)}, u32[]{:S(2)}) %collective-permute-start.5) | collective-permute-done | bytes 1310752 | tf_op jit(solution)/shard_map/ppermute | solution.py:168
  151.6 3.4 %collective-permute-done.4.refs_2_.refs_6_ = f32[2,4,160,256]{3,2,1,0:T(8,128)} collective-permute-done((f32[2,4,160,256]{3,2,1,0:T(8,128)}, f32[2,4,160,256]{3,2,1,0:T(8,128)}, u32[]{:S(2)}, u32[]{:S(2)}) %collective-permute-start.4) | collective-permute-done | bytes 1310752 | tf_op jit(solution)/shard_map/ppermute | solution.py:168
  155.0 3.2 %shard_map.94 = (f32[4,160,256]{2,1,0:T(8,128)}, f32[4,160,256]{2,1,0:T(8,128)}) custom-call(f32[4,4,320,256]{3,2,1,0:T(8,128)} %get-tuple-element.44.refs_4_.refs_0_.refs_2_.refs_6_.refs_3_, f32[2,4,160,256]{3,2,1,0:T(8,128)} %collective-permute-done.2.refs_1_.refs_4_, f32[2,4,160,256]{3,2,1,0:T(8,128)} %collective-permute-done.4.refs_2_.refs_6_, ...), custom_call_target="tpu_custom_call" | custom-call | flops 4000000000 | bytes 1000 | tf_op jit(solution)/shard_map/pallas_call | solution.py:153
  163.9 2.6 %shard_map.96 = (f32[2,160,256]{2,1,0:T(8,128)}, f32[2,160,256]{2,1,0:T(8,128)}) custom-call(f32[2,4,160,256]{3,2,1,0:T(8,128)} %get-tuple-element.51.refs_0_.refs_9_, f32[2,4,160,256]{3,2,1,0:T(8,128)} %copy-done, f32[2,4,160,256]{3,2,1,0:T(8,128)} %collective-permute-done.7.refs_2_.refs_11_, f32[2,2,160,256]{3,2,1,0:T(8,128)} %copy-done.9, ...), custom_call_target="tpu_custom_call" | custom-call | flops 4000000000 | bytes 1000 | tf_op jit(solution)/shard_map/pallas_call | solution.py:153
  166.5 6.5 %collective-permute-done.16.refs_1_.refs_5_ = f32[2,4,160,256]{3,2,1,0:T(8,128)} collective-permute-done((f32[2,4,160,256]{3,2,1,0:T(8,128)}, f32[2,4,160,256]{3,2,1,0:T(8,128)}, u32[]{:S(2)}, u32[]{:S(2)}) %collective-permute-start.16) | collective-permute-done | bytes 1310752 | tf_op jit(solution)/shard_map/ppermute | solution.py:172
  176.0 4.0 %shard_map.97.refs_10_ = f32[4,320,256]{2,1,0:T(8,128)} custom-call(f32[4,4,320,256]{3,2,1,0:T(8,128)} %get-tuple-element.44.refs_4_.refs_0_.refs_2_.refs_6_.refs_3_, f32[2,4,160,256]{3,2,1,0:T(8,128)} %collective-permute-done.16.refs_1_.refs_5_, f32[2,4,160,256]{3,2,1,0:T(8,128)} %collective-permute-done.5.refs_5_.refs_2_, f32[4,160,256]{2,1,0:T(8,128)} %copy-done.3, ...), custom_call_target="tpu_custom_call" | custom-call | flops 4000000000 | bytes 1000 | tf_op jit(solution)/shard_map/pallas_call | solution.py:153
  182.1 2.8 %collective-permute-start.15 = (f32[2,160,256]{2,1,0:T(8,128)S(1)}, f32[2,160,256]{2,1,0:T(8,128)S(1)}, u32[]{:S(2)}, u32[]{:S(2)}) collective-permute-start(f32[2,160,256]{2,1,0:T(8,128)S(1)} %copy-done.13), channel_id=1, source_target_pairs={{0,3},{1,0},{2,1},{3,2},{4,7},{5,4},{6,5},{7,6},{8,11},{9,8},{10,9... | collective-permute-start | bytes 983048 | tf_op jit(solution)/shard_map/ppermute | solution.py:168
  185.0 6.4 %collective-permute-done.15.refs_9_ = f32[2,160,256]{2,1,0:T(8,128)S(1)} collective-permute-done((f32[2,160,256]{2,1,0:T(8,128)S(1)}, f32[2,160,256]{2,1,0:T(8,128)S(1)}, u32[]{:S(2)}, u32[]{:S(2)}) %collective-permute-start.15) | collective-permute-done | bytes 327712 | tf_op jit(solution)/shard_map/ppermute | solution.py:168
  191.3 4.4 %collective-permute-done.14.refs_4_ = f32[2,160,256]{2,1,0:T(8,128)S(1)} collective-permute-done((f32[2,160,256]{2,1,0:T(8,128)S(1)}, f32[2,160,256]{2,1,0:T(8,128)S(1)}, u32[]{:S(2)}, u32[]{:S(2)}) %collective-permute-start.14) | collective-permute-done | bytes 327712 | tf_op jit(solution)/shard_map/ppermute | solution.py:168
  196.5 2.8 %shard_map.98 = (f32[320,256]{1,0:T(8,128)}, f32[320,256]{1,0:T(8,128)}) custom-call(f32[2,4,160,256]{3,2,1,0:T(8,128)} %get-tuple-element.51.refs_0_.refs_9_, f32[2,4,160,256]{3,2,1,0:T(8,128)} %copy-done, f32[2,4,160,256]{3,2,1,0:T(8,128)} %collective-permute-done.7.refs_2_.refs_11_, f32[2,2,160,256]{3,2,1,0:T(8,128)} %copy-done.8, ...), custom_call_target="tpu_custom_call" | custom-call | flops 4000000000 | bytes 1000 | tf_op jit(solution)/shard_map/pallas_call | solution.py:153
  206.9 5.1 %collective-permute-done.21.refs_7_.refs_3_ = f32[320,256]{1,0:T(8,128)S(1)} collective-permute-done((f32[320,256]{1,0:T(8,128)S(1)}, f32[320,256]{1,0:T(8,128)S(1)}, u32[]{:S(2)}, u32[]{:S(2)}) %collective-permute-start.21) | collective-permute-done | bytes 327712 | tf_op jit(solution)/shard_map/ppermute | solution.py:172
  214.5 2.6 %shard_map.100 = (f32[384,256]{1,0:T(8,128)}, f32[384,256]{1,0:T(8,128)}) custom-call(f32[2,4,384,256]{3,2,1,0:T(8,128)} %bitcast.11, f32[2,2,192,256]{3,2,1,0:T(8,128)} %copy-done.7, f32[2,192,256]{2,1,0:T(8,128)} %copy-done.11, f32[2,4,384,256]{3,2,1,0:T(8,128)} %bitcast.12, f32[2,2,192,256]{3,2,1,0:T(8,128)} %collective-permute-done.11.refs_1_.refs_4_, ...), custom_call_target="tpu_custom_call" | custom-call | flops 4000000000 | bytes 1000 | tf_op jit(solution)/shard_map/pallas_call | solution.py:153
  218.7 6.4 %collective-permute-done.22.refs_1_ = f32[384,256]{1,0:T(8,128)S(1)} collective-permute-done((f32[384,256]{1,0:T(8,128)}, f32[384,256]{1,0:T(8,128)S(1)}, u32[]{:S(2)}, u32[]{:S(2)}) %collective-permute-start.22) | collective-permute-done | bytes 393248 | tf_op jit(solution)/shard_map/ppermute | solution.py:172
  225.8 2.7 %shard_map.101 = f32[1,256,1024]{2,1,0:T(8,128)} custom-call(f32[384,256]{1,0:T(8,128)} %get-tuple-element.69.refs_0_, f32[384,256]{1,0:T(8,128)} %copy-done.12, f32[320,256]{1,0:T(8,128)} %get-tuple-element.65.refs_4_.refs_2_, f32[320,256]{1,0:T(8,128)} %copy-done.15, f32[320,256]{1,0:T(8,128)} %bitcast.13), custom_call_target="tpu_custom_call" | custom-call | flops 4000000000 | bytes 1000 | tf_op jit(solution)/shard_map/pallas_call | solution.py:153
  (79 shorter events, 33.7 us)
Async XLA Ops:
  8.0 72.1 %all-reduce.2.cloned.1.call-start = ((), (), s32[]{:S(2)}) async-start(), calls=%async_computation.2 | async-start | bytes 2097152 | tf_op jit(solution)/shard_map/psum | solution.py:238
  12.6 147.7 %reduce-scatter.3.cloned.1.call-start = ((), (), s32[]{:S(2)}) async-start(), calls=%async_computation.3 | async-start | bytes 15728640 | tf_op jit(solution)/shard_map/reduce_scatter | solution.py:176
  30.9 194.1 %reduce-scatter.5.cloned.1.call-start = ((), (), s32[]{:S(2)}) async-start(), calls=%async_computation.4 | async-start | bytes 1638400 | tf_op jit(solution)/shard_map/reduce_scatter | solution.py:176
  35.9 36.8 %collective-permute-start.1 = (f32[2,4,160,256]{3,2,1,0:T(8,128)}, f32[2,4,160,256]{3,2,1,0:T(8,128)}, u32[]{:S(2)}, u32[]{:S(2)}) collective-permute-start(f32[2,4,160,256]{3,2,1,0:T(8,128)} %get-tuple-element.43), channel_id=1, source_target_pairs={{0,12},{1,13},{2,14},{3,15},{4,0},{5,1},{6,2},{7,3},{8,4},{9,5},{1... | collective-permute-start | bytes 3932168 | tf_op jit(solution)/shard_map/ppermute | solution.py:168
  39.0 33.7 %collective-permute-start = (f32[2,4,160,256]{3,2,1,0:T(8,128)}, f32[2,4,160,256]{3,2,1,0:T(8,128)}, u32[]{:S(2)}, u32[]{:S(2)}) collective-permute-start(f32[2,4,160,256]{3,2,1,0:T(8,128)} %get-tuple-element.39.refs_0_), channel_id=1, source_target_pairs={{0,4},{1,5},{2,6},{3,7},{4,8},{5,9},{6,10},{7,11},{8,12},{9,13},{1... | collective-permute-start | bytes 3932168 | tf_op jit(solution)/shard_map/ppermute | solution.py:168
  48.4 65.7 %collective-permute-start.3 = (f32[4,4,160,256]{3,2,1,0:T(8,128)}, f32[4,4,160,256]{3,2,1,0:T(8,128)}, u32[]{:S(2)}, u32[]{:S(2)}) collective-permute-start(f32[4,4,160,256]{3,2,1,0:T(8,128)} %get-tuple-element.40.refs_0_), channel_id=1, source_target_pairs={{0,16},{1,17},{2,18},{3,19},{4,20},{5,21},{6,22},{7,23},{8,24},{9,... | collective-permute-start | bytes 7864328 | tf_op jit(solution)/shard_map/ppermute | solution.py:172
  58.9 59.8 %collective-permute-start.6 = (f32[2,4,160,256]{3,2,1,0:T(8,128)}, f32[2,4,160,256]{3,2,1,0:T(8,128)S(1)}, u32[]{:S(2)}, u32[]{:S(2)}) collective-permute-start(f32[2,4,160,256]{3,2,1,0:T(8,128)} %get-tuple-element.52), channel_id=1, source_target_pairs={{0,12},{1,13},{2,14},{3,15},{4,0},{5,1},{6,2},{7,3},{8,4},{9,5},{1... | collective-permute-start | bytes 3932168 | tf_op jit(solution)/shard_map/ppermute | solution.py:168
  62.0 59.8 %collective-permute-start.8 = (f32[2,4,160,256]{3,2,1,0:T(8,128)}, f32[2,4,160,256]{3,2,1,0:T(8,128)}, u32[]{:S(2)}, u32[]{:S(2)}) collective-permute-start(f32[2,4,160,256]{3,2,1,0:T(8,128)} %get-tuple-element.54), channel_id=1, source_target_pairs={{0,4},{1,5},{2,6},{3,7},{4,8},{5,9},{6,10},{7,11},{8,12},{9,13},{1... | collective-permute-start | bytes 3932168 | tf_op jit(solution)/shard_map/ppermute | solution.py:168
  76.9 47.8 %collective-permute-start.9 = (f32[2,4,160,256]{3,2,1,0:T(8,128)}, f32[2,4,160,256]{3,2,1,0:T(8,128)S(1)}, u32[]{:S(2)}, u32[]{:S(2)}) collective-permute-start(f32[2,4,160,256]{3,2,1,0:T(8,128)} %get-tuple-element.55), channel_id=1, source_target_pairs={{0,12},{1,13},{2,14},{3,15},{4,0},{5,1},{6,2},{7,3},{8,4},{9,5},{1... | collective-permute-start | bytes 3932168 | tf_op jit(solution)/shard_map/ppermute | solution.py:168
  80.1 48.3 %collective-permute-start.7 = (f32[2,4,160,256]{3,2,1,0:T(8,128)}, f32[2,4,160,256]{3,2,1,0:T(8,128)}, u32[]{:S(2)}, u32[]{:S(2)}) collective-permute-start(f32[2,4,160,256]{3,2,1,0:T(8,128)} %get-tuple-element.45.refs_3_), channel_id=1, source_target_pairs={{0,4},{1,5},{2,6},{3,7},{4,8},{5,9},{6,10},{7,11},{8,12},{9,13},{1... | collective-permute-start | bytes 3932168 | tf_op jit(solution)/shard_map/ppermute | solution.py:168
  114.0 32.0 %collective-permute-start.2 = (f32[2,4,160,256]{3,2,1,0:T(8,128)}, f32[2,4,160,256]{3,2,1,0:T(8,128)}, u32[]{:S(2)}, u32[]{:S(2)}) collective-permute-start(f32[2,4,160,256]{3,2,1,0:T(8,128)} %get-tuple-element.48), channel_id=1, source_target_pairs={{0,16},{1,17},{2,18},{3,19},{4,20},{5,21},{6,22},{7,23},{8,24},{9,... | collective-permute-start | bytes 3932168 | tf_op jit(solution)/shard_map/ppermute | solution.py:172
  118.7 9.7 %copy-start = (f32[2,4,160,256]{3,2,1,0:T(8,128)}, f32[2,4,160,256]{3,2,1,0:T(8,128)S(1)}, u32[]{:S(2)}) copy-start(f32[2,4,160,256]{3,2,1,0:T(8,128)S(1)} %collective-permute-done.6.refs_1_.refs_10_) | copy-start | bytes 3932164
  118.7 32.9 %collective-permute-start.5 = (f32[2,4,160,256]{3,2,1,0:T(8,128)}, f32[2,4,160,256]{3,2,1,0:T(8,128)}, u32[]{:S(2)}, u32[]{:S(2)}) collective-permute-start(f32[2,4,160,256]{3,2,1,0:T(8,128)} %get-tuple-element.50), channel_id=1, source_target_pairs={{0,12},{1,13},{2,14},{3,15},{4,0},{5,1},{6,2},{7,3},{8,4},{9,5},{1... | collective-permute-start | bytes 3932168 | tf_op jit(solution)/shard_map/ppermute | solution.py:168
  121.8 33.2 %collective-permute-start.4 = (f32[2,4,160,256]{3,2,1,0:T(8,128)}, f32[2,4,160,256]{3,2,1,0:T(8,128)}, u32[]{:S(2)}, u32[]{:S(2)}) collective-permute-start(f32[2,4,160,256]{3,2,1,0:T(8,128)} %get-tuple-element.49.refs_12_), channel_id=1, source_target_pairs={{0,4},{1,5},{2,6},{3,7},{4,8},{5,9},{6,10},{7,11},{8,12},{9,13},{1... | collective-permute-start | bytes 3932168 | tf_op jit(solution)/shard_map/ppermute | solution.py:168
  124.7 48.3 %collective-permute-start.16 = (f32[2,4,160,256]{3,2,1,0:T(8,128)}, f32[2,4,160,256]{3,2,1,0:T(8,128)}, u32[]{:S(2)}, u32[]{:S(2)}) collective-permute-start(f32[2,4,160,256]{3,2,1,0:T(8,128)} %get-tuple-element.63), channel_id=1, source_target_pairs={{0,16},{1,17},{2,18},{3,19},{4,20},{5,21},{6,22},{7,23},{8,24},{9,... | collective-permute-start | bytes 3932168 | tf_op jit(solution)/shard_map/ppermute | solution.py:172
  131.7 31.1 %collective-permute-start.12 = (f32[2,2,160,256]{3,2,1,0:T(8,128)}, f32[2,2,160,256]{3,2,1,0:T(8,128)S(1)}, u32[]{:S(2)}, u32[]{:S(2)}) collective-permute-start(f32[2,2,160,256]{3,2,1,0:T(8,128)} %get-tuple-element.60), channel_id=1, source_target_pairs={{0,3},{1,0},{2,1},{3,2},{4,7},{5,4},{6,5},{7,6},{8,11},{9,8},{10,9... | collective-permute-start | bytes 1966088 | tf_op jit(solution)/shard_map/ppermute | solution.py:168
  146.0 16.8 %collective-permute-start.13 = (f32[2,2,160,256]{3,2,1,0:T(8,128)}, f32[2,2,160,256]{3,2,1,0:T(8,128)S(1)}, u32[]{:S(2)}, u32[]{:S(2)}) collective-permute-start(f32[2,2,160,256]{3,2,1,0:T(8,128)} %get-tuple-element.56.refs_6_), channel_id=1, source_target_pairs={{0,1},{1,2},{2,3},{3,0},{4,5},{5,6},{6,7},{7,4},{8,9},{9,10},{10,1... | collective-permute-start | bytes 1966088 | tf_op jit(solution)/shard_map/ppermute | solution.py:168
  158.2 15.4 %collective-permute-start.18 = (f32[4,160,256]{2,1,0:T(8,128)}, f32[4,160,256]{2,1,0:T(8,128)S(1)}, u32[]{:S(2)}, u32[]{:S(2)}) collective-permute-start(f32[4,160,256]{2,1,0:T(8,128)} %get-tuple-element.64), channel_id=1, source_target_pairs={{0,12},{1,13},{2,14},{3,15},{4,0},{5,1},{6,2},{7,3},{8,4},{9,5},{1... | collective-permute-start | bytes 1966088 | tf_op jit(solution)/shard_map/ppermute | solution.py:168
  158.5 16.7 %collective-permute-start.17 = (f32[4,160,256]{2,1,0:T(8,128)}, f32[4,160,256]{2,1,0:T(8,128)S(1)}, u32[]{:S(2)}, u32[]{:S(2)}) collective-permute-start(f32[4,160,256]{2,1,0:T(8,128)} %get-tuple-element.57.refs_4_), channel_id=1, source_target_pairs={{0,4},{1,5},{2,6},{3,7},{4,8},{5,9},{6,10},{7,11},{8,12},{9,13},{1... | collective-permute-start | bytes 1966088 | tf_op jit(solution)/shard_map/ppermute | solution.py:168
  176.0 4.0 %copy-start.6 = (f32[2,2,192,256]{3,2,1,0:T(8,128)S(1)}, f32[2,2,192,256]{3,2,1,0:T(8,128)}, u32[]{:S(2)}) copy-start(f32[2,2,192,256]{3,2,1,0:T(8,128)} %get-tuple-element.58) | copy-start | bytes 2359300
  176.0 6.1 %copy-start.13 = (f32[2,160,256]{2,1,0:T(8,128)S(1)}, f32[2,160,256]{2,1,0:T(8,128)}, u32[]{:S(2)}) copy-start(f32[2,160,256]{2,1,0:T(8,128)} %get-tuple-element.62) | copy-start | bytes 983044
  180.0 5.0 %copy-start.4 = (f32[2,160,256]{2,1,0:T(8,128)S(1)}, f32[2,160,256]{2,1,0:T(8,128)}, u32[]{:S(2)}) copy-start(f32[2,160,256]{2,1,0:T(8,128)} %get-tuple-element.61.refs_8_) | copy-start | bytes 983044
  180.0 19.3 %collective-permute-start.10 = (f32[2,2,192,256]{3,2,1,0:T(8,128)S(1)}, f32[2,2,192,256]{3,2,1,0:T(8,128)S(1)}, u32[]{:S(2)}, u32[]{:S(2)}) collective-permute-start(f32[2,2,192,256]{3,2,1,0:T(8,128)S(1)} %copy-done.6), channel_id=1, source_target_pairs={{0,12},{1,13},{2,14},{3,15},{4,0},{5,1},{6,2},{7,3},{8,4},{9,5},{1... | collective-permute-start | bytes 2359304 | tf_op jit(solution)/shard_map/ppermute | solution.py:168
  181.1 19.0 %collective-permute-start.11 = (f32[2,2,192,256]{3,2,1,0:T(8,128)S(1)}, f32[2,2,192,256]{3,2,1,0:T(8,128)}, u32[]{:S(2)}, u32[]{:S(2)}) collective-permute-start(f32[2,2,192,256]{3,2,1,0:T(8,128)S(1)} %copy-done.5), channel_id=1, source_target_pairs={{0,4},{1,5},{2,6},{3,7},{4,8},{5,9},{6,10},{7,11},{8,12},{9,13},{1... | collective-permute-start | bytes 2359304 | tf_op jit(solution)/shard_map/ppermute | solution.py:168
  182.1 9.2 %collective-permute-start.15 = (f32[2,160,256]{2,1,0:T(8,128)S(1)}, f32[2,160,256]{2,1,0:T(8,128)S(1)}, u32[]{:S(2)}, u32[]{:S(2)}) collective-permute-start(f32[2,160,256]{2,1,0:T(8,128)S(1)} %copy-done.13), channel_id=1, source_target_pairs={{0,3},{1,0},{2,1},{3,2},{4,7},{5,4},{6,5},{7,6},{8,11},{9,8},{10,9... | collective-permute-start | bytes 983048 | tf_op jit(solution)/shard_map/ppermute | solution.py:168
  185.0 10.8 %collective-permute-start.14 = (f32[2,160,256]{2,1,0:T(8,128)S(1)}, f32[2,160,256]{2,1,0:T(8,128)S(1)}, u32[]{:S(2)}, u32[]{:S(2)}) collective-permute-start(f32[2,160,256]{2,1,0:T(8,128)S(1)} %copy-done.4), channel_id=1, source_target_pairs={{0,1},{1,2},{2,3},{3,0},{4,5},{5,6},{6,7},{7,4},{8,9},{9,10},{10,1... | collective-permute-start | bytes 983048 | tf_op jit(solution)/shard_map/ppermute | solution.py:168
  191.3 4.4 %copy-start.16 = (f32[2,160,256]{2,1,0:T(8,128)}, f32[2,160,256]{2,1,0:T(8,128)S(1)}, u32[]{:S(2)}) copy-start(f32[2,160,256]{2,1,0:T(8,128)S(1)} %collective-permute-done.15.refs_9_) | copy-start | bytes 983044
  200.2 4.4 %copy-start.14 = (f32[320,256]{1,0:T(8,128)S(1)}, f32[320,256]{1,0:T(8,128)}, u32[]{:S(2)}) copy-start(f32[320,256]{1,0:T(8,128)} %get-tuple-element.68) | copy-start | bytes 983044
  202.5 9.5 %collective-permute-start.20 = (f32[2,192,256]{2,1,0:T(8,128)}, f32[2,192,256]{2,1,0:T(8,128)S(1)}, u32[]{:S(2)}, u32[]{:S(2)}) collective-permute-start(f32[2,192,256]{2,1,0:T(8,128)} %get-tuple-element.67), channel_id=1, source_target_pairs={{0,12},{1,13},{2,14},{3,15},{4,0},{5,1},{6,2},{7,3},{8,4},{9,5},{1... | collective-permute-start | bytes 1179656 | tf_op jit(solution)/shard_map/ppermute | solution.py:168
  204.3 9.4 %collective-permute-start.19 = (f32[2,192,256]{2,1,0:T(8,128)}, f32[2,192,256]{2,1,0:T(8,128)S(1)}, u32[]{:S(2)}, u32[]{:S(2)}) collective-permute-start(f32[2,192,256]{2,1,0:T(8,128)} %get-tuple-element.66.refs_6_), channel_id=1, source_target_pairs={{0,4},{1,5},{2,6},{3,7},{4,8},{5,9},{6,10},{7,11},{8,12},{9,13},{1... | collective-permute-start | bytes 1179656 | tf_op jit(solution)/shard_map/ppermute | solution.py:168
  204.6 7.4 %collective-permute-start.21 = (f32[320,256]{1,0:T(8,128)S(1)}, f32[320,256]{1,0:T(8,128)S(1)}, u32[]{:S(2)}, u32[]{:S(2)}) collective-permute-start(f32[320,256]{1,0:T(8,128)S(1)} %copy-done.14), channel_id=1, source_target_pairs={{0,16},{1,17},{2,18},{3,19},{4,20},{5,21},{6,22},{7,23},{8,24},{9,... | collective-permute-start | bytes 983048 | tf_op jit(solution)/shard_map/ppermute | solution.py:172
  217.1 8.0 %collective-permute-start.22 = (f32[384,256]{1,0:T(8,128)}, f32[384,256]{1,0:T(8,128)S(1)}, u32[]{:S(2)}, u32[]{:S(2)}) collective-permute-start(f32[384,256]{1,0:T(8,128)} %get-tuple-element.70), channel_id=1, source_target_pairs={{0,16},{1,17},{2,18},{3,19},{4,20},{5,21},{6,22},{7,23},{8,24},{9,... | collective-permute-start | bytes 1179656 | tf_op jit(solution)/shard_map/ppermute | solution.py:172
  (12 other events, 15.9 us)
Sparse Core Ops, SparseCore 0:
  12.7 51.5 all-reduce.1
Sparse Core Ops, SparseCore 1:
  31.0 128.1 reduce-scatter.2
  180.1 25.7 reduce-scatter.4

commit v10 on v6

--- a/solution.py
+++ b/solution.py
@@ -231,7 +231,7 @@
     table = 4 * ((me // 16 + at // 4) % 2) + (me // 4 + at) % 4
     table = jnp.where(at == STRIPS, me % 4, table).astype(jnp.int32)
 
-    picked = jnp.sum(jnp.where(jnp.arange(groups) == group, exps, 0))
+    picked = lax.dynamic_index_in_dim(exps, group, keepdims=False)
     scale_up = jnp.left_shift(1, picked).astype(jnp.float32)
     delta = params - local_params[0].astype(jnp.float32)
     coded = jnp.clip(delta * scale_up, -448.0, 448.0).astype(jnp.bfloat16)

time: 235 us -> 235 us (level)
  no operation moved by 1% of the time
where the time goes in v10:
time: 235 us; the launch traced here: 234 us
  Pallas kernels  92.4 us (39%)
  waiting for transfers between devices  70.9 us (30%)
  starting transfers between devices  40.8 us (17%)
  between operations  16.2 us (7%)
  local copies, waits for them, and re-layouts  10.4 us (4%)
  other arithmetic  3.07 us (1%)
    ppermute x5, waiting for transfers between devices, along_z(): return lax.ppermute(array, 'fsdp', [(f, (f + 16) % 32) for f in range(32)])  53.7 us
    pallas_call x14, Pallas kernels, combine(): pl.pallas_call(kernel, grid=(1,), in_specs=[pl.BlockSpec(block, lambda i,...  41.1 us
    ppermute x22, starting transfers between devices, along(): return lax.ppermute(array, 'fsdp', pairs)  32.3 us
    pallas_call x3, Pallas kernels, products(): pl.pallas_call(body, grid_spec=pltpu.PrefetchScalarGridSpec(num_scalar_pr...  24.3 us
    pallas_call x1, Pallas kernels, all_products(): pl.pallas_call(body, grid_spec=pltpu.PrefetchScalarGridSpec(num_scalar_pr...  17.7 us
    ppermute x22, waiting for transfers between devices, along(): return lax.ppermute(array, 'fsdp', pairs)  17.1 us
    pallas_call x1, Pallas kernels, crossing_products(): pl.pallas_call(body, grid_spec=pltpu.PrefetchScalarGridSpec(num_scalar_pr...  9.28 us
    unnamed x34, local copies, waits for them, and re-layouts  9.14 us
  transfers between devices with their start and end apart: 29, of which 13 were waited for; matrix products, arithmetic and copies ran while one was open for 0% of the time, Pallas kernels for 37%

profile of v10, /device:TPU:0, one launch (start us, length us, event | category | flops | bytes accessed | tf_op | source)
XLA Modules:
  0.0 233.7 jit_solution(12079995397075009825)
XLA Ops:
  9.9 2.5 %convert_divide_fusion = f32[256,1024]{1,0:T(8,128)} fusion(f32[256,1024]{1,0:T(8,128)} %refs_0_.1, bf16[1,256,1024]{2,1,0:T(8,128)(2,1)} %param.8, f32[]{:T(128)} %bitcast.1), kind=kLoop, calls=%fused_computation.4 | loop fusion | flops 1835008 | bytes 2621444 | tf_op jit(solution)/shard_map/div | solution.py:238
  13.1 17.7 %shard_map.85 = (f32[4,8,384,256]{3,2,1,0:T(8,128)}, bf16[1024,1024]{1,0:T(8,128)(2,1)S(1)}) custom-call(s32[9]{0:T(128)} %compare_select_fusion.4.table, bf16[1024,8192]{1,0:T(8,128)(2,1)} %x.9, bf16[1024,1024]{1,0:T(8,128)(2,1)} %k.1), custom_call_target="tpu_custom_call" | custom-call | flops 20000000000 | bytes 1000 | tf_op jit(solution)/shard_map/pallas_call | solution.py:35
  30.9 4.9 %shard_map.86 = (f32[2,4,160,256]{3,2,1,0:T(8,128)}, f32[2,4,160,256]{3,2,1,0:T(8,128)}) custom-call(s32[9]{0:T(128)} %compare_select_fusion.4.table, bf16[1024,8192]{1,0:T(8,128)(2,1)} %x.9, bf16[1024,1024]{1,0:T(8,128)(2,1)S(1)} %get-tuple-element.41.k, f32[4,8,384,256]{3,2,1,0:T(8,128)} %get-tuple-element.42.refs_0_), custom_call_target="tpu_custom_call" | custom-call | flops 20000000000 | bytes 1000 | tf_op jit(solution)/shard_map/pallas_call | solution.py:129
  35.8 3.1 %collective-permute-start.1 = (f32[2,4,160,256]{3,2,1,0:T(8,128)}, f32[2,4,160,256]{3,2,1,0:T(8,128)}, u32[]{:S(2)}, u32[]{:S(2)}) collective-permute-start(f32[2,4,160,256]{3,2,1,0:T(8,128)} %get-tuple-element.47), channel_id=1, source_target_pairs={{0,12},{1,13},{2,14},{3,15},{4,0},{5,1},{6,2},{7,3},{8,4},{9,5},{1... | collective-permute-start | bytes 3932168 | tf_op jit(solution)/shard_map/ppermute | solution.py:168
  38.9 9.3 %shard_map.87 = (f32[4,4,160,256]{3,2,1,0:T(8,128)}, f32[2,4,160,256]{3,2,1,0:T(8,128)}, f32[2,4,160,256]{3,2,1,0:T(8,128)}) custom-call(s32[9]{0:T(128)} %compare_select_fusion.4.table, bf16[1024,8192]{1,0:T(8,128)(2,1)} %x.9, bf16[1024,1024]{1,0:T(8,128)(2,1)S(1)} %get-tuple-element.41.k, f32[2,4,160,256]{3,2,1,0:T(8,128)} %get-tuple-element.43.refs_0_), custom_call_target="tpu_custom_call" | custom-call | flops 20000000000 | bytes 1000 | tf_op jit(solution)/shard_map/pallas_call | solution.py:79
  50.1 8.7 %shard_map.88 = (f32[2,4,160,256]{3,2,1,0:T(8,128)}, f32[2,4,160,256]{3,2,1,0:T(8,128)}, f32[2,4,160,256]{3,2,1,0:T(8,128)}, f32[2,4,160,256]{3,2,1,0:T(8,128)}) custom-call(s32[9]{0:T(128)} %compare_select_fusion.4.table, bf16[1024,8192]{1,0:T(8,128)(2,1)} %x.9, bf16[1024,1024]{1,0:T(8,128)(2,1)S(1)} %get-tuple-element.41.k, ...), custom_call_target="tpu_custom_call" | custom-call | flops 20000000000 | bytes 1000 | tf_op jit(solution)/shard_map/pallas_call | solution.py:129
  58.7 3.1 %collective-permute-start.6 = (f32[2,4,160,256]{3,2,1,0:T(8,128)}, f32[2,4,160,256]{3,2,1,0:T(8,128)S(1)}, u32[]{:S(2)}, u32[]{:S(2)}) collective-permute-start(f32[2,4,160,256]{3,2,1,0:T(8,128)} %get-tuple-element.56), channel_id=1, source_target_pairs={{0,12},{1,13},{2,14},{3,15},{4,0},{5,1},{6,2},{7,3},{8,4},{9,5},{1... | collective-permute-start | bytes 3932168 | tf_op jit(solution)/shard_map/ppermute | solution.py:168
  61.8 10.7 %shard_map.89 = (f32[2,4,160,256]{3,2,1,0:T(8,128)}, f32[2,4,160,256]{3,2,1,0:T(8,128)}, f32[4,4,320,256]{3,2,1,0:T(8,128)}) custom-call(s32[9]{0:T(128)} %compare_select_fusion.4.table, bf16[1024,8192]{1,0:T(8,128)(2,1)} %x.9, bf16[1024,1024]{1,0:T(8,128)(2,1)S(1)} %get-tuple-element.41.k, f32[2,4,160,256]{3,2,1,0:T(8,128)} %get-tuple-element.45.refs_0_), custom_call_target="tpu_custom_call" | custom-call | flops 20000000000 | bytes 1000 | tf_op jit(solution)/shard_map/pallas_call | solution.py:129
  72.5 4.1 %shard_map.90 = (f32[2,4,160,256]{3,2,1,0:T(8,128)}, f32[2,4,160,256]{3,2,1,0:T(8,128)}) custom-call(f32[2,4,160,256]{3,2,1,0:T(8,128)} %get-tuple-element.45.refs_0_, f32[2,4,160,256]{3,2,1,0:T(8,128)} %get-tuple-element.46.refs_1_, f32[2,4,160,256]{3,2,1,0:T(8,128)} %collective-permute-done.refs_2_, f32[2,4,160,256]{3,2,1,0:T(8,128)} %collective-permute-done.1.refs_3_, ...), custom_call_target="tpu_custom_call" | custom-call | flops 4000000000 | bytes 1000 | tf_op jit(solution)/shard_map/pallas_call | solution.py:153
  76.7 3.3 %collective-permute-start.9 = (f32[2,4,160,256]{3,2,1,0:T(8,128)}, f32[2,4,160,256]{3,2,1,0:T(8,128)S(1)}, u32[]{:S(2)}, u32[]{:S(2)}) collective-permute-start(f32[2,4,160,256]{3,2,1,0:T(8,128)} %get-tuple-element.59), channel_id=1, source_target_pairs={{0,12},{1,13},{2,14},{3,15},{4,0},{5,1},{6,2},{7,3},{8,4},{9,5},{1... | collective-permute-start | bytes 3932168 | tf_op jit(solution)/shard_map/ppermute | solution.py:168
  79.9 3.4 %shard_map.91 = (f32[256,1024]{1,0:T(8,128)}, f32[256,1024]{1,0:T(8,128)}) custom-call(f32[256,1024]{1,0:T(8,128)} %refs_0_.1, f32[256,1024]{1,0:T(8,128)} %refs_1_.1, f32[256,1024]{1,0:T(8,128)} %all-reduce.2.cloned.1.call-done.refs_2_, f32[2,4,160,256]{3,2,1,0:T(8,128)} %get-tuple-element.49.refs_3_), custom_call_target="tpu_custom_call" | custom-call | flops 4000000000 | bytes 1000 | tf_op jit(solution)/shard_map/pallas_call | solution.py:153
  83.3 30.6 %collective-permute-done.3.refs_1_.refs_3_.refs_5_.refs_7_ = f32[4,4,160,256]{3,2,1,0:T(8,128)} collective-permute-done((f32[4,4,160,256]{3,2,1,0:T(8,128)}, f32[4,4,160,256]{3,2,1,0:T(8,128)}, u32[]{:S(2)}, u32[]{:S(2)}) %collective-permute-start.3) | collective-permute-done | bytes 2621472 | tf_op jit(solution)/shard_map/ppermute | solution.py:172
  114.4 4.2 %shard_map.92 = (f32[2,4,160,256]{3,2,1,0:T(8,128)}, f32[2,4,160,256]{3,2,1,0:T(8,128)}) custom-call(f32[4,4,320,256]{3,2,1,0:T(8,128)} %get-tuple-element.48.refs_4_.refs_0_.refs_2_.refs_6_.refs_3_.refs_8_.refs_12_.refs_5_, f32[4,4,160,256]{3,2,1,0:T(8,128)} %collective-permute-done.3.refs_1_.refs_3_.refs_5_.refs_7_, ...), custom_call_target="tpu_custom_call" | custom-call | flops 4000000000 | bytes 1000 | tf_op jit(solution)/shard_map/pallas_call | solution.py:153
  119.8 2.9 %collective-permute-start.5 = (f32[2,4,160,256]{3,2,1,0:T(8,128)}, f32[2,4,160,256]{3,2,1,0:T(8,128)S(1)}, u32[]{:S(2)}, u32[]{:S(2)}) collective-permute-start(f32[2,4,160,256]{3,2,1,0:T(8,128)} %get-tuple-element.54), channel_id=1, source_target_pairs={{0,12},{1,13},{2,14},{3,15},{4,0},{5,1},{6,2},{7,3},{8,4},{9,5},{1... | collective-permute-start | bytes 3932168 | tf_op jit(solution)/shard_map/ppermute | solution.py:168
  127.9 3.2 %shard_map.93 = (f32[2,2,160,256]{3,2,1,0:T(8,128)}, f32[2,2,160,256]{3,2,1,0:T(8,128)}) custom-call(f32[2,4,160,256]{3,2,1,0:T(8,128)} %get-tuple-element.55.refs_0_.refs_9_, f32[2,4,160,256]{3,2,1,0:T(8,128)} %copy-done.4, f32[2,4,160,256]{3,2,1,0:T(8,128)} %collective-permute-done.7.refs_2_.refs_11_, ...), custom_call_target="tpu_custom_call" | custom-call | flops 4000000000 | bytes 1000 | tf_op jit(solution)/shard_map/pallas_call | solution.py:153
  131.1 2.7 %collective-permute-start.16 = (f32[2,2,160,256]{3,2,1,0:T(8,128)}, f32[2,2,160,256]{3,2,1,0:T(8,128)S(1)}, u32[]{:S(2)}, u32[]{:S(2)}) collective-permute-start(f32[2,2,160,256]{3,2,1,0:T(8,128)} %get-tuple-element.66), channel_id=1, source_target_pairs={{0,3},{1,0},{2,1},{3,2},{4,7},{5,4},{6,5},{7,6},{8,11},{9,8},{10,9... | collective-permute-start | bytes 1966088 | tf_op jit(solution)/shard_map/ppermute | solution.py:168
  133.9 12.1 %collective-permute-done.2.refs_1_.refs_4_ = f32[2,4,160,256]{3,2,1,0:T(8,128)} collective-permute-done((f32[2,4,160,256]{3,2,1,0:T(8,128)}, f32[2,4,160,256]{3,2,1,0:T(8,128)}, u32[]{:S(2)}, u32[]{:S(2)}) %collective-permute-start.2) | collective-permute-done | bytes 1310752 | tf_op jit(solution)/shard_map/ppermute | solution.py:172
  147.4 4.1 %collective-permute-done.5.refs_5_.refs_2_.refs_14_ = f32[2,4,160,256]{3,2,1,0:T(8,128)S(1)} collective-permute-done((f32[2,4,160,256]{3,2,1,0:T(8,128)}, f32[2,4,160,256]{3,2,1,0:T(8,128)S(1)}, u32[]{:S(2)}, u32[]{:S(2)}) %collective-permute-start.5) | collective-permute-done | bytes 1310752 | tf_op jit(solution)/shard_map/ppermute | solution.py:168
  151.5 3.4 %collective-permute-done.4.refs_2_.refs_6_.refs_10_.refs_7_.refs_8_ = f32[2,4,160,256]{3,2,1,0:T(8,128)} collective-permute-done((f32[2,4,160,256]{3,2,1,0:T(8,128)}, f32[2,4,160,256]{3,2,1,0:T(8,128)}, u32[]{:S(2)}, u32[]{:S(2)}) %collective-permute-start.4) | collective-permute-done | bytes 1310752 | tf_op jit(solution)/shard_map/ppermute | solution.py:168
  154.9 3.2 %shard_map.94 = (f32[4,160,256]{2,1,0:T(8,128)}, f32[4,160,256]{2,1,0:T(8,128)}) custom-call(f32[4,4,320,256]{3,2,1,0:T(8,128)} %get-tuple-element.48.refs_4_.refs_0_.refs_2_.refs_6_.refs_3_.refs_8_.refs_12_.refs_5_, f32[2,4,160,256]{3,2,1,0:T(8,128)} %collective-permute-done.2.refs_1_.refs_4_, ...), custom_call_target="tpu_custom_call" | custom-call | flops 4000000000 | bytes 1000 | tf_op jit(solution)/shard_map/pallas_call | solution.py:153
  160.2 2.6 %shard_map.95 = (f32[2,2,192,256]{3,2,1,0:T(8,128)}, f32[2,2,192,256]{3,2,1,0:T(8,128)}) custom-call(f32[2,4,384,256]{3,2,1,0:T(8,128)} %bitcast.5, f32[2,4,384,256]{3,2,1,0:T(8,128)} %bitcast.6, f32[2,4,384,256]{3,2,1,0:T(8,128)} %bitcast.7, f32[2,4,384,256]{3,2,1,0:T(8,128)} %bitcast.8, f32[4,160,256]{2,1,0:T(8,128)} %get-tuple-element.61.refs_4_), custom_call_target="tpu_custom_call" | custom-call | flops 4000000000 | bytes 1000 | tf_op jit(solution)/shard_map/pallas_call | solution.py:153
  164.8 2.6 %shard_map.96 = (f32[2,160,256]{2,1,0:T(8,128)}, f32[2,160,256]{2,1,0:T(8,128)}) custom-call(f32[2,4,160,256]{3,2,1,0:T(8,128)} %get-tuple-element.55.refs_0_.refs_9_, f32[2,4,160,256]{3,2,1,0:T(8,128)} %copy-done.4, f32[2,4,160,256]{3,2,1,0:T(8,128)} %collective-permute-done.7.refs_2_.refs_11_, f32[2,2,160,256]{3,2,1,0:T(8,128)} %collective-permute-done.15.refs_3_.refs_8_, ...), custom_call_target="tpu_custom_call" | custom-call | flops 4000000000 | bytes 1000 | tf_op jit(solution)/shard_map/pallas_call | solution.py:153
  169.0 3.6 %collective-permute-done.12.refs_1_.refs_5_.refs_9_.refs_13_.refs_6_.refs_7_ = f32[2,4,160,256]{3,2,1,0:T(8,128)S(1)} collective-permute-done((f32[2,4,160,256]{3,2,1,0:T(8,128)}, f32[2,4,160,256]{3,2,1,0:T(8,128)S(1)}, u32[]{:S(2)}, u32[]{:S(2)}) %collective-permute-start.12) | collective-permute-done | bytes 1310752 | tf_op jit(solution)/shard_map/ppermute | solution.py:172
  174.1 2.8 %collective-permute-start.10 = (f32[2,2,192,256]{3,2,1,0:T(8,128)}, f32[2,2,192,256]{3,2,1,0:T(8,128)}, u32[]{:S(2)}, u32[]{:S(2)}) collective-permute-start(f32[2,2,192,256]{3,2,1,0:T(8,128)} %get-tuple-element.62), channel_id=1, source_target_pairs={{0,12},{1,13},{2,14},{3,15},{4,0},{5,1},{6,2},{7,3},{8,4},{9,5},{1... | collective-permute-start | bytes 2359304 | tf_op jit(solution)/shard_map/ppermute | solution.py:168
  179.3 2.7 %shard_map.97 = (f32[2,1,160,256]{3,2,1,0:T(8,128)}, f32[2,1,160,256]{3,2,1,0:T(8,128)}) custom-call(f32[4,4,320,256]{3,2,1,0:T(8,128)} %get-tuple-element.48.refs_4_.refs_0_.refs_2_.refs_6_.refs_3_.refs_8_.refs_12_.refs_5_, f32[2,4,160,256]{3,2,1,0:T(8,128)} %copy-done, f32[2,4,160,256]{3,2,1,0:T(8,128)} %copy-done.1, f32[4,160,256]{2,1,0:T(8,128)} %copy-done.3, ...), custom_call_target="tpu_custom_call" | custom-call | flops 4000000000 | bytes 1000 | tf_op jit(solution)/shard_map/pallas_call | solution.py:153
  182.0 2.7 %collective-permute-start.18 = (f32[2,1,160,256]{3,2,1,0:T(8,128)}, f32[2,1,160,256]{3,2,1,0:T(8,128)S(1)}, u32[]{:S(2)}, u32[]{:S(2)}) collective-permute-start(f32[2,1,160,256]{3,2,1,0:T(8,128)} %get-tuple-element.69), channel_id=1, source_target_pairs={{0,3},{1,0},{2,1},{3,2},{4,7},{5,4},{6,5},{7,6},{8,11},{9,8},{10,9... | collective-permute-start | bytes 983048 | tf_op jit(solution)/shard_map/ppermute | solution.py:168
  184.8 2.8 %shard_map.98 = (f32[320,256]{1,0:T(8,128)}, f32[320,256]{1,0:T(8,128)}) custom-call(f32[2,4,160,256]{3,2,1,0:T(8,128)} %get-tuple-element.55.refs_0_.refs_9_, f32[2,4,160,256]{3,2,1,0:T(8,128)} %copy-done.4, f32[2,4,160,256]{3,2,1,0:T(8,128)} %collective-permute-done.7.refs_2_.refs_11_, f32[2,2,160,256]{3,2,1,0:T(8,128)} %copy-done.11, ...), custom_call_target="tpu_custom_call" | custom-call | flops 4000000000 | bytes 1000 | tf_op jit(solution)/shard_map/pallas_call | solution.py:153
  189.7 3.6 %collective-permute-done.17.refs_4_.refs_10_ = f32[2,1,160,256]{3,2,1,0:T(8,128)S(1)} collective-permute-done((f32[2,1,160,256]{3,2,1,0:T(8,128)}, f32[2,1,160,256]{3,2,1,0:T(8,128)S(1)}, u32[]{:S(2)}, u32[]{:S(2)}) %collective-permute-start.17) | collective-permute-done | bytes 327712 | tf_op jit(solution)/shard_map/ppermute | solution.py:168
  206.9 2.4 %shard_map.101.refs_6_.refs_4_ = f32[320,256]{1,0:T(8,128)} custom-call(f32[4,4,320,256]{3,2,1,0:T(8,128)} %get-tuple-element.48.refs_4_.refs_0_.refs_2_.refs_6_.refs_3_.refs_8_.refs_12_.refs_5_, f32[2,4,160,256]{3,2,1,0:T(8,128)} %copy-done, f32[2,4,160,256]{3,2,1,0:T(8,128)} %copy-done.1, f32[4,160,256]{2,1,0:T(8,128)} %copy-done.3, ...), custom_call_target="tpu_custom_call" | custom-call | flops 4000000000 | bytes 1000 | tf_op jit(solution)/shard_map/pallas_call | solution.py:153
  212.2 2.5 %shard_map.102 = (f32[384,256]{1,0:T(8,128)}, f32[384,256]{1,0:T(8,128)}) custom-call(f32[2,4,384,256]{3,2,1,0:T(8,128)} %bitcast.11, f32[2,2,192,256]{3,2,1,0:T(8,128)} %collective-permute-done.10.refs_3_.refs_1_, f32[2,192,256]{2,1,0:T(8,128)} %copy-done.13, f32[2,4,384,256]{3,2,1,0:T(8,128)} %bitcast.12, f32[2,2,192,256]{3,2,1,0:T(8,128)} %copy-done.10, ...), custom_call_target="tpu_custom_call" | custom-call | flops 4000000000 | bytes 1000 | tf_op jit(solution)/shard_map/pallas_call | solution.py:153
  216.8 6.0 %collective-permute-done.26.refs_1_ = f32[384,256]{1,0:T(8,128)S(1)} collective-permute-done((f32[384,256]{1,0:T(8,128)}, f32[384,256]{1,0:T(8,128)S(1)}, u32[]{:S(2)}, u32[]{:S(2)}) %collective-permute-start.26) | collective-permute-done | bytes 393248 | tf_op jit(solution)/shard_map/ppermute | solution.py:172
  223.5 2.7 %shard_map.103 = f32[1,256,1024]{2,1,0:T(8,128)} custom-call(f32[384,256]{1,0:T(8,128)} %get-tuple-element.77.refs_0_, f32[384,256]{1,0:T(8,128)} %copy-done.14, f32[320,256]{1,0:T(8,128)} %get-tuple-element.71.refs_10_.refs_2_, f32[320,256]{1,0:T(8,128)} %copy-done.16, f32[320,256]{1,0:T(8,128)} %shard_map.101.refs_6_.refs_4_), custom_call_target="tpu_custom_call" | custom-call | flops 4000000000 | bytes 1000 | tf_op jit(solution)/shard_map/pallas_call | solution.py:153
  (84 shorter events, 43.2 us)
Async XLA Ops:
  8.0 71.9 %all-reduce.2.cloned.1.call-start = ((), (), s32[]{:S(2)}) async-start(), calls=%async_computation.1 | async-start | bytes 2097152 | tf_op jit(solution)/shard_map/psum | solution.py:238
  12.5 147.7 %reduce-scatter.2.cloned.1.call-start = ((), (), s32[]{:S(2)}) async-start(), calls=%async_computation.2 | async-start | bytes 15728640 | tf_op jit(solution)/shard_map/reduce_scatter | solution.py:176
  35.8 36.7 %collective-permute-start.1 = (f32[2,4,160,256]{3,2,1,0:T(8,128)}, f32[2,4,160,256]{3,2,1,0:T(8,128)}, u32[]{:S(2)}, u32[]{:S(2)}) collective-permute-start(f32[2,4,160,256]{3,2,1,0:T(8,128)} %get-tuple-element.47), channel_id=1, source_target_pairs={{0,12},{1,13},{2,14},{3,15},{4,0},{5,1},{6,2},{7,3},{8,4},{9,5},{1... | collective-permute-start | bytes 3932168 | tf_op jit(solution)/shard_map/ppermute | solution.py:168
  38.9 33.6 %collective-permute-start = (f32[2,4,160,256]{3,2,1,0:T(8,128)}, f32[2,4,160,256]{3,2,1,0:T(8,128)}, u32[]{:S(2)}, u32[]{:S(2)}) collective-permute-start(f32[2,4,160,256]{3,2,1,0:T(8,128)} %get-tuple-element.43.refs_0_), channel_id=1, source_target_pairs={{0,4},{1,5},{2,6},{3,7},{4,8},{5,9},{6,10},{7,11},{8,12},{9,13},{1... | collective-permute-start | bytes 3932168 | tf_op jit(solution)/shard_map/ppermute | solution.py:168
  48.2 65.8 %collective-permute-start.3 = (f32[4,4,160,256]{3,2,1,0:T(8,128)}, f32[4,4,160,256]{3,2,1,0:T(8,128)}, u32[]{:S(2)}, u32[]{:S(2)}) collective-permute-start(f32[4,4,160,256]{3,2,1,0:T(8,128)} %get-tuple-element.44.refs_0_), channel_id=1, source_target_pairs={{0,16},{1,17},{2,18},{3,19},{4,20},{5,21},{6,22},{7,23},{8,24},{9,... | collective-permute-start | bytes 7864328 | tf_op jit(solution)/shard_map/ppermute | solution.py:172
  58.7 59.9 %collective-permute-start.6 = (f32[2,4,160,256]{3,2,1,0:T(8,128)}, f32[2,4,160,256]{3,2,1,0:T(8,128)S(1)}, u32[]{:S(2)}, u32[]{:S(2)}) collective-permute-start(f32[2,4,160,256]{3,2,1,0:T(8,128)} %get-tuple-element.56), channel_id=1, source_target_pairs={{0,12},{1,13},{2,14},{3,15},{4,0},{5,1},{6,2},{7,3},{8,4},{9,5},{1... | collective-permute-start | bytes 3932168 | tf_op jit(solution)/shard_map/ppermute | solution.py:168
  61.8 60.8 %collective-permute-start.8 = (f32[2,4,160,256]{3,2,1,0:T(8,128)}, f32[2,4,160,256]{3,2,1,0:T(8,128)}, u32[]{:S(2)}, u32[]{:S(2)}) collective-permute-start(f32[2,4,160,256]{3,2,1,0:T(8,128)} %get-tuple-element.58), channel_id=1, source_target_pairs={{0,4},{1,5},{2,6},{3,7},{4,8},{5,9},{6,10},{7,11},{8,12},{9,13},{1... | collective-permute-start | bytes 3932168 | tf_op jit(solution)/shard_map/ppermute | solution.py:168
  76.7 47.9 %collective-permute-start.9 = (f32[2,4,160,256]{3,2,1,0:T(8,128)}, f32[2,4,160,256]{3,2,1,0:T(8,128)S(1)}, u32[]{:S(2)}, u32[]{:S(2)}) collective-permute-start(f32[2,4,160,256]{3,2,1,0:T(8,128)} %get-tuple-element.59), channel_id=1, source_target_pairs={{0,12},{1,13},{2,14},{3,15},{4,0},{5,1},{6,2},{7,3},{8,4},{9,5},{1... | collective-permute-start | bytes 3932168 | tf_op jit(solution)/shard_map/ppermute | solution.py:168
  79.9 48.0 %collective-permute-start.7 = (f32[2,4,160,256]{3,2,1,0:T(8,128)}, f32[2,4,160,256]{3,2,1,0:T(8,128)}, u32[]{:S(2)}, u32[]{:S(2)}) collective-permute-start(f32[2,4,160,256]{3,2,1,0:T(8,128)} %get-tuple-element.49.refs_3_), channel_id=1, source_target_pairs={{0,4},{1,5},{2,6},{3,7},{4,8},{5,9},{6,10},{7,11},{8,12},{9,13},{1... | collective-permute-start | bytes 3932168 | tf_op jit(solution)/shard_map/ppermute | solution.py:168
  113.9 32.0 %collective-permute-start.2 = (f32[2,4,160,256]{3,2,1,0:T(8,128)}, f32[2,4,160,256]{3,2,1,0:T(8,128)}, u32[]{:S(2)}, u32[]{:S(2)}) collective-permute-start(f32[2,4,160,256]{3,2,1,0:T(8,128)} %get-tuple-element.52), channel_id=1, source_target_pairs={{0,16},{1,17},{2,18},{3,19},{4,20},{5,21},{6,22},{7,23},{8,24},{9,... | collective-permute-start | bytes 3932168 | tf_op jit(solution)/shard_map/ppermute | solution.py:172
  119.8 31.7 %collective-permute-start.5 = (f32[2,4,160,256]{3,2,1,0:T(8,128)}, f32[2,4,160,256]{3,2,1,0:T(8,128)S(1)}, u32[]{:S(2)}, u32[]{:S(2)}) collective-permute-start(f32[2,4,160,256]{3,2,1,0:T(8,128)} %get-tuple-element.54), channel_id=1, source_target_pairs={{0,12},{1,13},{2,14},{3,15},{4,0},{5,1},{6,2},{7,3},{8,4},{9,5},{1... | collective-permute-start | bytes 3932168 | tf_op jit(solution)/shard_map/ppermute | solution.py:168
  122.6 32.3 %collective-permute-start.4 = (f32[2,4,160,256]{3,2,1,0:T(8,128)}, f32[2,4,160,256]{3,2,1,0:T(8,128)}, u32[]{:S(2)}, u32[]{:S(2)}) collective-permute-start(f32[2,4,160,256]{3,2,1,0:T(8,128)} %get-tuple-element.53.refs_12_), channel_id=1, source_target_pairs={{0,4},{1,5},{2,6},{3,7},{4,8},{5,9},{6,10},{7,11},{8,12},{9,13},{1... | collective-permute-start | bytes 3932168 | tf_op jit(solution)/shard_map/ppermute | solution.py:168
  125.6 47.0 %collective-permute-start.12 = (f32[2,4,160,256]{3,2,1,0:T(8,128)}, f32[2,4,160,256]{3,2,1,0:T(8,128)S(1)}, u32[]{:S(2)}, u32[]{:S(2)}) collective-permute-start(f32[2,4,160,256]{3,2,1,0:T(8,128)} %get-tuple-element.64), channel_id=1, source_target_pairs={{0,16},{1,17},{2,18},{3,19},{4,20},{5,21},{6,22},{7,23},{8,24},{9,... | collective-permute-start | bytes 3932168 | tf_op jit(solution)/shard_map/ppermute | solution.py:172
  131.1 31.6 %collective-permute-start.16 = (f32[2,2,160,256]{3,2,1,0:T(8,128)}, f32[2,2,160,256]{3,2,1,0:T(8,128)S(1)}, u32[]{:S(2)}, u32[]{:S(2)}) collective-permute-start(f32[2,2,160,256]{3,2,1,0:T(8,128)} %get-tuple-element.66), channel_id=1, source_target_pairs={{0,3},{1,0},{2,1},{3,2},{4,7},{5,4},{6,5},{7,6},{8,11},{9,8},{10,9... | collective-permute-start | bytes 1966088 | tf_op jit(solution)/shard_map/ppermute | solution.py:168
  145.9 18.9 %collective-permute-start.15 = (f32[2,2,160,256]{3,2,1,0:T(8,128)}, f32[2,2,160,256]{3,2,1,0:T(8,128)}, u32[]{:S(2)}, u32[]{:S(2)}) collective-permute-start(f32[2,2,160,256]{3,2,1,0:T(8,128)} %get-tuple-element.60.refs_6_), channel_id=1, source_target_pairs={{0,1},{1,2},{2,3},{3,0},{4,5},{5,6},{6,7},{7,4},{8,9},{9,10},{10,1... | collective-permute-start | bytes 1966088 | tf_op jit(solution)/shard_map/ppermute | solution.py:168
  158.1 15.9 %collective-permute-start.14 = (f32[4,160,256]{2,1,0:T(8,128)}, f32[4,160,256]{2,1,0:T(8,128)S(1)}, u32[]{:S(2)}, u32[]{:S(2)}) collective-permute-start(f32[4,160,256]{2,1,0:T(8,128)} %get-tuple-element.65), channel_id=1, source_target_pairs={{0,12},{1,13},{2,14},{3,15},{4,0},{5,1},{6,2},{7,3},{8,4},{9,5},{1... | collective-permute-start | bytes 1966088 | tf_op jit(solution)/shard_map/ppermute | solution.py:168
  159.4 19.1 %collective-permute-start.13 = (f32[4,160,256]{2,1,0:T(8,128)}, f32[4,160,256]{2,1,0:T(8,128)S(1)}, u32[]{:S(2)}, u32[]{:S(2)}) collective-permute-start(f32[4,160,256]{2,1,0:T(8,128)} %get-tuple-element.61.refs_4_), channel_id=1, source_target_pairs={{0,4},{1,5},{2,6},{3,7},{4,8},{5,9},{6,10},{7,11},{8,12},{9,13},{1... | collective-permute-start | bytes 1966088 | tf_op jit(solution)/shard_map/ppermute | solution.py:168
  163.6 34.7 %collective-permute-start.11 = (f32[2,2,192,256]{3,2,1,0:T(8,128)}, f32[2,2,192,256]{3,2,1,0:T(8,128)S(1)}, u32[]{:S(2)}, u32[]{:S(2)}) collective-permute-start(f32[2,2,192,256]{3,2,1,0:T(8,128)} %get-tuple-element.63.refs_8_), channel_id=1, source_target_pairs={{0,4},{1,5},{2,6},{3,7},{4,8},{5,9},{6,10},{7,11},{8,12},{9,13},{1... | collective-permute-start | bytes 2359304 | tf_op jit(solution)/shard_map/ppermute | solution.py:168
  167.4 17.4 %collective-permute-start.20 = (f32[2,160,256]{2,1,0:T(8,128)}, f32[2,160,256]{2,1,0:T(8,128)}, u32[]{:S(2)}, u32[]{:S(2)}) collective-permute-start(f32[2,160,256]{2,1,0:T(8,128)} %get-tuple-element.70), channel_id=1, source_target_pairs={{0,3},{1,0},{2,1},{3,2},{4,7},{5,4},{6,5},{7,6},{8,11},{9,8},{10,9... | collective-permute-start | bytes 983048 | tf_op jit(solution)/shard_map/ppermute | solution.py:168
  172.6 5.9 %copy-start = (f32[2,4,160,256]{3,2,1,0:T(8,128)}, f32[2,4,160,256]{3,2,1,0:T(8,128)S(1)}, u32[]{:S(2)}) copy-start(f32[2,4,160,256]{3,2,1,0:T(8,128)S(1)} %collective-permute-done.12.refs_1_.refs_5_.refs_9_.refs_13_.refs_6_.refs_7_) | copy-start | bytes 3932164
  172.6 12.2 %collective-permute-start.19 = (f32[2,160,256]{2,1,0:T(8,128)}, f32[2,160,256]{2,1,0:T(8,128)}, u32[]{:S(2)}, u32[]{:S(2)}) collective-permute-start(f32[2,160,256]{2,1,0:T(8,128)} %get-tuple-element.67.refs_16_), channel_id=1, source_target_pairs={{0,1},{1,2},{2,3},{3,0},{4,5},{5,6},{6,7},{7,4},{8,9},{9,10},{10,1... | collective-permute-start | bytes 983048 | tf_op jit(solution)/shard_map/ppermute | solution.py:168
  174.1 4.4 %copy-start.2 = (f32[4,160,256]{2,1,0:T(8,128)}, f32[4,160,256]{2,1,0:T(8,128)S(1)}, u32[]{:S(2)}) copy-start(f32[4,160,256]{2,1,0:T(8,128)S(1)} %collective-permute-done.14.refs_7_.refs_11_.refs_8_.refs_9_) | copy-start | bytes 1966084
  174.1 24.2 %collective-permute-start.10 = (f32[2,2,192,256]{3,2,1,0:T(8,128)}, f32[2,2,192,256]{3,2,1,0:T(8,128)}, u32[]{:S(2)}, u32[]{:S(2)}) collective-permute-start(f32[2,2,192,256]{3,2,1,0:T(8,128)} %get-tuple-element.62), channel_id=1, source_target_pairs={{0,12},{1,13},{2,14},{3,15},{4,0},{5,1},{6,2},{7,3},{8,4},{9,5},{1... | collective-permute-start | bytes 2359304 | tf_op jit(solution)/shard_map/ppermute | solution.py:168
  182.0 7.7 %collective-permute-start.18 = (f32[2,1,160,256]{3,2,1,0:T(8,128)}, f32[2,1,160,256]{3,2,1,0:T(8,128)S(1)}, u32[]{:S(2)}, u32[]{:S(2)}) collective-permute-start(f32[2,1,160,256]{3,2,1,0:T(8,128)} %get-tuple-element.69), channel_id=1, source_target_pairs={{0,3},{1,0},{2,1},{3,2},{4,7},{5,4},{6,5},{7,6},{8,11},{9,8},{10,9... | collective-permute-start | bytes 983048 | tf_op jit(solution)/shard_map/ppermute | solution.py:168
  184.8 8.5 %collective-permute-start.17 = (f32[2,1,160,256]{3,2,1,0:T(8,128)}, f32[2,1,160,256]{3,2,1,0:T(8,128)S(1)}, u32[]{:S(2)}, u32[]{:S(2)}) collective-permute-start(f32[2,1,160,256]{3,2,1,0:T(8,128)} %get-tuple-element.68.refs_10_), channel_id=1, source_target_pairs={{0,1},{1,2},{2,3},{3,0},{4,5},{5,6},{6,7},{7,4},{8,9},{9,10},{10,1... | collective-permute-start | bytes 983048 | tf_op jit(solution)/shard_map/ppermute | solution.py:168
  196.3 9.2 %collective-permute-start.24 = (f32[1,160,256]{2,1,0:T(8,128)}, f32[1,160,256]{2,1,0:T(8,128)S(1)}, u32[]{:S(2)}, u32[]{:S(2)}) collective-permute-start(f32[1,160,256]{2,1,0:T(8,128)} %get-tuple-element.75), channel_id=1, source_target_pairs={{0,3},{1,0},{2,1},{3,2},{4,7},{5,4},{6,5},{7,6},{8,11},{9,8},{10,9... | collective-permute-start | bytes 491528 | tf_op jit(solution)/shard_map/ppermute | solution.py:168
  196.4 7.1 %copy-start.15 = (f32[320,256]{1,0:T(8,128)S(1)}, f32[320,256]{1,0:T(8,128)}, u32[]{:S(2)}) copy-start(f32[320,256]{1,0:T(8,128)} %get-tuple-element.76) | copy-start | bytes 983044
  196.4 9.1 %collective-permute-start.23 = (f32[1,160,256]{2,1,0:T(8,128)}, f32[1,160,256]{2,1,0:T(8,128)S(1)}, u32[]{:S(2)}, u32[]{:S(2)}) collective-permute-start(f32[1,160,256]{2,1,0:T(8,128)} %get-tuple-element.72.refs_4_), channel_id=1, source_target_pairs={{0,1},{1,2},{2,3},{3,0},{4,5},{5,6},{6,7},{7,4},{8,9},{9,10},{10,1... | collective-permute-start | bytes 491528 | tf_op jit(solution)/shard_map/ppermute | solution.py:168
  201.5 9.1 %collective-permute-start.22 = (f32[2,192,256]{2,1,0:T(8,128)}, f32[2,192,256]{2,1,0:T(8,128)S(1)}, u32[]{:S(2)}, u32[]{:S(2)}) collective-permute-start(f32[2,192,256]{2,1,0:T(8,128)} %get-tuple-element.74), channel_id=1, source_target_pairs={{0,12},{1,13},{2,14},{3,15},{4,0},{5,1},{6,2},{7,3},{8,4},{9,5},{1... | collective-permute-start | bytes 1179656 | tf_op jit(solution)/shard_map/ppermute | solution.py:168
  201.5 9.2 %collective-permute-start.21 = (f32[2,192,256]{2,1,0:T(8,128)}, f32[2,192,256]{2,1,0:T(8,128)S(1)}, u32[]{:S(2)}, u32[]{:S(2)}) collective-permute-start(f32[2,192,256]{2,1,0:T(8,128)} %get-tuple-element.73.refs_12_), channel_id=1, source_target_pairs={{0,4},{1,5},{2,6},{3,7},{4,8},{5,9},{6,10},{7,11},{8,12},{9,13},{1... | collective-permute-start | bytes 1179656 | tf_op jit(solution)/shard_map/ppermute | solution.py:168
  203.5 7.1 %collective-permute-start.25 = (f32[320,256]{1,0:T(8,128)S(1)}, f32[320,256]{1,0:T(8,128)S(1)}, u32[]{:S(2)}, u32[]{:S(2)}) collective-permute-start(f32[320,256]{1,0:T(8,128)S(1)} %copy-done.15), channel_id=1, source_target_pairs={{0,16},{1,17},{2,18},{3,19},{4,20},{5,21},{6,22},{7,23},{8,24},{9,... | collective-permute-start | bytes 983048 | tf_op jit(solution)/shard_map/ppermute | solution.py:172
  214.8 8.0 %collective-permute-start.26 = (f32[384,256]{1,0:T(8,128)}, f32[384,256]{1,0:T(8,128)S(1)}, u32[]{:S(2)}, u32[]{:S(2)}) collective-permute-start(f32[384,256]{1,0:T(8,128)} %get-tuple-element.78), channel_id=1, source_target_pairs={{0,16},{1,17},{2,18},{3,19},{4,20},{5,21},{6,22},{7,23},{8,24},{9,... | collective-permute-start | bytes 1179656 | tf_op jit(solution)/shard_map/ppermute | solution.py:172
  (14 other events, 17.0 us)
Sparse Core Ops, SparseCore 0:
  12.6 51.6 all-reduce.1
Sparse Core Ops, SparseCore 1:
  30.9 128.3 reduce-scatter.1
